TPU v7x, 32 devices: a whole 2x2x4 slice. The times are simulated.
32 devices in a mesh: seq: 32 (over z, y, x, core).
Axes of the slice: x: 2, y: 2, z: 4, core: 2. Of those that a mesh axis runs over, the one named last changes fastest.
Arguments:
- queries: bfloat16 [32768, 1024], P('seq'), may hold values from -8 to 8, as said below
- keys: bfloat16 [32768, 1024], P('seq'), may hold values from -8 to 8
- values: bfloat16 [32768, 1024], P('seq'), may hold values from -6 to 6
- w_out: bfloat16 [1024, 2048], replicated, may hold values from -0.1875 to 0.1875
Outputs:
- output: bfloat16 [32768, 2048], P('seq')
Inputs may be any that keep to these rules, and one draw needn't show every extreme that they name: `queries`: query entries lie in the range.
All inputs are finite; a program needn't handle non-finite values.
Results may differ from a plain program's by a relative error of at most 0.0023.
The roundings to bfloat16 on the way count: a program that leaves them out, or rounds other values in their place, can miss the bound.
Values may be sent and summed in bfloat16 or wider, within the bound.
No kernel may reach another device: no remote copies, remote signals or barrier semaphores. Data moves between devices by JAX's collectives and lax.ppermute only.
A program may use at most 128 MiB of HBM per device.

v0:
```python
import functools

import jax
import jax.numpy as jnp
import numpy as np
from jax import lax
from jax.experimental import pallas as pl
from jax.experimental.pallas import tpu as pltpu
from jax.sharding import PartitionSpec as P

HEADS = 8
HEAD = 128
BLOCK = 256
TOK = 1024
UNITS = TOK // BLOCK
WIDTH = HEADS * HEAD
NEG = -1e30
FIRST = 2
SCALE = HEAD**-0.5
LOG2E = 1.4426950408889634
MIB = 1 << 20
SLICES = 4
VMEM_CLAIM = 60 * MIB
HBM = pl.BlockSpec(memory_space=pltpu.HBM)


def token_of(position):
    token = (position & 7) << 5
    for bit in range(5):
        token = token | (((position >> (3 + bit)) & 1) << (4 - bit))
    return token


def count_of(level):
    return max(BLOCK >> level, 8)


def pool_rows(level):
    rows = token_of(np.arange(count_of(level))) >> level
    columns = np.arange(BLOCK) >> level
    return (rows[:, None] == columns[None, :]) * 2.0**-level


def natural_pool(level, span):
    rows = np.arange(span >> level)
    return (rows[:, None] == (np.arange(span) >> level)[None, :]) * 2.0**-level


def padded(array, multiple):
    return np.pad(array, ((0, -len(array) % multiple), (0, 0)))


def as_bf16(array):
    return jnp.asarray(array.astype(np.float32)).astype(jnp.bfloat16)


def dot(a, b):
    return jnp.dot(a, b, preferred_element_type=jnp.float32)


def dot_t(a, b):
    return lax.dot_general(a, b, (((1,), (1,)), ((), ())), preferred_element_type=jnp.float32)


def twice(array):
    return jnp.concatenate([array, array], axis=0)


def merge(first, second):
    top = jnp.maximum(first[1], second[1])
    a = jnp.exp(first[1] - top)
    b = jnp.exp(second[1] - top)
    return (a * first[0] + b * second[0], top, a * first[2] + b * second[2])


def soft_rows(sources, targets, biases, rows, chunk):
    peaks, totals = [], []
    for start in range(0, rows, chunk):
        span = slice(start, start + chunk)
        scores = [
            source[span, :] if bias is None else source[span, :] + bias[span, :]
            for source, bias in zip(sources, biases)
        ]
        peak = functools.reduce(jnp.maximum, [jnp.max(item, axis=1, keepdims=True) for item in scores])
        total = 0.0
        for item, target in zip(scores, targets):
            probs = jnp.exp2((item - peak) * (SCALE * LOG2E))
            total = total + jnp.sum(probs, axis=1, keepdims=True)
            target[span, :] = probs.astype(jnp.bfloat16)
        peaks.append(peak * SCALE)
        totals.append(total)
    return jnp.concatenate(peaks, axis=0), jnp.concatenate(totals, axis=0)


def pool_kernel(levels, small_ref, large_ref, keys_ref, values_ref, *refs):
    count = levels - FIRST + 1
    targets, (small, large, buffers, *outs, sems, out_sems) = refs[:count], refs[count:]
    step = WIDTH // 4
    fixed = [pltpu.make_async_copy(small_ref, small, sems.at[8]), pltpu.make_async_copy(large_ref, large, sems.at[9])]
    copies = []
    for index, source in enumerate((keys_ref, values_ref)):
        for part in range(4):
            cols = slice(part * step, (part + 1) * step)
            copies.append(pltpu.make_async_copy(source.at[:, cols], buffers.at[index, :, cols], sems.at[index * 4 + part]))
    for copy in fixed + copies:
        copy.start()
    for copy in fixed:
        copy.wait()
    sends = []
    for index in range(2):
        for part in range(4):
            cols = slice(part * step, (part + 1) * step)
            copies[index * 4 + part].wait()
            tiles = [
                dot(small[...], buffers[index, i * 2 * BLOCK : (i + 1) * 2 * BLOCK, cols]) for i in range(UNITS // 2)
            ]
            offset = 0
            for level in range(FIRST, min(levels, 6) + 1):
                rows = 2 * BLOCK >> level
                both = jnp.concatenate([tile[offset : offset + rows] for tile in tiles], axis=0)
                outs[level - FIRST][index, :, cols] = both.astype(jnp.bfloat16)
                offset += rows
            if levels > 6:
                rest = dot(large[...], buffers[index, :, cols])
                for level in range(7, levels + 1):
                    start = (level - 7) * 8
                    outs[level - FIRST][index, :, cols] = rest[start : start + (TOK >> level)].astype(jnp.bfloat16)
        for place, (out, target) in enumerate(zip(outs, targets)):
            sends.append(pltpu.make_async_copy(out.at[index], target.at[index], out_sems.at[index, place]))
            sends[-1].start()
    for send in sends:
        send.wait()


def pool_call(keys, values, levels):
    small = as_bf16(padded(np.concatenate([natural_pool(level, 2 * BLOCK) for level in range(FIRST, min(levels, 6) + 1)]), 16))
    parts = [padded(natural_pool(level, TOK), 8) for level in range(7, levels + 1)] + [np.zeros((8, TOK))]
    large = as_bf16(padded(np.concatenate(parts), 16))
    crossing = range(FIRST, levels + 1)
    return pl.pallas_call(
        functools.partial(pool_kernel, levels),
        in_specs=[HBM] * 4,
        out_specs=[HBM] * len(crossing),
        out_shape=[jax.ShapeDtypeStruct((2, TOK >> level, WIDTH), jnp.bfloat16) for level in crossing],
        scratch_shapes=[
            pltpu.VMEM(small.shape, jnp.bfloat16),
            pltpu.VMEM(large.shape, jnp.bfloat16),
            pltpu.VMEM((2, TOK, WIDTH), jnp.bfloat16),
        ]
        + [pltpu.VMEM((2, TOK >> level, WIDTH), jnp.bfloat16) for level in crossing]
        + [
            pltpu.SemaphoreType.DMA((10,)),
            pltpu.SemaphoreType.DMA((2, len(crossing))),
        ],
        compiler_params=pltpu.CompilerParams(vmem_limit_bytes=VMEM_CLAIM),
        cost_estimate=pl.CostEstimate(flops=2 * 256 * 512 * 4096, bytes_accessed=6 * MIB, transcendentals=0),
        name="pool_keys_values",
    )(small, large, keys, values)


def far_offsets(levels):
    offsets, total = {}, 0
    for level in range(FIRST, levels + 1):
        offsets[level] = total
        total += UNITS * count_of(level)
    return offsets, total


def near_kernel(levels, first, pool_ref, q_ref, k_ref, v_ref, num_out, stat_out, far_out, *scratch):
    (pool, q, k, v, num, stat, far, ordered, coarse_q, coarse_k, coarse_v, bias, scores_a, scores_b, scores_c) = scratch[:15]
    probs_a, probs_b, probs_c, sems = scratch[15:]
    heads = HEADS // SLICES
    width = heads * HEAD
    cols = slice(first * HEAD, first * HEAD + width)
    copies = [pltpu.make_async_copy(pool_ref, pool, sems.at[0])]
    copies += [
        pltpu.make_async_copy(source.at[:, cols], target, sems.at[1 + index])
        for index, (source, target) in enumerate(((q_ref, q), (k_ref, k), (v_ref, v)))
    ]
    for copy in copies:
        copy.start()
    position = lax.broadcasted_iota(jnp.int32, (BLOCK, BLOCK), 0)
    column = lax.broadcasted_iota(jnp.int32, (BLOCK, BLOCK), 1)
    bias[...] = jnp.where(column <= token_of(position), 0.0, NEG)
    stat[...] = jnp.zeros_like(stat)
    for copy in copies:
        copy.wait()

    far_parts = []
    for unit in range(UNITS):
        pooled = dot(pool[...], q[unit * BLOCK : (unit + 1) * BLOCK, :])
        ordered[unit] = pooled[:BLOCK].astype(jnp.bfloat16)
        if unit >= 2:
            coarse_q[unit - 2] = pooled[BLOCK : BLOCK + 128].astype(jnp.bfloat16)
        far_parts.append(pooled[BLOCK + 128 :])
    offsets, _ = far_offsets(levels)
    start = 0
    for level in range(FIRST, levels + 1):
        count = count_of(level)
        parts = [item[start : start + count].reshape(count // 8, 1, 8, width) for item in far_parts]
        both = jnp.concatenate(parts, axis=1).reshape(UNITS * count, width)
        far[offsets[level] : offsets[level] + UNITS * count, :] = both.astype(jnp.bfloat16)
        start += count
    for unit in range(2):
        rows = slice(unit * BLOCK, (unit + 1) * BLOCK)
        half = slice(unit * 128, (unit + 1) * 128)
        coarse_k[half, :] = dot(pool[BLOCK : BLOCK + 128, :], k[rows, :]).astype(jnp.bfloat16)
        coarse_v[half, :] = dot(pool[BLOCK : BLOCK + 128, :], v[rows, :]).astype(jnp.bfloat16)
    sends = [pltpu.make_async_copy(far, far_out, sems.at[4])]
    sends[0].start()

    lane = lax.broadcasted_iota(jnp.int32, (BLOCK, HEAD), 1)

    def one_head(head, carry):
        own = pl.ds(pl.multiple_of(head * HEAD, HEAD), HEAD)

        def dots(tile):
            rows_a = slice(2 * tile * BLOCK, (2 * tile + 1) * BLOCK)
            rows_b = slice((2 * tile + 1) * BLOCK, (2 * tile + 2) * BLOCK)
            both = ordered[2 * tile : 2 * tile + 2, :, own].reshape(2 * BLOCK, HEAD)
            scores_a[tile] = dot_t(both, k[rows_a, own])
            scores_b[tile] = dot_t(ordered[2 * tile + 1, :, own], k[rows_b, own])

        def soft(tile):
            first_half = soft_rows([scores_a.at[tile, :BLOCK]], [probs_a.at[tile, :BLOCK]], [bias], BLOCK, 64)
            second_half = soft_rows(
                [scores_a.at[tile, BLOCK:], scores_b.at[tile]],
                [probs_a.at[tile, BLOCK:], probs_b.at[tile]],
                [None, bias],
                BLOCK,
                64,
            )
            return first_half, second_half

        def weigh(tile, stats):
            rows_a = slice(2 * tile * BLOCK, (2 * tile + 1) * BLOCK)
            rows_b = slice((2 * tile + 1) * BLOCK, (2 * tile + 2) * BLOCK)
            both = dot(probs_a[tile], v[rows_a, own])
            more = dot(probs_b[tile], v[rows_b, own])
            return (both[:BLOCK],) + stats[0], (both[BLOCK:] + more,) + stats[1]

        def finish(unit, state):
            num[:, unit, :, own] = state[0].reshape(BLOCK // 8, 8, HEAD)
            old = stat[:, unit].reshape(BLOCK, HEAD)
            old = jnp.where(lane == first + head, state[1], old)
            old = jnp.where(lane == first + head + HEADS, state[2], old)
            stat[:, unit] = old.reshape(BLOCK // 8, 8, HEAD)

        dots(0)
        scores_c[...] = dot_t(coarse_q[:, :, own].reshape(BLOCK, HEAD), coarse_k[:, own])
        dots(1)
        stats0 = soft(0)
        states = weigh(0, stats0)
        peak1, total1 = soft_rows([scores_c], [probs_c], [None], BLOCK, 64)
        stats1 = soft(1)
        num1 = 2.0 * dot(probs_c[...], coarse_v[:, own])
        total1 = 2.0 * total1
        states = states + weigh(1, stats1)
        for unit in range(UNITS):
            state = states[unit]
            if unit >= 2:
                half = slice((unit - 2) * 128, (unit - 1) * 128)
                state = merge(state, (twice(num1[half]), twice(peak1[half]), twice(total1[half])))
            finish(unit, state)
        return carry

    lax.fori_loop(0, heads, one_head, 0)
    sends += [pltpu.make_async_copy(num, num_out, sems.at[5]), pltpu.make_async_copy(stat, stat_out, sems.at[6])]
    for send in sends[1:]:
        send.start()
    for send in sends:
        send.wait()


def near_call(queries, keys, values, levels, index):
    pool = as_bf16(padded(np.concatenate([pool_rows(level) for level in range(levels + 1)]), 16))
    heads = HEADS // SLICES
    width = heads * HEAD
    _, far_rows = far_offsets(levels)
    bf16, f32 = jnp.bfloat16, jnp.float32
    return pl.pallas_call(
        functools.partial(near_kernel, levels, index * heads),
        in_specs=[HBM] * 4,
        out_specs=[HBM] * 3,
        out_shape=[
            jax.ShapeDtypeStruct((BLOCK // 8, UNITS, 8, width), f32),
            jax.ShapeDtypeStruct((BLOCK // 8, UNITS, 8, HEAD), f32),
            jax.ShapeDtypeStruct((far_rows, width), bf16),
        ],
        scratch_shapes=[
            pltpu.VMEM(pool.shape, bf16),
            pltpu.VMEM((TOK, width), bf16),
            pltpu.VMEM((TOK, width), bf16),
            pltpu.VMEM((TOK, width), bf16),
            pltpu.VMEM((BLOCK // 8, UNITS, 8, width), f32),
            pltpu.VMEM((BLOCK // 8, UNITS, 8, HEAD), f32),
            pltpu.VMEM((far_rows, width), bf16),
            pltpu.VMEM((UNITS, BLOCK, width), bf16),
            pltpu.VMEM((2, 128, width), bf16),
            pltpu.VMEM((BLOCK, width), bf16),
            pltpu.VMEM((BLOCK, width), bf16),
            pltpu.VMEM((BLOCK, BLOCK), f32),
            pltpu.VMEM((2, 2 * BLOCK, BLOCK), f32),
            pltpu.VMEM((2, BLOCK, BLOCK), f32),
            pltpu.VMEM((BLOCK, BLOCK), f32),
            pltpu.VMEM((2, 2 * BLOCK, BLOCK), bf16),
            pltpu.VMEM((2, BLOCK, BLOCK), bf16),
            pltpu.VMEM((BLOCK, BLOCK), bf16),
            pltpu.SemaphoreType.DMA((7,)),
        ],
        compiler_params=pltpu.CompilerParams(vmem_limit_bytes=VMEM_CLAIM),
        cost_estimate=pl.CostEstimate(flops=2_000_000_000, bytes_accessed=4 * MIB, transcendentals=1_000_000),
        name="near_levels",
    )(pool, queries, keys, values)


def far_kernel(levels, plan, flags_ref, *refs):
    crossing = range(FIRST, levels + 1)
    bundles = 1 + max(bundle for _, bundle, _ in plan)
    kv_refs = refs[:bundles]
    refs = refs[bundles:]
    far_refs, num_refs, stat_refs = refs[:SLICES], refs[SLICES : 2 * SLICES], refs[2 * SLICES : 3 * SLICES]
    turn_ref, w_ref, out_ref = refs[3 * SLICES : 3 * SLICES + 3]
    kv, queries, num, stat, turn, weights, scores, probs = refs[3 * SLICES + 3 : 3 * SLICES + 11]
    wide, peaks, totals, mixed, natural, stage, kv_sems, near_sems, out_sems = refs[3 * SLICES + 11 :]
    heads = HEADS // SLICES
    width = heads * HEAD
    model = w_ref.shape[1]
    step = 512
    offsets, far_rows = far_offsets(levels)

    def kv_copies(index):
        cols = pl.ds(pl.multiple_of(index * width, width), width)
        made = []
        for number, (level, bundle, spans) in enumerate(plan):
            source_start, target_start, rows = spans
            made.append(
                pltpu.make_async_copy(
                    kv_refs[bundle].at[:, source_start : source_start + rows, cols],
                    kv.at[level - FIRST, :, target_start : target_start + rows, cols],
                    kv_sems.at[index, number],
                )
            )
        return made

    near_copies = []
    for index in range(SLICES):
        cols = slice(index * width, (index + 1) * width)
        near_copies.append(pltpu.make_async_copy(far_refs[index], queries.at[:, cols], near_sems.at[index]))
    for index in range(SLICES):
        cols = slice(index * width, (index + 1) * width)
        near_copies.append(pltpu.make_async_copy(num_refs[index], num.at[:, :, :, cols], near_sems.at[SLICES + index]))
    for index in range(SLICES):
        near_copies.append(pltpu.make_async_copy(stat_refs[index], stat.at[index], near_sems.at[2 * SLICES + index]))
    near_copies.append(pltpu.make_async_copy(turn_ref, turn, near_sems.at[3 * SLICES]))
    near_copies.append(pltpu.make_async_copy(w_ref, weights, near_sems.at[3 * SLICES + 1]))
    for copy in near_copies[:SLICES]:
        copy.start()
    for index in range(SLICES):
        for copy in kv_copies(index):
            copy.start()
    for copy in near_copies[SLICES:]:
        copy.start()
    for copy in near_copies[:SLICES]:
        copy.wait()

    rows2 = UNITS * count_of(FIRST)
    lane = lax.broadcasted_iota(jnp.int32, (rows2, HEAD), 1)
    peaks[...] = jnp.full_like(peaks, NEG)
    totals[...] = jnp.zeros_like(totals)

    def group(index, carry):
        for copy in kv_copies(index):
            copy.wait()
        stats = []
        for inner in range(heads):
            own = pl.ds(pl.multiple_of(index * width + inner * HEAD, HEAD), HEAD)
            for level in crossing:
                span = slice(offsets[level], offsets[level] + UNITS * count_of(level))
                scores[inner, span, :] = dot_t(queries[span, own], kv[level - FIRST, 0, :, own])
        for inner in range(heads):
            stats.append(soft_rows([scores.at[inner]], [probs.at[inner]], [None], far_rows, 64))
        for inner in range(heads):
            own = pl.ds(pl.multiple_of(index * width + inner * HEAD, HEAD), HEAD)
            state = None
            for level in reversed(crossing):
                span = slice(offsets[level], offsets[level] + UNITS * count_of(level))
                live = flags_ref[level - FIRST] == 1
                factor = jnp.where(live, 2.0**level, 0.0)
                term = (
                    factor * dot(probs[inner, span, :], kv[level - FIRST, 1, :, own]),
                    jnp.where(live, stats[inner][0][span], NEG),
                    factor * stats[inner][1][span],
                )
                if state is None:
                    state = term
                else:
                    if count_of(level) > count_of(level + 1):
                        state = tuple(twice(item) for item in state)
                    state = merge(state, term)
            wide[:, :, :, own] = state[0].reshape(rows2 // (8 * UNITS), UNITS, 8, HEAD)
            head = index * heads + inner
            peaks[...] = jnp.where(lane == head, state[1], peaks[...])
            totals[...] = jnp.where(lane == head, state[2], totals[...])
        return carry

    lax.fori_loop(0, SLICES, group, 0)

    for copy in near_copies[SLICES:]:
        copy.wait()

    def widened(array, unit):
        array = array.reshape(rows2 // (8 * UNITS), UNITS, 8, HEAD)[:, unit]
        return twice(twice(array.reshape(rows2 // UNITS, HEAD)))

    def mix(unit):
        near = sum(stat[index, :, unit] for index in range(SLICES)).reshape(BLOCK, HEAD)
        near_total = pltpu.roll(near, HEAD - HEADS, 1)
        far_peak = widened(peaks[...], unit)
        far_total = widened(totals[...], unit)
        top = jnp.maximum(near, far_peak)
        a = jnp.exp(near - top)
        b = jnp.exp(far_peak - top)
        inverse = 1.0 / (a * near_total + b * far_total)
        a = a * inverse
        b = b * inverse
        for head in range(HEADS):
            own = slice(head * HEAD, (head + 1) * HEAD)
            far_num = twice(twice(wide[:, unit, :, own].reshape(rows2 // UNITS, HEAD)))
            near_num = num[:, unit, :, own].reshape(BLOCK, HEAD)
            both = a[:, head : head + 1] * near_num + b[:, head : head + 1] * far_num
            mixed[unit, :, own] = both.astype(jnp.bfloat16)
        natural[unit * BLOCK : (unit + 1) * BLOCK, :] = dot(turn[...], mixed[unit]).astype(jnp.bfloat16)

    sends = []

    def project(half):
        rows = slice(half * 2 * BLOCK, (half + 1) * 2 * BLOCK)
        for index in range(model // step):
            cols = slice(index * step, (index + 1) * step)
            stage[rows, cols] = dot(natural[rows, :], weights[:, cols]).astype(jnp.bfloat16)
            sends.append(
                pltpu.make_async_copy(stage.at[rows, cols], out_ref.at[rows, cols], out_sems.at[half * (model // step) + index])
            )
            sends[-1].start()

    mix(0)
    mix(1)
    project(0)
    mix(2)
    mix(3)
    project(1)
    for send in sends:
        send.wait()


def far_call(flags, bundles, plan, near, w_out, levels):
    turn = np.zeros((BLOCK, BLOCK))
    turn[token_of(np.arange(BLOCK)), np.arange(BLOCK)] = 1.0
    nums, stats, fars = [[item[place] for item in near] for place in range(3)]
    model = w_out.shape[1]
    _, far_rows = far_offsets(levels)
    count = levels - FIRST + 1
    heads = HEADS // SLICES
    rows2 = UNITS * count_of(FIRST)
    bf16, f32 = jnp.bfloat16, jnp.float32
    return pl.pallas_call(
        functools.partial(far_kernel, levels, plan),
        in_specs=[pl.BlockSpec(memory_space=pltpu.SMEM)]
        + [pl.BlockSpec(memory_space=pl.ANY)] * len(bundles)
        + [HBM] * (3 * SLICES + 2),
        out_specs=HBM,
        out_shape=jax.ShapeDtypeStruct((TOK, model), bf16),
        scratch_shapes=[
            pltpu.VMEM((count, 2, BLOCK, WIDTH), bf16),
            pltpu.VMEM((far_rows, WIDTH), bf16),
            pltpu.VMEM((BLOCK // 8, UNITS, 8, WIDTH), f32),
            pltpu.VMEM((SLICES, BLOCK // 8, UNITS, 8, HEAD), f32),
            pltpu.VMEM((BLOCK, BLOCK), bf16),
            pltpu.VMEM((WIDTH, model), bf16),
            pltpu.VMEM((heads, far_rows, BLOCK), f32),
            pltpu.VMEM((heads, far_rows, BLOCK), bf16),
            pltpu.VMEM((rows2 // (8 * UNITS), UNITS, 8, WIDTH), f32),
            pltpu.VMEM((rows2, HEAD), f32),
            pltpu.VMEM((rows2, HEAD), f32),
            pltpu.VMEM((UNITS, BLOCK, WIDTH), bf16),
            pltpu.VMEM((TOK, WIDTH), bf16),
            pltpu.VMEM((TOK, model), bf16),
            pltpu.SemaphoreType.DMA((SLICES, len(plan))),
            pltpu.SemaphoreType.DMA((3 * SLICES + 2,)),
            pltpu.SemaphoreType.DMA((2 * model // 512,)),
        ],
        compiler_params=pltpu.CompilerParams(vmem_limit_bytes=VMEM_CLAIM),
        cost_estimate=pl.CostEstimate(flops=6_500_000_000, bytes_accessed=18 * MIB, transcendentals=3_000_000),
        name="far_levels_projection",
    )(flags, *bundles, *fars, *nums, *stats, as_bf16(turn), w_out)


def moved(array, distance, upper_of=0):
    size = lax.axis_size("seq")
    pairs = [(i ^ distance, i) for i in range(size) if not upper_of or i & upper_of]
    return lax.ppermute(array, "seq", pairs)


def gathered(blocks, distance):
    sent = jnp.concatenate(blocks, axis=1) if len(blocks) > 1 else blocks[0]
    got = moved(sent, distance)
    joined, start = [], 0
    for block in blocks:
        rows = block.shape[1]
        joined.append(jnp.concatenate([block, got[:, start : start + rows]], axis=1))
        start += rows
    return joined


def after(arrays, others):
    return lax.optimization_barrier((arrays, others))[0]


def on_device(queries, keys, values, w_out):
    size = lax.axis_size("seq")
    levels = (TOK * size // (2 * BLOCK)).bit_length() - 1
    position = lax.axis_index("seq")
    flags = jnp.stack([(position >> (level - FIRST)) & 1 for level in range(FIRST, levels + 1)]).astype(jnp.int32)
    pooled = pool_call(keys, values, levels)
    blocks = {}
    for level in range(levels, FIRST - 1, -1):
        distance = 1 << (level - FIRST)
        blocks[level] = moved(pooled[level - FIRST], distance, distance)
    high = list(range(5, levels + 1))
    near = []
    for index in range(SLICES):
        source = after(queries, near[-1] if near else pooled)
        near.append(near_call(source, keys, values, levels, index))
    rounds = [1 << bit for bit in range(1, levels - FIRST)]
    for number, distance in enumerate(rounds):
        members = [level for level in high if (1 << (level - FIRST)) > distance]
        if members:
            items = after([blocks[level] for level in members], near[min(number, SLICES - 1)])
            for level, item in zip(members, gathered(items, distance)):
                blocks[level] = item
        if distance == 2:
            blocks[4] = gathered([after(blocks[4], near[min(1, SLICES - 1)])], 2)[0]
    low = jnp.concatenate([after(blocks[3], near[2]), blocks[4]], axis=1)
    low_got = moved(low, 1)
    top = jnp.concatenate([after(blocks[level], near[SLICES - 1]) for level in high], axis=1)
    top_got = moved(top, 1)
    plan = [(2, 0, (0, 0, BLOCK))]
    for place, level in enumerate((3, 4)):
        plan += [(level, 1, (place * 128, 0, 128)), (level, 2, (place * 128, 128, 128))]
    for place, level in enumerate(high):
        plan += [(level, 3, (place * 128, 0, 128)), (level, 4, (place * 128, 128, 128))]
    return far_call(flags, [blocks[2], low, low_got, top, top_got], plan, near, w_out, levels)


def solution(mesh):
    return jax.shard_map(
        on_device,
        mesh=mesh,
        in_specs=(P("seq", None), P("seq", None), P("seq", None), P()),
        out_specs=P("seq", None),
        check_vma=False,
    )
```

profile of v0, /device:TPU:0, one launch (start us, length us, event | category | flops | bytes accessed | tf_op | source)
XLA Modules:
  0.0 76.1 jit_solution(10315358641849862681)
XLA Ops:
  0.0 0.6 broadcast.1.large_ref
  0.6 4.7 %pool_keys_values.1 = (bf16[2,256,1024]{2,1,0:T(8,128)(2,1)}, bf16[2,128,1024]{2,1,0:T(8,128)(2,1)}, bf16[2,64,1024]{2,1,0:T(8,128)(2,1)}, bf16[2,32,1024]{2,1,0:T(8,128)(2,1)}, bf16[2,16,1024]{2,1,0:T(8,128)(2,1)}) custom-call(bf16[256,512]{1,0:T(8,128)(2,1)} %constant.26.small_ref, bf16[16,1024]{1,0:T(8,128)(2,1)} %broadcast.1.large_ref, ...), custom_call_target="tpu_custom_call" | custom-call | flops 1073741824 | bytes 6291456 | tf_op jit(solution)/shard_map/pool_keys_values/pallas_call | solution.py:140
  5.3 6.0 %collective-permute-start.6 = (bf16[2,16,1024]{2,1,0:T(8,128)(2,1)}, bf16[2,16,1024]{2,1,0:T(8,128)(2,1)S(1)}, u32[]{:S(2)}, u32[]{:S(2)}) collective-permute-start(bf16[2,16,1024]{2,1,0:T(8,128)(2,1)} %get-tuple-element.39), channel_id=1, source_target_pairs={{0,16},{1,17},{2,18},{3,19},{4,20},{5,21},{6,22},{7,23},{8,24},{9,... | collective-permute-start | bytes 196616 | tf_op jit(solution)/shard_map/ppermute | solution.py:502
  11.3 3.5 %collective-permute-start.5 = (bf16[2,32,1024]{2,1,0:T(8,128)(2,1)}, bf16[2,32,1024]{2,1,0:T(8,128)(2,1)S(1)}, u32[]{:S(2)}, u32[]{:S(2)}) collective-permute-start(bf16[2,32,1024]{2,1,0:T(8,128)(2,1)} %get-tuple-element.38), channel_id=1, source_target_pairs={{0,8},{1,9},{2,10},{3,11},{4,12},{5,13},{6,14},{7,15},{16,24},{17,... | collective-permute-start | bytes 393224 | tf_op jit(solution)/shard_map/ppermute | solution.py:502
  14.8 3.4 %collective-permute-start.2 = (bf16[2,64,1024]{2,1,0:T(8,128)(2,1)}, bf16[2,64,1024]{2,1,0:T(8,128)(2,1)S(1)}, u32[]{:S(2)}, u32[]{:S(2)}) collective-permute-start(bf16[2,64,1024]{2,1,0:T(8,128)(2,1)} %get-tuple-element.37), channel_id=1, source_target_pairs={{0,4},{1,5},{2,6},{3,7},{8,12},{9,13},{10,14},{11,15},{16,20},{17,... | collective-permute-start | bytes 786440 | tf_op jit(solution)/shard_map/ppermute | solution.py:502
  18.2 3.4 %collective-permute-start.1 = (bf16[2,128,1024]{2,1,0:T(8,128)(2,1)}, bf16[2,128,1024]{2,1,0:T(8,128)(2,1)S(1)}, u32[]{:S(2)}, u32[]{:S(2)}) collective-permute-start(bf16[2,128,1024]{2,1,0:T(8,128)(2,1)} %get-tuple-element.36), channel_id=1, source_target_pairs={{0,2},{1,3},{4,6},{5,7},{8,10},{9,11},{12,14},{13,15},{16,18},{17,... | collective-permute-start | bytes 1572872 | tf_op jit(solution)/shard_map/ppermute | solution.py:502
  21.6 1.4 %collective-permute-start = (bf16[2,256,1024]{2,1,0:T(8,128)(2,1)}, bf16[2,256,1024]{2,1,0:T(8,128)(2,1)S(1)}, u32[]{:S(2)}, u32[]{:S(2)}) collective-permute-start(bf16[2,256,1024]{2,1,0:T(8,128)(2,1)} %get-tuple-element.35), channel_id=1, source_target_pairs={{0,1},{2,3},{4,5},{6,7},{8,9},{10,11},{12,13},{14,15},{16,17},{18,... | collective-permute-start | bytes 3145736 | tf_op jit(solution)/shard_map/ppermute | solution.py:502
  23.0 6.0 %near_levels.4 = (f32[32,4,8,256]{3,2,1,0:T(8,128)}, f32[32,4,8,128]{3,2,1,0:T(8,128)}, bf16[512,256]{1,0:T(8,128)(2,1)}) custom-call(bf16[512,256]{1,0:T(8,128)(2,1)} %constant.28.pool_ref, bf16[1024,1024]{1,0:T(8,128)(2,1)} %q_ref.3, bf16[1024,1024]{1,0:T(8,128)(2,1)} %k_ref.7, bf16[1024,1024]{1,0:T(8,128)(2,1)} %v_ref.7), custom_call_target="tpu_custom_call" | custom-call | flops 2000000000 | bytes 4194304 | tf_op jit(solution)/shard_map/near_levels/pallas_call | solution.py:281
  29.1 0.0 collective-permute-done.6
  29.1 0.0 collective-permute-done.5
  29.1 0.1 collective-permute-start.7
  29.2 6.0 %near_levels.5 = (f32[32,4,8,256]{3,2,1,0:T(8,128)}, f32[32,4,8,128]{3,2,1,0:T(8,128)}, bf16[512,256]{1,0:T(8,128)(2,1)}) custom-call(bf16[512,256]{1,0:T(8,128)(2,1)} %constant.28.pool_ref, bf16[1024,1024]{1,0:T(8,128)(2,1)} %q_ref.3, bf16[1024,1024]{1,0:T(8,128)(2,1)} %k_ref.7, bf16[1024,1024]{1,0:T(8,128)(2,1)} %v_ref.7), custom_call_target="tpu_custom_call" | custom-call | flops 2000000000 | bytes 4194304 | tf_op jit(solution)/shard_map/near_levels/pallas_call | solution.py:281
  35.2 6.0 %near_levels.6 = (f32[32,4,8,256]{3,2,1,0:T(8,128)}, f32[32,4,8,128]{3,2,1,0:T(8,128)}, bf16[512,256]{1,0:T(8,128)(2,1)}) custom-call(bf16[512,256]{1,0:T(8,128)(2,1)} %constant.28.pool_ref, bf16[1024,1024]{1,0:T(8,128)(2,1)} %q_ref.3, bf16[1024,1024]{1,0:T(8,128)(2,1)} %k_ref.7, bf16[1024,1024]{1,0:T(8,128)(2,1)} %v_ref.7), custom_call_target="tpu_custom_call" | custom-call | flops 2000000000 | bytes 4194304 | tf_op jit(solution)/shard_map/near_levels/pallas_call | solution.py:281
  41.3 0.0 collective-permute-done.7
  41.4 0.1 collective-permute-start.8
  41.5 6.0 %near_levels.7 = (f32[32,4,8,256]{3,2,1,0:T(8,128)}, f32[32,4,8,128]{3,2,1,0:T(8,128)}, bf16[512,256]{1,0:T(8,128)(2,1)}) custom-call(bf16[512,256]{1,0:T(8,128)(2,1)} %constant.28.pool_ref, bf16[1024,1024]{1,0:T(8,128)(2,1)} %q_ref.3, bf16[1024,1024]{1,0:T(8,128)(2,1)} %k_ref.7, bf16[1024,1024]{1,0:T(8,128)(2,1)} %v_ref.7), custom_call_target="tpu_custom_call" | custom-call | flops 2000000000 | bytes 4194304 | tf_op jit(solution)/shard_map/near_levels/pallas_call | solution.py:281
  47.5 0.0 collective-permute-done.2
  47.5 2.1 %collective-permute-start.3 = (bf16[2,64,1024]{2,1,0:T(8,128)(2,1)S(1)}, bf16[2,64,1024]{2,1,0:T(8,128)(2,1)S(1)}, u32[]{:S(2)}, u32[]{:S(2)}) collective-permute-start(bf16[2,64,1024]{2,1,0:T(8,128)(2,1)S(1)} %collective-permute-done.2), channel_id=1, source_target_pairs={{2,0},{3,1},{0,2},{1,3},{6,4},{7,5},{4,6},{5,7},{10,8},{11,9},{8,1... | collective-permute-start | bytes 786440 | tf_op jit(solution)/shard_map/ppermute | solution.py:502
  49.5 0.0 collective-permute-done.1
  49.6 1.5 %collective-permute-done.8 = bf16[2,96,1024]{2,1,0:T(8,128)(2,1)S(1)} collective-permute-done((bf16[2,96,1024]{2,1,0:T(8,128)(2,1)S(1)}, bf16[2,96,1024]{2,1,0:T(8,128)(2,1)S(1)}, u32[]{:S(2)}, u32[]{:S(2)}) %collective-permute-start.8) | collective-permute-done | bytes 393248 | tf_op jit(solution)/shard_map/ppermute | solution.py:502
  51.2 0.1 collective-permute-start.9
  51.2 3.2 %collective-permute-done.3 = bf16[2,64,1024]{2,1,0:T(8,128)(2,1)S(1)} collective-permute-done((bf16[2,64,1024]{2,1,0:T(8,128)(2,1)S(1)}, bf16[2,64,1024]{2,1,0:T(8,128)(2,1)S(1)}, u32[]{:S(2)}, u32[]{:S(2)}) %collective-permute-start.3) | collective-permute-done | bytes 262176 | tf_op jit(solution)/shard_map/ppermute | solution.py:502
  54.4 0.0 copy-start.1
  54.4 0.1 collective-permute-start.4
  54.6 3.0 %collective-permute-done.9 = bf16[2,64,1024]{2,1,0:T(8,128)(2,1)S(1)} collective-permute-done((bf16[2,64,1024]{2,1,0:T(8,128)(2,1)S(1)}, bf16[2,64,1024]{2,1,0:T(8,128)(2,1)S(1)}, u32[]{:S(2)}, u32[]{:S(2)}) %collective-permute-start.9) | collective-permute-done | bytes 262176 | tf_op jit(solution)/shard_map/ppermute | solution.py:502
  57.7 0.0 copy-done.1
  57.7 0.0 copy-start
  57.7 0.1 collective-permute-start.10
  57.8 0.8 %stack.23.flags_ref = s32[5]{0:T(128)} concatenate(s32[1]{0:T(128)} %bitcast, s32[1]{0:T(128)} %bitcast.1, s32[1]{0:T(128)} %bitcast.2, s32[1]{0:T(128)} %bitcast.3, s32[1]{0:T(128)} %bitcast.4), dimensions={0} | concatenate | bytes 40 | tf_op jit(solution)/shard_map/stack | solution.py:524
  58.6 0.0 collective-permute-done.refs_0_
  58.6 0.0 copy-start.2
  58.6 0.0 collective-permute-done.4.refs_2_
  58.6 2.0 %collective-permute-done.10.refs_4_ = bf16[2,256,1024]{2,1,0:T(8,128)(2,1)} collective-permute-done((bf16[2,256,1024]{2,1,0:T(8,128)(2,1)S(1)}, bf16[2,256,1024]{2,1,0:T(8,128)(2,1)}, u32[]{:S(2)}, u32[]{:S(2)}) %collective-permute-start.10) | collective-permute-done | bytes 1048608 | tf_op jit(solution)/shard_map/ppermute | solution.py:502
  60.6 0.0 copy-done
  60.6 0.0 copy-done.2
  60.6 15.4 %far_levels_projection.1 = bf16[1024,2048]{1,0:T(8,128)(2,1)} custom-call(s32[5]{0:T(128)} %stack.23.flags_ref, bf16[2,256,1024]{2,1,0:T(8,128)(2,1)} %copy-done.2, bf16[2,256,1024]{2,1,0:T(8,128)(2,1)} %copy-done.1, bf16[2,256,1024]{2,1,0:T(8,128)(2,1)} %collective-permute-done.4.refs_2_, bf16[2,256,1024]{2,1,0:T(8,128)(2,1)} %copy-done, ...), custom_call_target="tpu_custom_call" | custom-call | flops 6499999744 | bytes 18874368 | tf_op jit(solution)/shard_map/far_levels_projection/pallas_call | solution.py:467
  (16 shorter events, 0.4 us)
Async XLA Ops:
  5.3 23.8 %collective-permute-start.6 = (bf16[2,16,1024]{2,1,0:T(8,128)(2,1)}, bf16[2,16,1024]{2,1,0:T(8,128)(2,1)S(1)}, u32[]{:S(2)}, u32[]{:S(2)}) collective-permute-start(bf16[2,16,1024]{2,1,0:T(8,128)(2,1)} %get-tuple-element.39), channel_id=1, source_target_pairs={{0,16},{1,17},{2,18},{3,19},{4,20},{5,21},{6,22},{7,23},{8,24},{9,... | collective-permute-start | bytes 196616 | tf_op jit(solution)/shard_map/ppermute | solution.py:502
  11.3 17.8 %collective-permute-start.5 = (bf16[2,32,1024]{2,1,0:T(8,128)(2,1)}, bf16[2,32,1024]{2,1,0:T(8,128)(2,1)S(1)}, u32[]{:S(2)}, u32[]{:S(2)}) collective-permute-start(bf16[2,32,1024]{2,1,0:T(8,128)(2,1)} %get-tuple-element.38), channel_id=1, source_target_pairs={{0,8},{1,9},{2,10},{3,11},{4,12},{5,13},{6,14},{7,15},{16,24},{17,... | collective-permute-start | bytes 393224 | tf_op jit(solution)/shard_map/ppermute | solution.py:502
  14.8 32.7 %collective-permute-start.2 = (bf16[2,64,1024]{2,1,0:T(8,128)(2,1)}, bf16[2,64,1024]{2,1,0:T(8,128)(2,1)S(1)}, u32[]{:S(2)}, u32[]{:S(2)}) collective-permute-start(bf16[2,64,1024]{2,1,0:T(8,128)(2,1)} %get-tuple-element.37), channel_id=1, source_target_pairs={{0,4},{1,5},{2,6},{3,7},{8,12},{9,13},{10,14},{11,15},{16,20},{17,... | collective-permute-start | bytes 786440 | tf_op jit(solution)/shard_map/ppermute | solution.py:502
  18.2 31.3 %collective-permute-start.1 = (bf16[2,128,1024]{2,1,0:T(8,128)(2,1)}, bf16[2,128,1024]{2,1,0:T(8,128)(2,1)S(1)}, u32[]{:S(2)}, u32[]{:S(2)}) collective-permute-start(bf16[2,128,1024]{2,1,0:T(8,128)(2,1)} %get-tuple-element.36), channel_id=1, source_target_pairs={{0,2},{1,3},{4,6},{5,7},{8,10},{9,11},{12,14},{13,15},{16,18},{17,... | collective-permute-start | bytes 1572872 | tf_op jit(solution)/shard_map/ppermute | solution.py:502
  21.6 36.9 %collective-permute-start = (bf16[2,256,1024]{2,1,0:T(8,128)(2,1)}, bf16[2,256,1024]{2,1,0:T(8,128)(2,1)S(1)}, u32[]{:S(2)}, u32[]{:S(2)}) collective-permute-start(bf16[2,256,1024]{2,1,0:T(8,128)(2,1)} %get-tuple-element.35), channel_id=1, source_target_pairs={{0,1},{2,3},{4,5},{6,7},{8,9},{10,11},{12,13},{14,15},{16,17},{18,... | collective-permute-start | bytes 3145736 | tf_op jit(solution)/shard_map/ppermute | solution.py:502
  29.1 12.1 %collective-permute-start.7 = (bf16[2,48,1024]{2,1,0:T(8,128)(2,1)S(1)}, bf16[2,48,1024]{2,1,0:T(8,128)(2,1)S(1)}, u32[]{:S(2)}, u32[]{:S(2)}) collective-permute-start(bf16[2,48,1024]{2,1,0:T(8,128)(2,1)S(1)} %pad_maximum_fusion.5), channel_id=1, source_target_pairs={{2,0},{3,1},{0,2},{1,3},{6,4},{7,5},{4,6},{5,7},{10,8},{11,9},{8,1... | collective-permute-start | bytes 589832 | tf_op jit(solution)/shard_map/ppermute | solution.py:502
  41.4 9.7 %collective-permute-start.8 = (bf16[2,96,1024]{2,1,0:T(8,128)(2,1)S(1)}, bf16[2,96,1024]{2,1,0:T(8,128)(2,1)S(1)}, u32[]{:S(2)}, u32[]{:S(2)}) collective-permute-start(bf16[2,96,1024]{2,1,0:T(8,128)(2,1)S(1)} %pad_maximum_fusion.2), channel_id=1, source_target_pairs={{4,0},{5,1},{6,2},{7,3},{0,4},{1,5},{2,6},{3,7},{12,8},{13,9},{14,... | collective-permute-start | bytes 1179656 | tf_op jit(solution)/shard_map/ppermute | solution.py:502
  47.5 6.9 %collective-permute-start.3 = (bf16[2,64,1024]{2,1,0:T(8,128)(2,1)S(1)}, bf16[2,64,1024]{2,1,0:T(8,128)(2,1)S(1)}, u32[]{:S(2)}, u32[]{:S(2)}) collective-permute-start(bf16[2,64,1024]{2,1,0:T(8,128)(2,1)S(1)} %collective-permute-done.2), channel_id=1, source_target_pairs={{2,0},{3,1},{0,2},{1,3},{6,4},{7,5},{4,6},{5,7},{10,8},{11,9},{8,1... | collective-permute-start | bytes 786440 | tf_op jit(solution)/shard_map/ppermute | solution.py:502
  51.2 6.4 %collective-permute-start.9 = (bf16[2,64,1024]{2,1,0:T(8,128)(2,1)S(1)}, bf16[2,64,1024]{2,1,0:T(8,128)(2,1)S(1)}, u32[]{:S(2)}, u32[]{:S(2)}) collective-permute-start(bf16[2,64,1024]{2,1,0:T(8,128)(2,1)S(1)} %pad_maximum_fusion.4), channel_id=1, source_target_pairs={{8,0},{9,1},{10,2},{11,3},{12,4},{13,5},{14,6},{15,7},{0,8},{1,9},... | collective-permute-start | bytes 786440 | tf_op jit(solution)/shard_map/ppermute | solution.py:502
  54.4 3.3 %copy-start.1 = (bf16[2,256,1024]{2,1,0:T(8,128)(2,1)}, bf16[2,256,1024]{2,1,0:T(8,128)(2,1)S(1)}, u32[]{:S(2)}) copy-start(bf16[2,256,1024]{2,1,0:T(8,128)(2,1)S(1)} %constant_dynamic-update-slice_fusion.refs_1_) | copy-start | bytes 3145732
  54.4 4.2 %collective-permute-start.4 = (bf16[2,256,1024]{2,1,0:T(8,128)(2,1)S(1)}, bf16[2,256,1024]{2,1,0:T(8,128)(2,1)}, u32[]{:S(2)}, u32[]{:S(2)}) collective-permute-start(bf16[2,256,1024]{2,1,0:T(8,128)(2,1)S(1)} %constant_dynamic-update-slice_fusion.refs_1_), channel_id=1, source_target_pairs={{1,0},{0,1},{3,2},{2,3},{5,4},{4,5},{7,6},{6,7},{9,8},{8,9},{11,10... | collective-permute-start | bytes 3145736 | tf_op jit(solution)/shard_map/ppermute | solution.py:502
  57.7 2.9 %copy-start = (bf16[2,256,1024]{2,1,0:T(8,128)(2,1)}, bf16[2,256,1024]{2,1,0:T(8,128)(2,1)S(1)}, u32[]{:S(2)}) copy-start(bf16[2,256,1024]{2,1,0:T(8,128)(2,1)S(1)} %constant_dynamic-update-slice_fusion.3.refs_3_) | copy-start | bytes 3145732
  57.7 2.9 %collective-permute-start.10 = (bf16[2,256,1024]{2,1,0:T(8,128)(2,1)S(1)}, bf16[2,256,1024]{2,1,0:T(8,128)(2,1)}, u32[]{:S(2)}, u32[]{:S(2)}) collective-permute-start(bf16[2,256,1024]{2,1,0:T(8,128)(2,1)S(1)} %constant_dynamic-update-slice_fusion.3.refs_3_), channel_id=1, source_target_pairs={{1,0},{0,1},{3,2},{2,3},{5,4},{4,5},{7,6},{6,7},{9,8},{8,9},{11,10... | collective-permute-start | bytes 3145736 | tf_op jit(solution)/shard_map/ppermute | solution.py:502
  58.6 2.0 %copy-start.2 = (bf16[2,256,1024]{2,1,0:T(8,128)(2,1)}, bf16[2,256,1024]{2,1,0:T(8,128)(2,1)S(1)}, u32[]{:S(2)}) copy-start(bf16[2,256,1024]{2,1,0:T(8,128)(2,1)S(1)} %collective-permute-done.refs_0_) | copy-start | bytes 3145732
where the time goes:
time: 76.5 us; the launch traced here: 76.1 us
  Pallas kernels  44.2 us (58%)
  starting transfers between devices  20.1 us (26%)
  waiting for transfers between devices  9.63 us (13%)
  local copies, waits for them, and re-layouts  1.61 us (2%)
    pallas_call x4, Pallas kernels, near_call(): pl.pallas_call(functools.partial(near_kernel, levels, index * heads), in_...  24.1 us
    ppermute x11, starting transfers between devices, moved(): return lax.ppermute(array, 'seq', pairs)  20.1 us
    pallas_call x1, Pallas kernels, far_call(): pl.pallas_call(functools.partial(far_kernel, levels, plan), in_specs=[pl....  15.4 us
    ppermute x11, waiting for transfers between devices, moved(): return lax.ppermute(array, 'seq', pairs)  9.63 us
    pallas_call x1, Pallas kernels, pool_call(): pl.pallas_call(functools.partial(pool_kernel, levels), in_specs=[HBM] * 4...  4.69 us
  transfers between devices with their start and end apart: 11, of which 4 were waited for; matrix products, arithmetic and copies ran while one was open for 2% of the time, Pallas kernels for 32%

commit v1 on v0

v1 whole, which is shorter than its diff:
```python
import functools

import jax
import jax.numpy as jnp
import numpy as np
from jax import lax
from jax.experimental import pallas as pl
from jax.experimental.pallas import tpu as pltpu
from jax.sharding import PartitionSpec as P

HEADS = 8
HEAD = 128
BLOCK = 256
TOK = 1024
UNITS = TOK // BLOCK
WIDTH = HEADS * HEAD
NEG = -1e30
FIRST = 2
SCALE = HEAD**-0.5
LOG2E = 1.4426950408889634
MIB = 1 << 20
SLICES = 2
VMEM_CLAIM = 60 * MIB
HBM = pl.BlockSpec(memory_space=pltpu.HBM)


def token_of(position):
    return ((position & 31) << 3) | (((position >> 5) & 1) << 2) | (((position >> 6) & 1) << 1) | (position >> 7)


def count_of(level):
    return max(BLOCK >> level, 32)


def pool_rows(level):
    rows = token_of(np.arange(count_of(level))) >> level
    columns = np.arange(BLOCK) >> level
    return (rows[:, None] == columns[None, :]) * 2.0**-level


def natural_pool(level, span):
    rows = np.arange(span >> level)
    return (rows[:, None] == (np.arange(span) >> level)[None, :]) * 2.0**-level


def padded(array, multiple):
    return np.pad(array, ((0, -len(array) % multiple), (0, 0)))


def as_bf16(array):
    return jnp.asarray(array.astype(np.float32)).astype(jnp.bfloat16)


def dot(a, b):
    return jnp.dot(a, b, preferred_element_type=jnp.float32)


def dot_t(a, b):
    return lax.dot_general(a, b, (((1,), (1,)), ((), ())), preferred_element_type=jnp.float32)


def dot_first(a, b):
    return lax.dot_general(a, b, (((0,), (0,)), ((), ())), preferred_element_type=jnp.float32)


def merge(first, second):
    top = jnp.maximum(first[1], second[1])
    a = jnp.exp(first[1] - top)
    b = jnp.exp(second[1] - top)
    return (a * first[0] + b * second[0], top, a * first[2] + b * second[2])


ROWS = 64


def soft_columns(loads, targets):
    spans = [slice(start, start + ROWS) for start in range(0, BLOCK, ROWS)]
    peak = None
    for load in loads:
        for span in spans:
            rows = jnp.max(load(span).reshape(ROWS // 8, 8, HEAD), axis=0)
            peak = rows if peak is None else jnp.maximum(peak, rows)
    peak = jnp.max(peak, axis=0, keepdims=True)
    total = jnp.zeros((8, HEAD), jnp.float32)
    for load, target in zip(loads, targets):
        for span in spans:
            probs = jnp.exp2((load(span) - peak) * (SCALE * LOG2E))
            total = total + jnp.sum(probs.reshape(ROWS // 8, 8, HEAD), axis=0)
            target[span, :] = probs.astype(jnp.bfloat16)
    return peak * SCALE, jnp.sum(total, axis=0, keepdims=True)


def pool_kernel(levels, small_ref, large_ref, keys_ref, values_ref, *refs):
    count = levels - FIRST + 1
    targets, (small, large, buffers, *outs, sems, out_sems) = refs[:count], refs[count:]
    step = WIDTH // 4
    fixed = [pltpu.make_async_copy(small_ref, small, sems.at[8]), pltpu.make_async_copy(large_ref, large, sems.at[9])]
    copies = []
    for index, source in enumerate((keys_ref, values_ref)):
        for part in range(4):
            cols = slice(part * step, (part + 1) * step)
            copies.append(pltpu.make_async_copy(source.at[:, cols], buffers.at[index, :, cols], sems.at[index * 4 + part]))
    for copy in fixed + copies:
        copy.start()
    for copy in fixed:
        copy.wait()
    sends = []
    for index in range(2):
        for part in range(4):
            cols = slice(part * step, (part + 1) * step)
            copies[index * 4 + part].wait()
            tiles = [
                dot(small[...], buffers[index, i * 2 * BLOCK : (i + 1) * 2 * BLOCK, cols]) for i in range(UNITS // 2)
            ]
            offset = 0
            for level in range(FIRST, min(levels, 6) + 1):
                rows = 2 * BLOCK >> level
                both = jnp.concatenate([tile[offset : offset + rows] for tile in tiles], axis=0)
                outs[level - FIRST][index, :, cols] = both.astype(jnp.bfloat16)
                offset += rows
            if levels > 6:
                rest = dot(large[...], buffers[index, :, cols])
                for level in range(7, levels + 1):
                    start = (level - 7) * 8
                    outs[level - FIRST][index, :, cols] = rest[start : start + (TOK >> level)].astype(jnp.bfloat16)
        for place, (out, target) in enumerate(zip(outs, targets)):
            sends.append(pltpu.make_async_copy(out.at[index], target.at[index], out_sems.at[index, place]))
            sends[-1].start()
    for send in sends:
        send.wait()


def pool_call(keys, values, levels):
    small = as_bf16(padded(np.concatenate([natural_pool(level, 2 * BLOCK) for level in range(FIRST, min(levels, 6) + 1)]), 16))
    parts = [padded(natural_pool(level, TOK), 8) for level in range(7, levels + 1)] + [np.zeros((8, TOK))]
    large = as_bf16(padded(np.concatenate(parts), 16))
    crossing = range(FIRST, levels + 1)
    return pl.pallas_call(
        functools.partial(pool_kernel, levels),
        in_specs=[HBM] * 4,
        out_specs=[HBM] * len(crossing),
        out_shape=[jax.ShapeDtypeStruct((2, TOK >> level, WIDTH), jnp.bfloat16) for level in crossing],
        scratch_shapes=[
            pltpu.VMEM(small.shape, jnp.bfloat16),
            pltpu.VMEM(large.shape, jnp.bfloat16),
            pltpu.VMEM((2, TOK, WIDTH), jnp.bfloat16),
        ]
        + [pltpu.VMEM((2, TOK >> level, WIDTH), jnp.bfloat16) for level in crossing]
        + [
            pltpu.SemaphoreType.DMA((10,)),
            pltpu.SemaphoreType.DMA((2, len(crossing))),
        ],
        compiler_params=pltpu.CompilerParams(vmem_limit_bytes=VMEM_CLAIM),
        cost_estimate=pl.CostEstimate(flops=2 * 256 * 512 * 4096, bytes_accessed=6 * MIB, transcendentals=0),
        name="pool_keys_values",
    )(small, large, keys, values)


def far_offsets(levels):
    offsets, total = {}, 0
    for level in range(FIRST, levels + 1):
        offsets[level] = total
        total += UNITS * count_of(level)
    return offsets, total


def lane_block(index):
    return slice(index * HEAD, (index + 1) * HEAD)


def near_kernel(levels, first, pool_ref, q_ref, k_ref, v_ref, num_out, stat_out, far_out, *scratch):
    (pool, q, k, v, num, stat, far, ordered, coarse_q, coarse_k, coarse_v, bias, scores_a, scores_b, scores_c) = scratch[:15]
    probs_a, probs_b, probs_c, sems, head_sems = scratch[15:]
    heads = HEADS // SLICES
    width = heads * HEAD
    cols = slice(first * HEAD, first * HEAD + width)
    copies = [
        pltpu.make_async_copy(pool_ref, pool, sems.at[0]),
        pltpu.make_async_copy(q_ref.at[:, cols], q, sems.at[1]),
        pltpu.make_async_copy(k_ref.at[:, cols], k, sems.at[2]),
        pltpu.make_async_copy(v_ref.at[:, cols], v, sems.at[3]),
    ]
    for copy in copies:
        copy.start()
    row = lax.broadcasted_iota(jnp.int32, (BLOCK, BLOCK), 0)
    position = lax.broadcasted_iota(jnp.int32, (BLOCK, BLOCK), 1)
    bias[...] = jnp.where(row <= token_of(position), 0.0, NEG)
    copies[0].wait()
    copies[1].wait()

    offsets, _ = far_offsets(levels)
    for unit in range(UNITS):
        pooled = dot(pool[...], q[unit * BLOCK : (unit + 1) * BLOCK, :])
        ordered[unit * BLOCK : (unit + 1) * BLOCK, :] = pooled[:BLOCK].astype(jnp.bfloat16)
        if unit >= 2:
            coarse_q[(unit - 2) * 128 : (unit - 1) * 128, :] = pooled[BLOCK : BLOCK + 128].astype(jnp.bfloat16)
        start = BLOCK + 128
        for level in range(FIRST, levels + 1):
            count = count_of(level)
            place = offsets[level] + unit * count
            far[place : place + count, :] = pooled[start : start + count].astype(jnp.bfloat16)
            start += count
    sends = [pltpu.make_async_copy(far, far_out, sems.at[4])]
    sends[0].start()
    copies[2].wait()
    copies[3].wait()
    for unit in range(2):
        rows = slice(unit * BLOCK, (unit + 1) * BLOCK)
        half = slice(unit * 128, (unit + 1) * 128)
        coarse_k[half, :] = dot(pool[BLOCK : BLOCK + 128, :], k[rows, :]).astype(jnp.bfloat16)
        coarse_v[half, :] = dot(pool[BLOCK : BLOCK + 128, :], v[rows, :]).astype(jnp.bfloat16)

    def num_copy(head):
        rows = pl.ds(pl.multiple_of(head * HEAD, HEAD), HEAD)
        return pltpu.make_async_copy(num.at[rows, :], num_out.at[rows, :], head_sems.at[head])

    def one_head(head, carry):
        own = pl.ds(pl.multiple_of(head * HEAD, HEAD), HEAD)

        def dots(tile):
            base = 2 * tile * BLOCK
            both = ordered[base : base + 2 * BLOCK, own]
            scores_a[tile] = dot_t(k[base : base + BLOCK, own], both)
            scores_b[tile] = dot_t(k[base + BLOCK : base + 2 * BLOCK, own], ordered[base + BLOCK : base + 2 * BLOCK, own])

        def soft(tile):
            stats = []
            for block in range(2):
                lanes = lane_block(block)
                stats.append(
                    soft_columns(
                        [lambda span: scores_a[tile, span, lanes] + bias[span, lanes]], [probs_a.at[tile, :, lanes]]
                    )
                )
            for block in range(2):
                lanes, late = lane_block(block), lane_block(2 + block)
                stats.append(
                    soft_columns(
                        [
                            lambda span: scores_a[tile, span, late],
                            lambda span: scores_b[tile, span, lanes] + bias[span, lanes],
                        ],
                        [probs_a.at[tile, :, late], probs_b.at[tile, :, lanes]],
                    )
                )
            return stats

        def weigh(tile, stats):
            base = 2 * tile * BLOCK
            both = dot_first(v[base : base + BLOCK, own], probs_a[tile])
            more = dot_first(v[base + BLOCK : base + 2 * BLOCK, own], probs_b[tile])
            nums = [both[:, lane_block(0)], both[:, lane_block(1)]]
            nums += [both[:, lane_block(2 + block)] + more[:, lane_block(block)] for block in range(2)]
            return [(item,) + pair for item, pair in zip(nums, stats)]

        dots(0)
        scores_c[...] = dot_t(coarse_k[:, own], coarse_q[:, own])
        dots(1)
        stats0 = soft(0)
        states = weigh(0, stats0)
        stats_c = [
            soft_columns([lambda span: scores_c[span, lane_block(block)]], [probs_c.at[:, lane_block(block)]])
            for block in range(2)
        ]
        stats1 = soft(1)
        num_c = 2.0 * dot_first(coarse_v[:, own], probs_c[...])
        late = weigh(1, stats1)
        for block, state in enumerate(late):
            unit = block // 2
            coarse = (num_c[:, lane_block(unit)], stats_c[unit][0], 2.0 * stats_c[unit][1])
            states.append(merge(state, coarse))
        for block, state in enumerate(states):
            num[own, lane_block(block)] = state[0]
            stat[head, 0:1, lane_block(block)] = state[1]
            stat[head, 1:2, lane_block(block)] = state[2]
        num_copy(head).start()
        return carry

    lax.fori_loop(0, heads, one_head, 0)
    sends.append(pltpu.make_async_copy(stat, stat_out, sems.at[5]))
    sends[-1].start()
    for send in sends:
        send.wait()
    for head in range(heads):
        num_copy(head).wait()


def near_call(queries, keys, values, levels, index):
    pool = as_bf16(padded(np.concatenate([pool_rows(level) for level in range(levels + 1)]), 16))
    heads = HEADS // SLICES
    width = heads * HEAD
    _, far_rows = far_offsets(levels)
    bf16, f32 = jnp.bfloat16, jnp.float32
    return pl.pallas_call(
        functools.partial(near_kernel, levels, index * heads),
        in_specs=[HBM] * 4,
        out_specs=[HBM] * 3,
        out_shape=[
            jax.ShapeDtypeStruct((width, TOK), f32),
            jax.ShapeDtypeStruct((heads, 8, TOK), f32),
            jax.ShapeDtypeStruct((far_rows, width), bf16),
        ],
        scratch_shapes=[
            pltpu.VMEM(pool.shape, bf16),
            pltpu.VMEM((TOK, width), bf16),
            pltpu.VMEM((TOK, width), bf16),
            pltpu.VMEM((TOK, width), bf16),
            pltpu.VMEM((width, TOK), f32),
            pltpu.VMEM((heads, 8, TOK), f32),
            pltpu.VMEM((far_rows, width), bf16),
            pltpu.VMEM((TOK, width), bf16),
            pltpu.VMEM((BLOCK, width), bf16),
            pltpu.VMEM((BLOCK, width), bf16),
            pltpu.VMEM((BLOCK, width), bf16),
            pltpu.VMEM((BLOCK, BLOCK), f32),
            pltpu.VMEM((2, BLOCK, 2 * BLOCK), f32),
            pltpu.VMEM((2, BLOCK, BLOCK), f32),
            pltpu.VMEM((BLOCK, BLOCK), f32),
            pltpu.VMEM((2, BLOCK, 2 * BLOCK), bf16),
            pltpu.VMEM((2, BLOCK, BLOCK), bf16),
            pltpu.VMEM((BLOCK, BLOCK), bf16),
            pltpu.SemaphoreType.DMA((6,)),
            pltpu.SemaphoreType.DMA((heads,)),
        ],
        compiler_params=pltpu.CompilerParams(vmem_limit_bytes=VMEM_CLAIM),
        cost_estimate=pl.CostEstimate(flops=4_000_000_000, bytes_accessed=8 * MIB, transcendentals=2_000_000),
        name="near_levels",
    )(pool, queries, keys, values)


def by_lane_group(arrays, size):
    lane = lax.broadcasted_iota(jnp.int32, arrays[0].shape, 1)
    result = arrays[-1]
    for index in range(len(arrays) - 2, -1, -1):
        result = jnp.where(lane < (index + 1) * size, arrays[index], result)
    return result


def widen_to_second(array):
    r32, r64, r96 = [pltpu.roll(array, shift, 1) for shift in (32, 64, 96)]
    return [by_lane_group([array, r32, r32, r64], 32), by_lane_group([r64, r96, r96, array], 32)]


def widen_to_units(arrays):
    units = []
    for array in arrays:
        turned = pltpu.roll(array, 64, 1)
        units += [by_lane_group([array, turned], 64), by_lane_group([turned, array], 64)]
    return units


def far_kernel(levels, plan, flags_ref, *refs):
    crossing = range(FIRST, levels + 1)
    bundles = 1 + max(bundle for _, bundle, _ in plan)
    kv_refs = refs[:bundles]
    refs = refs[bundles:]
    far_refs, num_refs, stat_refs = refs[:SLICES], refs[SLICES : 2 * SLICES], refs[2 * SLICES : 3 * SLICES]
    turn_ref, w_ref, out_ref = refs[3 * SLICES : 3 * SLICES + 3]
    kv, queries, num, stat, turn, weights, scores, probs = refs[3 * SLICES + 3 : 3 * SLICES + 11]
    mixed, natural, stage, kv_sems, near_sems, out_sems = refs[3 * SLICES + 11 :]
    heads = HEADS // SLICES
    width = heads * HEAD
    pair = 2 * HEAD
    model = w_ref.shape[1]
    step = 512
    offsets, far_rows = far_offsets(levels)

    def kv_copies(index):
        cols = pl.ds(pl.multiple_of(index * pair, pair), pair)
        made = []
        for number, (level, bundle, spans) in enumerate(plan):
            source_start, target_start, rows = spans
            made.append(
                pltpu.make_async_copy(
                    kv_refs[bundle].at[:, source_start : source_start + rows, cols],
                    kv.at[level - FIRST, :, target_start : target_start + rows, cols],
                    kv_sems.at[index, number],
                )
            )
        return made

    far_copies, near_copies = [], []
    for index in range(SLICES):
        cols = slice(index * width, (index + 1) * width)
        group = slice(index * heads, (index + 1) * heads)
        sems = [near_sems.at[place * SLICES + index] for place in range(3)]
        far_copies.append(pltpu.make_async_copy(far_refs[index], queries.at[:, cols], sems[0]))
        near_copies.append(pltpu.make_async_copy(num_refs[index], num.at[cols, :], sems[1]))
        near_copies.append(pltpu.make_async_copy(stat_refs[index], stat.at[group], sems[2]))
    last_copies = [
        pltpu.make_async_copy(turn_ref, turn, near_sems.at[3 * SLICES]),
        pltpu.make_async_copy(w_ref, weights, near_sems.at[3 * SLICES + 1]),
    ]
    for copy in far_copies + kv_copies(0) + near_copies:
        copy.start()
    for index in range(1, HEADS // 2):
        for copy in kv_copies(index):
            copy.start()
    for copy in last_copies:
        copy.start()
    for copy in far_copies:
        copy.wait()

    def group(index, carry):
        for copy in kv_copies(index):
            copy.wait()
        stats = []
        for inner in range(2):
            own = pl.ds(pl.multiple_of(index * pair + inner * HEAD, HEAD), HEAD)
            for level in crossing:
                span = slice(offsets[level], offsets[level] + UNITS * count_of(level))
                scores[inner, :, span] = dot_t(kv[level - FIRST, 0, :, own], queries[span, own])
        for inner in range(2):
            stats.append(
                [
                    soft_columns(
                        [lambda span: scores[inner, span, lane_block(block)]], [probs.at[inner, :, lane_block(block)]]
                    )
                    for block in range(far_rows // HEAD)
                ]
            )

        @pl.when(index == 0)
        def _():
            for copy in near_copies:
                copy.wait()

        for inner in range(2):
            head = 2 * index + inner
            own = pl.ds(pl.multiple_of(head * HEAD, HEAD), HEAD)
            state = None
            for level in reversed(crossing):
                span = slice(offsets[level], offsets[level] + UNITS * count_of(level))
                live = flags_ref[level - FIRST] == 1
                factor = jnp.where(live, 2.0**level, 0.0)
                weighted = factor * dot_first(kv[level - FIRST, 1, :, own], probs[inner, :, span])
                terms = []
                for block in range(UNITS * count_of(level) // HEAD):
                    peak, total = stats[inner][offsets[level] // HEAD + block]
                    terms.append((weighted[:, lane_block(block)], jnp.where(live, peak, NEG), factor * total))
                if state is None:
                    state = terms
                    continue
                if len(terms) > len(state):
                    wide = [widen_to_second(item) for item in state[0]]
                    state = [tuple(item[side] for item in wide) for side in range(2)]
                state = [merge(old, new) for old, new in zip(state, terms)]
            wide = [widen_to_units([half[place] for half in state]) for place in range(3)]
            for unit in range(UNITS):
                far_num, far_peak, far_total = [item[unit] for item in wide]
                for block in range(2 * unit, 2 * unit + 2):
                    peak = stat[head, 0:1, lane_block(block)]
                    total = stat[head, 1:2, lane_block(block)]
                    top = jnp.maximum(peak, far_peak)
                    a = jnp.exp(peak - top)
                    b = jnp.exp(far_peak - top)
                    inverse = 1.0 / (a * total + b * far_total)
                    both = (a * inverse) * num[own, lane_block(block)] + (b * inverse) * far_num
                    mixed[own, lane_block(block)] = both.astype(jnp.bfloat16)
        return carry

    lax.fori_loop(0, HEADS // 2, group, 0)

    for copy in last_copies:
        copy.wait()
    for unit in range(UNITS):
        rows = slice(unit * BLOCK, (unit + 1) * BLOCK)
        natural[rows, :] = dot_t(turn[...], mixed[:, rows]).astype(jnp.bfloat16)
    sends = []
    for index in range(model // step):
        cols = slice(index * step, (index + 1) * step)
        stage[:, cols] = dot(natural[...], weights[:, cols]).astype(jnp.bfloat16)
        sends.append(pltpu.make_async_copy(stage.at[:, cols], out_ref.at[:, cols], out_sems.at[index]))
        sends[-1].start()
    for send in sends:
        send.wait()


def far_call(flags, bundles, plan, near, w_out, levels):
    turn = np.zeros((BLOCK, BLOCK))
    turn[token_of(np.arange(BLOCK)), np.arange(BLOCK)] = 1.0
    nums, stats, fars = [[item[place] for item in near] for place in range(3)]
    model = w_out.shape[1]
    _, far_rows = far_offsets(levels)
    count = levels - FIRST + 1
    bf16, f32 = jnp.bfloat16, jnp.float32
    return pl.pallas_call(
        functools.partial(far_kernel, levels, plan),
        in_specs=[pl.BlockSpec(memory_space=pltpu.SMEM)] + [HBM] * (len(bundles) + 3 * SLICES + 2),
        out_specs=HBM,
        out_shape=jax.ShapeDtypeStruct((TOK, model), bf16),
        scratch_shapes=[
            pltpu.VMEM((count, 2, BLOCK, WIDTH), bf16),
            pltpu.VMEM((far_rows, WIDTH), bf16),
            pltpu.VMEM((WIDTH, TOK), f32),
            pltpu.VMEM((HEADS, 8, TOK), f32),
            pltpu.VMEM((BLOCK, BLOCK), bf16),
            pltpu.VMEM((WIDTH, model), bf16),
            pltpu.VMEM((2, BLOCK, far_rows), f32),
            pltpu.VMEM((2, BLOCK, far_rows), bf16),
            pltpu.VMEM((WIDTH, TOK), bf16),
            pltpu.VMEM((TOK, WIDTH), bf16),
            pltpu.VMEM((TOK, model), bf16),
            pltpu.SemaphoreType.DMA((HEADS // 2, len(plan))),
            pltpu.SemaphoreType.DMA((3 * SLICES + 2,)),
            pltpu.SemaphoreType.DMA((model // 512,)),
        ],
        compiler_params=pltpu.CompilerParams(vmem_limit_bytes=VMEM_CLAIM),
        cost_estimate=pl.CostEstimate(flops=6_500_000_000, bytes_accessed=18 * MIB, transcendentals=3_000_000),
        name="far_levels_projection",
    )(flags, *bundles, *fars, *nums, *stats, as_bf16(turn), w_out)


def moved(array, distance, upper_of=0):
    size = lax.axis_size("seq")
    pairs = [(i ^ distance, i) for i in range(size) if not upper_of or i & upper_of]
    return lax.ppermute(array, "seq", pairs)


def gathered(blocks, distance):
    sent = jnp.concatenate(blocks, axis=1) if len(blocks) > 1 else blocks[0]
    got = moved(sent, distance)
    joined, start = [], 0
    for block in blocks:
        rows = block.shape[1]
        joined.append(jnp.concatenate([block, got[:, start : start + rows]], axis=1))
        start += rows
    return joined


def after(arrays, others):
    return lax.optimization_barrier((arrays, others))[0]


def on_device(queries, keys, values, w_out):
    size = lax.axis_size("seq")
    levels = (TOK * size // (2 * BLOCK)).bit_length() - 1
    position = lax.axis_index("seq")
    flags = jnp.stack([(position >> (level - FIRST)) & 1 for level in range(FIRST, levels + 1)]).astype(jnp.int32)
    pooled = pool_call(keys, values, levels)
    blocks = {}
    for level in range(levels, FIRST - 1, -1):
        distance = 1 << (level - FIRST)
        blocks[level] = moved(pooled[level - FIRST], distance, distance)
    high = list(range(5, levels + 1))
    near = []
    for index in range(SLICES):
        source = after(queries, (near[-1], [blocks[level] for level in range(4, levels + 1)]) if near else pooled)
        near.append(near_call(source, keys, values, levels, index))
    rounds = [1 << bit for bit in range(1, levels - FIRST)]
    for number, distance in enumerate(rounds):
        members = [level for level in high if (1 << (level - FIRST)) > distance]
        if members:
            items = after([blocks[level] for level in members], near[min(number, SLICES - 1)])
            for level, item in zip(members, gathered(items, distance)):
                blocks[level] = item
        if distance == 2:
            blocks[4] = gathered([after(blocks[4], near[0])], 2)[0]
    low = jnp.concatenate([after(blocks[3], near[SLICES - 1]), blocks[4]], axis=1)
    low_got = moved(low, 1)
    top = jnp.concatenate([blocks[level] for level in high], axis=1)
    top_got = moved(top, 1)
    plan = [(2, 0, (0, 0, BLOCK))]
    for place, level in enumerate((3, 4)):
        plan += [(level, 1, (place * 128, 0, 128)), (level, 2, (place * 128, 128, 128))]
    for place, level in enumerate(high):
        plan += [(level, 3, (place * 128, 0, 128)), (level, 4, (place * 128, 128, 128))]
    return far_call(flags, [blocks[2], low, low_got, top, top_got], plan, near, w_out, levels)


def solution(mesh):
    return jax.shard_map(
        on_device,
        mesh=mesh,
        in_specs=(P("seq", None), P("seq", None), P("seq", None), P()),
        out_specs=P("seq", None),
        check_vma=False,
    )
```

time: 76.5 us -> 70.7 us (0.924)
  Pallas kernels: 44.2 us -> 34 us
  waiting for transfers between devices: 9.63 us -> 13 us
  starting transfers between devices: 20.1 us -> 21.4 us
    pallas_call x4 -> x2, Pallas kernels: 24.1 us -> 14.2 us  [near_call(): pl.pallas_call(functools.partial(near_kernel, levels, index * heads), in_...]
    ppermute x11, waiting for transfers between devices: 9.63 us -> 13 us  [moved(): return lax.ppermute(array, 'seq', pairs)]
    ppermute x11, starting transfers between devices: 20.1 us -> 21.4 us  [moved(): return lax.ppermute(array, 'seq', pairs)]
  transfers between devices with their start and end apart: 11 -> 11, of which waited for: 4 -> 4; matrix products, arithmetic and copies ran while one was open for 2% -> 2% of each run, Pallas kernels for 32% -> 20%
where the time goes in v1:
time: 70.7 us; the launch traced here: 70.5 us
  Pallas kernels  34 us (48%)
  starting transfers between devices  21.4 us (30%)
  waiting for transfers between devices  13 us (18%)
  local copies, waits for them, and re-layouts  1.58 us (2%)
    ppermute x11, starting transfers between devices, moved(): return lax.ppermute(array, 'seq', pairs)  21.4 us
    pallas_call x1, Pallas kernels, far_call(): pl.pallas_call(functools.partial(far_kernel, levels, plan), in_specs=[pl....  15.1 us
    pallas_call x2, Pallas kernels, near_call(): pl.pallas_call(functools.partial(near_kernel, levels, index * heads), in_...  14.2 us
    ppermute x11, waiting for transfers between devices, moved(): return lax.ppermute(array, 'seq', pairs)  13 us
    pallas_call x1, Pallas kernels, pool_call(): pl.pallas_call(functools.partial(pool_kernel, levels), in_specs=[HBM] * 4...  4.7 us
  transfers between devices with their start and end apart: 11, of which 4 were waited for; matrix products, arithmetic and copies ran while one was open for 2% of the time, Pallas kernels for 20%

profile of v1, /device:TPU:0, one launch (start us, length us, event | category | flops | bytes accessed | tf_op | source)
XLA Modules:
  0.0 70.5 jit_solution(2835480338618754144)
XLA Ops:
  0.0 0.6 broadcast.1.large_ref
  0.6 4.7 %pool_keys_values.1 = (bf16[2,256,1024]{2,1,0:T(8,128)(2,1)}, bf16[2,128,1024]{2,1,0:T(8,128)(2,1)}, bf16[2,64,1024]{2,1,0:T(8,128)(2,1)}, bf16[2,32,1024]{2,1,0:T(8,128)(2,1)}, bf16[2,16,1024]{2,1,0:T(8,128)(2,1)}) custom-call(bf16[256,512]{1,0:T(8,128)(2,1)} %constant.26.small_ref, bf16[16,1024]{1,0:T(8,128)(2,1)} %broadcast.1.large_ref, ...), custom_call_target="tpu_custom_call" | custom-call | flops 1073741824 | bytes 6291456 | tf_op jit(solution)/shard_map/pool_keys_values/pallas_call | solution.py:138
  5.3 5.9 %collective-permute-start.4 = (bf16[2,16,1024]{2,1,0:T(8,128)(2,1)}, bf16[2,16,1024]{2,1,0:T(8,128)(2,1)S(1)}, u32[]{:S(2)}, u32[]{:S(2)}) collective-permute-start(bf16[2,16,1024]{2,1,0:T(8,128)(2,1)} %get-tuple-element.29), channel_id=1, source_target_pairs={{0,16},{1,17},{2,18},{3,19},{4,20},{5,21},{6,22},{7,23},{8,24},{9,... | collective-permute-start | bytes 196616 | tf_op jit(solution)/shard_map/ppermute | solution.py:517
  11.3 3.5 %collective-permute-start.3 = (bf16[2,32,1024]{2,1,0:T(8,128)(2,1)}, bf16[2,32,1024]{2,1,0:T(8,128)(2,1)S(1)}, u32[]{:S(2)}, u32[]{:S(2)}) collective-permute-start(bf16[2,32,1024]{2,1,0:T(8,128)(2,1)} %get-tuple-element.28), channel_id=1, source_target_pairs={{0,8},{1,9},{2,10},{3,11},{4,12},{5,13},{6,14},{7,15},{16,24},{17,... | collective-permute-start | bytes 393224 | tf_op jit(solution)/shard_map/ppermute | solution.py:517
  14.8 3.4 %collective-permute-start.2 = (bf16[2,64,1024]{2,1,0:T(8,128)(2,1)}, bf16[2,64,1024]{2,1,0:T(8,128)(2,1)S(1)}, u32[]{:S(2)}, u32[]{:S(2)}) collective-permute-start(bf16[2,64,1024]{2,1,0:T(8,128)(2,1)} %get-tuple-element.27), channel_id=1, source_target_pairs={{0,4},{1,5},{2,6},{3,7},{8,12},{9,13},{10,14},{11,15},{16,20},{17,... | collective-permute-start | bytes 786440 | tf_op jit(solution)/shard_map/ppermute | solution.py:517
  18.2 3.4 %collective-permute-start.1 = (bf16[2,128,1024]{2,1,0:T(8,128)(2,1)}, bf16[2,128,1024]{2,1,0:T(8,128)(2,1)S(1)}, u32[]{:S(2)}, u32[]{:S(2)}) collective-permute-start(bf16[2,128,1024]{2,1,0:T(8,128)(2,1)} %get-tuple-element.26), channel_id=1, source_target_pairs={{0,2},{1,3},{4,6},{5,7},{8,10},{9,11},{12,14},{13,15},{16,18},{17,... | collective-permute-start | bytes 1572872 | tf_op jit(solution)/shard_map/ppermute | solution.py:517
  21.6 7.1 %near_levels.2 = (f32[512,1024]{1,0:T(8,128)}, f32[4,8,1024]{2,1,0:T(8,128)}, bf16[768,512]{1,0:T(8,128)(2,1)}) custom-call(bf16[576,256]{1,0:T(8,128)(2,1)} %constant.28.pool_ref, bf16[1024,1024]{1,0:T(8,128)(2,1)} %q_ref.1, bf16[1024,1024]{1,0:T(8,128)(2,1)} %k_ref.3, bf16[1024,1024]{1,0:T(8,128)(2,1)} %v_ref.3), custom_call_target="tpu_custom_call" | custom-call | flops 4000000000 | bytes 8388608 | tf_op jit(solution)/shard_map/near_levels/pallas_call | solution.py:294
  28.7 0.0 collective-permute-done.4
  28.7 0.0 collective-permute-done.3
  28.8 0.0 copy-start.2
  28.8 0.1 collective-permute-start.7
  28.9 0.0 collective-permute-done.2
  28.9 7.1 %near_levels.3 = (f32[512,1024]{1,0:T(8,128)}, f32[4,8,1024]{2,1,0:T(8,128)}, bf16[768,512]{1,0:T(8,128)(2,1)}) custom-call(bf16[576,256]{1,0:T(8,128)(2,1)} %constant.28.pool_ref, bf16[1024,1024]{1,0:T(8,128)(2,1)} %q_ref.1, bf16[1024,1024]{1,0:T(8,128)(2,1)} %k_ref.3, bf16[1024,1024]{1,0:T(8,128)(2,1)} %v_ref.3), custom_call_target="tpu_custom_call" | custom-call | flops 4000000000 | bytes 8388608 | tf_op jit(solution)/shard_map/near_levels/pallas_call | solution.py:294
  36.0 0.3 collective-permute-done.7
  36.5 0.1 collective-permute-start.8
  36.5 0.0 copy-done.2
  36.6 2.3 %collective-permute-start = (bf16[2,256,1024]{2,1,0:T(8,128)(2,1)S(1)}, bf16[2,256,1024]{2,1,0:T(8,128)(2,1)}, u32[]{:S(2)}, u32[]{:S(2)}) collective-permute-start(bf16[2,256,1024]{2,1,0:T(8,128)(2,1)S(1)} %copy-done.2), channel_id=1, source_target_pairs={{0,1},{2,3},{4,5},{6,7},{8,9},{10,11},{12,13},{14,15},{16,17},{18,... | collective-permute-start | bytes 3145736 | tf_op jit(solution)/shard_map/ppermute | solution.py:517
  38.8 2.5 %collective-permute-start.5 = (bf16[2,64,1024]{2,1,0:T(8,128)(2,1)S(1)}, bf16[2,64,1024]{2,1,0:T(8,128)(2,1)S(1)}, u32[]{:S(2)}, u32[]{:S(2)}) collective-permute-start(bf16[2,64,1024]{2,1,0:T(8,128)(2,1)S(1)} %collective-permute-done.2), channel_id=1, source_target_pairs={{2,0},{3,1},{0,2},{1,3},{6,4},{7,5},{4,6},{5,7},{10,8},{11,9},{8,1... | collective-permute-start | bytes 786440 | tf_op jit(solution)/shard_map/ppermute | solution.py:517
  41.3 0.0 collective-permute-done.1
  41.3 4.6 %collective-permute-done.8 = bf16[2,96,1024]{2,1,0:T(8,128)(2,1)S(1)} collective-permute-done((bf16[2,96,1024]{2,1,0:T(8,128)(2,1)S(1)}, bf16[2,96,1024]{2,1,0:T(8,128)(2,1)S(1)}, u32[]{:S(2)}, u32[]{:S(2)}) %collective-permute-start.8) | collective-permute-done | bytes 393248 | tf_op jit(solution)/shard_map/ppermute | solution.py:517
  46.0 0.1 collective-permute-start.9
  46.1 0.0 collective-permute-done.5
  46.2 0.0 copy-start.1
  46.2 0.1 collective-permute-start.6
  46.3 6.1 %collective-permute-done.9 = bf16[2,64,1024]{2,1,0:T(8,128)(2,1)S(1)} collective-permute-done((bf16[2,64,1024]{2,1,0:T(8,128)(2,1)S(1)}, bf16[2,64,1024]{2,1,0:T(8,128)(2,1)S(1)}, u32[]{:S(2)}, u32[]{:S(2)}) %collective-permute-start.9) | collective-permute-done | bytes 262176 | tf_op jit(solution)/shard_map/ppermute | solution.py:517
  52.4 0.1 pad_maximum_fusion.refs_3_
  52.5 0.0 copy-start
  52.5 0.1 collective-permute-start.10
  52.6 0.8 %stack.23.flags_ref = s32[5]{0:T(128)} concatenate(s32[1]{0:T(128)} %bitcast, s32[1]{0:T(128)} %bitcast.1, s32[1]{0:T(128)} %bitcast.2, s32[1]{0:T(128)} %bitcast.3, s32[1]{0:T(128)} %bitcast.4), dimensions={0} | concatenate | bytes 40 | tf_op jit(solution)/shard_map/stack | solution.py:539
  53.4 0.0 collective-permute-done.refs_0_
  53.4 0.0 collective-permute-done.6.refs_2_
  53.4 1.9 %collective-permute-done.10.refs_4_ = bf16[2,256,1024]{2,1,0:T(8,128)(2,1)} collective-permute-done((bf16[2,256,1024]{2,1,0:T(8,128)(2,1)S(1)}, bf16[2,256,1024]{2,1,0:T(8,128)(2,1)}, u32[]{:S(2)}, u32[]{:S(2)}) %collective-permute-start.10) | collective-permute-done | bytes 1048608 | tf_op jit(solution)/shard_map/ppermute | solution.py:517
  55.4 0.0 copy-done.1
  55.4 0.0 copy-done
  55.4 15.1 %far_levels_projection.1 = bf16[1024,2048]{1,0:T(8,128)(2,1)} custom-call(s32[5]{0:T(128)} %stack.23.flags_ref, bf16[2,256,1024]{2,1,0:T(8,128)(2,1)} %collective-permute-done.refs_0_, bf16[2,256,1024]{2,1,0:T(8,128)(2,1)} %copy-done.1, bf16[2,256,1024]{2,1,0:T(8,128)(2,1)} %collective-permute-done.6.refs_2_, bf16[2,256,1024]{2,1,0:T(8,128)(2,1)} %copy-done, ...), custom_call_target="tpu_custom_call" | custom-call | flops 6499999744 | bytes 18874368 | tf_op jit(solution)/shard_map/far_levels_projection/pallas_call | solution.py:487
  (12 shorter events, 0.2 us)
Async XLA Ops:
  5.3 23.4 %collective-permute-start.4 = (bf16[2,16,1024]{2,1,0:T(8,128)(2,1)}, bf16[2,16,1024]{2,1,0:T(8,128)(2,1)S(1)}, u32[]{:S(2)}, u32[]{:S(2)}) collective-permute-start(bf16[2,16,1024]{2,1,0:T(8,128)(2,1)} %get-tuple-element.29), channel_id=1, source_target_pairs={{0,16},{1,17},{2,18},{3,19},{4,20},{5,21},{6,22},{7,23},{8,24},{9,... | collective-permute-start | bytes 196616 | tf_op jit(solution)/shard_map/ppermute | solution.py:517
  11.3 17.5 %collective-permute-start.3 = (bf16[2,32,1024]{2,1,0:T(8,128)(2,1)}, bf16[2,32,1024]{2,1,0:T(8,128)(2,1)S(1)}, u32[]{:S(2)}, u32[]{:S(2)}) collective-permute-start(bf16[2,32,1024]{2,1,0:T(8,128)(2,1)} %get-tuple-element.28), channel_id=1, source_target_pairs={{0,8},{1,9},{2,10},{3,11},{4,12},{5,13},{6,14},{7,15},{16,24},{17,... | collective-permute-start | bytes 393224 | tf_op jit(solution)/shard_map/ppermute | solution.py:517
  14.8 14.1 %collective-permute-start.2 = (bf16[2,64,1024]{2,1,0:T(8,128)(2,1)}, bf16[2,64,1024]{2,1,0:T(8,128)(2,1)S(1)}, u32[]{:S(2)}, u32[]{:S(2)}) collective-permute-start(bf16[2,64,1024]{2,1,0:T(8,128)(2,1)} %get-tuple-element.27), channel_id=1, source_target_pairs={{0,4},{1,5},{2,6},{3,7},{8,12},{9,13},{10,14},{11,15},{16,20},{17,... | collective-permute-start | bytes 786440 | tf_op jit(solution)/shard_map/ppermute | solution.py:517
  18.2 23.1 %collective-permute-start.1 = (bf16[2,128,1024]{2,1,0:T(8,128)(2,1)}, bf16[2,128,1024]{2,1,0:T(8,128)(2,1)S(1)}, u32[]{:S(2)}, u32[]{:S(2)}) collective-permute-start(bf16[2,128,1024]{2,1,0:T(8,128)(2,1)} %get-tuple-element.26), channel_id=1, source_target_pairs={{0,2},{1,3},{4,6},{5,7},{8,10},{9,11},{12,14},{13,15},{16,18},{17,... | collective-permute-start | bytes 1572872 | tf_op jit(solution)/shard_map/ppermute | solution.py:517
  28.8 7.8 %copy-start.2 = (bf16[2,256,1024]{2,1,0:T(8,128)(2,1)S(1)}, bf16[2,256,1024]{2,1,0:T(8,128)(2,1)}, u32[]{:S(2)}) copy-start(bf16[2,256,1024]{2,1,0:T(8,128)(2,1)} %get-tuple-element.25) | copy-start | bytes 3145732
  28.8 7.6 %collective-permute-start.7 = (bf16[2,48,1024]{2,1,0:T(8,128)(2,1)S(1)}, bf16[2,48,1024]{2,1,0:T(8,128)(2,1)S(1)}, u32[]{:S(2)}, u32[]{:S(2)}) collective-permute-start(bf16[2,48,1024]{2,1,0:T(8,128)(2,1)S(1)} %pad_maximum_fusion.4), channel_id=1, source_target_pairs={{2,0},{3,1},{0,2},{1,3},{6,4},{7,5},{4,6},{5,7},{10,8},{11,9},{8,1... | collective-permute-start | bytes 589832 | tf_op jit(solution)/shard_map/ppermute | solution.py:517
  36.5 9.5 %collective-permute-start.8 = (bf16[2,96,1024]{2,1,0:T(8,128)(2,1)S(1)}, bf16[2,96,1024]{2,1,0:T(8,128)(2,1)S(1)}, u32[]{:S(2)}, u32[]{:S(2)}) collective-permute-start(bf16[2,96,1024]{2,1,0:T(8,128)(2,1)S(1)} %pad_maximum_fusion.1), channel_id=1, source_target_pairs={{4,0},{5,1},{6,2},{7,3},{0,4},{1,5},{2,6},{3,7},{12,8},{13,9},{14,... | collective-permute-start | bytes 1179656 | tf_op jit(solution)/shard_map/ppermute | solution.py:517
  36.6 16.9 %collective-permute-start = (bf16[2,256,1024]{2,1,0:T(8,128)(2,1)S(1)}, bf16[2,256,1024]{2,1,0:T(8,128)(2,1)}, u32[]{:S(2)}, u32[]{:S(2)}) collective-permute-start(bf16[2,256,1024]{2,1,0:T(8,128)(2,1)S(1)} %copy-done.2), channel_id=1, source_target_pairs={{0,1},{2,3},{4,5},{6,7},{8,9},{10,11},{12,13},{14,15},{16,17},{18,... | collective-permute-start | bytes 3145736 | tf_op jit(solution)/shard_map/ppermute | solution.py:517
  38.8 7.3 %collective-permute-start.5 = (bf16[2,64,1024]{2,1,0:T(8,128)(2,1)S(1)}, bf16[2,64,1024]{2,1,0:T(8,128)(2,1)S(1)}, u32[]{:S(2)}, u32[]{:S(2)}) collective-permute-start(bf16[2,64,1024]{2,1,0:T(8,128)(2,1)S(1)} %collective-permute-done.2), channel_id=1, source_target_pairs={{2,0},{3,1},{0,2},{1,3},{6,4},{7,5},{4,6},{5,7},{10,8},{11,9},{8,1... | collective-permute-start | bytes 786440 | tf_op jit(solution)/shard_map/ppermute | solution.py:517
  46.0 6.4 %collective-permute-start.9 = (bf16[2,64,1024]{2,1,0:T(8,128)(2,1)S(1)}, bf16[2,64,1024]{2,1,0:T(8,128)(2,1)S(1)}, u32[]{:S(2)}, u32[]{:S(2)}) collective-permute-start(bf16[2,64,1024]{2,1,0:T(8,128)(2,1)S(1)} %pad_maximum_fusion.3), channel_id=1, source_target_pairs={{8,0},{9,1},{10,2},{11,3},{12,4},{13,5},{14,6},{15,7},{0,8},{1,9},... | collective-permute-start | bytes 786440 | tf_op jit(solution)/shard_map/ppermute | solution.py:517
  46.2 9.2 %copy-start.1 = (bf16[2,256,1024]{2,1,0:T(8,128)(2,1)}, bf16[2,256,1024]{2,1,0:T(8,128)(2,1)S(1)}, u32[]{:S(2)}) copy-start(bf16[2,256,1024]{2,1,0:T(8,128)(2,1)S(1)} %constant_dynamic-update-slice_fusion.refs_1_) | copy-start | bytes 3145732
  46.2 7.3 %collective-permute-start.6 = (bf16[2,256,1024]{2,1,0:T(8,128)(2,1)S(1)}, bf16[2,256,1024]{2,1,0:T(8,128)(2,1)}, u32[]{:S(2)}, u32[]{:S(2)}) collective-permute-start(bf16[2,256,1024]{2,1,0:T(8,128)(2,1)S(1)} %constant_dynamic-update-slice_fusion.refs_1_), channel_id=1, source_target_pairs={{1,0},{0,1},{3,2},{2,3},{5,4},{4,5},{7,6},{6,7},{9,8},{8,9},{11,10... | collective-permute-start | bytes 3145736 | tf_op jit(solution)/shard_map/ppermute | solution.py:517
  52.5 2.9 %copy-start = (bf16[2,256,1024]{2,1,0:T(8,128)(2,1)}, bf16[2,256,1024]{2,1,0:T(8,128)(2,1)S(1)}, u32[]{:S(2)}) copy-start(bf16[2,256,1024]{2,1,0:T(8,128)(2,1)S(1)} %pad_maximum_fusion.refs_3_) | copy-start | bytes 3145732
  52.5 2.9 %collective-permute-start.10 = (bf16[2,256,1024]{2,1,0:T(8,128)(2,1)S(1)}, bf16[2,256,1024]{2,1,0:T(8,128)(2,1)}, u32[]{:S(2)}, u32[]{:S(2)}) collective-permute-start(bf16[2,256,1024]{2,1,0:T(8,128)(2,1)S(1)} %pad_maximum_fusion.refs_3_), channel_id=1, source_target_pairs={{1,0},{0,1},{3,2},{2,3},{5,4},{4,5},{7,6},{6,7},{9,8},{8,9},{11,10... | collective-permute-start | bytes 3145736 | tf_op jit(solution)/shard_map/ppermute | solution.py:517

commit v2 on v1

--- a/solution.py
+++ b/solution.py
@@ -19,7 +19,8 @@
 SCALE = HEAD**-0.5
 LOG2E = 1.4426950408889634
 MIB = 1 << 20
-SLICES = 2
+SLICES = 4
+NEAR_FLOPS = 8_000_000_000
 VMEM_CLAIM = 60 * MIB
 HBM = pl.BlockSpec(memory_space=pltpu.HBM)
 
@@ -210,79 +211,87 @@
         coarse_k[half, :] = dot(pool[BLOCK : BLOCK + 128, :], k[rows, :]).astype(jnp.bfloat16)
         coarse_v[half, :] = dot(pool[BLOCK : BLOCK + 128, :], v[rows, :]).astype(jnp.bfloat16)
 
-    def num_copy(head):
-        rows = pl.ds(pl.multiple_of(head * HEAD, HEAD), HEAD)
-        return pltpu.make_async_copy(num.at[rows, :], num_out.at[rows, :], head_sems.at[head])
-
-    def one_head(head, carry):
-        own = pl.ds(pl.multiple_of(head * HEAD, HEAD), HEAD)
-
-        def dots(tile):
-            base = 2 * tile * BLOCK
-            both = ordered[base : base + 2 * BLOCK, own]
-            scores_a[tile] = dot_t(k[base : base + BLOCK, own], both)
-            scores_b[tile] = dot_t(k[base + BLOCK : base + 2 * BLOCK, own], ordered[base + BLOCK : base + 2 * BLOCK, own])
-
-        def soft(tile):
-            stats = []
-            for block in range(2):
-                lanes = lane_block(block)
-                stats.append(
-                    soft_columns(
-                        [lambda span: scores_a[tile, span, lanes] + bias[span, lanes]], [probs_a.at[tile, :, lanes]]
-                    )
+    def num_copy(head, tile):
+        rows = lane_block(head)
+        lanes = slice(tile * 2 * BLOCK, (tile + 1) * 2 * BLOCK)
+        return pltpu.make_async_copy(num.at[rows, lanes], num_out.at[rows, lanes], head_sems.at[head, tile])
+
+    def dots(head, tile):
+        own, base = lane_block(head), 2 * tile * BLOCK
+        both = ordered[base : base + 2 * BLOCK, own]
+        scores_a[head, tile] = dot_t(k[base : base + BLOCK, own], both)
+        scores_b[head, tile] = dot_t(k[base + BLOCK : base + 2 * BLOCK, own], ordered[base + BLOCK : base + 2 * BLOCK, own])
+
+    def dots_coarse(head):
+        own = lane_block(head)
+        scores_c[head] = dot_t(coarse_k[:, own], coarse_q[:, own])
+
+    def soft(head, tile):
+        stats = []
+        for block in range(2):
+            lanes = lane_block(block)
+            stats.append(
+                soft_columns(
+                    [lambda span: scores_a[head, tile, span, lanes] + bias[span, lanes]],
+                    [probs_a.at[head, tile, :, lanes]],
                 )
-            for block in range(2):
-                lanes, late = lane_block(block), lane_block(2 + block)
-                stats.append(
-                    soft_columns(
-                        [
-                            lambda span: scores_a[tile, span, late],
-                            lambda span: scores_b[tile, span, lanes] + bias[span, lanes],
-                        ],
-                        [probs_a.at[tile, :, late], probs_b.at[tile, :, lanes]],
-                    )
+            )
+        for block in range(2):
+            lanes, late = lane_block(block), lane_block(2 + block)
+            stats.append(
+                soft_columns(
+                    [
+                        lambda span: scores_a[head, tile, span, late],
+                        lambda span: scores_b[head, tile, span, lanes] + bias[span, lanes],
+                    ],
+                    [probs_a.at[head, tile, :, late], probs_b.at[head, tile, :, lanes]],
                 )
-            return stats
-
-        def weigh(tile, stats):
-            base = 2 * tile * BLOCK
-            both = dot_first(v[base : base + BLOCK, own], probs_a[tile])
-            more = dot_first(v[base + BLOCK : base + 2 * BLOCK, own], probs_b[tile])
-            nums = [both[:, lane_block(0)], both[:, lane_block(1)]]
-            nums += [both[:, lane_block(2 + block)] + more[:, lane_block(block)] for block in range(2)]
-            return [(item,) + pair for item, pair in zip(nums, stats)]
-
-        dots(0)
-        scores_c[...] = dot_t(coarse_k[:, own], coarse_q[:, own])
-        dots(1)
-        stats0 = soft(0)
-        states = weigh(0, stats0)
-        stats_c = [
-            soft_columns([lambda span: scores_c[span, lane_block(block)]], [probs_c.at[:, lane_block(block)]])
+            )
+        return stats
+
+    def soft_coarse(head):
+        return [
+            soft_columns([lambda span: scores_c[head, span, lane_block(block)]], [probs_c.at[head, :, lane_block(block)]])
             for block in range(2)
         ]
-        stats1 = soft(1)
-        num_c = 2.0 * dot_first(coarse_v[:, own], probs_c[...])
-        late = weigh(1, stats1)
-        for block, state in enumerate(late):
+
+    def weigh(head, tile, stats):
+        own, base = lane_block(head), 2 * tile * BLOCK
+        both = dot_first(v[base : base + BLOCK, own], probs_a[head, tile])
+        more = dot_first(v[base + BLOCK : base + 2 * BLOCK, own], probs_b[head, tile])
+        nums = [both[:, lane_block(0)], both[:, lane_block(1)]]
+        nums += [both[:, lane_block(2 + block)] + more[:, lane_block(block)] for block in range(2)]
+        return [(item,) + pair for item, pair in zip(nums, stats)]
+
+    def keep(head, tile, states):
+        for index, state in enumerate(states):
+            lanes = lane_block(4 * tile + index)
+            num[lane_block(head), lanes] = state[0]
+            stat[head, 0:1, lanes] = state[1]
+            stat[head, 1:2, lanes] = state[2]
+        num_copy(head, tile).start()
+
+    for head in range(heads):
+        dots_coarse(head)
+        dots(head, 1)
+        dots(head, 0)
+    for head in range(heads):
+        coarse_stats = soft_coarse(head)
+        coarse_num = 2.0 * dot_first(coarse_v[:, lane_block(head)], probs_c[head])
+        states = []
+        for block, state in enumerate(weigh(head, 1, soft(head, 1))):
             unit = block // 2
-            coarse = (num_c[:, lane_block(unit)], stats_c[unit][0], 2.0 * stats_c[unit][1])
+            coarse = (coarse_num[:, lane_block(unit)], coarse_stats[unit][0], 2.0 * coarse_stats[unit][1])
             states.append(merge(state, coarse))
-        for block, state in enumerate(states):
-            num[own, lane_block(block)] = state[0]
-            stat[head, 0:1, lane_block(block)] = state[1]
-            stat[head, 1:2, lane_block(block)] = state[2]
-        num_copy(head).start()
-        return carry
-
-    lax.fori_loop(0, heads, one_head, 0)
+        keep(head, 1, states)
+        keep(head, 0, weigh(head, 0, soft(head, 0)))
     sends.append(pltpu.make_async_copy(stat, stat_out, sems.at[5]))
     sends[-1].start()
     for send in sends:
         send.wait()
     for head in range(heads):
-        num_copy(head).wait()
+        for tile in range(2):
+            num_copy(head, tile).wait()
 
 
 def near_call(queries, keys, values, levels, index):
@@ -313,17 +322,17 @@
             pltpu.VMEM((BLOCK, width), bf16),
             pltpu.VMEM((BLOCK, width), bf16),
             pltpu.VMEM((BLOCK, BLOCK), f32),
-            pltpu.VMEM((2, BLOCK, 2 * BLOCK), f32),
-            pltpu.VMEM((2, BLOCK, BLOCK), f32),
-            pltpu.VMEM((BLOCK, BLOCK), f32),
-            pltpu.VMEM((2, BLOCK, 2 * BLOCK), bf16),
-            pltpu.VMEM((2, BLOCK, BLOCK), bf16),
-            pltpu.VMEM((BLOCK, BLOCK), bf16),
+            pltpu.VMEM((heads, 2, BLOCK, 2 * BLOCK), f32),
+            pltpu.VMEM((heads, 2, BLOCK, BLOCK), f32),
+            pltpu.VMEM((heads, BLOCK, BLOCK), f32),
+            pltpu.VMEM((heads, 2, BLOCK, 2 * BLOCK), bf16),
+            pltpu.VMEM((heads, 2, BLOCK, BLOCK), bf16),
+            pltpu.VMEM((heads, BLOCK, BLOCK), bf16),
             pltpu.SemaphoreType.DMA((6,)),
-            pltpu.SemaphoreType.DMA((heads,)),
+            pltpu.SemaphoreType.DMA((heads, 2)),
         ],
         compiler_params=pltpu.CompilerParams(vmem_limit_bytes=VMEM_CLAIM),
-        cost_estimate=pl.CostEstimate(flops=4_000_000_000, bytes_accessed=8 * MIB, transcendentals=2_000_000),
+        cost_estimate=pl.CostEstimate(flops=NEAR_FLOPS, bytes_accessed=MIB // 4, transcendentals=0),
         name="near_levels",
     )(pool, queries, keys, values)
 
@@ -357,7 +366,7 @@
     far_refs, num_refs, stat_refs = refs[:SLICES], refs[SLICES : 2 * SLICES], refs[2 * SLICES : 3 * SLICES]
     turn_ref, w_ref, out_ref = refs[3 * SLICES : 3 * SLICES + 3]
     kv, queries, num, stat, turn, weights, scores, probs = refs[3 * SLICES + 3 : 3 * SLICES + 11]
-    mixed, natural, stage, kv_sems, near_sems, out_sems = refs[3 * SLICES + 11 :]
+    mixed, natural, stage, kv_sems, near_sems, last_sems, out_sems = refs[3 * SLICES + 11 :]
     heads = HEADS // SLICES
     width = heads * HEAD
     pair = 2 * HEAD
@@ -379,52 +388,72 @@
             )
         return made
 
-    far_copies, near_copies = [], []
+    def near_copies(index):
+        cols = slice(index * pair, (index + 1) * pair)
+        group = slice(index * heads, (index + 1) * heads)
+        sems = [near_sems.at[place, index] for place in range(3)]
+        return [
+            pltpu.make_async_copy(far_refs[index], queries.at[:, cols], sems[0]),
+            pltpu.make_async_copy(num_refs[index], num.at[cols, :], sems[1]),
+            pltpu.make_async_copy(stat_refs[index], stat.at[group], sems[2]),
+        ]
+
+    turn_copy = pltpu.make_async_copy(turn_ref, turn, last_sems.at[0])
+    w_copies = [
+        pltpu.make_async_copy(
+            w_ref.at[:, index * step : (index + 1) * step], weights.at[:, index * step : (index + 1) * step], last_sems.at[1 + index]
+        )
+        for index in range(model // step)
+    ]
     for index in range(SLICES):
-        cols = slice(index * width, (index + 1) * width)
-        group = slice(index * heads, (index + 1) * heads)
-        sems = [near_sems.at[place * SLICES + index] for place in range(3)]
-        far_copies.append(pltpu.make_async_copy(far_refs[index], queries.at[:, cols], sems[0]))
-        near_copies.append(pltpu.make_async_copy(num_refs[index], num.at[cols, :], sems[1]))
-        near_copies.append(pltpu.make_async_copy(stat_refs[index], stat.at[group], sems[2]))
-    last_copies = [
-        pltpu.make_async_copy(turn_ref, turn, near_sems.at[3 * SLICES]),
-        pltpu.make_async_copy(w_ref, weights, near_sems.at[3 * SLICES + 1]),
-    ]
-    for copy in far_copies + kv_copies(0) + near_copies:
+        for copy in near_copies(index)[:1] + kv_copies(index) + near_copies(index)[1:]:
+            copy.start()
+    for copy in [turn_copy] + w_copies:
         copy.start()
-    for index in range(1, HEADS // 2):
-        for copy in kv_copies(index):
-            copy.start()
-    for copy in last_copies:
-        copy.start()
-    for copy in far_copies:
-        copy.wait()
-
-    def group(index, carry):
-        for copy in kv_copies(index):
-            copy.wait()
-        stats = []
+
+    def wait_scores(index):
+        for number in range(SLICES):
+
+            @pl.when(index == number)
+            def _():
+                near_copies(number)[0].wait()
+                for copy in kv_copies(number):
+                    copy.wait()
+
+    def wait_near(index):
+        for number in range(SLICES):
+
+            @pl.when(index == number)
+            def _():
+                for copy in near_copies(number)[1:]:
+                    copy.wait()
+
+    def dots(index, slot):
         for inner in range(2):
             own = pl.ds(pl.multiple_of(index * pair + inner * HEAD, HEAD), HEAD)
             for level in crossing:
                 span = slice(offsets[level], offsets[level] + UNITS * count_of(level))
-                scores[inner, :, span] = dot_t(kv[level - FIRST, 0, :, own], queries[span, own])
+                scores[slot, inner, :, span] = dot_t(kv[level - FIRST, 0, :, own], queries[span, own])
+
+    wait_scores(0)
+    dots(0, 0)
+
+    def group(index, carry):
+        slot = lax.rem(index, 2)
+        following = lax.rem(index + 1, SLICES)
+        wait_scores(index + 1)
+        wait_near(index)
+        dots(following, 1 - slot)
+        stats = []
         for inner in range(2):
             stats.append(
                 [
                     soft_columns(
-                        [lambda span: scores[inner, span, lane_block(block)]], [probs.at[inner, :, lane_block(block)]]
+                        [lambda span: scores[slot, inner, span, lane_block(block)]], [probs.at[inner, :, lane_block(block)]]
                     )
                     for block in range(far_rows // HEAD)
                 ]
             )
-
-        @pl.when(index == 0)
-        def _():
-            for copy in near_copies:
-                copy.wait()
-
         for inner in range(2):
             head = 2 * index + inner
             own = pl.ds(pl.multiple_of(head * HEAD, HEAD), HEAD)
@@ -459,16 +488,16 @@
                     mixed[own, lane_block(block)] = both.astype(jnp.bfloat16)
         return carry
 
-    lax.fori_loop(0, HEADS // 2, group, 0)
-
-    for copy in last_copies:
-        copy.wait()
+    lax.fori_loop(0, SLICES, group, 0)
+
+    turn_copy.wait()
     for unit in range(UNITS):
         rows = slice(unit * BLOCK, (unit + 1) * BLOCK)
         natural[rows, :] = dot_t(turn[...], mixed[:, rows]).astype(jnp.bfloat16)
     sends = []
     for index in range(model // step):
         cols = slice(index * step, (index + 1) * step)
+        w_copies[index].wait()
         stage[:, cols] = dot(natural[...], weights[:, cols]).astype(jnp.bfloat16)
         sends.append(pltpu.make_async_copy(stage.at[:, cols], out_ref.at[:, cols], out_sems.at[index]))
         sends[-1].start()
@@ -496,13 +525,14 @@
             pltpu.VMEM((HEADS, 8, TOK), f32),
             pltpu.VMEM((BLOCK, BLOCK), bf16),
             pltpu.VMEM((WIDTH, model), bf16),
-            pltpu.VMEM((2, BLOCK, far_rows), f32),
+            pltpu.VMEM((2, 2, BLOCK, far_rows), f32),
             pltpu.VMEM((2, BLOCK, far_rows), bf16),
             pltpu.VMEM((WIDTH, TOK), bf16),
             pltpu.VMEM((TOK, WIDTH), bf16),
             pltpu.VMEM((TOK, model), bf16),
             pltpu.SemaphoreType.DMA((HEADS // 2, len(plan))),
-            pltpu.SemaphoreType.DMA((3 * SLICES + 2,)),
+            pltpu.SemaphoreType.DMA((3, SLICES)),
+            pltpu.SemaphoreType.DMA((1 + model // 512,)),
             pltpu.SemaphoreType.DMA((model // 512,)),
         ],
         compiler_params=pltpu.CompilerParams(vmem_limit_bytes=VMEM_CLAIM),
@@ -544,27 +574,32 @@
         blocks[level] = moved(pooled[level - FIRST], distance, distance)
     high = list(range(5, levels + 1))
     near = []
-    for index in range(SLICES):
-        source = after(queries, (near[-1], [blocks[level] for level in range(4, levels + 1)]) if near else pooled)
-        near.append(near_call(source, keys, values, levels, index))
+
+    def near_slice(arrived):
+        source = after(queries, (near[-1:], arrived))
+        near.append(near_call(source, keys, values, levels, len(near)))
+
+    near_slice(pooled)
     rounds = [1 << bit for bit in range(1, levels - FIRST)]
     for number, distance in enumerate(rounds):
+        arrived = dict(blocks)
         members = [level for level in high if (1 << (level - FIRST)) > distance]
+        if number == 0:
+            blocks[4] = gathered([blocks[4]], 2)[0]
         if members:
-            items = after([blocks[level] for level in members], near[min(number, SLICES - 1)])
-            for level, item in zip(members, gathered(items, distance)):
+            waited = after([blocks[level] for level in members], near[-1])
+            for level, item in zip(members, gathered(waited, distance)):
                 blocks[level] = item
-        if distance == 2:
-            blocks[4] = gathered([after(blocks[4], near[0])], 2)[0]
-    low = jnp.concatenate([after(blocks[3], near[SLICES - 1]), blocks[4]], axis=1)
+        if len(near) < SLICES:
+            near_slice([arrived[level] for level in range(max(4 - number, 2), levels + 1)])
+    low = jnp.concatenate([after(blocks[3], near[2]), blocks[4]], axis=1)
     low_got = moved(low, 1)
-    top = jnp.concatenate([blocks[level] for level in high], axis=1)
+    top = jnp.concatenate(after([blocks[level] for level in high], near[-1]), axis=1)
     top_got = moved(top, 1)
     plan = [(2, 0, (0, 0, BLOCK))]
-    for place, level in enumerate((3, 4)):
-        plan += [(level, 1, (place * 128, 0, 128)), (level, 2, (place * 128, 128, 128))]
-    for place, level in enumerate(high):
-        plan += [(level, 3, (place * 128, 0, 128)), (level, 4, (place * 128, 128, 128))]
+    for first, members in ((1, (3, 4)), (3, high)):
+        for place, level in enumerate(members):
+            plan += [(level, first, (place * 128, 0, 128)), (level, first + 1, (place * 128, 128, 128))]
     return far_call(flags, [blocks[2], low, low_got, top, top_got], plan, near, w_out, levels)
 
 

time: 70.7 us -> 78.1 us (1.10)
  Pallas kernels: 34 us -> 38.4 us
  waiting for transfers between devices: 13 us -> 15.2 us
  local copies, waits for them, and re-layouts: 1.58 us -> 2.66 us
    pallas_call x2 -> x4, Pallas kernels: 14.2 us -> 17.1 us  [near_call(): pl.pallas_call(functools.partial(near_kernel, levels, index * heads), in_...]
    ppermute x11, waiting for transfers between devices: 13 us -> 15.2 us  [moved(): return lax.ppermute(array, 'seq', pairs)]
    pallas_call x1, Pallas kernels: 15.1 us -> 16.6 us  [far_call(): pl.pallas_call(functools.partial(far_kernel, levels, plan), in_specs=[pl....]
    unnamed x8 -> x9, local copies, waits for them, and re-layouts: 0.07 us -> 1.15 us
  transfers between devices with their start and end apart: 11 -> 11, of which waited for: 4 -> 5; matrix products, arithmetic and copies ran while one was open for 2% -> 1% of each run, Pallas kernels for 20% -> 22%
where the time goes in v2:
time: 78.1 us; the launch traced here: 77.8 us
  Pallas kernels  38.4 us (49%)
  starting transfers between devices  21 us (27%)
  waiting for transfers between devices  15.2 us (19%)
  local copies, waits for them, and re-layouts  2.66 us (3%)
    ppermute x11, starting transfers between devices, moved(): return lax.ppermute(array, 'seq', pairs)  21 us
    pallas_call x4, Pallas kernels, near_call(): pl.pallas_call(functools.partial(near_kernel, levels, index * heads), in_...  17.1 us
    pallas_call x1, Pallas kernels, far_call(): pl.pallas_call(functools.partial(far_kernel, levels, plan), in_specs=[pl....  16.6 us
    ppermute x11, waiting for transfers between devices, moved(): return lax.ppermute(array, 'seq', pairs)  15.2 us
    pallas_call x1, Pallas kernels, pool_call(): pl.pallas_call(functools.partial(pool_kernel, levels), in_specs=[HBM] * 4...  4.7 us
  transfers between devices with their start and end apart: 11, of which 5 were waited for; matrix products, arithmetic and copies ran while one was open for 1% of the time, Pallas kernels for 22%

profile of v2, /device:TPU:0, one launch (start us, length us, event | category | flops | bytes accessed | tf_op | source)
XLA Modules:
  0.0 77.8 jit_solution(11068256534845436209)
XLA Ops:
  0.0 0.6 broadcast.1.large_ref
  0.6 4.7 %pool_keys_values.1 = (bf16[2,256,1024]{2,1,0:T(8,128)(2,1)}, bf16[2,128,1024]{2,1,0:T(8,128)(2,1)}, bf16[2,64,1024]{2,1,0:T(8,128)(2,1)}, bf16[2,32,1024]{2,1,0:T(8,128)(2,1)}, bf16[2,16,1024]{2,1,0:T(8,128)(2,1)}) custom-call(bf16[256,512]{1,0:T(8,128)(2,1)} %constant.26.small_ref, bf16[16,1024]{1,0:T(8,128)(2,1)} %broadcast.1.large_ref, ...), custom_call_target="tpu_custom_call" | custom-call | flops 1073741824 | bytes 6291456 | tf_op jit(solution)/shard_map/pool_keys_values/pallas_call | solution.py:139
  5.3 5.9 %collective-permute-start.4 = (bf16[2,16,1024]{2,1,0:T(8,128)(2,1)}, bf16[2,16,1024]{2,1,0:T(8,128)(2,1)S(1)}, u32[]{:S(2)}, u32[]{:S(2)}) collective-permute-start(bf16[2,16,1024]{2,1,0:T(8,128)(2,1)} %get-tuple-element.38), channel_id=1, source_target_pairs={{0,16},{1,17},{2,18},{3,19},{4,20},{5,21},{6,22},{7,23},{8,24},{9,... | collective-permute-start | bytes 196616 | tf_op jit(solution)/shard_map/ppermute | solution.py:547
  11.3 3.5 %collective-permute-start.3 = (bf16[2,32,1024]{2,1,0:T(8,128)(2,1)}, bf16[2,32,1024]{2,1,0:T(8,128)(2,1)S(1)}, u32[]{:S(2)}, u32[]{:S(2)}) collective-permute-start(bf16[2,32,1024]{2,1,0:T(8,128)(2,1)} %get-tuple-element.37), channel_id=1, source_target_pairs={{0,8},{1,9},{2,10},{3,11},{4,12},{5,13},{6,14},{7,15},{16,24},{17,... | collective-permute-start | bytes 393224 | tf_op jit(solution)/shard_map/ppermute | solution.py:547
  14.8 3.4 %collective-permute-start.2 = (bf16[2,64,1024]{2,1,0:T(8,128)(2,1)}, bf16[2,64,1024]{2,1,0:T(8,128)(2,1)S(1)}, u32[]{:S(2)}, u32[]{:S(2)}) collective-permute-start(bf16[2,64,1024]{2,1,0:T(8,128)(2,1)} %get-tuple-element.36), channel_id=1, source_target_pairs={{0,4},{1,5},{2,6},{3,7},{8,12},{9,13},{10,14},{11,15},{16,20},{17,... | collective-permute-start | bytes 786440 | tf_op jit(solution)/shard_map/ppermute | solution.py:547
  18.2 3.4 %collective-permute-start.1 = (bf16[2,128,1024]{2,1,0:T(8,128)(2,1)}, bf16[2,128,1024]{2,1,0:T(8,128)(2,1)S(1)}, u32[]{:S(2)}, u32[]{:S(2)}) collective-permute-start(bf16[2,128,1024]{2,1,0:T(8,128)(2,1)} %get-tuple-element.35), channel_id=1, source_target_pairs={{0,2},{1,3},{4,6},{5,7},{8,10},{9,11},{12,14},{13,15},{16,18},{17,... | collective-permute-start | bytes 1572872 | tf_op jit(solution)/shard_map/ppermute | solution.py:547
  21.7 2.3 %collective-permute-start = (bf16[2,256,1024]{2,1,0:T(8,128)(2,1)}, bf16[2,256,1024]{2,1,0:T(8,128)(2,1)}, u32[]{:S(2)}, u32[]{:S(2)}) collective-permute-start(bf16[2,256,1024]{2,1,0:T(8,128)(2,1)} %get-tuple-element.34), channel_id=1, source_target_pairs={{0,1},{2,3},{4,5},{6,7},{8,9},{10,11},{12,13},{14,15},{16,17},{18,... | collective-permute-start | bytes 3145736 | tf_op jit(solution)/shard_map/ppermute | solution.py:547
  23.9 4.3 %near_levels.4 = (f32[256,1024]{1,0:T(8,128)}, f32[2,8,1024]{2,1,0:T(8,128)}, bf16[768,256]{1,0:T(8,128)(2,1)}) custom-call(bf16[576,256]{1,0:T(8,128)(2,1)} %constant.28.pool_ref, bf16[1024,1024]{1,0:T(8,128)(2,1)} %q_ref.3, bf16[1024,1024]{1,0:T(8,128)(2,1)} %k_ref.7, bf16[1024,1024]{1,0:T(8,128)(2,1)} %v_ref.7), custom_call_target="tpu_custom_call" | custom-call | flops 8000000000 | bytes 262144 | tf_op jit(solution)/shard_map/near_levels/pallas_call | solution.py:303
  28.2 0.0 collective-permute-done.4
  28.2 0.0 collective-permute-done.3
  28.2 0.1 collective-permute-start.6
  28.3 0.0 collective-permute-done.2
  28.3 4.3 %near_levels.5 = (f32[256,1024]{1,0:T(8,128)}, f32[2,8,1024]{2,1,0:T(8,128)}, bf16[768,256]{1,0:T(8,128)(2,1)}) custom-call(bf16[576,256]{1,0:T(8,128)(2,1)} %constant.28.pool_ref, bf16[1024,1024]{1,0:T(8,128)(2,1)} %q_ref.3, bf16[1024,1024]{1,0:T(8,128)(2,1)} %k_ref.7, bf16[1024,1024]{1,0:T(8,128)(2,1)} %v_ref.7), custom_call_target="tpu_custom_call" | custom-call | flops 8000000000 | bytes 262144 | tf_op jit(solution)/shard_map/near_levels/pallas_call | solution.py:303
  32.6 2.1 %collective-permute-start.5 = (bf16[2,64,1024]{2,1,0:T(8,128)(2,1)S(1)}, bf16[2,64,1024]{2,1,0:T(8,128)(2,1)S(1)}, u32[]{:S(2)}, u32[]{:S(2)}) collective-permute-start(bf16[2,64,1024]{2,1,0:T(8,128)(2,1)S(1)} %collective-permute-done.2), channel_id=1, source_target_pairs={{2,0},{3,1},{0,2},{1,3},{6,4},{7,5},{4,6},{5,7},{10,8},{11,9},{8,1... | collective-permute-start | bytes 786440 | tf_op jit(solution)/shard_map/ppermute | solution.py:547
  34.7 3.7 %collective-permute-done.6 = bf16[2,48,1024]{2,1,0:T(8,128)(2,1)S(1)} collective-permute-done((bf16[2,48,1024]{2,1,0:T(8,128)(2,1)S(1)}, bf16[2,48,1024]{2,1,0:T(8,128)(2,1)S(1)}, u32[]{:S(2)}, u32[]{:S(2)}) %collective-permute-start.6) | collective-permute-done | bytes 196640 | tf_op jit(solution)/shard_map/ppermute | solution.py:547
  38.5 0.1 collective-permute-start.8
  38.6 3.4 %collective-permute-done.5 = bf16[2,64,1024]{2,1,0:T(8,128)(2,1)S(1)} collective-permute-done((bf16[2,64,1024]{2,1,0:T(8,128)(2,1)S(1)}, bf16[2,64,1024]{2,1,0:T(8,128)(2,1)S(1)}, u32[]{:S(2)}, u32[]{:S(2)}) %collective-permute-start.5) | collective-permute-done | bytes 262176 | tf_op jit(solution)/shard_map/ppermute | solution.py:547
  42.0 0.0 collective-permute-done.1
  42.0 4.3 %near_levels.6 = (f32[256,1024]{1,0:T(8,128)}, f32[2,8,1024]{2,1,0:T(8,128)}, bf16[768,256]{1,0:T(8,128)(2,1)}) custom-call(bf16[576,256]{1,0:T(8,128)(2,1)} %constant.28.pool_ref, bf16[1024,1024]{1,0:T(8,128)(2,1)} %q_ref.3, bf16[1024,1024]{1,0:T(8,128)(2,1)} %k_ref.7, bf16[1024,1024]{1,0:T(8,128)(2,1)} %v_ref.7), custom_call_target="tpu_custom_call" | custom-call | flops 8000000000 | bytes 262144 | tf_op jit(solution)/shard_map/near_levels/pallas_call | solution.py:303
  46.3 0.1 collective-permute-done.8
  46.4 0.1 collective-permute-start.9
  46.5 0.0 copy-start
  46.5 0.1 collective-permute-start.7
  46.7 6.1 %collective-permute-done.9 = bf16[2,64,1024]{2,1,0:T(8,128)(2,1)S(1)} collective-permute-done((bf16[2,64,1024]{2,1,0:T(8,128)(2,1)S(1)}, bf16[2,64,1024]{2,1,0:T(8,128)(2,1)S(1)}, u32[]{:S(2)}, u32[]{:S(2)}) %collective-permute-start.9) | collective-permute-done | bytes 262176 | tf_op jit(solution)/shard_map/ppermute | solution.py:547
  52.9 0.0 collective-permute-done.refs_0_
  52.9 4.3 %near_levels.7 = (f32[256,1024]{1,0:T(8,128)}, f32[2,8,1024]{2,1,0:T(8,128)}, bf16[768,256]{1,0:T(8,128)(2,1)}) custom-call(bf16[576,256]{1,0:T(8,128)(2,1)} %constant.28.pool_ref, bf16[1024,1024]{1,0:T(8,128)(2,1)} %q_ref.3, bf16[1024,1024]{1,0:T(8,128)(2,1)} %k_ref.7, bf16[1024,1024]{1,0:T(8,128)(2,1)} %v_ref.7), custom_call_target="tpu_custom_call" | custom-call | flops 8000000000 | bytes 262144 | tf_op jit(solution)/shard_map/near_levels/pallas_call | solution.py:303
  57.2 0.0 copy-done
  57.3 0.0 copy-start.1
  57.3 0.1 collective-permute-start.10
  57.4 0.8 %stack.23.flags_ref = s32[5]{0:T(128)} concatenate(s32[1]{0:T(128)} %bitcast, s32[1]{0:T(128)} %bitcast.1, s32[1]{0:T(128)} %bitcast.2, s32[1]{0:T(128)} %bitcast.3, s32[1]{0:T(128)} %bitcast.4), dimensions={0} | concatenate | bytes 40 | tf_op jit(solution)/shard_map/stack | solution.py:569
  58.2 0.0 collective-permute-done.7.refs_2_
  58.2 1.8 %collective-permute-done.10.refs_4_ = bf16[2,256,1024]{2,1,0:T(8,128)(2,1)S(1)} collective-permute-done((bf16[2,256,1024]{2,1,0:T(8,128)(2,1)S(1)}, bf16[2,256,1024]{2,1,0:T(8,128)(2,1)S(1)}, u32[]{:S(2)}, u32[]{:S(2)}) %collective-permute-start.10) | collective-permute-done | bytes 1048608 | tf_op jit(solution)/shard_map/ppermute | solution.py:547
  60.0 0.0 copy-done.1
  60.0 0.0 copy-start.2
  60.0 1.0 %copy-done.2 = bf16[2,256,1024]{2,1,0:T(8,128)(2,1)} copy-done((bf16[2,256,1024]{2,1,0:T(8,128)(2,1)}, bf16[2,256,1024]{2,1,0:T(8,128)(2,1)S(1)}, u32[]{:S(2)}) %copy-start.2) | copy-done | bytes 1048600
  61.1 16.6 %far_levels_projection.1 = bf16[1024,2048]{1,0:T(8,128)(2,1)} custom-call(s32[5]{0:T(128)} %stack.23.flags_ref, bf16[2,256,1024]{2,1,0:T(8,128)(2,1)} %collective-permute-done.refs_0_, bf16[2,256,1024]{2,1,0:T(8,128)(2,1)} %copy-done, bf16[2,256,1024]{2,1,0:T(8,128)(2,1)} %collective-permute-done.7.refs_2_, bf16[2,256,1024]{2,1,0:T(8,128)(2,1)} %copy-done.1, ...), custom_call_target="tpu_custom_call" | custom-call | flops 6499999744 | bytes 18874368 | tf_op jit(solution)/shard_map/far_levels_projection/pallas_call | solution.py:516
  (16 shorter events, 0.4 us)
Async XLA Ops:
  5.3 22.9 %collective-permute-start.4 = (bf16[2,16,1024]{2,1,0:T(8,128)(2,1)}, bf16[2,16,1024]{2,1,0:T(8,128)(2,1)S(1)}, u32[]{:S(2)}, u32[]{:S(2)}) collective-permute-start(bf16[2,16,1024]{2,1,0:T(8,128)(2,1)} %get-tuple-element.38), channel_id=1, source_target_pairs={{0,16},{1,17},{2,18},{3,19},{4,20},{5,21},{6,22},{7,23},{8,24},{9,... | collective-permute-start | bytes 196616 | tf_op jit(solution)/shard_map/ppermute | solution.py:547
  11.3 16.9 %collective-permute-start.3 = (bf16[2,32,1024]{2,1,0:T(8,128)(2,1)}, bf16[2,32,1024]{2,1,0:T(8,128)(2,1)S(1)}, u32[]{:S(2)}, u32[]{:S(2)}) collective-permute-start(bf16[2,32,1024]{2,1,0:T(8,128)(2,1)} %get-tuple-element.37), channel_id=1, source_target_pairs={{0,8},{1,9},{2,10},{3,11},{4,12},{5,13},{6,14},{7,15},{16,24},{17,... | collective-permute-start | bytes 393224 | tf_op jit(solution)/shard_map/ppermute | solution.py:547
  14.8 13.6 %collective-permute-start.2 = (bf16[2,64,1024]{2,1,0:T(8,128)(2,1)}, bf16[2,64,1024]{2,1,0:T(8,128)(2,1)S(1)}, u32[]{:S(2)}, u32[]{:S(2)}) collective-permute-start(bf16[2,64,1024]{2,1,0:T(8,128)(2,1)} %get-tuple-element.36), channel_id=1, source_target_pairs={{0,4},{1,5},{2,6},{3,7},{8,12},{9,13},{10,14},{11,15},{16,20},{17,... | collective-permute-start | bytes 786440 | tf_op jit(solution)/shard_map/ppermute | solution.py:547
  18.2 23.8 %collective-permute-start.1 = (bf16[2,128,1024]{2,1,0:T(8,128)(2,1)}, bf16[2,128,1024]{2,1,0:T(8,128)(2,1)S(1)}, u32[]{:S(2)}, u32[]{:S(2)}) collective-permute-start(bf16[2,128,1024]{2,1,0:T(8,128)(2,1)} %get-tuple-element.35), channel_id=1, source_target_pairs={{0,2},{1,3},{4,6},{5,7},{8,10},{9,11},{12,14},{13,15},{16,18},{17,... | collective-permute-start | bytes 1572872 | tf_op jit(solution)/shard_map/ppermute | solution.py:547
  21.7 31.2 %collective-permute-start = (bf16[2,256,1024]{2,1,0:T(8,128)(2,1)}, bf16[2,256,1024]{2,1,0:T(8,128)(2,1)}, u32[]{:S(2)}, u32[]{:S(2)}) collective-permute-start(bf16[2,256,1024]{2,1,0:T(8,128)(2,1)} %get-tuple-element.34), channel_id=1, source_target_pairs={{0,1},{2,3},{4,5},{6,7},{8,9},{10,11},{12,13},{14,15},{16,17},{18,... | collective-permute-start | bytes 3145736 | tf_op jit(solution)/shard_map/ppermute | solution.py:547
  28.2 10.2 %collective-permute-start.6 = (bf16[2,48,1024]{2,1,0:T(8,128)(2,1)S(1)}, bf16[2,48,1024]{2,1,0:T(8,128)(2,1)S(1)}, u32[]{:S(2)}, u32[]{:S(2)}) collective-permute-start(bf16[2,48,1024]{2,1,0:T(8,128)(2,1)S(1)} %pad_maximum_fusion.5), channel_id=1, source_target_pairs={{2,0},{3,1},{0,2},{1,3},{6,4},{7,5},{4,6},{5,7},{10,8},{11,9},{8,1... | collective-permute-start | bytes 589832 | tf_op jit(solution)/shard_map/ppermute | solution.py:547
  32.6 9.4 %collective-permute-start.5 = (bf16[2,64,1024]{2,1,0:T(8,128)(2,1)S(1)}, bf16[2,64,1024]{2,1,0:T(8,128)(2,1)S(1)}, u32[]{:S(2)}, u32[]{:S(2)}) collective-permute-start(bf16[2,64,1024]{2,1,0:T(8,128)(2,1)S(1)} %collective-permute-done.2), channel_id=1, source_target_pairs={{2,0},{3,1},{0,2},{1,3},{6,4},{7,5},{4,6},{5,7},{10,8},{11,9},{8,1... | collective-permute-start | bytes 786440 | tf_op jit(solution)/shard_map/ppermute | solution.py:547
  38.5 7.8 %collective-permute-start.8 = (bf16[2,96,1024]{2,1,0:T(8,128)(2,1)S(1)}, bf16[2,96,1024]{2,1,0:T(8,128)(2,1)S(1)}, u32[]{:S(2)}, u32[]{:S(2)}) collective-permute-start(bf16[2,96,1024]{2,1,0:T(8,128)(2,1)S(1)} %pad_maximum_fusion.2), channel_id=1, source_target_pairs={{4,0},{5,1},{6,2},{7,3},{0,4},{1,5},{2,6},{3,7},{12,8},{13,9},{14,... | collective-permute-start | bytes 1179656 | tf_op jit(solution)/shard_map/ppermute | solution.py:547
  46.4 6.4 %collective-permute-start.9 = (bf16[2,64,1024]{2,1,0:T(8,128)(2,1)S(1)}, bf16[2,64,1024]{2,1,0:T(8,128)(2,1)S(1)}, u32[]{:S(2)}, u32[]{:S(2)}) collective-permute-start(bf16[2,64,1024]{2,1,0:T(8,128)(2,1)S(1)} %pad_maximum_fusion.4), channel_id=1, source_target_pairs={{8,0},{9,1},{10,2},{11,3},{12,4},{13,5},{14,6},{15,7},{0,8},{1,9},... | collective-permute-start | bytes 786440 | tf_op jit(solution)/shard_map/ppermute | solution.py:547
  46.5 10.7 %copy-start = (bf16[2,256,1024]{2,1,0:T(8,128)(2,1)}, bf16[2,256,1024]{2,1,0:T(8,128)(2,1)S(1)}, u32[]{:S(2)}) copy-start(bf16[2,256,1024]{2,1,0:T(8,128)(2,1)S(1)} %constant_dynamic-update-slice_fusion.2.refs_1_) | copy-start | bytes 3145732
  46.5 11.7 %collective-permute-start.7 = (bf16[2,256,1024]{2,1,0:T(8,128)(2,1)S(1)}, bf16[2,256,1024]{2,1,0:T(8,128)(2,1)}, u32[]{:S(2)}, u32[]{:S(2)}) collective-permute-start(bf16[2,256,1024]{2,1,0:T(8,128)(2,1)S(1)} %constant_dynamic-update-slice_fusion.2.refs_1_), channel_id=1, source_target_pairs={{1,0},{0,1},{3,2},{2,3},{5,4},{4,5},{7,6},{6,7},{9,8},{8,9},{11,10... | collective-permute-start | bytes 3145736 | tf_op jit(solution)/shard_map/ppermute | solution.py:547
  57.3 2.7 %copy-start.1 = (bf16[2,256,1024]{2,1,0:T(8,128)(2,1)}, bf16[2,256,1024]{2,1,0:T(8,128)(2,1)S(1)}, u32[]{:S(2)}) copy-start(bf16[2,256,1024]{2,1,0:T(8,128)(2,1)S(1)} %constant_dynamic-update-slice_fusion.5.refs_3_) | copy-start | bytes 3145732
  57.3 2.7 %collective-permute-start.10 = (bf16[2,256,1024]{2,1,0:T(8,128)(2,1)S(1)}, bf16[2,256,1024]{2,1,0:T(8,128)(2,1)S(1)}, u32[]{:S(2)}, u32[]{:S(2)}) collective-permute-start(bf16[2,256,1024]{2,1,0:T(8,128)(2,1)S(1)} %constant_dynamic-update-slice_fusion.5.refs_3_), channel_id=1, source_target_pairs={{1,0},{0,1},{3,2},{2,3},{5,4},{4,5},{7,6},{6,7},{9,8},{8,9},{11,10... | collective-permute-start | bytes 3145736 | tf_op jit(solution)/shard_map/ppermute | solution.py:547
  60.0 1.0 %copy-start.2 = (bf16[2,256,1024]{2,1,0:T(8,128)(2,1)}, bf16[2,256,1024]{2,1,0:T(8,128)(2,1)S(1)}, u32[]{:S(2)}) copy-start(bf16[2,256,1024]{2,1,0:T(8,128)(2,1)S(1)} %collective-permute-done.10.refs_4_) | copy-start | bytes 3145732

commit v3 on v1

--- a/solution.py
+++ b/solution.py
@@ -16,6 +16,8 @@
 WIDTH = HEADS * HEAD
 NEG = -1e30
 FIRST = 2
+TOP = 5
+GROUP = 8
 SCALE = HEAD**-0.5
 LOG2E = 1.4426950408889634
 MIB = 1 << 20
@@ -323,7 +325,7 @@
             pltpu.SemaphoreType.DMA((heads,)),
         ],
         compiler_params=pltpu.CompilerParams(vmem_limit_bytes=VMEM_CLAIM),
-        cost_estimate=pl.CostEstimate(flops=4_000_000_000, bytes_accessed=8 * MIB, transcendentals=2_000_000),
+        cost_estimate=pl.CostEstimate(flops=8_000_000_000, bytes_accessed=4 * MIB, transcendentals=0),
         name="near_levels",
     )(pool, queries, keys, values)
 
@@ -538,33 +540,28 @@
     position = lax.axis_index("seq")
     flags = jnp.stack([(position >> (level - FIRST)) & 1 for level in range(FIRST, levels + 1)]).astype(jnp.int32)
     pooled = pool_call(keys, values, levels)
+
     blocks = {}
-    for level in range(levels, FIRST - 1, -1):
-        distance = 1 << (level - FIRST)
-        blocks[level] = moved(pooled[level - FIRST], distance, distance)
-    high = list(range(5, levels + 1))
-    near = []
-    for index in range(SLICES):
-        source = after(queries, (near[-1], [blocks[level] for level in range(4, levels + 1)]) if near else pooled)
-        near.append(near_call(source, keys, values, levels, index))
-    rounds = [1 << bit for bit in range(1, levels - FIRST)]
-    for number, distance in enumerate(rounds):
-        members = [level for level in high if (1 << (level - FIRST)) > distance]
-        if members:
-            items = after([blocks[level] for level in members], near[min(number, SLICES - 1)])
-            for level, item in zip(members, gathered(items, distance)):
-                blocks[level] = item
-        if distance == 2:
-            blocks[4] = gathered([after(blocks[4], near[0])], 2)[0]
-    low = jnp.concatenate([after(blocks[3], near[SLICES - 1]), blocks[4]], axis=1)
+    for level in list(range(levels, TOP - 1, -1)) + [3, 4, 2]:
+        cross = 1 << (level - FIRST)
+        parts = max(cross // GROUP, 1)
+        pieces = [moved(pooled[level - FIRST], cross + GROUP * part, cross) for part in range(parts)]
+        blocks[level] = jnp.concatenate(pieces, axis=1) if parts > 1 else pieces[0]
+    high = list(range(TOP, levels + 1))
+
+    first = gathered([blocks[level] for level in high], 2)
+    near = [near_call(after(queries, [blocks[level] for level in high]), keys, values, levels, 0)]
+    second = gathered(after(first, near[0]), 4)
+    blocks[4] = gathered([after(blocks[4], near[0])], 2)[0]
+    near.append(near_call(after(queries, (near[0], first)), keys, values, levels, 1))
+    low = jnp.concatenate([after(blocks[3], near[0]), blocks[4]], axis=1)
     low_got = moved(low, 1)
-    top = jnp.concatenate([blocks[level] for level in high], axis=1)
+    top = jnp.concatenate(after(second, near[1]), axis=1)
     top_got = moved(top, 1)
     plan = [(2, 0, (0, 0, BLOCK))]
-    for place, level in enumerate((3, 4)):
-        plan += [(level, 1, (place * 128, 0, 128)), (level, 2, (place * 128, 128, 128))]
-    for place, level in enumerate(high):
-        plan += [(level, 3, (place * 128, 0, 128)), (level, 4, (place * 128, 128, 128))]
+    for number, members in ((1, (3, 4)), (3, high)):
+        for place, level in enumerate(members):
+            plan += [(level, number, (place * 128, 0, 128)), (level, number + 1, (place * 128, 128, 128))]
     return far_call(flags, [blocks[2], low, low_got, top, top_got], plan, near, w_out, levels)
 
 

time: 70.7 us -> 69.6 us (0.984)
  waiting for transfers between devices: 13 us -> 11.1 us
  starting transfers between devices: 21.4 us -> 22.2 us
    ppermute x11, waiting for transfers between devices: 13 us -> 11.1 us  [moved(): return lax.ppermute(array, 'seq', pairs)]
    ppermute x11, starting transfers between devices: 21.4 us -> 22.2 us  [moved(): return lax.ppermute(array, 'seq', pairs)]
  transfers between devices with their start and end apart: 11 -> 11, of which waited for: 4 -> 3; matrix products, arithmetic and copies ran while one was open for 2% -> 2% of each run, Pallas kernels for 20% -> 20%
where the time goes in v3:
time: 69.6 us; the launch traced here: 69.3 us
  Pallas kernels  33.9 us (49%)
  starting transfers between devices  22.2 us (32%)
  waiting for transfers between devices  11.1 us (16%)
  local copies, waits for them, and re-layouts  1.67 us (2%)
    ppermute x11, starting transfers between devices, moved(): return lax.ppermute(array, 'seq', pairs)  22.2 us
    pallas_call x1, Pallas kernels, far_call(): pl.pallas_call(functools.partial(far_kernel, levels, plan), in_specs=[pl....  15.1 us
    pallas_call x2, Pallas kernels, near_call(): pl.pallas_call(functools.partial(near_kernel, levels, index * heads), in_...  14.1 us
    ppermute x11, waiting for transfers between devices, moved(): return lax.ppermute(array, 'seq', pairs)  11.1 us
    pallas_call x1, Pallas kernels, pool_call(): pl.pallas_call(functools.partial(pool_kernel, levels), in_specs=[HBM] * 4...  4.69 us
  transfers between devices with their start and end apart: 11, of which 3 were waited for; matrix products, arithmetic and copies ran while one was open for 2% of the time, Pallas kernels for 20%

profile of v3, /device:TPU:0, one launch (start us, length us, event | category | flops | bytes accessed | tf_op | source)
XLA Modules:
  0.0 69.3 jit_solution(5740819657683264818)
XLA Ops:
  0.0 0.6 broadcast.1.large_ref
  0.6 4.7 %pool_keys_values.1 = (bf16[2,256,1024]{2,1,0:T(8,128)(2,1)}, bf16[2,128,1024]{2,1,0:T(8,128)(2,1)}, bf16[2,64,1024]{2,1,0:T(8,128)(2,1)}, bf16[2,32,1024]{2,1,0:T(8,128)(2,1)}, bf16[2,16,1024]{2,1,0:T(8,128)(2,1)}) custom-call(bf16[256,512]{1,0:T(8,128)(2,1)} %constant.26.small_ref, bf16[16,1024]{1,0:T(8,128)(2,1)} %broadcast.1.large_ref, ...), custom_call_target="tpu_custom_call" | custom-call | flops 1073741824 | bytes 6291456 | tf_op jit(solution)/shard_map/pool_keys_values/pallas_call | solution.py:140
  5.3 4.9 %collective-permute-start.2 = (bf16[2,32,1024]{2,1,0:T(8,128)(2,1)}, bf16[2,32,1024]{2,1,0:T(8,128)(2,1)S(1)}, u32[]{:S(2)}, u32[]{:S(2)}) collective-permute-start(bf16[2,32,1024]{2,1,0:T(8,128)(2,1)} %get-tuple-element.26), channel_id=1, source_target_pairs={{0,8},{1,9},{2,10},{3,11},{4,12},{5,13},{6,14},{7,15},{16,24},{17,... | collective-permute-start | bytes 393224 | tf_op jit(solution)/shard_map/ppermute | solution.py:519
  10.3 3.3 %collective-permute-start.7 = (bf16[2,16,1024]{2,1,0:T(8,128)(2,1)}, bf16[2,16,1024]{2,1,0:T(8,128)(2,1)S(1)}, u32[]{:S(2)}, u32[]{:S(2)}) collective-permute-start(bf16[2,16,1024]{2,1,0:T(8,128)(2,1)} %get-tuple-element.34), channel_id=1, source_target_pairs={{8,16},{9,17},{10,18},{11,19},{12,20},{13,21},{14,22},{15,23},{0,2... | collective-permute-start | bytes 196616 | tf_op jit(solution)/shard_map/ppermute | solution.py:519
  13.6 2.5 %collective-permute-start.6 = (bf16[2,16,1024]{2,1,0:T(8,128)(2,1)}, bf16[2,16,1024]{2,1,0:T(8,128)(2,1)S(1)}, u32[]{:S(2)}, u32[]{:S(2)}) collective-permute-start(bf16[2,16,1024]{2,1,0:T(8,128)(2,1)} %get-tuple-element.34), channel_id=1, source_target_pairs={{0,16},{1,17},{2,18},{3,19},{4,20},{5,21},{6,22},{7,23},{8,24},{9,... | collective-permute-start | bytes 196616 | tf_op jit(solution)/shard_map/ppermute | solution.py:519
  16.1 3.4 %collective-permute-start.3 = (bf16[2,64,1024]{2,1,0:T(8,128)(2,1)}, bf16[2,64,1024]{2,1,0:T(8,128)(2,1)S(1)}, u32[]{:S(2)}, u32[]{:S(2)}) collective-permute-start(bf16[2,64,1024]{2,1,0:T(8,128)(2,1)} %get-tuple-element.32), channel_id=1, source_target_pairs={{0,4},{1,5},{2,6},{3,7},{8,12},{9,13},{10,14},{11,15},{16,20},{17,... | collective-permute-start | bytes 786440 | tf_op jit(solution)/shard_map/ppermute | solution.py:519
  19.5 3.4 %collective-permute-start.1 = (bf16[2,128,1024]{2,1,0:T(8,128)(2,1)}, bf16[2,128,1024]{2,1,0:T(8,128)(2,1)S(1)}, u32[]{:S(2)}, u32[]{:S(2)}) collective-permute-start(bf16[2,128,1024]{2,1,0:T(8,128)(2,1)} %get-tuple-element.25), channel_id=1, source_target_pairs={{0,2},{1,3},{4,6},{5,7},{8,10},{9,11},{12,14},{13,15},{16,18},{17,... | collective-permute-start | bytes 1572872 | tf_op jit(solution)/shard_map/ppermute | solution.py:519
  22.9 0.0 collective-permute-done.2
  23.0 2.3 %collective-permute-start = (bf16[2,256,1024]{2,1,0:T(8,128)(2,1)}, bf16[2,256,1024]{2,1,0:T(8,128)(2,1)}, u32[]{:S(2)}, u32[]{:S(2)}) collective-permute-start(bf16[2,256,1024]{2,1,0:T(8,128)(2,1)} %get-tuple-element.24), channel_id=1, source_target_pairs={{0,1},{2,3},{4,5},{6,7},{8,9},{10,11},{12,13},{14,15},{16,17},{18,... | collective-permute-start | bytes 3145736 | tf_op jit(solution)/shard_map/ppermute | solution.py:519
  25.2 0.0 collective-permute-done.7
  25.2 0.0 collective-permute-done.6
  25.3 0.1 collective-permute-start.8
  25.3 7.1 %near_levels.2 = (f32[512,1024]{1,0:T(8,128)}, f32[4,8,1024]{2,1,0:T(8,128)}, bf16[768,512]{1,0:T(8,128)(2,1)}) custom-call(bf16[576,256]{1,0:T(8,128)(2,1)} %constant.28.pool_ref, bf16[1024,1024]{1,0:T(8,128)(2,1)} %q_ref.1, bf16[1024,1024]{1,0:T(8,128)(2,1)} %k_ref.3, bf16[1024,1024]{1,0:T(8,128)(2,1)} %v_ref.3), custom_call_target="tpu_custom_call" | custom-call | flops 8000000000 | bytes 4194304 | tf_op jit(solution)/shard_map/near_levels/pallas_call | solution.py:296
  32.4 0.0 collective-permute-done.3
  32.4 2.1 %collective-permute-start.4 = (bf16[2,64,1024]{2,1,0:T(8,128)(2,1)S(1)}, bf16[2,64,1024]{2,1,0:T(8,128)(2,1)S(1)}, u32[]{:S(2)}, u32[]{:S(2)}) collective-permute-start(bf16[2,64,1024]{2,1,0:T(8,128)(2,1)S(1)} %collective-permute-done.3), channel_id=1, source_target_pairs={{2,0},{3,1},{0,2},{1,3},{6,4},{7,5},{4,6},{5,7},{10,8},{11,9},{8,1... | collective-permute-start | bytes 786440 | tf_op jit(solution)/shard_map/ppermute | solution.py:519
  34.5 6.6 %collective-permute-done.8 = bf16[2,64,1024]{2,1,0:T(8,128)(2,1)S(1)} collective-permute-done((bf16[2,64,1024]{2,1,0:T(8,128)(2,1)S(1)}, bf16[2,64,1024]{2,1,0:T(8,128)(2,1)S(1)}, u32[]{:S(2)}, u32[]{:S(2)}) %collective-permute-start.8) | collective-permute-done | bytes 262176 | tf_op jit(solution)/shard_map/ppermute | solution.py:519
  41.2 0.1 collective-permute-start.9
  41.3 7.1 %near_levels.3 = (f32[512,1024]{1,0:T(8,128)}, f32[4,8,1024]{2,1,0:T(8,128)}, bf16[768,512]{1,0:T(8,128)(2,1)}) custom-call(bf16[576,256]{1,0:T(8,128)(2,1)} %constant.28.pool_ref, bf16[1024,1024]{1,0:T(8,128)(2,1)} %q_ref.1, bf16[1024,1024]{1,0:T(8,128)(2,1)} %k_ref.3, bf16[1024,1024]{1,0:T(8,128)(2,1)} %v_ref.3), custom_call_target="tpu_custom_call" | custom-call | flops 8000000000 | bytes 4194304 | tf_op jit(solution)/shard_map/near_levels/pallas_call | solution.py:296
  48.4 0.0 collective-permute-done.1
  48.4 0.0 collective-permute-done.4
  48.5 0.0 copy-start.1
  48.5 0.1 collective-permute-start.5
  48.6 2.6 %collective-permute-done.9 = bf16[2,128,1024]{2,1,0:T(8,128)(2,1)S(1)} collective-permute-done((bf16[2,128,1024]{2,1,0:T(8,128)(2,1)S(1)}, bf16[2,128,1024]{2,1,0:T(8,128)(2,1)S(1)}, u32[]{:S(2)}, u32[]{:S(2)}) %collective-permute-start.9) | collective-permute-done | bytes 524320 | tf_op jit(solution)/shard_map/ppermute | solution.py:519
  51.3 0.0 copy-done.1
  51.4 0.0 copy-start
  51.4 0.1 collective-permute-start.10
  51.5 0.8 %stack.23.flags_ref = s32[5]{0:T(128)} concatenate(s32[1]{0:T(128)} %bitcast, s32[1]{0:T(128)} %bitcast.1, s32[1]{0:T(128)} %bitcast.2, s32[1]{0:T(128)} %bitcast.3, s32[1]{0:T(128)} %bitcast.4), dimensions={0} | concatenate | bytes 40 | tf_op jit(solution)/shard_map/stack | solution.py:541
  52.3 0.0 collective-permute-done.refs_0_
  52.3 0.0 collective-permute-done.5.refs_2_
  52.3 1.9 %collective-permute-done.10.refs_4_ = bf16[2,256,1024]{2,1,0:T(8,128)(2,1)} collective-permute-done((bf16[2,256,1024]{2,1,0:T(8,128)(2,1)S(1)}, bf16[2,256,1024]{2,1,0:T(8,128)(2,1)}, u32[]{:S(2)}, u32[]{:S(2)}) %collective-permute-start.10) | collective-permute-done | bytes 1048608 | tf_op jit(solution)/shard_map/ppermute | solution.py:519
  54.2 0.0 copy-done
  54.2 15.1 %far_levels_projection.1 = bf16[1024,2048]{1,0:T(8,128)(2,1)} custom-call(s32[5]{0:T(128)} %stack.23.flags_ref, bf16[2,256,1024]{2,1,0:T(8,128)(2,1)} %collective-permute-done.refs_0_, bf16[2,256,1024]{2,1,0:T(8,128)(2,1)} %copy-done.1, bf16[2,256,1024]{2,1,0:T(8,128)(2,1)} %collective-permute-done.5.refs_2_, bf16[2,256,1024]{2,1,0:T(8,128)(2,1)} %copy-done, ...), custom_call_target="tpu_custom_call" | custom-call | flops 6499999744 | bytes 18874368 | tf_op jit(solution)/shard_map/far_levels_projection/pallas_call | solution.py:489
  (12 shorter events, 0.4 us)
Async XLA Ops:
  5.3 17.6 %collective-permute-start.2 = (bf16[2,32,1024]{2,1,0:T(8,128)(2,1)}, bf16[2,32,1024]{2,1,0:T(8,128)(2,1)S(1)}, u32[]{:S(2)}, u32[]{:S(2)}) collective-permute-start(bf16[2,32,1024]{2,1,0:T(8,128)(2,1)} %get-tuple-element.26), channel_id=1, source_target_pairs={{0,8},{1,9},{2,10},{3,11},{4,12},{5,13},{6,14},{7,15},{16,24},{17,... | collective-permute-start | bytes 393224 | tf_op jit(solution)/shard_map/ppermute | solution.py:519
  10.3 15.0 %collective-permute-start.7 = (bf16[2,16,1024]{2,1,0:T(8,128)(2,1)}, bf16[2,16,1024]{2,1,0:T(8,128)(2,1)S(1)}, u32[]{:S(2)}, u32[]{:S(2)}) collective-permute-start(bf16[2,16,1024]{2,1,0:T(8,128)(2,1)} %get-tuple-element.34), channel_id=1, source_target_pairs={{8,16},{9,17},{10,18},{11,19},{12,20},{13,21},{14,22},{15,23},{0,2... | collective-permute-start | bytes 196616 | tf_op jit(solution)/shard_map/ppermute | solution.py:519
  13.6 11.7 %collective-permute-start.6 = (bf16[2,16,1024]{2,1,0:T(8,128)(2,1)}, bf16[2,16,1024]{2,1,0:T(8,128)(2,1)S(1)}, u32[]{:S(2)}, u32[]{:S(2)}) collective-permute-start(bf16[2,16,1024]{2,1,0:T(8,128)(2,1)} %get-tuple-element.34), channel_id=1, source_target_pairs={{0,16},{1,17},{2,18},{3,19},{4,20},{5,21},{6,22},{7,23},{8,24},{9,... | collective-permute-start | bytes 196616 | tf_op jit(solution)/shard_map/ppermute | solution.py:519
  16.1 16.4 %collective-permute-start.3 = (bf16[2,64,1024]{2,1,0:T(8,128)(2,1)}, bf16[2,64,1024]{2,1,0:T(8,128)(2,1)S(1)}, u32[]{:S(2)}, u32[]{:S(2)}) collective-permute-start(bf16[2,64,1024]{2,1,0:T(8,128)(2,1)} %get-tuple-element.32), channel_id=1, source_target_pairs={{0,4},{1,5},{2,6},{3,7},{8,12},{9,13},{10,14},{11,15},{16,20},{17,... | collective-permute-start | bytes 786440 | tf_op jit(solution)/shard_map/ppermute | solution.py:519
  19.5 28.9 %collective-permute-start.1 = (bf16[2,128,1024]{2,1,0:T(8,128)(2,1)}, bf16[2,128,1024]{2,1,0:T(8,128)(2,1)S(1)}, u32[]{:S(2)}, u32[]{:S(2)}) collective-permute-start(bf16[2,128,1024]{2,1,0:T(8,128)(2,1)} %get-tuple-element.25), channel_id=1, source_target_pairs={{0,2},{1,3},{4,6},{5,7},{8,10},{9,11},{12,14},{13,15},{16,18},{17,... | collective-permute-start | bytes 1572872 | tf_op jit(solution)/shard_map/ppermute | solution.py:519
  23.0 29.4 %collective-permute-start = (bf16[2,256,1024]{2,1,0:T(8,128)(2,1)}, bf16[2,256,1024]{2,1,0:T(8,128)(2,1)}, u32[]{:S(2)}, u32[]{:S(2)}) collective-permute-start(bf16[2,256,1024]{2,1,0:T(8,128)(2,1)} %get-tuple-element.24), channel_id=1, source_target_pairs={{0,1},{2,3},{4,5},{6,7},{8,9},{10,11},{12,13},{14,15},{16,17},{18,... | collective-permute-start | bytes 3145736 | tf_op jit(solution)/shard_map/ppermute | solution.py:519
  25.3 15.8 %collective-permute-start.8 = (bf16[2,64,1024]{2,1,0:T(8,128)(2,1)S(1)}, bf16[2,64,1024]{2,1,0:T(8,128)(2,1)S(1)}, u32[]{:S(2)}, u32[]{:S(2)}) collective-permute-start(bf16[2,64,1024]{2,1,0:T(8,128)(2,1)S(1)} %fusion), channel_id=1, source_target_pairs={{2,0},{3,1},{0,2},{1,3},{6,4},{7,5},{4,6},{5,7},{10,8},{11,9},{8,1... | collective-permute-start | bytes 786440 | tf_op jit(solution)/shard_map/ppermute | solution.py:519
  32.4 16.0 %collective-permute-start.4 = (bf16[2,64,1024]{2,1,0:T(8,128)(2,1)S(1)}, bf16[2,64,1024]{2,1,0:T(8,128)(2,1)S(1)}, u32[]{:S(2)}, u32[]{:S(2)}) collective-permute-start(bf16[2,64,1024]{2,1,0:T(8,128)(2,1)S(1)} %collective-permute-done.3), channel_id=1, source_target_pairs={{2,0},{3,1},{0,2},{1,3},{6,4},{7,5},{4,6},{5,7},{10,8},{11,9},{8,1... | collective-permute-start | bytes 786440 | tf_op jit(solution)/shard_map/ppermute | solution.py:519
  41.2 9.9 %collective-permute-start.9 = (bf16[2,128,1024]{2,1,0:T(8,128)(2,1)S(1)}, bf16[2,128,1024]{2,1,0:T(8,128)(2,1)S(1)}, u32[]{:S(2)}, u32[]{:S(2)}) collective-permute-start(bf16[2,128,1024]{2,1,0:T(8,128)(2,1)S(1)} %pad_maximum_fusion), channel_id=1, source_target_pairs={{4,0},{5,1},{6,2},{7,3},{0,4},{1,5},{2,6},{3,7},{12,8},{13,9},{14,... | collective-permute-start | bytes 1572872 | tf_op jit(solution)/shard_map/ppermute | solution.py:519
  48.5 2.8 %copy-start.1 = (bf16[2,256,1024]{2,1,0:T(8,128)(2,1)}, bf16[2,256,1024]{2,1,0:T(8,128)(2,1)S(1)}, u32[]{:S(2)}) copy-start(bf16[2,256,1024]{2,1,0:T(8,128)(2,1)S(1)} %constant_dynamic-update-slice_fusion.refs_1_) | copy-start | bytes 3145732
  48.5 3.8 %collective-permute-start.5 = (bf16[2,256,1024]{2,1,0:T(8,128)(2,1)S(1)}, bf16[2,256,1024]{2,1,0:T(8,128)(2,1)}, u32[]{:S(2)}, u32[]{:S(2)}) collective-permute-start(bf16[2,256,1024]{2,1,0:T(8,128)(2,1)S(1)} %constant_dynamic-update-slice_fusion.refs_1_), channel_id=1, source_target_pairs={{1,0},{0,1},{3,2},{2,3},{5,4},{4,5},{7,6},{6,7},{9,8},{8,9},{11,10... | collective-permute-start | bytes 3145736 | tf_op jit(solution)/shard_map/ppermute | solution.py:519
  51.4 2.9 %copy-start = (bf16[2,256,1024]{2,1,0:T(8,128)(2,1)}, bf16[2,256,1024]{2,1,0:T(8,128)(2,1)S(1)}, u32[]{:S(2)}) copy-start(bf16[2,256,1024]{2,1,0:T(8,128)(2,1)S(1)} %constant_dynamic-update-slice_fusion.3.refs_3_) | copy-start | bytes 3145732
  51.4 2.9 %collective-permute-start.10 = (bf16[2,256,1024]{2,1,0:T(8,128)(2,1)S(1)}, bf16[2,256,1024]{2,1,0:T(8,128)(2,1)}, u32[]{:S(2)}, u32[]{:S(2)}) collective-permute-start(bf16[2,256,1024]{2,1,0:T(8,128)(2,1)S(1)} %constant_dynamic-update-slice_fusion.3.refs_3_), channel_id=1, source_target_pairs={{1,0},{0,1},{3,2},{2,3},{5,4},{4,5},{7,6},{6,7},{9,8},{8,9},{11,10... | collective-permute-start | bytes 3145736 | tf_op jit(solution)/shard_map/ppermute | solution.py:519

commit v4 on v3

v4 whole, which is shorter than its diff:
```python
import functools

import jax
import jax.numpy as jnp
import numpy as np
from jax import lax
from jax.experimental import pallas as pl
from jax.experimental.pallas import tpu as pltpu
from jax.sharding import PartitionSpec as P

HEADS = 8
HEAD = 128
BLOCK = 256
TOK = 1024
UNITS = TOK // BLOCK
WIDTH = HEADS * HEAD
NEG = -1e30
FIRST = 2
TOP = 5
GROUP = 8
SCALE = HEAD**-0.5
LOG2E = 1.4426950408889634
MIB = 1 << 20
SLICES = ((0, 3), (3, 3), (6, 2))
VMEM_CLAIM = 60 * MIB
HBM = pl.BlockSpec(memory_space=pltpu.HBM)


def token_of(position):
    return ((position & 31) << 3) | (((position >> 5) & 1) << 2) | (((position >> 6) & 1) << 1) | (position >> 7)


def count_of(level):
    return max(BLOCK >> level, 32)


def pool_rows(level):
    rows = token_of(np.arange(count_of(level))) >> level
    columns = np.arange(BLOCK) >> level
    return (rows[:, None] == columns[None, :]) * 2.0**-level


def natural_pool(level, span):
    rows = np.arange(span >> level)
    return (rows[:, None] == (np.arange(span) >> level)[None, :]) * 2.0**-level


def padded(array, multiple):
    return np.pad(array, ((0, -len(array) % multiple), (0, 0)))


def as_bf16(array):
    return jnp.asarray(array.astype(np.float32)).astype(jnp.bfloat16)


def dot(a, b):
    return jnp.dot(a, b, preferred_element_type=jnp.float32)


def dot_t(a, b):
    return lax.dot_general(a, b, (((1,), (1,)), ((), ())), preferred_element_type=jnp.float32)


def dot_first(a, b):
    return lax.dot_general(a, b, (((0,), (0,)), ((), ())), preferred_element_type=jnp.float32)


def merge(first, second):
    top = jnp.maximum(first[1], second[1])
    a = jnp.exp(first[1] - top)
    b = jnp.exp(second[1] - top)
    return (a * first[0] + b * second[0], top, a * first[2] + b * second[2])


ROWS = 64


def soft_columns(loads, targets):
    spans = [slice(start, start + ROWS) for start in range(0, BLOCK, ROWS)]
    peak = None
    for load in loads:
        for span in spans:
            rows = jnp.max(load(span).reshape(ROWS // 8, 8, HEAD), axis=0)
            peak = rows if peak is None else jnp.maximum(peak, rows)
    peak = jnp.max(peak, axis=0, keepdims=True)
    total = jnp.zeros((8, HEAD), jnp.float32)
    for load, target in zip(loads, targets):
        for span in spans:
            probs = jnp.exp2((load(span) - peak) * (SCALE * LOG2E))
            total = total + jnp.sum(probs.reshape(ROWS // 8, 8, HEAD), axis=0)
            target[span, :] = probs.astype(jnp.bfloat16)
    return peak * SCALE, jnp.sum(total, axis=0, keepdims=True)


def packed(levels):
    places, rows = {level: (level - FIRST, 0) for level in range(FIRST, TOP)}, 0
    for level in range(TOP, levels + 1):
        places[level] = (TOP - FIRST, rows)
        rows += TOK >> level
    return places, [TOK >> level for level in range(FIRST, TOP)] + [rows]


def pool_kernel(levels, small_ref, large_ref, keys_ref, values_ref, *refs):
    places, sizes = packed(levels)
    count = len(sizes)
    targets, (small, large, buffers, *outs, sems, out_sems) = refs[:count], refs[count:]
    step = WIDTH // 4
    fixed = [pltpu.make_async_copy(small_ref, small, sems.at[8]), pltpu.make_async_copy(large_ref, large, sems.at[9])]
    copies = []
    for index, source in enumerate((keys_ref, values_ref)):
        for part in range(4):
            cols = slice(part * step, (part + 1) * step)
            copies.append(pltpu.make_async_copy(source.at[:, cols], buffers.at[index, :, cols], sems.at[index * 4 + part]))
    for copy in fixed + copies:
        copy.start()
    for copy in fixed:
        copy.wait()
    sends = []
    for index in range(2):
        for part in range(4):
            cols = slice(part * step, (part + 1) * step)
            copies[index * 4 + part].wait()
            tiles = [
                dot(small[...], buffers[index, i * 2 * BLOCK : (i + 1) * 2 * BLOCK, cols]) for i in range(UNITS // 2)
            ]
            offset = 0
            for level in range(FIRST, min(levels, 6) + 1):
                rows = 2 * BLOCK >> level
                both = jnp.concatenate([tile[offset : offset + rows] for tile in tiles], axis=0)
                place, first = places[level]
                outs[place][index, first : first + 2 * rows, cols] = both.astype(jnp.bfloat16)
                offset += rows
            if levels > 6:
                rest = dot(large[...], buffers[index, :, cols])
                for level in range(7, levels + 1):
                    start = (level - 7) * 8
                    place, first = places[level]
                    outs[place][index, first : first + (TOK >> level), cols] = rest[start : start + (TOK >> level)].astype(jnp.bfloat16)
        for place, (out, target) in enumerate(zip(outs, targets)):
            sends.append(pltpu.make_async_copy(out.at[index], target.at[index], out_sems.at[index, place]))
            sends[-1].start()
    for send in sends:
        send.wait()


def pool_call(keys, values, levels):
    small = as_bf16(padded(np.concatenate([natural_pool(level, 2 * BLOCK) for level in range(FIRST, min(levels, 6) + 1)]), 16))
    parts = [padded(natural_pool(level, TOK), 8) for level in range(7, levels + 1)] + [np.zeros((8, TOK))]
    large = as_bf16(padded(np.concatenate(parts), 16))
    _, sizes = packed(levels)
    return pl.pallas_call(
        functools.partial(pool_kernel, levels),
        in_specs=[HBM] * 4,
        out_specs=[HBM] * len(sizes),
        out_shape=[jax.ShapeDtypeStruct((2, rows, WIDTH), jnp.bfloat16) for rows in sizes],
        scratch_shapes=[
            pltpu.VMEM(small.shape, jnp.bfloat16),
            pltpu.VMEM(large.shape, jnp.bfloat16),
            pltpu.VMEM((2, TOK, WIDTH), jnp.bfloat16),
        ]
        + [pltpu.VMEM((2, rows, WIDTH), jnp.bfloat16) for rows in sizes]
        + [
            pltpu.SemaphoreType.DMA((10,)),
            pltpu.SemaphoreType.DMA((2, len(sizes))),
        ],
        compiler_params=pltpu.CompilerParams(vmem_limit_bytes=VMEM_CLAIM),
        cost_estimate=pl.CostEstimate(flops=2 * 256 * 512 * 4096, bytes_accessed=6 * MIB, transcendentals=0),
        name="pool_keys_values",
    )(small, large, keys, values)


def far_offsets(levels):
    offsets, total = {}, 0
    for level in range(FIRST, levels + 1):
        offsets[level] = total
        total += UNITS * count_of(level)
    return offsets, total


def lane_block(index):
    return slice(index * HEAD, (index + 1) * HEAD)


def near_kernel(levels, first, heads, pool_ref, q_ref, k_ref, v_ref, num_out, stat_out, far_out, *scratch):
    (pool, q, k, v, num, stat, far, ordered, coarse_q, coarse_k, coarse_v, bias, scores_a, scores_b, scores_c) = scratch[:15]
    probs_a, probs_b, probs_c, sems, head_sems = scratch[15:]
    width = heads * HEAD
    cols = slice(first * HEAD, first * HEAD + width)
    copies = [
        pltpu.make_async_copy(pool_ref, pool, sems.at[0]),
        pltpu.make_async_copy(q_ref.at[:, cols], q, sems.at[1]),
        pltpu.make_async_copy(k_ref.at[:, cols], k, sems.at[2]),
        pltpu.make_async_copy(v_ref.at[:, cols], v, sems.at[3]),
    ]
    for copy in copies:
        copy.start()
    row = lax.broadcasted_iota(jnp.int32, (BLOCK, BLOCK), 0)
    position = lax.broadcasted_iota(jnp.int32, (BLOCK, BLOCK), 1)
    bias[...] = jnp.where(row <= token_of(position), 0.0, NEG)
    copies[0].wait()
    copies[1].wait()

    offsets, _ = far_offsets(levels)
    for unit in range(UNITS):
        pooled = dot(pool[...], q[unit * BLOCK : (unit + 1) * BLOCK, :])
        ordered[unit * BLOCK : (unit + 1) * BLOCK, :] = pooled[:BLOCK].astype(jnp.bfloat16)
        if unit >= 2:
            coarse_q[(unit - 2) * 128 : (unit - 1) * 128, :] = pooled[BLOCK : BLOCK + 128].astype(jnp.bfloat16)
        start = BLOCK + 128
        for level in range(FIRST, levels + 1):
            count = count_of(level)
            place = offsets[level] + unit * count
            far[place : place + count, :] = pooled[start : start + count].astype(jnp.bfloat16)
            start += count
    sends = [pltpu.make_async_copy(far, far_out, sems.at[4])]
    sends[0].start()
    copies[2].wait()
    copies[3].wait()
    for unit in range(2):
        rows = slice(unit * BLOCK, (unit + 1) * BLOCK)
        half = slice(unit * 128, (unit + 1) * 128)
        coarse_k[half, :] = dot(pool[BLOCK : BLOCK + 128, :], k[rows, :]).astype(jnp.bfloat16)
        coarse_v[half, :] = dot(pool[BLOCK : BLOCK + 128, :], v[rows, :]).astype(jnp.bfloat16)

    def num_copy(head, tile):
        rows = lane_block(head)
        lanes = slice(tile * 2 * BLOCK, (tile + 1) * 2 * BLOCK)
        return pltpu.make_async_copy(num.at[rows, lanes], num_out.at[rows, lanes], head_sems.at[head, tile])

    def dot_pieces(head):
        slot, own = head % 2, lane_block(head)

        def coarse():
            scores_c[slot] = dot_t(coarse_k[:, own], coarse_q[:, own])

        def part(tile, piece):
            base = 2 * tile * BLOCK
            if piece < 2:
                rows = slice(base + piece * BLOCK, base + (piece + 1) * BLOCK)
                scores_a[slot, tile, :, piece * BLOCK : (piece + 1) * BLOCK] = dot_t(
                    k[base : base + BLOCK, own], ordered[rows, own]
                )
            else:
                rows = slice(base + BLOCK, base + 2 * BLOCK)
                scores_b[slot, tile] = dot_t(k[rows, own], ordered[rows, own])

        return [coarse] + [functools.partial(part, tile, piece) for tile in (1, 0) for piece in range(3)]

    def soft_a(head, tile, block):
        slot, lanes = head % 2, lane_block(block)
        return soft_columns(
            [lambda span: scores_a[slot, tile, span, lanes] + bias[span, lanes]], [probs_a.at[slot, tile, :, lanes]]
        )

    def soft_b(head, tile, block):
        slot, lanes, late = head % 2, lane_block(block), lane_block(2 + block)
        return soft_columns(
            [
                lambda span: scores_a[slot, tile, span, late],
                lambda span: scores_b[slot, tile, span, lanes] + bias[span, lanes],
            ],
            [probs_a.at[slot, tile, :, late], probs_b.at[slot, tile, :, lanes]],
        )

    def soft_c(head, block):
        slot, lanes = head % 2, lane_block(block)
        return soft_columns([lambda span: scores_c[slot, span, lanes]], [probs_c.at[slot, :, lanes]])

    def weigh(head, tile):
        slot, own, base = head % 2, lane_block(head), 2 * tile * BLOCK
        both = dot_first(v[base : base + BLOCK, own], probs_a[slot, tile])
        more = dot_first(v[base + BLOCK : base + 2 * BLOCK, own], probs_b[slot, tile])
        nums = [both[:, lane_block(0)], both[:, lane_block(1)]]
        return nums + [both[:, lane_block(2 + block)] + more[:, lane_block(block)] for block in range(2)]

    def keep(head, tile, states):
        for index, state in enumerate(states):
            lanes = lane_block(4 * tile + index)
            num[lane_block(head), lanes] = state[0]
            stat[head, 0:1, lanes] = state[1]
            stat[head, 1:2, lanes] = state[2]
        num_copy(head, tile).start()

    def finish_late(head, nums, stats, coarse_num, coarse_stats):
        states = []
        for block in range(4):
            unit = block // 2
            coarse = (2.0 * coarse_num[:, lane_block(unit)], coarse_stats[unit][0], 2.0 * coarse_stats[unit][1])
            states.append(merge((nums[block],) + stats[block], coarse))
        keep(head, 1, states)

    for piece in dot_pieces(0):
        piece()
    pending = None
    for head in range(heads):
        pieces = dot_pieces(head + 1) if head + 1 < heads else []

        def more():
            if pieces:
                pieces.pop(0)()

        coarse_stats = [soft_c(head, 0)]
        more()
        if pending is not None:
            pending()
        coarse_stats.append(soft_c(head, 1))
        more()
        coarse_num = dot_first(coarse_v[:, lane_block(head)], probs_c[head % 2])
        late_stats = []
        for block in range(2):
            late_stats.append(soft_a(head, 1, block))
            more()
        for block in range(2):
            late_stats.append(soft_b(head, 1, block))
            more()
        nums = weigh(head, 1)
        stats = [soft_a(head, 0, 0)]
        more()
        stats.append(soft_a(head, 0, 1))
        finish_late(head, nums, late_stats, coarse_num, coarse_stats)
        for block in range(2):
            stats.append(soft_b(head, 0, block))

        def pending(head=head, stats=stats):
            keep(head, 0, [(item,) + pair for item, pair in zip(weigh(head, 0), stats)])

    pending()
    sends.append(pltpu.make_async_copy(stat, stat_out, sems.at[5]))
    sends[-1].start()
    for send in sends:
        send.wait()
    for head in range(heads):
        for tile in range(2):
            num_copy(head, tile).wait()


def near_call(queries, keys, values, levels, index):
    pool = as_bf16(padded(np.concatenate([pool_rows(level) for level in range(levels + 1)]), 16))
    first, heads = SLICES[index]
    width = heads * HEAD
    _, far_rows = far_offsets(levels)
    bf16, f32 = jnp.bfloat16, jnp.float32
    return pl.pallas_call(
        functools.partial(near_kernel, levels, first, heads),
        in_specs=[HBM] * 4,
        out_specs=[HBM] * 3,
        out_shape=[
            jax.ShapeDtypeStruct((width, TOK), f32),
            jax.ShapeDtypeStruct((heads, 8, TOK), f32),
            jax.ShapeDtypeStruct((far_rows, width), bf16),
        ],
        scratch_shapes=[
            pltpu.VMEM(pool.shape, bf16),
            pltpu.VMEM((TOK, width), bf16),
            pltpu.VMEM((TOK, width), bf16),
            pltpu.VMEM((TOK, width), bf16),
            pltpu.VMEM((width, TOK), f32),
            pltpu.VMEM((heads, 8, TOK), f32),
            pltpu.VMEM((far_rows, width), bf16),
            pltpu.VMEM((TOK, width), bf16),
            pltpu.VMEM((BLOCK, width), bf16),
            pltpu.VMEM((BLOCK, width), bf16),
            pltpu.VMEM((BLOCK, width), bf16),
            pltpu.VMEM((BLOCK, BLOCK), f32),
            pltpu.VMEM((2, 2, BLOCK, 2 * BLOCK), f32),
            pltpu.VMEM((2, 2, BLOCK, BLOCK), f32),
            pltpu.VMEM((2, BLOCK, BLOCK), f32),
            pltpu.VMEM((2, 2, BLOCK, 2 * BLOCK), bf16),
            pltpu.VMEM((2, 2, BLOCK, BLOCK), bf16),
            pltpu.VMEM((2, BLOCK, BLOCK), bf16),
            pltpu.SemaphoreType.DMA((6,)),
            pltpu.SemaphoreType.DMA((heads, 2)),
        ],
        compiler_params=pltpu.CompilerParams(vmem_limit_bytes=VMEM_CLAIM),
        cost_estimate=pl.CostEstimate(flops=8_000_000_000, bytes_accessed=4 * MIB, transcendentals=0),
        name="near_levels",
    )(pool, queries, keys, values)


def by_lane_group(arrays, size):
    lane = lax.broadcasted_iota(jnp.int32, arrays[0].shape, 1)
    result = arrays[-1]
    for index in range(len(arrays) - 2, -1, -1):
        result = jnp.where(lane < (index + 1) * size, arrays[index], result)
    return result


def widen_to_second(array):
    r32, r64, r96 = [pltpu.roll(array, shift, 1) for shift in (32, 64, 96)]
    return [by_lane_group([array, r32, r32, r64], 32), by_lane_group([r64, r96, r96, array], 32)]


def widen_to_units(arrays):
    units = []
    for array in arrays:
        turned = pltpu.roll(array, 64, 1)
        units += [by_lane_group([array, turned], 64), by_lane_group([turned, array], 64)]
    return units


def far_kernel(levels, plan, flags_ref, *refs):
    crossing = range(FIRST, levels + 1)
    bundles = 1 + max(bundle for _, bundle, _ in plan)
    kv_refs = refs[:bundles]
    refs = refs[bundles:]
    slices = len(SLICES)
    far_refs, num_refs, stat_refs = refs[:slices], refs[slices : 2 * slices], refs[2 * slices : 3 * slices]
    turn_ref, w_ref, out_ref = refs[3 * slices : 3 * slices + 3]
    kv, queries, num, stat, turn, weights, scores, probs = refs[3 * slices + 3 : 3 * slices + 11]
    mixed, natural, stage, kv_sems, near_sems, out_sems = refs[3 * slices + 11 :]
    pair = 2 * HEAD
    model = w_ref.shape[1]
    step = 512
    offsets, far_rows = far_offsets(levels)

    def kv_copies(index):
        cols = slice(index * pair, (index + 1) * pair)
        made = []
        for number, (level, bundle, spans) in enumerate(plan):
            source_start, target_start, rows = spans
            made.append(
                pltpu.make_async_copy(
                    kv_refs[bundle].at[:, source_start : source_start + rows, cols],
                    kv.at[level - FIRST, :, target_start : target_start + rows, cols],
                    kv_sems.at[index, number],
                )
            )
        return made

    far_copies, near_copies = [], []
    for index, (first, heads) in enumerate(SLICES):
        cols = slice(first * HEAD, (first + heads) * HEAD)
        group = slice(first, first + heads)
        sems = [near_sems.at[place * slices + index] for place in range(3)]
        far_copies.append(pltpu.make_async_copy(far_refs[index], queries.at[:, cols], sems[0]))
        near_copies.append(
            [
                pltpu.make_async_copy(num_refs[index], num.at[cols, :], sems[1]),
                pltpu.make_async_copy(stat_refs[index], stat.at[group], sems[2]),
            ]
        )
    last_copies = [
        pltpu.make_async_copy(turn_ref, turn, near_sems.at[3 * slices]),
        pltpu.make_async_copy(w_ref, weights, near_sems.at[3 * slices + 1]),
    ]
    for copy in far_copies + kv_copies(0) + kv_copies(1) + near_copies[0]:
        copy.start()
    for index in range(2, HEADS // 2):
        for copy in kv_copies(index):
            copy.start()
    for copies in near_copies[1:]:
        for copy in copies:
            copy.start()
    for copy in last_copies:
        copy.start()

    def score(head, level):
        own = lane_block(head)
        span = slice(offsets[level], offsets[level] + UNITS * count_of(level))
        scores[head % 2, :, span] = dot_t(kv[level - FIRST, 0, :, own], queries[span, own])

    def soft(head, level):
        blocks = range(offsets[level] // HEAD, (offsets[level] + UNITS * count_of(level)) // HEAD)
        return [
            soft_columns(
                [lambda span, block=block: scores[head % 2, span, lane_block(block)]], [probs.at[head % 2, :, lane_block(block)]]
            )
            for block in blocks
        ]

    def weigh(head, level, stats):
        own = lane_block(head)
        span = slice(offsets[level], offsets[level] + UNITS * count_of(level))
        live = flags_ref[level - FIRST] == 1
        factor = jnp.where(live, 2.0**level, 0.0)
        weighted = factor * dot_first(kv[level - FIRST, 1, :, own], probs[head % 2, :, span])
        return [
            (weighted[:, lane_block(block)], jnp.where(live, peak, NEG), factor * total)
            for block, (peak, total) in enumerate(stats)
        ]

    def join(state, terms):
        if state is None:
            return terms
        if len(terms) > len(state):
            wide = [widen_to_second(item) for item in state[0]]
            state = [tuple(item[side] for item in wide) for side in range(2)]
        return [merge(old, new) for old, new in zip(state, terms)]

    def mix(head, state):
        own = lane_block(head)
        wide = [widen_to_units([half[place] for half in state]) for place in range(3)]
        for unit in range(UNITS):
            far_num, far_peak, far_total = [item[unit] for item in wide]
            for block in range(2 * unit, 2 * unit + 2):
                peak = stat[head, 0:1, lane_block(block)]
                total = stat[head, 1:2, lane_block(block)]
                top = jnp.maximum(peak, far_peak)
                a = jnp.exp(peak - top)
                b = jnp.exp(far_peak - top)
                inverse = 1.0 / (a * total + b * far_total)
                both = (a * inverse) * num[own, lane_block(block)] + (b * inverse) * far_num
                mixed[own, lane_block(block)] = both.astype(jnp.bfloat16)

    order = list(range(levels, FIRST - 1, -1))
    for copy in far_copies + kv_copies(0):
        copy.wait()
    for level in order:
        score(0, level)
    for copy in near_copies[0]:
        copy.wait()
    pending = None
    for head in range(HEADS):
        if head % 2 == 1 and head + 1 < HEADS:
            for copy in kv_copies((head + 1) // 2):
                copy.wait()
        for index, (first, _) in enumerate(SLICES):
            if index and first == head:
                for copy in near_copies[index]:
                    copy.wait()
        terms = []
        for level in order:
            stats = soft(head, level)
            if head + 1 < HEADS:
                score(head + 1, level)
            if level == order[0] and pending is not None:
                pending()
            terms.append(weigh(head, level, stats))

        def pending(head=head, terms=terms):
            mix(head, functools.reduce(join, terms, None))

    pending()

    for copy in last_copies:
        copy.wait()
    for unit in range(UNITS):
        rows = slice(unit * BLOCK, (unit + 1) * BLOCK)
        natural[rows, :] = dot_t(turn[...], mixed[:, rows]).astype(jnp.bfloat16)
    sends = []
    for index in range(model // step):
        cols = slice(index * step, (index + 1) * step)
        stage[:, cols] = dot(natural[...], weights[:, cols]).astype(jnp.bfloat16)
        sends.append(pltpu.make_async_copy(stage.at[:, cols], out_ref.at[:, cols], out_sems.at[index]))
        sends[-1].start()
    for send in sends:
        send.wait()


def far_call(flags, bundles, plan, near, w_out, levels):
    turn = np.zeros((BLOCK, BLOCK))
    turn[token_of(np.arange(BLOCK)), np.arange(BLOCK)] = 1.0
    nums, stats, fars = [[item[place] for item in near] for place in range(3)]
    model = w_out.shape[1]
    _, far_rows = far_offsets(levels)
    count = levels - FIRST + 1
    bf16, f32 = jnp.bfloat16, jnp.float32
    return pl.pallas_call(
        functools.partial(far_kernel, levels, plan),
        in_specs=[pl.BlockSpec(memory_space=pltpu.SMEM)] + [HBM] * (len(bundles) + 3 * len(SLICES) + 2),
        out_specs=HBM,
        out_shape=jax.ShapeDtypeStruct((TOK, model), bf16),
        scratch_shapes=[
            pltpu.VMEM((count, 2, BLOCK, WIDTH), bf16),
            pltpu.VMEM((far_rows, WIDTH), bf16),
            pltpu.VMEM((WIDTH, TOK), f32),
            pltpu.VMEM((HEADS, 8, TOK), f32),
            pltpu.VMEM((BLOCK, BLOCK), bf16),
            pltpu.VMEM((WIDTH, model), bf16),
            pltpu.VMEM((2, BLOCK, far_rows), f32),
            pltpu.VMEM((2, BLOCK, far_rows), bf16),
            pltpu.VMEM((WIDTH, TOK), bf16),
            pltpu.VMEM((TOK, WIDTH), bf16),
            pltpu.VMEM((TOK, model), bf16),
            pltpu.SemaphoreType.DMA((HEADS // 2, len(plan))),
            pltpu.SemaphoreType.DMA((3 * len(SLICES) + 2,)),
            pltpu.SemaphoreType.DMA((model // 512,)),
        ],
        compiler_params=pltpu.CompilerParams(vmem_limit_bytes=VMEM_CLAIM),
        cost_estimate=pl.CostEstimate(flops=6_500_000_000, bytes_accessed=18 * MIB, transcendentals=3_000_000),
        name="far_levels_projection",
    )(flags, *bundles, *fars, *nums, *stats, as_bf16(turn), w_out)


def moved(array, distance, upper_of=0):
    size = lax.axis_size("seq")
    pairs = [(i ^ distance, i) for i in range(size) if not upper_of or i & upper_of]
    return lax.ppermute(array, "seq", pairs)


def gathered(blocks, distance):
    sent = jnp.concatenate(blocks, axis=1) if len(blocks) > 1 else blocks[0]
    got = moved(sent, distance)
    joined, start = [], 0
    for block in blocks:
        rows = block.shape[1]
        joined.append(jnp.concatenate([block, got[:, start : start + rows]], axis=1))
        start += rows
    return joined


def after(arrays, others):
    return lax.optimization_barrier((arrays, others))[0]


def on_device(queries, keys, values, w_out):
    size = lax.axis_size("seq")
    levels = (TOK * size // (2 * BLOCK)).bit_length() - 1
    position = lax.axis_index("seq")
    flags = jnp.stack([(position >> (level - FIRST)) & 1 for level in range(FIRST, levels + 1)]).astype(jnp.int32)
    pooled = pool_call(keys, values, levels)

    places, _ = packed(levels)
    blocks = {level: pooled[level - FIRST] for level in range(FIRST, TOP)}
    for level in range(TOP, levels + 1):
        place, first = places[level]
        blocks[level] = pooled[place][:, first : first + (TOK >> level)]
    high = list(range(TOP, levels + 1))

    for distance in [1 << (level - FIRST) for level in high]:
        members = [level for level in high if 1 << (level - FIRST) >= distance]
        sent = pooled[-1] if distance == GROUP else jnp.concatenate([blocks[level] for level in members], axis=1)
        got = moved(sent, distance, distance if len(members) == 1 else 0)
        start = 0
        for level in members:
            rows = blocks[level].shape[1]
            piece = got[:, start : start + rows]
            start += rows
            if 1 << (level - FIRST) == distance:
                blocks[level] = piece
            else:
                blocks[level] = jnp.concatenate([blocks[level], piece], axis=1)
        if distance == GROUP:
            fourth = moved(blocks[4], 4, 4)
            third = moved(blocks[3], 2, 2)
            second = moved(blocks[2], 1, 1)
            arrived = blocks[TOP]

    upper = [blocks[level] for level in high[1:]]
    five = gathered([arrived], 2)
    near = [near_call(after(queries, arrived), keys, values, levels, 0)]
    upper = gathered(after(upper, near[0]), 4)
    five_y = gathered(after(five, near[0]), 4)
    fourth = gathered([after(fourth, near[0])], 2)[0]
    near.append(near_call(after(queries, (near[0], five)), keys, values, levels, 1))
    upper_x = gathered(after(upper, near[1]), 2)
    low = jnp.concatenate([after(third, near[1]), fourth], axis=1)
    low_got = moved(low, 1)
    near.append(near_call(after(queries, (near[1], upper, five_y)), keys, values, levels, 2))
    top = jnp.concatenate(after(five_y + upper_x, near[2]), axis=1)
    top_got = moved(top, 1)
    plan = [(2, 4, (0, 0, BLOCK))]
    for level in (3, 4):
        plan += [(level, bundle, ((level - 3) * 128, bundle * 128, 128)) for bundle in (0, 1)]
    for level in high:
        plan += [(level, bundle, ((level - TOP) * 128, (bundle - 2) * 128, 128)) for bundle in (2, 3)]
    return far_call(flags, [low, low_got, top, top_got, second], plan, near, w_out, levels)


def solution(mesh):
    return jax.shard_map(
        on_device,
        mesh=mesh,
        in_specs=(P("seq", None), P("seq", None), P("seq", None), P()),
        out_specs=P("seq", None),
        check_vma=False,
    )
```

time: 69.6 us -> 63.5 us (0.912)
  waiting for transfers between devices: 11.1 us -> 1.76 us
  local copies, waits for them, and re-layouts: 1.67 us -> 3.43 us
  starting transfers between devices: 22.2 us -> 23.1 us
    ppermute x11 -> x12, waiting for transfers between devices: 11.1 us -> 1.76 us  [moved(): return lax.ppermute(array, 'seq', pairs)]
    unnamed x7 -> x11, local copies, waits for them, and re-layouts: 0.1 us -> 1.17 us
    pallas_call x2 -> x3, Pallas kernels: 14.1 us -> 15.1 us  [near_call(): pl.pallas_call(functools.partial(near_kernel, levels, first, heads), in_s...]
    ppermute x11 -> x12, starting transfers between devices: 22.2 us -> 23.1 us  [moved(): return lax.ppermute(array, 'seq', pairs)]
    slice x2 -> x3, local copies, waits for them, and re-layouts: 0.05 us -> 0.86 us  [the longest x1 0.84 us: on_device(): blocks[level] = pooled[place][:, first:first + (TOK >> level)]]
  transfers between devices with their start and end apart: 11 -> 12, of which waited for: 3 -> 1; matrix products, arithmetic and copies ran while one was open for 2% -> 3% of each run, Pallas kernels for 20% -> 24%
where the time goes in v4:
time: 63.5 us; the launch traced here: 63.2 us
  Pallas kernels  34.4 us (54%)
  starting transfers between devices  23.1 us (36%)
  local copies, waits for them, and re-layouts  3.43 us (5%)
  waiting for transfers between devices  1.76 us (3%)
    ppermute x12, starting transfers between devices, moved(): return lax.ppermute(array, 'seq', pairs)  23.1 us
    pallas_call x3, Pallas kernels, near_call(): pl.pallas_call(functools.partial(near_kernel, levels, first, heads), in_s...  15.1 us
    pallas_call x1, Pallas kernels, far_call(): pl.pallas_call(functools.partial(far_kernel, levels, plan), in_specs=[pl....  14.6 us
    pallas_call x1, Pallas kernels, pool_call(): pl.pallas_call(functools.partial(pool_kernel, levels), in_specs=[HBM] * 4...  4.68 us
    ppermute x12, waiting for transfers between devices, moved(): return lax.ppermute(array, 'seq', pairs)  1.76 us
  transfers between devices with their start and end apart: 12, of which 1 were waited for; matrix products, arithmetic and copies ran while one was open for 3% of the time, Pallas kernels for 24%

profile of v4, /device:TPU:0, one launch (start us, length us, event | category | flops | bytes accessed | tf_op | source)
XLA Modules:
  0.0 63.2 jit_solution(15512140150329638092)
XLA Ops:
  0.0 0.6 broadcast.1.large_ref
  0.6 4.7 %pool_keys_values.1 = (bf16[2,256,1024]{2,1,0:T(8,128)(2,1)}, bf16[2,128,1024]{2,1,0:T(8,128)(2,1)}, bf16[2,64,1024]{2,1,0:T(8,128)(2,1)}, bf16[2,48,1024]{2,1,0:T(8,128)(2,1)}) custom-call(bf16[256,512]{1,0:T(8,128)(2,1)} %constant.26.small_ref, bf16[16,1024]{1,0:T(8,128)(2,1)} %broadcast.1.large_ref, bf16[1024,1024]{1,0:T(8,128)(2,1)} %k_ref.5, ...), custom_call_target="tpu_custom_call" | custom-call | flops 1073741824 | bytes 6291456 | tf_op jit(solution)/shard_map/pool_keys_values/pallas_call | solution.py:151
  5.3 3.1 %collective-permute-start.1 = (bf16[2,48,1024]{2,1,0:T(8,128)(2,1)}, bf16[2,48,1024]{2,1,0:T(8,128)(2,1)S(1)}, u32[]{:S(2)}, u32[]{:S(2)}) collective-permute-start(bf16[2,48,1024]{2,1,0:T(8,128)(2,1)} %get-tuple-element.29), channel_id=1, source_target_pairs={{8,0},{9,1},{10,2},{11,3},{12,4},{13,5},{14,6},{15,7},{0,8},{1,9},... | collective-permute-start | bytes 589832 | tf_op jit(solution)/shard_map/ppermute | solution.py:588
  8.4 3.4 %collective-permute-start.3 = (bf16[2,64,1024]{2,1,0:T(8,128)(2,1)}, bf16[2,64,1024]{2,1,0:T(8,128)(2,1)S(1)}, u32[]{:S(2)}, u32[]{:S(2)}) collective-permute-start(bf16[2,64,1024]{2,1,0:T(8,128)(2,1)} %get-tuple-element.39), channel_id=1, source_target_pairs={{0,4},{1,5},{2,6},{3,7},{8,12},{9,13},{10,14},{11,15},{16,20},{17,... | collective-permute-start | bytes 786440 | tf_op jit(solution)/shard_map/ppermute | solution.py:588
  11.8 3.4 %collective-permute-start = (bf16[2,128,1024]{2,1,0:T(8,128)(2,1)}, bf16[2,128,1024]{2,1,0:T(8,128)(2,1)S(1)}, u32[]{:S(2)}, u32[]{:S(2)}) collective-permute-start(bf16[2,128,1024]{2,1,0:T(8,128)(2,1)} %get-tuple-element.28), channel_id=1, source_target_pairs={{0,2},{1,3},{4,6},{5,7},{8,10},{9,11},{12,14},{13,15},{16,18},{17,... | collective-permute-start | bytes 1572872 | tf_op jit(solution)/shard_map/ppermute | solution.py:588
  15.3 2.3 %collective-permute-start.11 = (bf16[2,256,1024]{2,1,0:T(8,128)(2,1)}, bf16[2,256,1024]{2,1,0:T(8,128)(2,1)}, u32[]{:S(2)}, u32[]{:S(2)}) collective-permute-start(bf16[2,256,1024]{2,1,0:T(8,128)(2,1)} %get-tuple-element.50), channel_id=1, source_target_pairs={{0,1},{2,3},{4,5},{6,7},{8,9},{10,11},{12,13},{14,15},{16,17},{18,... | collective-permute-start | bytes 3145736 | tf_op jit(solution)/shard_map/ppermute | solution.py:588
  17.6 0.8 %slice.10 = bf16[2,16,1024]{2,1,0:T(8,128)(2,1)S(1)} slice(bf16[2,48,1024]{2,1,0:T(8,128)(2,1)} %get-tuple-element.29), slice={[0:2], [32:48], [0:1024]} | slice | bytes 131072 | tf_op jit(solution)/shard_map/slice | solution.py:617
  18.4 0.0 collective-permute-done.1
  18.4 0.1 collective-permute-start.2
  18.5 4.5 %collective-permute-start.7 = (bf16[2,32,1024]{2,1,0:T(8,128)(2,1)S(1)}, bf16[2,32,1024]{2,1,0:T(8,128)(2,1)S(1)}, u32[]{:S(2)}, u32[]{:S(2)}) collective-permute-start(bf16[2,32,1024]{2,1,0:T(8,128)(2,1)S(1)} %pad_maximum_fusion.2), channel_id=1, source_target_pairs={{0,16},{1,17},{2,18},{3,19},{4,20},{5,21},{6,22},{7,23},{8,24},{9,... | collective-permute-start | bytes 393224 | tf_op jit(solution)/shard_map/ppermute | solution.py:588
  23.1 5.3 %near_levels.3 = (f32[384,1024]{1,0:T(8,128)}, f32[3,8,1024]{2,1,0:T(8,128)}, bf16[768,384]{1,0:T(8,128)(2,1)}) custom-call(bf16[576,256]{1,0:T(8,128)(2,1)} %constant.28.pool_ref, bf16[1024,1024]{1,0:T(8,128)(2,1)} %q_ref.2, bf16[1024,1024]{1,0:T(8,128)(2,1)} %k_ref.5, bf16[1024,1024]{1,0:T(8,128)(2,1)} %v_ref.5), custom_call_target="tpu_custom_call" | custom-call | flops 8000000000 | bytes 4194304 | tf_op jit(solution)/shard_map/near_levels/pallas_call | solution.py:343
  28.3 0.0 collective-permute-done.3
  28.4 2.1 %collective-permute-start.4 = (bf16[2,64,1024]{2,1,0:T(8,128)(2,1)S(1)}, bf16[2,64,1024]{2,1,0:T(8,128)(2,1)S(1)}, u32[]{:S(2)}, u32[]{:S(2)}) collective-permute-start(bf16[2,64,1024]{2,1,0:T(8,128)(2,1)S(1)} %collective-permute-done.3), channel_id=1, source_target_pairs={{2,0},{3,1},{0,2},{1,3},{6,4},{7,5},{4,6},{5,7},{10,8},{11,9},{8,1... | collective-permute-start | bytes 786440 | tf_op jit(solution)/shard_map/ppermute | solution.py:588
  30.4 0.0 collective-permute-done.2
  30.4 0.0 collective-permute-done.7
  30.5 0.1 collective-permute-start.8
  30.5 2.0 %collective-permute-start.6 = (bf16[2,64,1024]{2,1,0:T(8,128)(2,1)S(1)}, bf16[2,64,1024]{2,1,0:T(8,128)(2,1)S(1)}, u32[]{:S(2)}, u32[]{:S(2)}) collective-permute-start(bf16[2,64,1024]{2,1,0:T(8,128)(2,1)S(1)} %pad_maximum_fusion.1), channel_id=1, source_target_pairs={{4,0},{5,1},{6,2},{7,3},{0,4},{1,5},{2,6},{3,7},{12,8},{13,9},{14,... | collective-permute-start | bytes 786440 | tf_op jit(solution)/shard_map/ppermute | solution.py:588
  32.5 5.3 %near_levels.4 = (f32[384,1024]{1,0:T(8,128)}, f32[3,8,1024]{2,1,0:T(8,128)}, bf16[768,384]{1,0:T(8,128)(2,1)}) custom-call(bf16[576,256]{1,0:T(8,128)(2,1)} %constant.28.pool_ref, bf16[1024,1024]{1,0:T(8,128)(2,1)} %q_ref.2, bf16[1024,1024]{1,0:T(8,128)(2,1)} %k_ref.5, bf16[1024,1024]{1,0:T(8,128)(2,1)} %v_ref.5), custom_call_target="tpu_custom_call" | custom-call | flops 8000000000 | bytes 4194304 | tf_op jit(solution)/shard_map/near_levels/pallas_call | solution.py:343
  37.9 0.0 collective-permute-done.8
  37.9 1.8 %collective-permute-start.9 = (bf16[2,64,1024]{2,1,0:T(8,128)(2,1)S(1)}, bf16[2,64,1024]{2,1,0:T(8,128)(2,1)S(1)}, u32[]{:S(2)}, u32[]{:S(2)}) collective-permute-start(bf16[2,64,1024]{2,1,0:T(8,128)(2,1)S(1)} %constant_dynamic-update-slice_fusion.5), channel_id=1, source_target_pairs={{2,0},{3,1},{0,2},{1,3},{6,4},{7,5},{4,6},{5,7},{10,8},{11,9},{8,1... | collective-permute-start | bytes 786440 | tf_op jit(solution)/shard_map/ppermute | solution.py:588
  39.7 0.0 collective-permute-done
  39.8 0.0 collective-permute-done.4
  39.8 0.0 copy-start.1
  39.8 0.1 collective-permute-start.5
  39.9 0.0 collective-permute-done.6
  40.0 4.5 %near_levels.5 = (f32[256,1024]{1,0:T(8,128)}, f32[2,8,1024]{2,1,0:T(8,128)}, bf16[768,256]{1,0:T(8,128)(2,1)}) custom-call(bf16[576,256]{1,0:T(8,128)(2,1)} %constant.28.pool_ref, bf16[1024,1024]{1,0:T(8,128)(2,1)} %q_ref.2, bf16[1024,1024]{1,0:T(8,128)(2,1)} %k_ref.5, bf16[1024,1024]{1,0:T(8,128)(2,1)} %v_ref.5), custom_call_target="tpu_custom_call" | custom-call | flops 8000000000 | bytes 4194304 | tf_op jit(solution)/shard_map/near_levels/pallas_call | solution.py:343
  44.5 0.0 copy-done.1
  44.5 0.0 collective-permute-done.9
  44.6 0.0 copy-start
  44.6 0.3 collective-permute-start.10
  44.9 0.7 %stack.23.flags_ref = s32[5]{0:T(128)} concatenate(s32[1]{0:T(128)} %bitcast, s32[1]{0:T(128)} %bitcast.1, s32[1]{0:T(128)} %bitcast.2, s32[1]{0:T(128)} %bitcast.3, s32[1]{0:T(128)} %bitcast.4), dimensions={0} | concatenate | bytes 40 | tf_op jit(solution)/shard_map/stack | solution.py:610
  45.6 0.0 collective-permute-done.11.refs_4_
  45.6 0.0 collective-permute-done.5.refs_1_
  45.6 1.7 %collective-permute-done.10.refs_3_ = bf16[2,256,1024]{2,1,0:T(8,128)(2,1)S(1)} collective-permute-done((bf16[2,256,1024]{2,1,0:T(8,128)(2,1)S(1)}, bf16[2,256,1024]{2,1,0:T(8,128)(2,1)S(1)}, u32[]{:S(2)}, u32[]{:S(2)}) %collective-permute-start.10) | collective-permute-done | bytes 1048608 | tf_op jit(solution)/shard_map/ppermute | solution.py:588
  47.4 0.0 copy-done
  47.4 0.0 copy-start.2
  47.4 1.0 %copy-done.2 = bf16[2,256,1024]{2,1,0:T(8,128)(2,1)} copy-done((bf16[2,256,1024]{2,1,0:T(8,128)(2,1)}, bf16[2,256,1024]{2,1,0:T(8,128)(2,1)S(1)}, u32[]{:S(2)}) %copy-start.2) | copy-done | bytes 1048600
  48.4 14.6 %far_levels_projection.1 = bf16[1024,2048]{1,0:T(8,128)(2,1)} custom-call(s32[5]{0:T(128)} %stack.23.flags_ref, bf16[2,256,1024]{2,1,0:T(8,128)(2,1)} %copy-done.1, bf16[2,256,1024]{2,1,0:T(8,128)(2,1)} %collective-permute-done.5.refs_1_, bf16[2,256,1024]{2,1,0:T(8,128)(2,1)} %copy-done, bf16[2,256,1024]{2,1,0:T(8,128)(2,1)} %copy-done.2, ...), custom_call_target="tpu_custom_call" | custom-call | flops 6499999744 | bytes 18874368 | tf_op jit(solution)/shard_map/far_levels_projection/pallas_call | solution.py:558
  (14 shorter events, 0.3 us)
Async XLA Ops:
  5.3 13.1 %collective-permute-start.1 = (bf16[2,48,1024]{2,1,0:T(8,128)(2,1)}, bf16[2,48,1024]{2,1,0:T(8,128)(2,1)S(1)}, u32[]{:S(2)}, u32[]{:S(2)}) collective-permute-start(bf16[2,48,1024]{2,1,0:T(8,128)(2,1)} %get-tuple-element.29), channel_id=1, source_target_pairs={{8,0},{9,1},{10,2},{11,3},{12,4},{13,5},{14,6},{15,7},{0,8},{1,9},... | collective-permute-start | bytes 589832 | tf_op jit(solution)/shard_map/ppermute | solution.py:588
  8.4 19.9 %collective-permute-start.3 = (bf16[2,64,1024]{2,1,0:T(8,128)(2,1)}, bf16[2,64,1024]{2,1,0:T(8,128)(2,1)S(1)}, u32[]{:S(2)}, u32[]{:S(2)}) collective-permute-start(bf16[2,64,1024]{2,1,0:T(8,128)(2,1)} %get-tuple-element.39), channel_id=1, source_target_pairs={{0,4},{1,5},{2,6},{3,7},{8,12},{9,13},{10,14},{11,15},{16,20},{17,... | collective-permute-start | bytes 786440 | tf_op jit(solution)/shard_map/ppermute | solution.py:588
  11.8 27.9 %collective-permute-start = (bf16[2,128,1024]{2,1,0:T(8,128)(2,1)}, bf16[2,128,1024]{2,1,0:T(8,128)(2,1)S(1)}, u32[]{:S(2)}, u32[]{:S(2)}) collective-permute-start(bf16[2,128,1024]{2,1,0:T(8,128)(2,1)} %get-tuple-element.28), channel_id=1, source_target_pairs={{0,2},{1,3},{4,6},{5,7},{8,10},{9,11},{12,14},{13,15},{16,18},{17,... | collective-permute-start | bytes 1572872 | tf_op jit(solution)/shard_map/ppermute | solution.py:588
  15.3 30.4 %collective-permute-start.11 = (bf16[2,256,1024]{2,1,0:T(8,128)(2,1)}, bf16[2,256,1024]{2,1,0:T(8,128)(2,1)}, u32[]{:S(2)}, u32[]{:S(2)}) collective-permute-start(bf16[2,256,1024]{2,1,0:T(8,128)(2,1)} %get-tuple-element.50), channel_id=1, source_target_pairs={{0,1},{2,3},{4,5},{6,7},{8,9},{10,11},{12,13},{14,15},{16,17},{18,... | collective-permute-start | bytes 3145736 | tf_op jit(solution)/shard_map/ppermute | solution.py:588
  18.4 12.0 %collective-permute-start.2 = (bf16[2,32,1024]{2,1,0:T(8,128)(2,1)S(1)}, bf16[2,32,1024]{2,1,0:T(8,128)(2,1)S(1)}, u32[]{:S(2)}, u32[]{:S(2)}) collective-permute-start(bf16[2,32,1024]{2,1,0:T(8,128)(2,1)S(1)} %slice.12), channel_id=1, source_target_pairs={{2,0},{3,1},{0,2},{1,3},{6,4},{7,5},{4,6},{5,7},{10,8},{11,9},{8,1... | collective-permute-start | bytes 393224 | tf_op jit(solution)/shard_map/ppermute | solution.py:588
  18.5 11.9 %collective-permute-start.7 = (bf16[2,32,1024]{2,1,0:T(8,128)(2,1)S(1)}, bf16[2,32,1024]{2,1,0:T(8,128)(2,1)S(1)}, u32[]{:S(2)}, u32[]{:S(2)}) collective-permute-start(bf16[2,32,1024]{2,1,0:T(8,128)(2,1)S(1)} %pad_maximum_fusion.2), channel_id=1, source_target_pairs={{0,16},{1,17},{2,18},{3,19},{4,20},{5,21},{6,22},{7,23},{8,24},{9,... | collective-permute-start | bytes 393224 | tf_op jit(solution)/shard_map/ppermute | solution.py:588
  28.4 11.4 %collective-permute-start.4 = (bf16[2,64,1024]{2,1,0:T(8,128)(2,1)S(1)}, bf16[2,64,1024]{2,1,0:T(8,128)(2,1)S(1)}, u32[]{:S(2)}, u32[]{:S(2)}) collective-permute-start(bf16[2,64,1024]{2,1,0:T(8,128)(2,1)S(1)} %collective-permute-done.3), channel_id=1, source_target_pairs={{2,0},{3,1},{0,2},{1,3},{6,4},{7,5},{4,6},{5,7},{10,8},{11,9},{8,1... | collective-permute-start | bytes 786440 | tf_op jit(solution)/shard_map/ppermute | solution.py:588
  30.5 7.5 %collective-permute-start.8 = (bf16[2,32,1024]{2,1,0:T(8,128)(2,1)S(1)}, bf16[2,32,1024]{2,1,0:T(8,128)(2,1)S(1)}, u32[]{:S(2)}, u32[]{:S(2)}) collective-permute-start(bf16[2,32,1024]{2,1,0:T(8,128)(2,1)S(1)} %collective-permute-done.7), channel_id=1, source_target_pairs={{4,0},{5,1},{6,2},{7,3},{0,4},{1,5},{2,6},{3,7},{12,8},{13,9},{14,... | collective-permute-start | bytes 393224 | tf_op jit(solution)/shard_map/ppermute | solution.py:588
  30.5 9.4 %collective-permute-start.6 = (bf16[2,64,1024]{2,1,0:T(8,128)(2,1)S(1)}, bf16[2,64,1024]{2,1,0:T(8,128)(2,1)S(1)}, u32[]{:S(2)}, u32[]{:S(2)}) collective-permute-start(bf16[2,64,1024]{2,1,0:T(8,128)(2,1)S(1)} %pad_maximum_fusion.1), channel_id=1, source_target_pairs={{4,0},{5,1},{6,2},{7,3},{0,4},{1,5},{2,6},{3,7},{12,8},{13,9},{14,... | collective-permute-start | bytes 786440 | tf_op jit(solution)/shard_map/ppermute | solution.py:588
  37.9 6.6 %collective-permute-start.9 = (bf16[2,64,1024]{2,1,0:T(8,128)(2,1)S(1)}, bf16[2,64,1024]{2,1,0:T(8,128)(2,1)S(1)}, u32[]{:S(2)}, u32[]{:S(2)}) collective-permute-start(bf16[2,64,1024]{2,1,0:T(8,128)(2,1)S(1)} %constant_dynamic-update-slice_fusion.5), channel_id=1, source_target_pairs={{2,0},{3,1},{0,2},{1,3},{6,4},{7,5},{4,6},{5,7},{10,8},{11,9},{8,1... | collective-permute-start | bytes 786440 | tf_op jit(solution)/shard_map/ppermute | solution.py:588
  39.8 4.7 %copy-start.1 = (bf16[2,256,1024]{2,1,0:T(8,128)(2,1)}, bf16[2,256,1024]{2,1,0:T(8,128)(2,1)S(1)}, u32[]{:S(2)}) copy-start(bf16[2,256,1024]{2,1,0:T(8,128)(2,1)S(1)} %constant_dynamic-update-slice_fusion.refs_0_) | copy-start | bytes 3145732
  39.8 5.8 %collective-permute-start.5 = (bf16[2,256,1024]{2,1,0:T(8,128)(2,1)S(1)}, bf16[2,256,1024]{2,1,0:T(8,128)(2,1)}, u32[]{:S(2)}, u32[]{:S(2)}) collective-permute-start(bf16[2,256,1024]{2,1,0:T(8,128)(2,1)S(1)} %constant_dynamic-update-slice_fusion.refs_0_), channel_id=1, source_target_pairs={{1,0},{0,1},{3,2},{2,3},{5,4},{4,5},{7,6},{6,7},{9,8},{8,9},{11,10... | collective-permute-start | bytes 3145736 | tf_op jit(solution)/shard_map/ppermute | solution.py:588
  44.6 2.7 %copy-start = (bf16[2,256,1024]{2,1,0:T(8,128)(2,1)}, bf16[2,256,1024]{2,1,0:T(8,128)(2,1)S(1)}, u32[]{:S(2)}) copy-start(bf16[2,256,1024]{2,1,0:T(8,128)(2,1)S(1)} %constant_dynamic-update-slice_fusion.7.refs_2_) | copy-start | bytes 3145732
  44.6 2.7 %collective-permute-start.10 = (bf16[2,256,1024]{2,1,0:T(8,128)(2,1)S(1)}, bf16[2,256,1024]{2,1,0:T(8,128)(2,1)S(1)}, u32[]{:S(2)}, u32[]{:S(2)}) collective-permute-start(bf16[2,256,1024]{2,1,0:T(8,128)(2,1)S(1)} %constant_dynamic-update-slice_fusion.7.refs_2_), channel_id=1, source_target_pairs={{1,0},{0,1},{3,2},{2,3},{5,4},{4,5},{7,6},{6,7},{9,8},{8,9},{11,10... | collective-permute-start | bytes 3145736 | tf_op jit(solution)/shard_map/ppermute | solution.py:588
  47.4 1.0 %copy-start.2 = (bf16[2,256,1024]{2,1,0:T(8,128)(2,1)}, bf16[2,256,1024]{2,1,0:T(8,128)(2,1)S(1)}, u32[]{:S(2)}) copy-start(bf16[2,256,1024]{2,1,0:T(8,128)(2,1)S(1)} %collective-permute-done.10.refs_3_) | copy-start | bytes 3145732

commit v5 on v4

--- a/solution.py
+++ b/solution.py
@@ -582,10 +582,8 @@
     )(flags, *bundles, *fars, *nums, *stats, as_bf16(turn), w_out)
 
 
-def moved(array, distance, upper_of=0):
-    size = lax.axis_size("seq")
-    pairs = [(i ^ distance, i) for i in range(size) if not upper_of or i & upper_of]
-    return lax.ppermute(array, "seq", pairs)
+def moved(array, distance):
+    return lax.ppermute(array, "seq", [(i ^ distance, i) for i in range(lax.axis_size("seq"))])
 
 
 def gathered(blocks, distance):
@@ -620,7 +618,7 @@
     for distance in [1 << (level - FIRST) for level in high]:
         members = [level for level in high if 1 << (level - FIRST) >= distance]
         sent = pooled[-1] if distance == GROUP else jnp.concatenate([blocks[level] for level in members], axis=1)
-        got = moved(sent, distance, distance if len(members) == 1 else 0)
+        got = moved(sent, distance)
         start = 0
         for level in members:
             rows = blocks[level].shape[1]
@@ -631,9 +629,9 @@
             else:
                 blocks[level] = jnp.concatenate([blocks[level], piece], axis=1)
         if distance == GROUP:
-            fourth = moved(blocks[4], 4, 4)
-            third = moved(blocks[3], 2, 2)
-            second = moved(blocks[2], 1, 1)
+            fourth = moved(blocks[4], 4)
+            third = moved(blocks[3], 2)
+            second = moved(blocks[2], 1)
             arrived = blocks[TOP]
 
     upper = [blocks[level] for level in high[1:]]

time: 63.5 us -> 60.6 us (0.954)
  starting transfers between devices: 23.1 us -> 15.1 us
  waiting for transfers between devices: 1.76 us -> 6.95 us
    ppermute x12, starting transfers between devices: 23.1 us -> 15.1 us  [moved(): lax.ppermute(array, 'seq', [(i ^ distance, i) for i in range(lax.axis_siz...]
    ppermute x12, waiting for transfers between devices: 1.76 us -> 6.95 us  [moved(): lax.ppermute(array, 'seq', [(i ^ distance, i) for i in range(lax.axis_siz...]
  transfers between devices with their start and end apart: 12 -> 12, of which waited for: 1 -> 3; matrix products, arithmetic and copies ran while one was open for 3% -> 3% of each run, Pallas kernels for 24% -> 25%
where the time goes in v5:
time: 60.6 us; the launch traced here: 60.4 us
  Pallas kernels  34.4 us (57%)
  starting transfers between devices  15.1 us (25%)
  waiting for transfers between devices  6.95 us (11%)
  local copies, waits for them, and re-layouts  3.45 us (6%)
    ppermute x12, starting transfers between devices, moved(): lax.ppermute(array, 'seq', [(i ^ distance, i) for i in range(lax.axis_siz...  15.1 us
    pallas_call x3, Pallas kernels, near_call(): pl.pallas_call(functools.partial(near_kernel, levels, first, heads), in_s...  15.1 us
    pallas_call x1, Pallas kernels, far_call(): pl.pallas_call(functools.partial(far_kernel, levels, plan), in_specs=[pl....  14.6 us
    ppermute x12, waiting for transfers between devices, moved(): lax.ppermute(array, 'seq', [(i ^ distance, i) for i in range(lax.axis_siz...  6.95 us
    pallas_call x1, Pallas kernels, pool_call(): pl.pallas_call(functools.partial(pool_kernel, levels), in_specs=[HBM] * 4...  4.68 us
  transfers between devices with their start and end apart: 12, of which 3 were waited for; matrix products, arithmetic and copies ran while one was open for 3% of the time, Pallas kernels for 25%

profile of v5, /device:TPU:0, one launch (start us, length us, event | category | flops | bytes accessed | tf_op | source)
XLA Modules:
  0.0 60.4 jit_solution(12675050412454354441)
XLA Ops:
  0.0 0.6 %broadcast.1.large_ref = bf16[16,1024]{1,0:T(8,128)(2,1)} broadcast(bf16[]{:T(256)} %constant.27), dimensions={} | broadcast | bytes 32770 | tf_op jit(solution)
  0.6 4.7 %pool_keys_values.1 = (bf16[2,256,1024]{2,1,0:T(8,128)(2,1)}, bf16[2,128,1024]{2,1,0:T(8,128)(2,1)}, bf16[2,64,1024]{2,1,0:T(8,128)(2,1)}, bf16[2,48,1024]{2,1,0:T(8,128)(2,1)}) custom-call(bf16[256,512]{1,0:T(8,128)(2,1)} %constant.26.small_ref, bf16[16,1024]{1,0:T(8,128)(2,1)} %broadcast.1.large_ref, bf16[1024,1024]{1,0:T(8,128)(2,1)} %k_ref.5, ...), custom_call_target="tpu_custom_call" | custom-call | flops 1073741824 | bytes 6291456 | tf_op jit(solution)/shard_map/pool_keys_values/pallas_call | solution.py:151
  5.3 3.1 %collective-permute-start.1 = (bf16[2,48,1024]{2,1,0:T(8,128)(2,1)}, bf16[2,48,1024]{2,1,0:T(8,128)(2,1)S(1)}, u32[]{:S(2)}, u32[]{:S(2)}) collective-permute-start(bf16[2,48,1024]{2,1,0:T(8,128)(2,1)} %get-tuple-element.29), channel_id=1, source_target_pairs={{8,0},{9,1},{10,2},{11,3},{12,4},{13,5},{14,6},{15,7},{0,8},{1,9},... | collective-permute-start | bytes 589832 | tf_op jit(solution)/shard_map/ppermute | solution.py:586
  8.4 1.5 %collective-permute-start.3 = (bf16[2,64,1024]{2,1,0:T(8,128)(2,1)}, bf16[2,64,1024]{2,1,0:T(8,128)(2,1)S(1)}, u32[]{:S(2)}, u32[]{:S(2)}) collective-permute-start(bf16[2,64,1024]{2,1,0:T(8,128)(2,1)} %get-tuple-element.39), channel_id=1, source_target_pairs={{4,0},{5,1},{6,2},{7,3},{0,4},{1,5},{2,6},{3,7},{12,8},{13,9},{14,... | collective-permute-start | bytes 786440 | tf_op jit(solution)/shard_map/ppermute | solution.py:586
  9.9 1.5 %collective-permute-start = (bf16[2,128,1024]{2,1,0:T(8,128)(2,1)}, bf16[2,128,1024]{2,1,0:T(8,128)(2,1)S(1)}, u32[]{:S(2)}, u32[]{:S(2)}) collective-permute-start(bf16[2,128,1024]{2,1,0:T(8,128)(2,1)} %get-tuple-element.28), channel_id=1, source_target_pairs={{2,0},{3,1},{0,2},{1,3},{6,4},{7,5},{4,6},{5,7},{10,8},{11,9},{8,1... | collective-permute-start | bytes 1572872 | tf_op jit(solution)/shard_map/ppermute | solution.py:586
  11.4 0.0 collective-permute-start.11
  11.4 0.8 %slice.10 = bf16[2,16,1024]{2,1,0:T(8,128)(2,1)S(1)} slice(bf16[2,48,1024]{2,1,0:T(8,128)(2,1)} %get-tuple-element.29), slice={[0:2], [32:48], [0:1024]} | slice | bytes 131072 | tf_op jit(solution)/shard_map/slice | solution.py:615
  12.3 1.3 %collective-permute-done.1 = bf16[2,48,1024]{2,1,0:T(8,128)(2,1)S(1)} collective-permute-done((bf16[2,48,1024]{2,1,0:T(8,128)(2,1)}, bf16[2,48,1024]{2,1,0:T(8,128)(2,1)S(1)}, u32[]{:S(2)}, u32[]{:S(2)}) %collective-permute-start.1) | collective-permute-done | bytes 196640 | tf_op jit(solution)/shard_map/ppermute | solution.py:586
  13.5 1.7 %collective-permute-start.2 = (bf16[2,32,1024]{2,1,0:T(8,128)(2,1)S(1)}, bf16[2,32,1024]{2,1,0:T(8,128)(2,1)S(1)}, u32[]{:S(2)}, u32[]{:S(2)}) collective-permute-start(bf16[2,32,1024]{2,1,0:T(8,128)(2,1)S(1)} %slice.12), channel_id=1, source_target_pairs={{2,0},{3,1},{0,2},{1,3},{6,4},{7,5},{4,6},{5,7},{10,8},{11,9},{8,1... | collective-permute-start | bytes 393224 | tf_op jit(solution)/shard_map/ppermute | solution.py:586
  15.3 2.7 %collective-permute-start.7 = (bf16[2,32,1024]{2,1,0:T(8,128)(2,1)S(1)}, bf16[2,32,1024]{2,1,0:T(8,128)(2,1)S(1)}, u32[]{:S(2)}, u32[]{:S(2)}) collective-permute-start(bf16[2,32,1024]{2,1,0:T(8,128)(2,1)S(1)} %pad_maximum_fusion.2), channel_id=1, source_target_pairs={{16,0},{17,1},{18,2},{19,3},{20,4},{21,5},{22,6},{23,7},{24,8},{25... | collective-permute-start | bytes 393224 | tf_op jit(solution)/shard_map/ppermute | solution.py:586
  17.9 5.3 %near_levels.3 = (f32[384,1024]{1,0:T(8,128)}, f32[3,8,1024]{2,1,0:T(8,128)}, bf16[768,384]{1,0:T(8,128)(2,1)}) custom-call(bf16[576,256]{1,0:T(8,128)(2,1)} %constant.28.pool_ref, bf16[1024,1024]{1,0:T(8,128)(2,1)} %q_ref.2, bf16[1024,1024]{1,0:T(8,128)(2,1)} %k_ref.5, bf16[1024,1024]{1,0:T(8,128)(2,1)} %v_ref.5), custom_call_target="tpu_custom_call" | custom-call | flops 8000000000 | bytes 4194304 | tf_op jit(solution)/shard_map/near_levels/pallas_call | solution.py:343
  23.2 0.0 collective-permute-done.3
  23.2 0.6 collective-permute-start.4
  23.8 3.9 %collective-permute-done.2 = bf16[2,32,1024]{2,1,0:T(8,128)(2,1)S(1)} collective-permute-done((bf16[2,32,1024]{2,1,0:T(8,128)(2,1)S(1)}, bf16[2,32,1024]{2,1,0:T(8,128)(2,1)S(1)}, u32[]{:S(2)}, u32[]{:S(2)}) %collective-permute-start.2) | collective-permute-done | bytes 131104 | tf_op jit(solution)/shard_map/ppermute | solution.py:586
  27.8 0.0 collective-permute-done.7
  27.8 0.1 collective-permute-start.8
  27.8 2.0 %collective-permute-start.6 = (bf16[2,64,1024]{2,1,0:T(8,128)(2,1)S(1)}, bf16[2,64,1024]{2,1,0:T(8,128)(2,1)S(1)}, u32[]{:S(2)}, u32[]{:S(2)}) collective-permute-start(bf16[2,64,1024]{2,1,0:T(8,128)(2,1)S(1)} %pad_maximum_fusion.1), channel_id=1, source_target_pairs={{4,0},{5,1},{6,2},{7,3},{0,4},{1,5},{2,6},{3,7},{12,8},{13,9},{14,... | collective-permute-start | bytes 786440 | tf_op jit(solution)/shard_map/ppermute | solution.py:586
  29.9 5.3 %near_levels.4 = (f32[384,1024]{1,0:T(8,128)}, f32[3,8,1024]{2,1,0:T(8,128)}, bf16[768,384]{1,0:T(8,128)(2,1)}) custom-call(bf16[576,256]{1,0:T(8,128)(2,1)} %constant.28.pool_ref, bf16[1024,1024]{1,0:T(8,128)(2,1)} %q_ref.2, bf16[1024,1024]{1,0:T(8,128)(2,1)} %k_ref.5, bf16[1024,1024]{1,0:T(8,128)(2,1)} %v_ref.5), custom_call_target="tpu_custom_call" | custom-call | flops 8000000000 | bytes 4194304 | tf_op jit(solution)/shard_map/near_levels/pallas_call | solution.py:343
  35.2 0.0 collective-permute-done.8
  35.2 1.6 %collective-permute-start.9 = (bf16[2,64,1024]{2,1,0:T(8,128)(2,1)S(1)}, bf16[2,64,1024]{2,1,0:T(8,128)(2,1)S(1)}, u32[]{:S(2)}, u32[]{:S(2)}) collective-permute-start(bf16[2,64,1024]{2,1,0:T(8,128)(2,1)S(1)} %constant_dynamic-update-slice_fusion.5), channel_id=1, source_target_pairs={{2,0},{3,1},{0,2},{1,3},{6,4},{7,5},{4,6},{5,7},{10,8},{11,9},{8,1... | collective-permute-start | bytes 786440 | tf_op jit(solution)/shard_map/ppermute | solution.py:586
  36.9 0.0 collective-permute-done
  36.9 0.0 collective-permute-done.4
  37.0 0.0 copy-start.1
  37.0 0.1 collective-permute-start.5
  37.1 0.0 collective-permute-done.6
  37.1 4.5 %near_levels.5 = (f32[256,1024]{1,0:T(8,128)}, f32[2,8,1024]{2,1,0:T(8,128)}, bf16[768,256]{1,0:T(8,128)(2,1)}) custom-call(bf16[576,256]{1,0:T(8,128)(2,1)} %constant.28.pool_ref, bf16[1024,1024]{1,0:T(8,128)(2,1)} %q_ref.2, bf16[1024,1024]{1,0:T(8,128)(2,1)} %k_ref.5, bf16[1024,1024]{1,0:T(8,128)(2,1)} %v_ref.5), custom_call_target="tpu_custom_call" | custom-call | flops 8000000000 | bytes 4194304 | tf_op jit(solution)/shard_map/near_levels/pallas_call | solution.py:343
  41.6 0.0 copy-done.1
  41.6 0.0 collective-permute-done.9
  41.8 0.0 copy-start
  41.8 0.3 collective-permute-start.10
  42.1 0.7 %stack.23.flags_ref = s32[5]{0:T(128)} concatenate(s32[1]{0:T(128)} %bitcast, s32[1]{0:T(128)} %bitcast.1, s32[1]{0:T(128)} %bitcast.2, s32[1]{0:T(128)} %bitcast.3, s32[1]{0:T(128)} %bitcast.4), dimensions={0} | concatenate | bytes 40 | tf_op jit(solution)/shard_map/stack | solution.py:608
  42.8 0.0 collective-permute-done.11.refs_4_
  42.8 0.0 collective-permute-done.5.refs_1_
  42.8 1.7 %collective-permute-done.10.refs_3_ = bf16[2,256,1024]{2,1,0:T(8,128)(2,1)S(1)} collective-permute-done((bf16[2,256,1024]{2,1,0:T(8,128)(2,1)S(1)}, bf16[2,256,1024]{2,1,0:T(8,128)(2,1)S(1)}, u32[]{:S(2)}, u32[]{:S(2)}) %collective-permute-start.10) | collective-permute-done | bytes 1048608 | tf_op jit(solution)/shard_map/ppermute | solution.py:586
  44.5 0.0 copy-done
  44.5 0.0 copy-start.2
  44.5 1.0 %copy-done.2 = bf16[2,256,1024]{2,1,0:T(8,128)(2,1)} copy-done((bf16[2,256,1024]{2,1,0:T(8,128)(2,1)}, bf16[2,256,1024]{2,1,0:T(8,128)(2,1)S(1)}, u32[]{:S(2)}) %copy-start.2) | copy-done | bytes 1048600
  45.6 14.6 %far_levels_projection.1 = bf16[1024,2048]{1,0:T(8,128)(2,1)} custom-call(s32[5]{0:T(128)} %stack.23.flags_ref, bf16[2,256,1024]{2,1,0:T(8,128)(2,1)} %copy-done.1, bf16[2,256,1024]{2,1,0:T(8,128)(2,1)} %collective-permute-done.5.refs_1_, bf16[2,256,1024]{2,1,0:T(8,128)(2,1)} %copy-done, bf16[2,256,1024]{2,1,0:T(8,128)(2,1)} %copy-done.2, ...), custom_call_target="tpu_custom_call" | custom-call | flops 6499999744 | bytes 18874368 | tf_op jit(solution)/shard_map/far_levels_projection/pallas_call | solution.py:558
  (14 shorter events, 0.3 us)
Async XLA Ops:
  5.3 8.2 %collective-permute-start.1 = (bf16[2,48,1024]{2,1,0:T(8,128)(2,1)}, bf16[2,48,1024]{2,1,0:T(8,128)(2,1)S(1)}, u32[]{:S(2)}, u32[]{:S(2)}) collective-permute-start(bf16[2,48,1024]{2,1,0:T(8,128)(2,1)} %get-tuple-element.29), channel_id=1, source_target_pairs={{8,0},{9,1},{10,2},{11,3},{12,4},{13,5},{14,6},{15,7},{0,8},{1,9},... | collective-permute-start | bytes 589832 | tf_op jit(solution)/shard_map/ppermute | solution.py:586
  8.4 14.8 %collective-permute-start.3 = (bf16[2,64,1024]{2,1,0:T(8,128)(2,1)}, bf16[2,64,1024]{2,1,0:T(8,128)(2,1)S(1)}, u32[]{:S(2)}, u32[]{:S(2)}) collective-permute-start(bf16[2,64,1024]{2,1,0:T(8,128)(2,1)} %get-tuple-element.39), channel_id=1, source_target_pairs={{4,0},{5,1},{6,2},{7,3},{0,4},{1,5},{2,6},{3,7},{12,8},{13,9},{14,... | collective-permute-start | bytes 786440 | tf_op jit(solution)/shard_map/ppermute | solution.py:586
  9.9 27.0 %collective-permute-start = (bf16[2,128,1024]{2,1,0:T(8,128)(2,1)}, bf16[2,128,1024]{2,1,0:T(8,128)(2,1)S(1)}, u32[]{:S(2)}, u32[]{:S(2)}) collective-permute-start(bf16[2,128,1024]{2,1,0:T(8,128)(2,1)} %get-tuple-element.28), channel_id=1, source_target_pairs={{2,0},{3,1},{0,2},{1,3},{6,4},{7,5},{4,6},{5,7},{10,8},{11,9},{8,1... | collective-permute-start | bytes 1572872 | tf_op jit(solution)/shard_map/ppermute | solution.py:586
  11.4 31.4 %collective-permute-start.11 = (bf16[2,256,1024]{2,1,0:T(8,128)(2,1)}, bf16[2,256,1024]{2,1,0:T(8,128)(2,1)}, u32[]{:S(2)}, u32[]{:S(2)}) collective-permute-start(bf16[2,256,1024]{2,1,0:T(8,128)(2,1)} %get-tuple-element.50), channel_id=1, source_target_pairs={{1,0},{0,1},{3,2},{2,3},{5,4},{4,5},{7,6},{6,7},{9,8},{8,9},{11,10... | collective-permute-start | bytes 3145736 | tf_op jit(solution)/shard_map/ppermute | solution.py:586
  13.5 14.2 %collective-permute-start.2 = (bf16[2,32,1024]{2,1,0:T(8,128)(2,1)S(1)}, bf16[2,32,1024]{2,1,0:T(8,128)(2,1)S(1)}, u32[]{:S(2)}, u32[]{:S(2)}) collective-permute-start(bf16[2,32,1024]{2,1,0:T(8,128)(2,1)S(1)} %slice.12), channel_id=1, source_target_pairs={{2,0},{3,1},{0,2},{1,3},{6,4},{7,5},{4,6},{5,7},{10,8},{11,9},{8,1... | collective-permute-start | bytes 393224 | tf_op jit(solution)/shard_map/ppermute | solution.py:586
  15.3 12.5 %collective-permute-start.7 = (bf16[2,32,1024]{2,1,0:T(8,128)(2,1)S(1)}, bf16[2,32,1024]{2,1,0:T(8,128)(2,1)S(1)}, u32[]{:S(2)}, u32[]{:S(2)}) collective-permute-start(bf16[2,32,1024]{2,1,0:T(8,128)(2,1)S(1)} %pad_maximum_fusion.2), channel_id=1, source_target_pairs={{16,0},{17,1},{18,2},{19,3},{20,4},{21,5},{22,6},{23,7},{24,8},{25... | collective-permute-start | bytes 393224 | tf_op jit(solution)/shard_map/ppermute | solution.py:586
  23.2 13.7 %collective-permute-start.4 = (bf16[2,64,1024]{2,1,0:T(8,128)(2,1)S(1)}, bf16[2,64,1024]{2,1,0:T(8,128)(2,1)S(1)}, u32[]{:S(2)}, u32[]{:S(2)}) collective-permute-start(bf16[2,64,1024]{2,1,0:T(8,128)(2,1)S(1)} %collective-permute-done.3), channel_id=1, source_target_pairs={{2,0},{3,1},{0,2},{1,3},{6,4},{7,5},{4,6},{5,7},{10,8},{11,9},{8,1... | collective-permute-start | bytes 786440 | tf_op jit(solution)/shard_map/ppermute | solution.py:586
  27.8 7.5 %collective-permute-start.8 = (bf16[2,32,1024]{2,1,0:T(8,128)(2,1)S(1)}, bf16[2,32,1024]{2,1,0:T(8,128)(2,1)S(1)}, u32[]{:S(2)}, u32[]{:S(2)}) collective-permute-start(bf16[2,32,1024]{2,1,0:T(8,128)(2,1)S(1)} %collective-permute-done.7), channel_id=1, source_target_pairs={{4,0},{5,1},{6,2},{7,3},{0,4},{1,5},{2,6},{3,7},{12,8},{13,9},{14,... | collective-permute-start | bytes 393224 | tf_op jit(solution)/shard_map/ppermute | solution.py:586
  27.8 9.2 %collective-permute-start.6 = (bf16[2,64,1024]{2,1,0:T(8,128)(2,1)S(1)}, bf16[2,64,1024]{2,1,0:T(8,128)(2,1)S(1)}, u32[]{:S(2)}, u32[]{:S(2)}) collective-permute-start(bf16[2,64,1024]{2,1,0:T(8,128)(2,1)S(1)} %pad_maximum_fusion.1), channel_id=1, source_target_pairs={{4,0},{5,1},{6,2},{7,3},{0,4},{1,5},{2,6},{3,7},{12,8},{13,9},{14,... | collective-permute-start | bytes 786440 | tf_op jit(solution)/shard_map/ppermute | solution.py:586
  35.2 6.4 %collective-permute-start.9 = (bf16[2,64,1024]{2,1,0:T(8,128)(2,1)S(1)}, bf16[2,64,1024]{2,1,0:T(8,128)(2,1)S(1)}, u32[]{:S(2)}, u32[]{:S(2)}) collective-permute-start(bf16[2,64,1024]{2,1,0:T(8,128)(2,1)S(1)} %constant_dynamic-update-slice_fusion.5), channel_id=1, source_target_pairs={{2,0},{3,1},{0,2},{1,3},{6,4},{7,5},{4,6},{5,7},{10,8},{11,9},{8,1... | collective-permute-start | bytes 786440 | tf_op jit(solution)/shard_map/ppermute | solution.py:586
  37.0 4.7 %copy-start.1 = (bf16[2,256,1024]{2,1,0:T(8,128)(2,1)}, bf16[2,256,1024]{2,1,0:T(8,128)(2,1)S(1)}, u32[]{:S(2)}) copy-start(bf16[2,256,1024]{2,1,0:T(8,128)(2,1)S(1)} %constant_dynamic-update-slice_fusion.refs_0_) | copy-start | bytes 3145732
  37.0 5.8 %collective-permute-start.5 = (bf16[2,256,1024]{2,1,0:T(8,128)(2,1)S(1)}, bf16[2,256,1024]{2,1,0:T(8,128)(2,1)}, u32[]{:S(2)}, u32[]{:S(2)}) collective-permute-start(bf16[2,256,1024]{2,1,0:T(8,128)(2,1)S(1)} %constant_dynamic-update-slice_fusion.refs_0_), channel_id=1, source_target_pairs={{1,0},{0,1},{3,2},{2,3},{5,4},{4,5},{7,6},{6,7},{9,8},{8,9},{11,10... | collective-permute-start | bytes 3145736 | tf_op jit(solution)/shard_map/ppermute | solution.py:586
  41.8 2.7 %copy-start = (bf16[2,256,1024]{2,1,0:T(8,128)(2,1)}, bf16[2,256,1024]{2,1,0:T(8,128)(2,1)S(1)}, u32[]{:S(2)}) copy-start(bf16[2,256,1024]{2,1,0:T(8,128)(2,1)S(1)} %constant_dynamic-update-slice_fusion.7.refs_2_) | copy-start | bytes 3145732
  41.8 2.7 %collective-permute-start.10 = (bf16[2,256,1024]{2,1,0:T(8,128)(2,1)S(1)}, bf16[2,256,1024]{2,1,0:T(8,128)(2,1)S(1)}, u32[]{:S(2)}, u32[]{:S(2)}) collective-permute-start(bf16[2,256,1024]{2,1,0:T(8,128)(2,1)S(1)} %constant_dynamic-update-slice_fusion.7.refs_2_), channel_id=1, source_target_pairs={{1,0},{0,1},{3,2},{2,3},{5,4},{4,5},{7,6},{6,7},{9,8},{8,9},{11,10... | collective-permute-start | bytes 3145736 | tf_op jit(solution)/shard_map/ppermute | solution.py:586
  44.5 1.0 %copy-start.2 = (bf16[2,256,1024]{2,1,0:T(8,128)(2,1)}, bf16[2,256,1024]{2,1,0:T(8,128)(2,1)S(1)}, u32[]{:S(2)}) copy-start(bf16[2,256,1024]{2,1,0:T(8,128)(2,1)S(1)} %collective-permute-done.10.refs_3_) | copy-start | bytes 3145732

commit v6 on v5

--- a/solution.py
+++ b/solution.py
@@ -586,15 +586,10 @@
     return lax.ppermute(array, "seq", [(i ^ distance, i) for i in range(lax.axis_size("seq"))])
 
 
-def gathered(blocks, distance):
-    sent = jnp.concatenate(blocks, axis=1) if len(blocks) > 1 else blocks[0]
-    got = moved(sent, distance)
-    joined, start = [], 0
-    for block in blocks:
-        rows = block.shape[1]
-        joined.append(jnp.concatenate([block, got[:, start : start + rows]], axis=1))
-        start += rows
-    return joined
+def gathered(array, distances):
+    size = lax.axis_size("seq")
+    got = lax.ppermute(array, "seq", [(i ^ distances[i % 2], i) for i in range(size)])
+    return jnp.concatenate([array, got], axis=1)
 
 
 def after(arrays, others):
@@ -630,28 +625,28 @@
                 blocks[level] = jnp.concatenate([blocks[level], piece], axis=1)
         if distance == GROUP:
             fourth = moved(blocks[4], 4)
-            third = moved(blocks[3], 2)
-            second = moved(blocks[2], 1)
             arrived = blocks[TOP]
 
-    upper = [blocks[level] for level in high[1:]]
-    five = gathered([arrived], 2)
+    upper = jnp.concatenate([blocks[level] for level in high], axis=1)
     near = [near_call(after(queries, arrived), keys, values, levels, 0)]
-    upper = gathered(after(upper, near[0]), 4)
-    five_y = gathered(after(five, near[0]), 4)
-    fourth = gathered([after(fourth, near[0])], 2)[0]
-    near.append(near_call(after(queries, (near[0], five)), keys, values, levels, 1))
-    upper_x = gathered(after(upper, near[1]), 2)
-    low = jnp.concatenate([after(third, near[1]), fourth], axis=1)
+    once = gathered(after(upper, near[0]), (2, 4))
+    third = moved(after(blocks[3], (near[0], upper)), 2)
+    near.append(near_call(after(queries, (near[0], upper)), keys, values, levels, 1))
+    joined = gathered(after(once, near[1]), (4, 2))
+    fourth = gathered(after(fourth, near[1]), (2, 2))
+    second = moved(after(blocks[2], arrived), 1)
+    near.append(near_call(after(queries, (near[1], once)), keys, values, levels, 2))
+    low = jnp.concatenate([after(third, near[2]), fourth], axis=1)
     low_got = moved(low, 1)
-    near.append(near_call(after(queries, (near[1], upper, five_y)), keys, values, levels, 2))
-    top = jnp.concatenate(after(five_y + upper_x, near[2]), axis=1)
+    top = after(joined, near[2])
     top_got = moved(top, 1)
     plan = [(2, 4, (0, 0, BLOCK))]
     for level in (3, 4):
         plan += [(level, bundle, ((level - 3) * 128, bundle * 128, 128)) for bundle in (0, 1)]
     for level in high:
-        plan += [(level, bundle, ((level - TOP) * 128, (bundle - 2) * 128, 128)) for bundle in (2, 3)]
+        for piece in range(4):
+            start = (piece * len(high) + level - TOP) * 32
+            plan += [(level, bundle, (start, (bundle - 2) * 128 + piece * 32, 32)) for bundle in (2, 3)]
     return far_call(flags, [low, low_got, top, top_got, second], plan, near, w_out, levels)
 
 

time: 60.6 us -> 68.8 us (1.14)
  waiting for transfers between devices: 6.95 us -> 15.6 us
  local copies, waits for them, and re-layouts: 3.45 us -> 2.25 us
    ppermute x0 -> x3, waiting for transfers between devices: none -> 5.58 us  [gathered(): lax.ppermute(array, 'seq', [(i ^ distances[i % 2], i) for i in range(size)])]
    ppermute x0 -> x3, starting transfers between devices: none -> 4.55 us  [gathered(): lax.ppermute(array, 'seq', [(i ^ distances[i % 2], i) for i in range(size)])]
    ppermute x12 -> x7, starting transfers between devices: 15.1 us -> 11.1 us  [moved(): lax.ppermute(array, 'seq', [(i ^ distance, i) for i in range(lax.axis_siz...]
    ppermute x12 -> x7, waiting for transfers between devices: 6.95 us -> 10.1 us  [moved(): lax.ppermute(array, 'seq', [(i ^ distance, i) for i in range(lax.axis_siz...]
    unnamed x11 -> x9, local copies, waits for them, and re-layouts: 1.17 us -> 0.08 us
  transfers between devices with their start and end apart: 12 -> 10, of which waited for: 3 -> 5; matrix products, arithmetic and copies ran while one was open for 3% -> 3% of each run, Pallas kernels for 25% -> 22%
where the time goes in v6:
time: 68.8 us; the launch traced here: 68.6 us
  Pallas kernels  34.7 us (50%)
  starting transfers between devices  15.6 us (23%)
  waiting for transfers between devices  15.6 us (23%)
  local copies, waits for them, and re-layouts  2.25 us (3%)
    pallas_call x1, Pallas kernels, far_call(): pl.pallas_call(functools.partial(far_kernel, levels, plan), in_specs=[pl....  15.1 us
    pallas_call x3, Pallas kernels, near_call(): pl.pallas_call(functools.partial(near_kernel, levels, first, heads), in_s...  14.9 us
    ppermute x7, starting transfers between devices, moved(): lax.ppermute(array, 'seq', [(i ^ distance, i) for i in range(lax.axis_siz...  11.1 us
    ppermute x7, waiting for transfers between devices, moved(): lax.ppermute(array, 'seq', [(i ^ distance, i) for i in range(lax.axis_siz...  10.1 us
    ppermute x3, waiting for transfers between devices, gathered(): lax.ppermute(array, 'seq', [(i ^ distances[i % 2], i) for i in range(size)])  5.58 us
    pallas_call x1, Pallas kernels, pool_call(): pl.pallas_call(functools.partial(pool_kernel, levels), in_specs=[HBM] * 4...  4.69 us
    ppermute x3, starting transfers between devices, gathered(): lax.ppermute(array, 'seq', [(i ^ distances[i % 2], i) for i in range(size)])  4.55 us
  transfers between devices with their start and end apart: 10, of which 5 were waited for; matrix products, arithmetic and copies ran while one was open for 3% of the time, Pallas kernels for 22%

profile of v6, /device:TPU:0, one launch (start us, length us, event | category | flops | bytes accessed | tf_op | source)
XLA Modules:
  0.0 68.6 jit_solution(10605271651862729621)
XLA Ops:
  0.0 0.6 broadcast.1.large_ref
  0.6 4.7 %pool_keys_values.1 = (bf16[2,256,1024]{2,1,0:T(8,128)(2,1)}, bf16[2,128,1024]{2,1,0:T(8,128)(2,1)}, bf16[2,64,1024]{2,1,0:T(8,128)(2,1)}, bf16[2,48,1024]{2,1,0:T(8,128)(2,1)}) custom-call(bf16[256,512]{1,0:T(8,128)(2,1)} %constant.26.small_ref, bf16[16,1024]{1,0:T(8,128)(2,1)} %broadcast.1.large_ref, bf16[1024,1024]{1,0:T(8,128)(2,1)} %k_ref.5, ...), custom_call_target="tpu_custom_call" | custom-call | flops 1073741824 | bytes 6291456 | tf_op jit(solution)/shard_map/pool_keys_values/pallas_call | solution.py:151
  5.3 3.1 %collective-permute-start = (bf16[2,48,1024]{2,1,0:T(8,128)(2,1)}, bf16[2,48,1024]{2,1,0:T(8,128)(2,1)S(1)}, u32[]{:S(2)}, u32[]{:S(2)}) collective-permute-start(bf16[2,48,1024]{2,1,0:T(8,128)(2,1)} %get-tuple-element.29), channel_id=1, source_target_pairs={{8,0},{9,1},{10,2},{11,3},{12,4},{13,5},{14,6},{15,7},{0,8},{1,9},... | collective-permute-start | bytes 589832 | tf_op jit(solution)/shard_map/ppermute | solution.py:586
  8.4 1.5 %collective-permute-start.4 = (bf16[2,64,1024]{2,1,0:T(8,128)(2,1)}, bf16[2,64,1024]{2,1,0:T(8,128)(2,1)S(1)}, u32[]{:S(2)}, u32[]{:S(2)}) collective-permute-start(bf16[2,64,1024]{2,1,0:T(8,128)(2,1)} %get-tuple-element.45), channel_id=1, source_target_pairs={{4,0},{5,1},{6,2},{7,3},{0,4},{1,5},{2,6},{3,7},{12,8},{13,9},{14,... | collective-permute-start | bytes 786440 | tf_op jit(solution)/shard_map/ppermute | solution.py:586
  9.9 0.8 %slice.10 = bf16[2,16,1024]{2,1,0:T(8,128)(2,1)S(1)} slice(bf16[2,48,1024]{2,1,0:T(8,128)(2,1)} %get-tuple-element.29), slice={[0:2], [32:48], [0:1024]} | slice | bytes 131072 | tf_op jit(solution)/shard_map/slice | solution.py:610
  10.8 2.7 %collective-permute-done = bf16[2,48,1024]{2,1,0:T(8,128)(2,1)S(1)} collective-permute-done((bf16[2,48,1024]{2,1,0:T(8,128)(2,1)}, bf16[2,48,1024]{2,1,0:T(8,128)(2,1)S(1)}, u32[]{:S(2)}, u32[]{:S(2)}) %collective-permute-start) | collective-permute-done | bytes 196640 | tf_op jit(solution)/shard_map/ppermute | solution.py:586
  13.5 0.0 copy-start.2
  13.6 2.8 %collective-permute-start.1 = (bf16[2,32,1024]{2,1,0:T(8,128)(2,1)S(1)}, bf16[2,32,1024]{2,1,0:T(8,128)(2,1)S(1)}, u32[]{:S(2)}, u32[]{:S(2)}) collective-permute-start(bf16[2,32,1024]{2,1,0:T(8,128)(2,1)S(1)} %pad_maximum_fusion.2), channel_id=1, source_target_pairs={{16,0},{17,1},{18,2},{19,3},{20,4},{21,5},{22,6},{23,7},{24,8},{25... | collective-permute-start | bytes 393224 | tf_op jit(solution)/shard_map/ppermute | solution.py:586
  16.4 0.0 collective-permute-start.9
  16.4 5.3 %near_levels.3 = (f32[384,1024]{1,0:T(8,128)}, f32[3,8,1024]{2,1,0:T(8,128)}, bf16[768,384]{1,0:T(8,128)(2,1)}) custom-call(bf16[576,256]{1,0:T(8,128)(2,1)} %constant.28.pool_ref, bf16[1024,1024]{1,0:T(8,128)(2,1)} %q_ref.2, bf16[1024,1024]{1,0:T(8,128)(2,1)} %k_ref.5, bf16[1024,1024]{1,0:T(8,128)(2,1)} %v_ref.5), custom_call_target="tpu_custom_call" | custom-call | flops 8000000000 | bytes 4194304 | tf_op jit(solution)/shard_map/near_levels/pallas_call | solution.py:343
  21.7 0.4 collective-permute-done.1
  22.0 1.4 %collective-permute-start.3 = (bf16[2,64,1024]{2,1,0:T(8,128)(2,1)S(1)}, bf16[2,64,1024]{2,1,0:T(8,128)(2,1)S(1)}, u32[]{:S(2)}, u32[]{:S(2)}) collective-permute-start(bf16[2,64,1024]{2,1,0:T(8,128)(2,1)S(1)} %pad_maximum_fusion.1), channel_id=1, source_target_pairs={{2,0},{5,1},{0,2},{7,3},{6,4},{1,5},{4,6},{3,7},{10,8},{13,9},{8,1... | collective-permute-start | bytes 786440 | tf_op jit(solution)/shard_map/ppermute | solution.py:591
  23.5 0.0 copy-done.2
  23.5 0.7 collective-permute-start.2
  24.1 5.3 %near_levels.4 = (f32[384,1024]{1,0:T(8,128)}, f32[3,8,1024]{2,1,0:T(8,128)}, bf16[768,384]{1,0:T(8,128)(2,1)}) custom-call(bf16[576,256]{1,0:T(8,128)(2,1)} %constant.28.pool_ref, bf16[1024,1024]{1,0:T(8,128)(2,1)} %q_ref.2, bf16[1024,1024]{1,0:T(8,128)(2,1)} %k_ref.5, bf16[1024,1024]{1,0:T(8,128)(2,1)} %v_ref.5), custom_call_target="tpu_custom_call" | custom-call | flops 8000000000 | bytes 4194304 | tf_op jit(solution)/shard_map/near_levels/pallas_call | solution.py:343
  29.4 0.0 collective-permute-done.4
  29.4 1.4 %collective-permute-start.5 = (bf16[2,64,1024]{2,1,0:T(8,128)(2,1)S(1)}, bf16[2,64,1024]{2,1,0:T(8,128)(2,1)S(1)}, u32[]{:S(2)}, u32[]{:S(2)}) collective-permute-start(bf16[2,64,1024]{2,1,0:T(8,128)(2,1)S(1)} %collective-permute-done.4), channel_id=1, source_target_pairs={{2,0},{3,1},{0,2},{1,3},{6,4},{7,5},{4,6},{5,7},{10,8},{11,9},{8,1... | collective-permute-start | bytes 786440 | tf_op jit(solution)/shard_map/ppermute | solution.py:591
  30.9 0.0 collective-permute-done.3
  30.9 1.7 %collective-permute-start.7 = (bf16[2,128,1024]{2,1,0:T(8,128)(2,1)S(1)}, bf16[2,128,1024]{2,1,0:T(8,128)(2,1)S(1)}, u32[]{:S(2)}, u32[]{:S(2)}) collective-permute-start(bf16[2,128,1024]{2,1,0:T(8,128)(2,1)S(1)} %constant_dynamic-update-slice_fusion), channel_id=1, source_target_pairs={{4,0},{3,1},{6,2},{1,3},{0,4},{7,5},{2,6},{5,7},{12,8},{11,9},{14,... | collective-permute-start | bytes 1572872 | tf_op jit(solution)/shard_map/ppermute | solution.py:591
  32.6 4.3 %near_levels.5 = (f32[256,1024]{1,0:T(8,128)}, f32[2,8,1024]{2,1,0:T(8,128)}, bf16[768,256]{1,0:T(8,128)(2,1)}) custom-call(bf16[576,256]{1,0:T(8,128)(2,1)} %constant.28.pool_ref, bf16[1024,1024]{1,0:T(8,128)(2,1)} %q_ref.2, bf16[1024,1024]{1,0:T(8,128)(2,1)} %k_ref.5, bf16[1024,1024]{1,0:T(8,128)(2,1)} %v_ref.5), custom_call_target="tpu_custom_call" | custom-call | flops 8000000000 | bytes 4194304 | tf_op jit(solution)/shard_map/near_levels/pallas_call | solution.py:343
  36.9 5.2 %collective-permute-done.2 = bf16[2,128,1024]{2,1,0:T(8,128)(2,1)S(1)} collective-permute-done((bf16[2,128,1024]{2,1,0:T(8,128)(2,1)S(1)}, bf16[2,128,1024]{2,1,0:T(8,128)(2,1)S(1)}, u32[]{:S(2)}, u32[]{:S(2)}) %collective-permute-start.2) | collective-permute-done | bytes 524320 | tf_op jit(solution)/shard_map/ppermute | solution.py:586
  42.2 5.6 %collective-permute-done.5 = bf16[2,64,1024]{2,1,0:T(8,128)(2,1)S(1)} collective-permute-done((bf16[2,64,1024]{2,1,0:T(8,128)(2,1)S(1)}, bf16[2,64,1024]{2,1,0:T(8,128)(2,1)S(1)}, u32[]{:S(2)}, u32[]{:S(2)}) %collective-permute-start.5) | collective-permute-done | bytes 262176 | tf_op jit(solution)/shard_map/ppermute | solution.py:591
  47.8 0.0 copy-start.1
  47.8 0.1 collective-permute-start.6
  47.9 0.0 collective-permute-done.7
  47.9 0.1 pad_maximum_fusion.refs_2_
  48.0 0.0 copy-start
  48.0 2.9 %collective-permute-start.8 = (bf16[2,256,1024]{2,1,0:T(8,128)(2,1)S(1)}, bf16[2,256,1024]{2,1,0:T(8,128)(2,1)}, u32[]{:S(2)}, u32[]{:S(2)}) collective-permute-start(bf16[2,256,1024]{2,1,0:T(8,128)(2,1)S(1)} %pad_maximum_fusion.refs_2_), channel_id=1, source_target_pairs={{1,0},{0,1},{3,2},{2,3},{5,4},{4,5},{7,6},{6,7},{9,8},{8,9},{11,10... | collective-permute-start | bytes 3145736 | tf_op jit(solution)/shard_map/ppermute | solution.py:586
  50.9 0.7 stack.23.flags_ref
  51.6 0.0 collective-permute-done.9.refs_4_
  51.6 0.0 collective-permute-done.6.refs_1_
  51.6 1.7 %collective-permute-done.8.refs_3_ = bf16[2,256,1024]{2,1,0:T(8,128)(2,1)} collective-permute-done((bf16[2,256,1024]{2,1,0:T(8,128)(2,1)S(1)}, bf16[2,256,1024]{2,1,0:T(8,128)(2,1)}, u32[]{:S(2)}, u32[]{:S(2)}) %collective-permute-start.8) | collective-permute-done | bytes 1048608 | tf_op jit(solution)/shard_map/ppermute | solution.py:586
  53.3 0.0 copy-done.1
  53.3 0.0 copy-done
  53.3 15.1 %far_levels_projection.1 = bf16[1024,2048]{1,0:T(8,128)(2,1)} custom-call(s32[5]{0:T(128)} %stack.23.flags_ref, bf16[2,256,1024]{2,1,0:T(8,128)(2,1)} %copy-done.1, bf16[2,256,1024]{2,1,0:T(8,128)(2,1)} %collective-permute-done.6.refs_1_, bf16[2,256,1024]{2,1,0:T(8,128)(2,1)} %copy-done, bf16[2,256,1024]{2,1,0:T(8,128)(2,1)} %collective-permute-done.8.refs_3_, ...), custom_call_target="tpu_custom_call" | custom-call | flops 6499999744 | bytes 18874368 | tf_op jit(solution)/shard_map/far_levels_projection/pallas_call | solution.py:558
  (9 shorter events, 0.2 us)
Async XLA Ops:
  5.3 8.2 %collective-permute-start = (bf16[2,48,1024]{2,1,0:T(8,128)(2,1)}, bf16[2,48,1024]{2,1,0:T(8,128)(2,1)S(1)}, u32[]{:S(2)}, u32[]{:S(2)}) collective-permute-start(bf16[2,48,1024]{2,1,0:T(8,128)(2,1)} %get-tuple-element.29), channel_id=1, source_target_pairs={{8,0},{9,1},{10,2},{11,3},{12,4},{13,5},{14,6},{15,7},{0,8},{1,9},... | collective-permute-start | bytes 589832 | tf_op jit(solution)/shard_map/ppermute | solution.py:586
  8.4 21.0 %collective-permute-start.4 = (bf16[2,64,1024]{2,1,0:T(8,128)(2,1)}, bf16[2,64,1024]{2,1,0:T(8,128)(2,1)S(1)}, u32[]{:S(2)}, u32[]{:S(2)}) collective-permute-start(bf16[2,64,1024]{2,1,0:T(8,128)(2,1)} %get-tuple-element.45), channel_id=1, source_target_pairs={{4,0},{5,1},{6,2},{7,3},{0,4},{1,5},{2,6},{3,7},{12,8},{13,9},{14,... | collective-permute-start | bytes 786440 | tf_op jit(solution)/shard_map/ppermute | solution.py:586
  13.5 9.9 %copy-start.2 = (bf16[2,128,1024]{2,1,0:T(8,128)(2,1)S(1)}, bf16[2,128,1024]{2,1,0:T(8,128)(2,1)}, u32[]{:S(2)}) copy-start(bf16[2,128,1024]{2,1,0:T(8,128)(2,1)} %get-tuple-element.34) | copy-start | bytes 1572868
  13.6 8.5 %collective-permute-start.1 = (bf16[2,32,1024]{2,1,0:T(8,128)(2,1)S(1)}, bf16[2,32,1024]{2,1,0:T(8,128)(2,1)S(1)}, u32[]{:S(2)}, u32[]{:S(2)}) collective-permute-start(bf16[2,32,1024]{2,1,0:T(8,128)(2,1)S(1)} %pad_maximum_fusion.2), channel_id=1, source_target_pairs={{16,0},{17,1},{18,2},{19,3},{20,4},{21,5},{22,6},{23,7},{24,8},{25... | collective-permute-start | bytes 393224 | tf_op jit(solution)/shard_map/ppermute | solution.py:586
  16.4 35.2 %collective-permute-start.9 = (bf16[2,256,1024]{2,1,0:T(8,128)(2,1)}, bf16[2,256,1024]{2,1,0:T(8,128)(2,1)}, u32[]{:S(2)}, u32[]{:S(2)}) collective-permute-start(bf16[2,256,1024]{2,1,0:T(8,128)(2,1)} %get-tuple-element.50), channel_id=1, source_target_pairs={{1,0},{0,1},{3,2},{2,3},{5,4},{4,5},{7,6},{6,7},{9,8},{8,9},{11,10... | collective-permute-start | bytes 3145736 | tf_op jit(solution)/shard_map/ppermute | solution.py:586
  22.0 8.9 %collective-permute-start.3 = (bf16[2,64,1024]{2,1,0:T(8,128)(2,1)S(1)}, bf16[2,64,1024]{2,1,0:T(8,128)(2,1)S(1)}, u32[]{:S(2)}, u32[]{:S(2)}) collective-permute-start(bf16[2,64,1024]{2,1,0:T(8,128)(2,1)S(1)} %pad_maximum_fusion.1), channel_id=1, source_target_pairs={{2,0},{5,1},{0,2},{7,3},{6,4},{1,5},{4,6},{3,7},{10,8},{13,9},{8,1... | collective-permute-start | bytes 786440 | tf_op jit(solution)/shard_map/ppermute | solution.py:591
  23.5 18.7 %collective-permute-start.2 = (bf16[2,128,1024]{2,1,0:T(8,128)(2,1)S(1)}, bf16[2,128,1024]{2,1,0:T(8,128)(2,1)S(1)}, u32[]{:S(2)}, u32[]{:S(2)}) collective-permute-start(bf16[2,128,1024]{2,1,0:T(8,128)(2,1)S(1)} %copy-done.2), channel_id=1, source_target_pairs={{2,0},{3,1},{0,2},{1,3},{6,4},{7,5},{4,6},{5,7},{10,8},{11,9},{8,1... | collective-permute-start | bytes 1572872 | tf_op jit(solution)/shard_map/ppermute | solution.py:586
  29.4 18.3 %collective-permute-start.5 = (bf16[2,64,1024]{2,1,0:T(8,128)(2,1)S(1)}, bf16[2,64,1024]{2,1,0:T(8,128)(2,1)S(1)}, u32[]{:S(2)}, u32[]{:S(2)}) collective-permute-start(bf16[2,64,1024]{2,1,0:T(8,128)(2,1)S(1)} %collective-permute-done.4), channel_id=1, source_target_pairs={{2,0},{3,1},{0,2},{1,3},{6,4},{7,5},{4,6},{5,7},{10,8},{11,9},{8,1... | collective-permute-start | bytes 786440 | tf_op jit(solution)/shard_map/ppermute | solution.py:591
  30.9 16.9 %collective-permute-start.7 = (bf16[2,128,1024]{2,1,0:T(8,128)(2,1)S(1)}, bf16[2,128,1024]{2,1,0:T(8,128)(2,1)S(1)}, u32[]{:S(2)}, u32[]{:S(2)}) collective-permute-start(bf16[2,128,1024]{2,1,0:T(8,128)(2,1)S(1)} %constant_dynamic-update-slice_fusion), channel_id=1, source_target_pairs={{4,0},{3,1},{6,2},{1,3},{0,4},{7,5},{2,6},{5,7},{12,8},{11,9},{14,... | collective-permute-start | bytes 1572872 | tf_op jit(solution)/shard_map/ppermute | solution.py:591
  47.8 5.5 %copy-start.1 = (bf16[2,256,1024]{2,1,0:T(8,128)(2,1)}, bf16[2,256,1024]{2,1,0:T(8,128)(2,1)S(1)}, u32[]{:S(2)}) copy-start(bf16[2,256,1024]{2,1,0:T(8,128)(2,1)S(1)} %constant_dynamic-update-slice_fusion.2.refs_0_) | copy-start | bytes 3145732
  47.8 3.8 %collective-permute-start.6 = (bf16[2,256,1024]{2,1,0:T(8,128)(2,1)S(1)}, bf16[2,256,1024]{2,1,0:T(8,128)(2,1)}, u32[]{:S(2)}, u32[]{:S(2)}) collective-permute-start(bf16[2,256,1024]{2,1,0:T(8,128)(2,1)S(1)} %constant_dynamic-update-slice_fusion.2.refs_0_), channel_id=1, source_target_pairs={{1,0},{0,1},{3,2},{2,3},{5,4},{4,5},{7,6},{6,7},{9,8},{8,9},{11,10... | collective-permute-start | bytes 3145736 | tf_op jit(solution)/shard_map/ppermute | solution.py:586
  48.0 5.4 %copy-start = (bf16[2,256,1024]{2,1,0:T(8,128)(2,1)}, bf16[2,256,1024]{2,1,0:T(8,128)(2,1)S(1)}, u32[]{:S(2)}) copy-start(bf16[2,256,1024]{2,1,0:T(8,128)(2,1)S(1)} %pad_maximum_fusion.refs_2_) | copy-start | bytes 3145732
  48.0 5.3 %collective-permute-start.8 = (bf16[2,256,1024]{2,1,0:T(8,128)(2,1)S(1)}, bf16[2,256,1024]{2,1,0:T(8,128)(2,1)}, u32[]{:S(2)}, u32[]{:S(2)}) collective-permute-start(bf16[2,256,1024]{2,1,0:T(8,128)(2,1)S(1)} %pad_maximum_fusion.refs_2_), channel_id=1, source_target_pairs={{1,0},{0,1},{3,2},{2,3},{5,4},{4,5},{7,6},{6,7},{9,8},{8,9},{11,10... | collective-permute-start | bytes 3145736 | tf_op jit(solution)/shard_map/ppermute | solution.py:586

commit v7 on v5

--- a/solution.py
+++ b/solution.py
@@ -136,9 +136,10 @@
                     start = (level - 7) * 8
                     place, first = places[level]
                     outs[place][index, first : first + (TOK >> level), cols] = rest[start : start + (TOK >> level)].astype(jnp.bfloat16)
-        for place, (out, target) in enumerate(zip(outs, targets)):
-            sends.append(pltpu.make_async_copy(out.at[index], target.at[index], out_sems.at[index, place]))
-            sends[-1].start()
+            for place, (out, target) in enumerate(zip(outs, targets)):
+                span = (index, slice(None), cols)
+                sends.append(pltpu.make_async_copy(out.at[span], target.at[span], out_sems.at[index * 4 + part, place]))
+                sends[-1].start()
     for send in sends:
         send.wait()
 
@@ -161,7 +162,7 @@
         + [pltpu.VMEM((2, rows, WIDTH), jnp.bfloat16) for rows in sizes]
         + [
             pltpu.SemaphoreType.DMA((10,)),
-            pltpu.SemaphoreType.DMA((2, len(sizes))),
+            pltpu.SemaphoreType.DMA((8, len(sizes))),
         ],
         compiler_params=pltpu.CompilerParams(vmem_limit_bytes=VMEM_CLAIM),
         cost_estimate=pl.CostEstimate(flops=2 * 256 * 512 * 4096, bytes_accessed=6 * MIB, transcendentals=0),
@@ -398,7 +399,7 @@
     return units
 
 
-def far_kernel(levels, plan, flags_ref, *refs):
+def far_kernel(levels, plan, *refs):
     crossing = range(FIRST, levels + 1)
     bundles = 1 + max(bundle for _, bundle, _ in plan)
     kv_refs = refs[:bundles]
@@ -407,10 +408,10 @@
     far_refs, num_refs, stat_refs = refs[:slices], refs[slices : 2 * slices], refs[2 * slices : 3 * slices]
     turn_ref, w_ref, out_ref = refs[3 * slices : 3 * slices + 3]
     kv, queries, num, stat, turn, weights, scores, probs = refs[3 * slices + 3 : 3 * slices + 11]
-    mixed, natural, stage, kv_sems, near_sems, out_sems = refs[3 * slices + 11 :]
+    mixed, natural, stage, partial, kv_sems, near_sems, out_sems = refs[3 * slices + 11 :]
     pair = 2 * HEAD
     model = w_ref.shape[1]
-    step = 512
+    step = 256
     offsets, far_rows = far_offsets(levels)
 
     def kv_copies(index):
@@ -439,20 +440,28 @@
                 pltpu.make_async_copy(stat_refs[index], stat.at[group], sems[2]),
             ]
         )
-    last_copies = [
-        pltpu.make_async_copy(turn_ref, turn, near_sems.at[3 * slices]),
-        pltpu.make_async_copy(w_ref, weights, near_sems.at[3 * slices + 1]),
+    turn_copy = pltpu.make_async_copy(turn_ref, turn, near_sems.at[3 * slices])
+    half = WIDTH // 2
+    w_copies = [
+        pltpu.make_async_copy(w_ref.at[rows], weights.at[rows], near_sems.at[3 * slices + 1 + index])
+        for index, rows in enumerate((slice(0, half), slice(half, WIDTH)))
     ]
-    for copy in far_copies + kv_copies(0) + kv_copies(1) + near_copies[0]:
+    started = far_copies + kv_copies(0) + near_copies[0] + kv_copies(1) + [turn_copy] + near_copies[1]
+    started += [w_copies[0]] + kv_copies(2) + kv_copies(3)
+    for copies in near_copies[2:]:
+        started += copies
+    for copy in started + [w_copies[1]]:
         copy.start()
-    for index in range(2, HEADS // 2):
-        for copy in kv_copies(index):
-            copy.start()
-    for copies in near_copies[1:]:
-        for copy in copies:
-            copy.start()
-    for copy in last_copies:
-        copy.start()
+
+    def turned(part):
+        cols = slice(part * half, (part + 1) * half)
+        for unit in range(UNITS):
+            rows = slice(unit * BLOCK, (unit + 1) * BLOCK)
+            natural[rows, cols] = dot_t(turn[...], mixed[cols, rows]).astype(jnp.bfloat16)
+
+    def first_product(index):
+        cols = slice(index * step, (index + 1) * step)
+        partial[:, cols] = dot(natural[:, :half], weights[:half, cols])
 
     def score(head, level):
         own = lane_block(head)
@@ -471,7 +480,7 @@
     def weigh(head, level, stats):
         own = lane_block(head)
         span = slice(offsets[level], offsets[level] + UNITS * count_of(level))
-        live = flags_ref[level - FIRST] == 1
+        live = ((position >> (level - FIRST)) & 1) == 1
         factor = jnp.where(live, 2.0**level, 0.0)
         weighted = factor * dot_first(kv[level - FIRST, 1, :, own], probs[head % 2, :, span])
         return [
@@ -502,6 +511,7 @@
                 both = (a * inverse) * num[own, lane_block(block)] + (b * inverse) * far_num
                 mixed[own, lane_block(block)] = both.astype(jnp.bfloat16)
 
+    position = lax.axis_index("seq")
     order = list(range(levels, FIRST - 1, -1))
     for copy in far_copies + kv_copies(0):
         copy.wait()
@@ -510,6 +520,7 @@
     for copy in near_copies[0]:
         copy.wait()
     pending = None
+    products = [functools.partial(first_product, index) for index in range(model // step)]
     for head in range(HEADS):
         if head % 2 == 1 and head + 1 < HEADS:
             for copy in kv_copies((head + 1) // 2):
@@ -525,6 +536,12 @@
                 score(head + 1, level)
             if level == order[0] and pending is not None:
                 pending()
+                if head == HEADS // 2:
+                    turn_copy.wait()
+                    w_copies[0].wait()
+                    turned(0)
+            elif head >= HEADS // 2 and products:
+                products.pop(0)()
             terms.append(weigh(head, level, stats))
 
         def pending(head=head, terms=terms):
@@ -532,22 +549,21 @@
 
     pending()
 
-    for copy in last_copies:
-        copy.wait()
-    for unit in range(UNITS):
-        rows = slice(unit * BLOCK, (unit + 1) * BLOCK)
-        natural[rows, :] = dot_t(turn[...], mixed[:, rows]).astype(jnp.bfloat16)
+    for product in products:
+        product()
+    turned(1)
+    w_copies[1].wait()
     sends = []
     for index in range(model // step):
         cols = slice(index * step, (index + 1) * step)
-        stage[:, cols] = dot(natural[...], weights[:, cols]).astype(jnp.bfloat16)
+        stage[:, cols] = (partial[:, cols] + dot(natural[:, half:], weights[half:, cols])).astype(jnp.bfloat16)
         sends.append(pltpu.make_async_copy(stage.at[:, cols], out_ref.at[:, cols], out_sems.at[index]))
         sends[-1].start()
     for send in sends:
         send.wait()
 
 
-def far_call(flags, bundles, plan, near, w_out, levels):
+def far_call(bundles, plan, near, w_out, levels):
     turn = np.zeros((BLOCK, BLOCK))
     turn[token_of(np.arange(BLOCK)), np.arange(BLOCK)] = 1.0
     nums, stats, fars = [[item[place] for item in near] for place in range(3)]
@@ -557,7 +573,7 @@
     bf16, f32 = jnp.bfloat16, jnp.float32
     return pl.pallas_call(
         functools.partial(far_kernel, levels, plan),
-        in_specs=[pl.BlockSpec(memory_space=pltpu.SMEM)] + [HBM] * (len(bundles) + 3 * len(SLICES) + 2),
+        in_specs=[HBM] * (len(bundles) + 3 * len(SLICES) + 2),
         out_specs=HBM,
         out_shape=jax.ShapeDtypeStruct((TOK, model), bf16),
         scratch_shapes=[
@@ -572,14 +588,15 @@
             pltpu.VMEM((WIDTH, TOK), bf16),
             pltpu.VMEM((TOK, WIDTH), bf16),
             pltpu.VMEM((TOK, model), bf16),
+            pltpu.VMEM((TOK, model), f32),
             pltpu.SemaphoreType.DMA((HEADS // 2, len(plan))),
-            pltpu.SemaphoreType.DMA((3 * len(SLICES) + 2,)),
-            pltpu.SemaphoreType.DMA((model // 512,)),
+            pltpu.SemaphoreType.DMA((3 * len(SLICES) + 3,)),
+            pltpu.SemaphoreType.DMA((model // 256,)),
         ],
         compiler_params=pltpu.CompilerParams(vmem_limit_bytes=VMEM_CLAIM),
         cost_estimate=pl.CostEstimate(flops=6_500_000_000, bytes_accessed=18 * MIB, transcendentals=3_000_000),
         name="far_levels_projection",
-    )(flags, *bundles, *fars, *nums, *stats, as_bf16(turn), w_out)
+    )(*bundles, *fars, *nums, *stats, as_bf16(turn), w_out)
 
 
 def moved(array, distance):
@@ -604,8 +621,6 @@
 def on_device(queries, keys, values, w_out):
     size = lax.axis_size("seq")
     levels = (TOK * size // (2 * BLOCK)).bit_length() - 1
-    position = lax.axis_index("seq")
-    flags = jnp.stack([(position >> (level - FIRST)) & 1 for level in range(FIRST, levels + 1)]).astype(jnp.int32)
     pooled = pool_call(keys, values, levels)
 
     places, _ = packed(levels)
@@ -652,7 +667,7 @@
         plan += [(level, bundle, ((level - 3) * 128, bundle * 128, 128)) for bundle in (0, 1)]
     for level in high:
         plan += [(level, bundle, ((level - TOP) * 128, (bundle - 2) * 128, 128)) for bundle in (2, 3)]
-    return far_call(flags, [low, low_got, top, top_got, second], plan, near, w_out, levels)
+    return far_call([low, low_got, top, top_got, second], plan, near, w_out, levels)
 
 
 def solution(mesh):

time: 60.6 us -> 60.2 us (level)
  waiting for transfers between devices: 6.95 us -> 7.91 us
  local copies, waits for them, and re-layouts: 3.45 us -> 2.73 us
    ppermute x12, waiting for transfers between devices: 6.95 us -> 7.91 us  [moved(): lax.ppermute(array, 'seq', [(i ^ distance, i) for i in range(lax.axis_siz...]
    another operation x2 -> x1, local copies, waits for them, and re-layouts: 1.33 us -> 0.62 us  [the longest x1 0.71 us: on_device(): jnp.stack([position >> level - FIRST & 1 for level in range(FIRST, levels...]
  transfers between devices with their start and end apart: 12 -> 12, of which waited for: 3 -> 4; matrix products, arithmetic and copies ran while one was open for 3% -> 2% of each run, Pallas kernels for 25% -> 25%
where the time goes in v7:
time: 60.2 us; the launch traced here: 60 us
  Pallas kernels  34 us (56%)
  starting transfers between devices  15 us (25%)
  waiting for transfers between devices  7.91 us (13%)
  local copies, waits for them, and re-layouts  2.73 us (5%)
    pallas_call x3, Pallas kernels, near_call(): pl.pallas_call(functools.partial(near_kernel, levels, first, heads), in_s...  15.1 us
    ppermute x12, starting transfers between devices, moved(): lax.ppermute(array, 'seq', [(i ^ distance, i) for i in range(lax.axis_siz...  15 us
    pallas_call x1, Pallas kernels, far_call(): pl.pallas_call(functools.partial(far_kernel, levels, plan), in_specs=[HBM...  14.2 us
    ppermute x12, waiting for transfers between devices, moved(): lax.ppermute(array, 'seq', [(i ^ distance, i) for i in range(lax.axis_siz...  7.91 us
    pallas_call x1, Pallas kernels, pool_call(): pl.pallas_call(functools.partial(pool_kernel, levels), in_specs=[HBM] * 4...  4.64 us
  transfers between devices with their start and end apart: 12, of which 4 were waited for; matrix products, arithmetic and copies ran while one was open for 2% of the time, Pallas kernels for 25%

profile of v7, /device:TPU:0, one launch (start us, length us, event | category | flops | bytes accessed | tf_op | source)
XLA Modules:
  0.0 60.0 jit_solution(3522972793221805132)
XLA Ops:
  0.0 0.6 %broadcast.1.large_ref = bf16[16,1024]{1,0:T(8,128)(2,1)} broadcast(bf16[]{:T(256)} %constant.13), dimensions={} | broadcast | bytes 32770 | tf_op jit(solution)
  0.6 4.6 %pool_keys_values.1 = (bf16[2,256,1024]{2,1,0:T(8,128)(2,1)}, bf16[2,128,1024]{2,1,0:T(8,128)(2,1)}, bf16[2,64,1024]{2,1,0:T(8,128)(2,1)}, bf16[2,48,1024]{2,1,0:T(8,128)(2,1)}) custom-call(bf16[256,512]{1,0:T(8,128)(2,1)} %constant.12.small_ref, bf16[16,1024]{1,0:T(8,128)(2,1)} %broadcast.1.large_ref, bf16[1024,1024]{1,0:T(8,128)(2,1)} %k_ref.5, ...), custom_call_target="tpu_custom_call" | custom-call | flops 1073741824 | bytes 6291456 | tf_op jit(solution)/shard_map/pool_keys_values/pallas_call | solution.py:152
  5.3 3.1 %collective-permute-start.1 = (bf16[2,48,1024]{2,1,0:T(8,128)(2,1)}, bf16[2,48,1024]{2,1,0:T(8,128)(2,1)S(1)}, u32[]{:S(2)}, u32[]{:S(2)}) collective-permute-start(bf16[2,48,1024]{2,1,0:T(8,128)(2,1)} %get-tuple-element.29), channel_id=1, source_target_pairs={{8,0},{9,1},{10,2},{11,3},{12,4},{13,5},{14,6},{15,7},{0,8},{1,9},... | collective-permute-start | bytes 589832 | tf_op jit(solution)/shard_map/ppermute | solution.py:603
  8.4 1.5 %collective-permute-start.3 = (bf16[2,64,1024]{2,1,0:T(8,128)(2,1)}, bf16[2,64,1024]{2,1,0:T(8,128)(2,1)S(1)}, u32[]{:S(2)}, u32[]{:S(2)}) collective-permute-start(bf16[2,64,1024]{2,1,0:T(8,128)(2,1)} %get-tuple-element.39), channel_id=1, source_target_pairs={{4,0},{5,1},{6,2},{7,3},{0,4},{1,5},{2,6},{3,7},{12,8},{13,9},{14,... | collective-permute-start | bytes 786440 | tf_op jit(solution)/shard_map/ppermute | solution.py:603
  9.9 1.5 %collective-permute-start = (bf16[2,128,1024]{2,1,0:T(8,128)(2,1)}, bf16[2,128,1024]{2,1,0:T(8,128)(2,1)S(1)}, u32[]{:S(2)}, u32[]{:S(2)}) collective-permute-start(bf16[2,128,1024]{2,1,0:T(8,128)(2,1)} %get-tuple-element.28), channel_id=1, source_target_pairs={{2,0},{3,1},{0,2},{1,3},{6,4},{7,5},{4,6},{5,7},{10,8},{11,9},{8,1... | collective-permute-start | bytes 1572872 | tf_op jit(solution)/shard_map/ppermute | solution.py:603
  11.4 0.0 collective-permute-start.11
  11.4 0.8 %slice.10 = bf16[2,16,1024]{2,1,0:T(8,128)(2,1)S(1)} slice(bf16[2,48,1024]{2,1,0:T(8,128)(2,1)} %get-tuple-element.29), slice={[0:2], [32:48], [0:1024]} | slice | bytes 131072 | tf_op jit(solution)/shard_map/slice | solution.py:630
  12.2 1.3 %collective-permute-done.1 = bf16[2,48,1024]{2,1,0:T(8,128)(2,1)S(1)} collective-permute-done((bf16[2,48,1024]{2,1,0:T(8,128)(2,1)}, bf16[2,48,1024]{2,1,0:T(8,128)(2,1)S(1)}, u32[]{:S(2)}, u32[]{:S(2)}) %collective-permute-start.1) | collective-permute-done | bytes 196640 | tf_op jit(solution)/shard_map/ppermute | solution.py:603
  13.5 1.7 %collective-permute-start.2 = (bf16[2,32,1024]{2,1,0:T(8,128)(2,1)S(1)}, bf16[2,32,1024]{2,1,0:T(8,128)(2,1)S(1)}, u32[]{:S(2)}, u32[]{:S(2)}) collective-permute-start(bf16[2,32,1024]{2,1,0:T(8,128)(2,1)S(1)} %slice.12), channel_id=1, source_target_pairs={{2,0},{3,1},{0,2},{1,3},{6,4},{7,5},{4,6},{5,7},{10,8},{11,9},{8,1... | collective-permute-start | bytes 393224 | tf_op jit(solution)/shard_map/ppermute | solution.py:603
  15.2 2.7 %collective-permute-start.7 = (bf16[2,32,1024]{2,1,0:T(8,128)(2,1)S(1)}, bf16[2,32,1024]{2,1,0:T(8,128)(2,1)S(1)}, u32[]{:S(2)}, u32[]{:S(2)}) collective-permute-start(bf16[2,32,1024]{2,1,0:T(8,128)(2,1)S(1)} %pad_maximum_fusion.2), channel_id=1, source_target_pairs={{16,0},{17,1},{18,2},{19,3},{20,4},{21,5},{22,6},{23,7},{24,8},{25... | collective-permute-start | bytes 393224 | tf_op jit(solution)/shard_map/ppermute | solution.py:603
  17.9 5.3 %near_levels.3 = (f32[384,1024]{1,0:T(8,128)}, f32[3,8,1024]{2,1,0:T(8,128)}, bf16[768,384]{1,0:T(8,128)(2,1)}) custom-call(bf16[576,256]{1,0:T(8,128)(2,1)} %constant.14.pool_ref, bf16[1024,1024]{1,0:T(8,128)(2,1)} %q_ref.2, bf16[1024,1024]{1,0:T(8,128)(2,1)} %k_ref.5, bf16[1024,1024]{1,0:T(8,128)(2,1)} %v_ref.5), custom_call_target="tpu_custom_call" | custom-call | flops 8000000000 | bytes 4194304 | tf_op jit(solution)/shard_map/near_levels/pallas_call | solution.py:344
  23.2 0.0 collective-permute-done.3
  23.2 0.6 collective-permute-start.4
  23.8 4.0 %collective-permute-done.2 = bf16[2,32,1024]{2,1,0:T(8,128)(2,1)S(1)} collective-permute-done((bf16[2,32,1024]{2,1,0:T(8,128)(2,1)S(1)}, bf16[2,32,1024]{2,1,0:T(8,128)(2,1)S(1)}, u32[]{:S(2)}, u32[]{:S(2)}) %collective-permute-start.2) | collective-permute-done | bytes 131104 | tf_op jit(solution)/shard_map/ppermute | solution.py:603
  27.8 0.0 collective-permute-done.7
  27.8 0.1 collective-permute-start.8
  27.9 2.0 %collective-permute-start.6 = (bf16[2,64,1024]{2,1,0:T(8,128)(2,1)S(1)}, bf16[2,64,1024]{2,1,0:T(8,128)(2,1)S(1)}, u32[]{:S(2)}, u32[]{:S(2)}) collective-permute-start(bf16[2,64,1024]{2,1,0:T(8,128)(2,1)S(1)} %pad_maximum_fusion.1), channel_id=1, source_target_pairs={{4,0},{5,1},{6,2},{7,3},{0,4},{1,5},{2,6},{3,7},{12,8},{13,9},{14,... | collective-permute-start | bytes 786440 | tf_op jit(solution)/shard_map/ppermute | solution.py:603
  29.9 5.3 %near_levels.4 = (f32[384,1024]{1,0:T(8,128)}, f32[3,8,1024]{2,1,0:T(8,128)}, bf16[768,384]{1,0:T(8,128)(2,1)}) custom-call(bf16[576,256]{1,0:T(8,128)(2,1)} %constant.14.pool_ref, bf16[1024,1024]{1,0:T(8,128)(2,1)} %q_ref.2, bf16[1024,1024]{1,0:T(8,128)(2,1)} %k_ref.5, bf16[1024,1024]{1,0:T(8,128)(2,1)} %v_ref.5), custom_call_target="tpu_custom_call" | custom-call | flops 8000000000 | bytes 4194304 | tf_op jit(solution)/shard_map/near_levels/pallas_call | solution.py:344
  35.2 0.0 collective-permute-done.8
  35.3 1.6 %collective-permute-start.9 = (bf16[2,64,1024]{2,1,0:T(8,128)(2,1)S(1)}, bf16[2,64,1024]{2,1,0:T(8,128)(2,1)S(1)}, u32[]{:S(2)}, u32[]{:S(2)}) collective-permute-start(bf16[2,64,1024]{2,1,0:T(8,128)(2,1)S(1)} %constant_dynamic-update-slice_fusion.5), channel_id=1, source_target_pairs={{2,0},{3,1},{0,2},{1,3},{6,4},{7,5},{4,6},{5,7},{10,8},{11,9},{8,1... | collective-permute-start | bytes 786440 | tf_op jit(solution)/shard_map/ppermute | solution.py:603
  36.8 0.0 collective-permute-done
  36.9 0.0 collective-permute-done.4
  36.9 0.0 copy-start.1
  36.9 0.1 collective-permute-start.5
  37.0 0.0 collective-permute-done.6
  37.1 4.5 %near_levels.5 = (f32[256,1024]{1,0:T(8,128)}, f32[2,8,1024]{2,1,0:T(8,128)}, bf16[768,256]{1,0:T(8,128)(2,1)}) custom-call(bf16[576,256]{1,0:T(8,128)(2,1)} %constant.14.pool_ref, bf16[1024,1024]{1,0:T(8,128)(2,1)} %q_ref.2, bf16[1024,1024]{1,0:T(8,128)(2,1)} %k_ref.5, bf16[1024,1024]{1,0:T(8,128)(2,1)} %v_ref.5), custom_call_target="tpu_custom_call" | custom-call | flops 8000000000 | bytes 4194304 | tf_op jit(solution)/shard_map/near_levels/pallas_call | solution.py:344
  41.6 0.0 copy-done.1
  41.6 0.1 collective-permute-done.9
  41.8 0.0 copy-start
  41.8 0.2 collective-permute-start.10
  42.0 0.0 collective-permute-done.11.refs_4_
  42.0 0.0 collective-permute-done.5.refs_1_
  42.0 2.5 %collective-permute-done.10.refs_3_ = bf16[2,256,1024]{2,1,0:T(8,128)(2,1)S(1)} collective-permute-done((bf16[2,256,1024]{2,1,0:T(8,128)(2,1)S(1)}, bf16[2,256,1024]{2,1,0:T(8,128)(2,1)S(1)}, u32[]{:S(2)}, u32[]{:S(2)}) %collective-permute-start.10) | collective-permute-done | bytes 1048608 | tf_op jit(solution)/shard_map/ppermute | solution.py:603
  44.6 0.0 copy-done
  44.6 0.0 copy-start.2
  44.6 1.0 %copy-done.2 = bf16[2,256,1024]{2,1,0:T(8,128)(2,1)} copy-done((bf16[2,256,1024]{2,1,0:T(8,128)(2,1)}, bf16[2,256,1024]{2,1,0:T(8,128)(2,1)S(1)}, u32[]{:S(2)}) %copy-start.2) | copy-done | bytes 1048600
  45.6 14.2 %far_levels_projection.1 = bf16[1024,2048]{1,0:T(8,128)(2,1)} custom-call(bf16[2,256,1024]{2,1,0:T(8,128)(2,1)} %copy-done.1, bf16[2,256,1024]{2,1,0:T(8,128)(2,1)} %collective-permute-done.5.refs_1_, bf16[2,256,1024]{2,1,0:T(8,128)(2,1)} %copy-done, bf16[2,256,1024]{2,1,0:T(8,128)(2,1)} %copy-done.2, bf16[2,256,1024]{2,1,0:T(8,128)(2,1)} %collective-permute-done.11.refs_4_, ...), custom_call_target="tpu_custom_call" | custom-call | flops 6499999744 | bytes 18874368 | tf_op jit(solution)/shard_map/far_levels_projection/pallas_call | solution.py:574
  (14 shorter events, 0.3 us)
Async XLA Ops:
  5.3 8.2 %collective-permute-start.1 = (bf16[2,48,1024]{2,1,0:T(8,128)(2,1)}, bf16[2,48,1024]{2,1,0:T(8,128)(2,1)S(1)}, u32[]{:S(2)}, u32[]{:S(2)}) collective-permute-start(bf16[2,48,1024]{2,1,0:T(8,128)(2,1)} %get-tuple-element.29), channel_id=1, source_target_pairs={{8,0},{9,1},{10,2},{11,3},{12,4},{13,5},{14,6},{15,7},{0,8},{1,9},... | collective-permute-start | bytes 589832 | tf_op jit(solution)/shard_map/ppermute | solution.py:603
  8.4 14.8 %collective-permute-start.3 = (bf16[2,64,1024]{2,1,0:T(8,128)(2,1)}, bf16[2,64,1024]{2,1,0:T(8,128)(2,1)S(1)}, u32[]{:S(2)}, u32[]{:S(2)}) collective-permute-start(bf16[2,64,1024]{2,1,0:T(8,128)(2,1)} %get-tuple-element.39), channel_id=1, source_target_pairs={{4,0},{5,1},{6,2},{7,3},{0,4},{1,5},{2,6},{3,7},{12,8},{13,9},{14,... | collective-permute-start | bytes 786440 | tf_op jit(solution)/shard_map/ppermute | solution.py:603
  9.9 26.9 %collective-permute-start = (bf16[2,128,1024]{2,1,0:T(8,128)(2,1)}, bf16[2,128,1024]{2,1,0:T(8,128)(2,1)S(1)}, u32[]{:S(2)}, u32[]{:S(2)}) collective-permute-start(bf16[2,128,1024]{2,1,0:T(8,128)(2,1)} %get-tuple-element.28), channel_id=1, source_target_pairs={{2,0},{3,1},{0,2},{1,3},{6,4},{7,5},{4,6},{5,7},{10,8},{11,9},{8,1... | collective-permute-start | bytes 1572872 | tf_op jit(solution)/shard_map/ppermute | solution.py:603
  11.4 30.7 %collective-permute-start.11 = (bf16[2,256,1024]{2,1,0:T(8,128)(2,1)}, bf16[2,256,1024]{2,1,0:T(8,128)(2,1)}, u32[]{:S(2)}, u32[]{:S(2)}) collective-permute-start(bf16[2,256,1024]{2,1,0:T(8,128)(2,1)} %get-tuple-element.50), channel_id=1, source_target_pairs={{1,0},{0,1},{3,2},{2,3},{5,4},{4,5},{7,6},{6,7},{9,8},{8,9},{11,10... | collective-permute-start | bytes 3145736 | tf_op jit(solution)/shard_map/ppermute | solution.py:603
  13.5 14.3 %collective-permute-start.2 = (bf16[2,32,1024]{2,1,0:T(8,128)(2,1)S(1)}, bf16[2,32,1024]{2,1,0:T(8,128)(2,1)S(1)}, u32[]{:S(2)}, u32[]{:S(2)}) collective-permute-start(bf16[2,32,1024]{2,1,0:T(8,128)(2,1)S(1)} %slice.12), channel_id=1, source_target_pairs={{2,0},{3,1},{0,2},{1,3},{6,4},{7,5},{4,6},{5,7},{10,8},{11,9},{8,1... | collective-permute-start | bytes 393224 | tf_op jit(solution)/shard_map/ppermute | solution.py:603
  15.2 12.6 %collective-permute-start.7 = (bf16[2,32,1024]{2,1,0:T(8,128)(2,1)S(1)}, bf16[2,32,1024]{2,1,0:T(8,128)(2,1)S(1)}, u32[]{:S(2)}, u32[]{:S(2)}) collective-permute-start(bf16[2,32,1024]{2,1,0:T(8,128)(2,1)S(1)} %pad_maximum_fusion.2), channel_id=1, source_target_pairs={{16,0},{17,1},{18,2},{19,3},{20,4},{21,5},{22,6},{23,7},{24,8},{25... | collective-permute-start | bytes 393224 | tf_op jit(solution)/shard_map/ppermute | solution.py:603
  23.2 13.7 %collective-permute-start.4 = (bf16[2,64,1024]{2,1,0:T(8,128)(2,1)S(1)}, bf16[2,64,1024]{2,1,0:T(8,128)(2,1)S(1)}, u32[]{:S(2)}, u32[]{:S(2)}) collective-permute-start(bf16[2,64,1024]{2,1,0:T(8,128)(2,1)S(1)} %collective-permute-done.3), channel_id=1, source_target_pairs={{2,0},{3,1},{0,2},{1,3},{6,4},{7,5},{4,6},{5,7},{10,8},{11,9},{8,1... | collective-permute-start | bytes 786440 | tf_op jit(solution)/shard_map/ppermute | solution.py:603
  27.8 7.4 %collective-permute-start.8 = (bf16[2,32,1024]{2,1,0:T(8,128)(2,1)S(1)}, bf16[2,32,1024]{2,1,0:T(8,128)(2,1)S(1)}, u32[]{:S(2)}, u32[]{:S(2)}) collective-permute-start(bf16[2,32,1024]{2,1,0:T(8,128)(2,1)S(1)} %collective-permute-done.7), channel_id=1, source_target_pairs={{4,0},{5,1},{6,2},{7,3},{0,4},{1,5},{2,6},{3,7},{12,8},{13,9},{14,... | collective-permute-start | bytes 393224 | tf_op jit(solution)/shard_map/ppermute | solution.py:603
  27.9 9.2 %collective-permute-start.6 = (bf16[2,64,1024]{2,1,0:T(8,128)(2,1)S(1)}, bf16[2,64,1024]{2,1,0:T(8,128)(2,1)S(1)}, u32[]{:S(2)}, u32[]{:S(2)}) collective-permute-start(bf16[2,64,1024]{2,1,0:T(8,128)(2,1)S(1)} %pad_maximum_fusion.1), channel_id=1, source_target_pairs={{4,0},{5,1},{6,2},{7,3},{0,4},{1,5},{2,6},{3,7},{12,8},{13,9},{14,... | collective-permute-start | bytes 786440 | tf_op jit(solution)/shard_map/ppermute | solution.py:603
  35.3 6.4 %collective-permute-start.9 = (bf16[2,64,1024]{2,1,0:T(8,128)(2,1)S(1)}, bf16[2,64,1024]{2,1,0:T(8,128)(2,1)S(1)}, u32[]{:S(2)}, u32[]{:S(2)}) collective-permute-start(bf16[2,64,1024]{2,1,0:T(8,128)(2,1)S(1)} %constant_dynamic-update-slice_fusion.5), channel_id=1, source_target_pairs={{2,0},{3,1},{0,2},{1,3},{6,4},{7,5},{4,6},{5,7},{10,8},{11,9},{8,1... | collective-permute-start | bytes 786440 | tf_op jit(solution)/shard_map/ppermute | solution.py:603
  36.9 4.6 %copy-start.1 = (bf16[2,256,1024]{2,1,0:T(8,128)(2,1)}, bf16[2,256,1024]{2,1,0:T(8,128)(2,1)S(1)}, u32[]{:S(2)}) copy-start(bf16[2,256,1024]{2,1,0:T(8,128)(2,1)S(1)} %constant_dynamic-update-slice_fusion.refs_0_) | copy-start | bytes 3145732
  36.9 5.1 %collective-permute-start.5 = (bf16[2,256,1024]{2,1,0:T(8,128)(2,1)S(1)}, bf16[2,256,1024]{2,1,0:T(8,128)(2,1)}, u32[]{:S(2)}, u32[]{:S(2)}) collective-permute-start(bf16[2,256,1024]{2,1,0:T(8,128)(2,1)S(1)} %constant_dynamic-update-slice_fusion.refs_0_), channel_id=1, source_target_pairs={{1,0},{0,1},{3,2},{2,3},{5,4},{4,5},{7,6},{6,7},{9,8},{8,9},{11,10... | collective-permute-start | bytes 3145736 | tf_op jit(solution)/shard_map/ppermute | solution.py:603
  41.8 2.7 %copy-start = (bf16[2,256,1024]{2,1,0:T(8,128)(2,1)}, bf16[2,256,1024]{2,1,0:T(8,128)(2,1)S(1)}, u32[]{:S(2)}) copy-start(bf16[2,256,1024]{2,1,0:T(8,128)(2,1)S(1)} %constant_dynamic-update-slice_fusion.7.refs_2_) | copy-start | bytes 3145732
  41.8 2.7 %collective-permute-start.10 = (bf16[2,256,1024]{2,1,0:T(8,128)(2,1)S(1)}, bf16[2,256,1024]{2,1,0:T(8,128)(2,1)S(1)}, u32[]{:S(2)}, u32[]{:S(2)}) collective-permute-start(bf16[2,256,1024]{2,1,0:T(8,128)(2,1)S(1)} %constant_dynamic-update-slice_fusion.7.refs_2_), channel_id=1, source_target_pairs={{1,0},{0,1},{3,2},{2,3},{5,4},{4,5},{7,6},{6,7},{9,8},{8,9},{11,10... | collective-permute-start | bytes 3145736 | tf_op jit(solution)/shard_map/ppermute | solution.py:603
  44.6 1.0 %copy-start.2 = (bf16[2,256,1024]{2,1,0:T(8,128)(2,1)}, bf16[2,256,1024]{2,1,0:T(8,128)(2,1)S(1)}, u32[]{:S(2)}) copy-start(bf16[2,256,1024]{2,1,0:T(8,128)(2,1)S(1)} %collective-permute-done.10.refs_3_) | copy-start | bytes 3145732

commit v8 on v7

--- a/solution.py
+++ b/solution.py
@@ -93,11 +93,11 @@
 
 
 def packed(levels):
-    places, rows = {level: (level - FIRST, 0) for level in range(FIRST, TOP)}, 0
+    places, rows = {2: (0, 0), 3: (1, 0), 4: (3, 0)}, 0
     for level in range(TOP, levels + 1):
-        places[level] = (TOP - FIRST, rows)
+        places[level] = (4, rows)
         rows += TOK >> level
-    return places, [TOK >> level for level in range(FIRST, TOP)] + [rows]
+    return places, [TOK >> 2, TOK >> 4, TOK >> 4, TOK >> 4, rows]
 
 
 def pool_kernel(levels, small_ref, large_ref, keys_ref, values_ref, *refs):
@@ -126,6 +126,11 @@
             offset = 0
             for level in range(FIRST, min(levels, 6) + 1):
                 rows = 2 * BLOCK >> level
+                if level == 3:
+                    for place, tile in enumerate(tiles):
+                        outs[1 + place][index, :, cols] = tile[offset : offset + rows].astype(jnp.bfloat16)
+                    offset += rows
+                    continue
                 both = jnp.concatenate([tile[offset : offset + rows] for tile in tiles], axis=0)
                 place, first = places[level]
                 outs[place][index, first : first + 2 * rows, cols] = both.astype(jnp.bfloat16)
@@ -446,12 +451,19 @@
         pltpu.make_async_copy(w_ref.at[rows], weights.at[rows], near_sems.at[3 * slices + 1 + index])
         for index, rows in enumerate((slice(0, half), slice(half, WIDTH)))
     ]
-    started = far_copies + kv_copies(0) + near_copies[0] + kv_copies(1) + [turn_copy] + near_copies[1]
-    started += [w_copies[0]] + kv_copies(2) + kv_copies(3)
-    for copies in near_copies[2:]:
-        started += copies
-    for copy in started + [w_copies[1]]:
-        copy.start()
+    stages = [
+        far_copies[:1] + kv_copies(0) + near_copies[0],
+        far_copies[1:2] + kv_copies(1) + [turn_copy],
+        far_copies[2:] + kv_copies(2) + near_copies[1] + w_copies[:1],
+        kv_copies(3) + near_copies[2] + w_copies[1:],
+    ]
+
+    def start_stage(number):
+        for copy in stages[number]:
+            copy.start()
+
+    start_stage(0)
+    start_stage(1)
 
     def turned(part):
         cols = slice(part * half, (part + 1) * half)
@@ -513,8 +525,9 @@
 
     position = lax.axis_index("seq")
     order = list(range(levels, FIRST - 1, -1))
-    for copy in far_copies + kv_copies(0):
+    for copy in far_copies[:1] + kv_copies(0):
         copy.wait()
+    start_stage(2)
     for level in order:
         score(0, level)
     for copy in near_copies[0]:
@@ -525,6 +538,11 @@
         if head % 2 == 1 and head + 1 < HEADS:
             for copy in kv_copies((head + 1) // 2):
                 copy.wait()
+        for index, (first, _) in enumerate(SLICES):
+            if index and first == head + 1:
+                far_copies[index].wait()
+        if head == 1:
+            start_stage(3)
         for index, (first, _) in enumerate(SLICES):
             if index and first == head:
                 for copy in near_copies[index]:
@@ -624,7 +642,7 @@
     pooled = pool_call(keys, values, levels)
 
     places, _ = packed(levels)
-    blocks = {level: pooled[level - FIRST] for level in range(FIRST, TOP)}
+    blocks = {2: pooled[0], 4: pooled[3]}
     for level in range(TOP, levels + 1):
         place, first = places[level]
         blocks[level] = pooled[place][:, first : first + (TOK >> level)]
@@ -645,9 +663,10 @@
                 blocks[level] = jnp.concatenate([blocks[level], piece], axis=1)
         if distance == GROUP:
             fourth = moved(blocks[4], 4)
-            third = moved(blocks[3], 2)
-            second = moved(blocks[2], 1)
+            third = [moved(pooled[1], 2)]
             arrived = blocks[TOP]
+            third.append(moved(after(pooled[2], arrived), 2))
+            second = moved(after(blocks[2], arrived), 1)
 
     upper = [blocks[level] for level in high[1:]]
     five = gathered([arrived], 2)
@@ -657,7 +676,7 @@
     fourth = gathered([after(fourth, near[0])], 2)[0]
     near.append(near_call(after(queries, (near[0], five)), keys, values, levels, 1))
     upper_x = gathered(after(upper, near[1]), 2)
-    low = jnp.concatenate([after(third, near[1]), fourth], axis=1)
+    low = jnp.concatenate([*after(third, near[1]), fourth], axis=1)
     low_got = moved(low, 1)
     near.append(near_call(after(queries, (near[1], upper, five_y)), keys, values, levels, 2))
     top = jnp.concatenate(after(five_y + upper_x, near[2]), axis=1)

time: 60.2 us -> 62.1 us (1.032)
  waiting for transfers between devices: 7.91 us -> 10.8 us
  local copies, waits for them, and re-layouts: 2.73 us -> 1.68 us
    ppermute x12 -> x13, waiting for transfers between devices: 7.91 us -> 10.8 us  [moved(): lax.ppermute(array, 'seq', [(i ^ distance, i) for i in range(lax.axis_siz...]
    unnamed x11 -> x10, local copies, waits for them, and re-layouts: 1.16 us -> 0.13 us
    ppermute x12 -> x13, starting transfers between devices: 15 us -> 15.6 us  [moved(): lax.ppermute(array, 'seq', [(i ^ distance, i) for i in range(lax.axis_siz...]
  transfers between devices with their start and end apart: 12 -> 13, of which waited for: 4 -> 3; matrix products, arithmetic and copies ran while one was open for 2% -> 2% of each run, Pallas kernels for 25% -> 24%
where the time goes in v8:
time: 62.1 us; the launch traced here: 61.9 us
  Pallas kernels  33.4 us (54%)
  starting transfers between devices  15.6 us (25%)
  waiting for transfers between devices  10.8 us (17%)
  local copies, waits for them, and re-layouts  1.68 us (3%)
    ppermute x13, starting transfers between devices, moved(): lax.ppermute(array, 'seq', [(i ^ distance, i) for i in range(lax.axis_siz...  15.6 us
    pallas_call x3, Pallas kernels, near_call(): pl.pallas_call(functools.partial(near_kernel, levels, first, heads), in_s...  14.8 us
    pallas_call x1, Pallas kernels, far_call(): pl.pallas_call(functools.partial(far_kernel, levels, plan), in_specs=[HBM...  13.9 us
    ppermute x13, waiting for transfers between devices, moved(): lax.ppermute(array, 'seq', [(i ^ distance, i) for i in range(lax.axis_siz...  10.8 us
    pallas_call x1, Pallas kernels, pool_call(): pl.pallas_call(functools.partial(pool_kernel, levels), in_specs=[HBM] * 4...  4.71 us
  transfers between devices with their start and end apart: 13, of which 3 were waited for; matrix products, arithmetic and copies ran while one was open for 2% of the time, Pallas kernels for 24%

profile of v8, /device:TPU:0, one launch (start us, length us, event | category | flops | bytes accessed | tf_op | source)
XLA Modules:
  0.0 61.9 jit_solution(13393333251786335563)
XLA Ops:
  0.0 0.6 broadcast.1.large_ref
  0.6 4.7 %pool_keys_values.1 = (bf16[2,256,1024]{2,1,0:T(8,128)(2,1)}, bf16[2,64,1024]{2,1,0:T(8,128)(2,1)}, bf16[2,64,1024]{2,1,0:T(8,128)(2,1)}, bf16[2,64,1024]{2,1,0:T(8,128)(2,1)}, bf16[2,48,1024]{2,1,0:T(8,128)(2,1)}) custom-call(bf16[256,512]{1,0:T(8,128)(2,1)} %constant.12.small_ref, bf16[16,1024]{1,0:T(8,128)(2,1)} %broadcast.1.large_ref, ...), custom_call_target="tpu_custom_call" | custom-call | flops 1073741824 | bytes 6291456 | tf_op jit(solution)/shard_map/pool_keys_values/pallas_call | solution.py:157
  5.3 3.1 %collective-permute-start.1 = (bf16[2,48,1024]{2,1,0:T(8,128)(2,1)}, bf16[2,48,1024]{2,1,0:T(8,128)(2,1)S(1)}, u32[]{:S(2)}, u32[]{:S(2)}) collective-permute-start(bf16[2,48,1024]{2,1,0:T(8,128)(2,1)} %get-tuple-element.34), channel_id=1, source_target_pairs={{8,0},{9,1},{10,2},{11,3},{12,4},{13,5},{14,6},{15,7},{0,8},{1,9},... | collective-permute-start | bytes 589832 | tf_op jit(solution)/shard_map/ppermute | solution.py:621
  8.4 1.5 %collective-permute-start = (bf16[2,64,1024]{2,1,0:T(8,128)(2,1)}, bf16[2,64,1024]{2,1,0:T(8,128)(2,1)S(1)}, u32[]{:S(2)}, u32[]{:S(2)}) collective-permute-start(bf16[2,64,1024]{2,1,0:T(8,128)(2,1)} %get-tuple-element.32), channel_id=1, source_target_pairs={{2,0},{3,1},{0,2},{1,3},{6,4},{7,5},{4,6},{5,7},{10,8},{11,9},{8,1... | collective-permute-start | bytes 786440 | tf_op jit(solution)/shard_map/ppermute | solution.py:621
  9.9 1.5 %collective-permute-start.4 = (bf16[2,64,1024]{2,1,0:T(8,128)(2,1)}, bf16[2,64,1024]{2,1,0:T(8,128)(2,1)S(1)}, u32[]{:S(2)}, u32[]{:S(2)}) collective-permute-start(bf16[2,64,1024]{2,1,0:T(8,128)(2,1)} %get-tuple-element.46), channel_id=1, source_target_pairs={{4,0},{5,1},{6,2},{7,3},{0,4},{1,5},{2,6},{3,7},{12,8},{13,9},{14,... | collective-permute-start | bytes 786440 | tf_op jit(solution)/shard_map/ppermute | solution.py:621
  11.4 0.8 %slice.10 = bf16[2,16,1024]{2,1,0:T(8,128)(2,1)S(1)} slice(bf16[2,48,1024]{2,1,0:T(8,128)(2,1)} %get-tuple-element.34), slice={[0:2], [32:48], [0:1024]} | slice | bytes 131072 | tf_op jit(solution)/shard_map/slice | solution.py:648
  12.3 1.2 %collective-permute-done.1 = bf16[2,48,1024]{2,1,0:T(8,128)(2,1)S(1)} collective-permute-done((bf16[2,48,1024]{2,1,0:T(8,128)(2,1)}, bf16[2,48,1024]{2,1,0:T(8,128)(2,1)S(1)}, u32[]{:S(2)}, u32[]{:S(2)}) %collective-permute-start.1) | collective-permute-done | bytes 196640 | tf_op jit(solution)/shard_map/ppermute | solution.py:621
  13.5 1.7 %collective-permute-start.3 = (bf16[2,32,1024]{2,1,0:T(8,128)(2,1)S(1)}, bf16[2,32,1024]{2,1,0:T(8,128)(2,1)S(1)}, u32[]{:S(2)}, u32[]{:S(2)}) collective-permute-start(bf16[2,32,1024]{2,1,0:T(8,128)(2,1)S(1)} %slice.12), channel_id=1, source_target_pairs={{2,0},{3,1},{0,2},{1,3},{6,4},{7,5},{4,6},{5,7},{10,8},{11,9},{8,1... | collective-permute-start | bytes 393224 | tf_op jit(solution)/shard_map/ppermute | solution.py:621
  15.3 2.7 %collective-permute-start.8 = (bf16[2,32,1024]{2,1,0:T(8,128)(2,1)S(1)}, bf16[2,32,1024]{2,1,0:T(8,128)(2,1)S(1)}, u32[]{:S(2)}, u32[]{:S(2)}) collective-permute-start(bf16[2,32,1024]{2,1,0:T(8,128)(2,1)S(1)} %pad_maximum_fusion.2), channel_id=1, source_target_pairs={{16,0},{17,1},{18,2},{19,3},{20,4},{21,5},{22,6},{23,7},{24,8},{25... | collective-permute-start | bytes 393224 | tf_op jit(solution)/shard_map/ppermute | solution.py:621
  17.9 0.5 collective-permute-start.2
  18.5 5.3 %near_levels.3 = (f32[384,1024]{1,0:T(8,128)}, f32[3,8,1024]{2,1,0:T(8,128)}, bf16[768,384]{1,0:T(8,128)(2,1)}) custom-call(bf16[576,256]{1,0:T(8,128)(2,1)} %constant.14.pool_ref, bf16[1024,1024]{1,0:T(8,128)(2,1)} %q_ref.2, bf16[1024,1024]{1,0:T(8,128)(2,1)} %k_ref.5, bf16[1024,1024]{1,0:T(8,128)(2,1)} %v_ref.5), custom_call_target="tpu_custom_call" | custom-call | flops 8000000000 | bytes 4194304 | tf_op jit(solution)/shard_map/near_levels/pallas_call | solution.py:349
  23.8 0.0 collective-permute-done.4
  23.8 0.1 collective-permute-start.12
  23.9 0.0 collective-permute-done.8
  23.9 1.6 %collective-permute-start.5 = (bf16[2,64,1024]{2,1,0:T(8,128)(2,1)S(1)}, bf16[2,64,1024]{2,1,0:T(8,128)(2,1)S(1)}, u32[]{:S(2)}, u32[]{:S(2)}) collective-permute-start(bf16[2,64,1024]{2,1,0:T(8,128)(2,1)S(1)} %collective-permute-done.4), channel_id=1, source_target_pairs={{2,0},{3,1},{0,2},{1,3},{6,4},{7,5},{4,6},{5,7},{10,8},{11,9},{8,1... | collective-permute-start | bytes 786440 | tf_op jit(solution)/shard_map/ppermute | solution.py:621
  25.4 0.0 collective-permute-done.3
  25.4 1.6 %collective-permute-start.9 = (bf16[2,32,1024]{2,1,0:T(8,128)(2,1)S(1)}, bf16[2,32,1024]{2,1,0:T(8,128)(2,1)S(1)}, u32[]{:S(2)}, u32[]{:S(2)}) collective-permute-start(bf16[2,32,1024]{2,1,0:T(8,128)(2,1)S(1)} %collective-permute-done.8), channel_id=1, source_target_pairs={{4,0},{5,1},{6,2},{7,3},{0,4},{1,5},{2,6},{3,7},{12,8},{13,9},{14,... | collective-permute-start | bytes 393224 | tf_op jit(solution)/shard_map/ppermute | solution.py:621
  27.0 5.3 %near_levels.4 = (f32[384,1024]{1,0:T(8,128)}, f32[3,8,1024]{2,1,0:T(8,128)}, bf16[768,384]{1,0:T(8,128)(2,1)}) custom-call(bf16[576,256]{1,0:T(8,128)(2,1)} %constant.14.pool_ref, bf16[1024,1024]{1,0:T(8,128)(2,1)} %q_ref.2, bf16[1024,1024]{1,0:T(8,128)(2,1)} %k_ref.5, bf16[1024,1024]{1,0:T(8,128)(2,1)} %v_ref.5), custom_call_target="tpu_custom_call" | custom-call | flops 8000000000 | bytes 4194304 | tf_op jit(solution)/shard_map/near_levels/pallas_call | solution.py:349
  32.4 0.0 collective-permute-done.9
  32.4 0.6 collective-permute-start.7
  33.0 0.0 collective-permute-done
  33.0 0.0 collective-permute-done.2
  33.0 0.6 collective-permute-start.10
  33.7 0.0 collective-permute-done.5
  33.7 0.0 copy-start.1
  33.7 0.1 collective-permute-start.6
  33.8 6.7 %collective-permute-done.7 = bf16[2,64,1024]{2,1,0:T(8,128)(2,1)S(1)} collective-permute-done((bf16[2,64,1024]{2,1,0:T(8,128)(2,1)S(1)}, bf16[2,64,1024]{2,1,0:T(8,128)(2,1)S(1)}, u32[]{:S(2)}, u32[]{:S(2)}) %collective-permute-start.7) | collective-permute-done | bytes 262176 | tf_op jit(solution)/shard_map/ppermute | solution.py:621
  40.6 4.3 %near_levels.5 = (f32[256,1024]{1,0:T(8,128)}, f32[2,8,1024]{2,1,0:T(8,128)}, bf16[768,256]{1,0:T(8,128)(2,1)}) custom-call(bf16[576,256]{1,0:T(8,128)(2,1)} %constant.14.pool_ref, bf16[1024,1024]{1,0:T(8,128)(2,1)} %q_ref.2, bf16[1024,1024]{1,0:T(8,128)(2,1)} %k_ref.5, bf16[1024,1024]{1,0:T(8,128)(2,1)} %v_ref.5), custom_call_target="tpu_custom_call" | custom-call | flops 8000000000 | bytes 4194304 | tf_op jit(solution)/shard_map/near_levels/pallas_call | solution.py:349
  44.8 0.0 copy-done.1
  44.9 0.0 collective-permute-done.10
  45.0 0.0 copy-start
  45.0 0.1 collective-permute-start.11
  45.1 0.0 collective-permute-done.12.refs_4_
  45.1 0.0 collective-permute-done.6.refs_1_
  45.1 2.8 %collective-permute-done.11.refs_3_ = bf16[2,256,1024]{2,1,0:T(8,128)(2,1)} collective-permute-done((bf16[2,256,1024]{2,1,0:T(8,128)(2,1)S(1)}, bf16[2,256,1024]{2,1,0:T(8,128)(2,1)}, u32[]{:S(2)}, u32[]{:S(2)}) %collective-permute-start.11) | collective-permute-done | bytes 1048608 | tf_op jit(solution)/shard_map/ppermute | solution.py:621
  47.9 0.0 copy-done
  47.9 13.9 %far_levels_projection.1 = bf16[1024,2048]{1,0:T(8,128)(2,1)} custom-call(bf16[2,256,1024]{2,1,0:T(8,128)(2,1)} %copy-done.1, bf16[2,256,1024]{2,1,0:T(8,128)(2,1)} %collective-permute-done.6.refs_1_, bf16[2,256,1024]{2,1,0:T(8,128)(2,1)} %copy-done, bf16[2,256,1024]{2,1,0:T(8,128)(2,1)} %collective-permute-done.11.refs_3_, ...), custom_call_target="tpu_custom_call" | custom-call | flops 6499999744 | bytes 18874368 | tf_op jit(solution)/shard_map/far_levels_projection/pallas_call | solution.py:592
  (15 shorter events, 0.3 us)
Async XLA Ops:
  5.3 8.2 %collective-permute-start.1 = (bf16[2,48,1024]{2,1,0:T(8,128)(2,1)}, bf16[2,48,1024]{2,1,0:T(8,128)(2,1)S(1)}, u32[]{:S(2)}, u32[]{:S(2)}) collective-permute-start(bf16[2,48,1024]{2,1,0:T(8,128)(2,1)} %get-tuple-element.34), channel_id=1, source_target_pairs={{8,0},{9,1},{10,2},{11,3},{12,4},{13,5},{14,6},{15,7},{0,8},{1,9},... | collective-permute-start | bytes 589832 | tf_op jit(solution)/shard_map/ppermute | solution.py:621
  8.4 24.6 %collective-permute-start = (bf16[2,64,1024]{2,1,0:T(8,128)(2,1)}, bf16[2,64,1024]{2,1,0:T(8,128)(2,1)S(1)}, u32[]{:S(2)}, u32[]{:S(2)}) collective-permute-start(bf16[2,64,1024]{2,1,0:T(8,128)(2,1)} %get-tuple-element.32), channel_id=1, source_target_pairs={{2,0},{3,1},{0,2},{1,3},{6,4},{7,5},{4,6},{5,7},{10,8},{11,9},{8,1... | collective-permute-start | bytes 786440 | tf_op jit(solution)/shard_map/ppermute | solution.py:621
  9.9 13.9 %collective-permute-start.4 = (bf16[2,64,1024]{2,1,0:T(8,128)(2,1)}, bf16[2,64,1024]{2,1,0:T(8,128)(2,1)S(1)}, u32[]{:S(2)}, u32[]{:S(2)}) collective-permute-start(bf16[2,64,1024]{2,1,0:T(8,128)(2,1)} %get-tuple-element.46), channel_id=1, source_target_pairs={{4,0},{5,1},{6,2},{7,3},{0,4},{1,5},{2,6},{3,7},{12,8},{13,9},{14,... | collective-permute-start | bytes 786440 | tf_op jit(solution)/shard_map/ppermute | solution.py:621
  13.5 11.9 %collective-permute-start.3 = (bf16[2,32,1024]{2,1,0:T(8,128)(2,1)S(1)}, bf16[2,32,1024]{2,1,0:T(8,128)(2,1)S(1)}, u32[]{:S(2)}, u32[]{:S(2)}) collective-permute-start(bf16[2,32,1024]{2,1,0:T(8,128)(2,1)S(1)} %slice.12), channel_id=1, source_target_pairs={{2,0},{3,1},{0,2},{1,3},{6,4},{7,5},{4,6},{5,7},{10,8},{11,9},{8,1... | collective-permute-start | bytes 393224 | tf_op jit(solution)/shard_map/ppermute | solution.py:621
  15.3 8.6 %collective-permute-start.8 = (bf16[2,32,1024]{2,1,0:T(8,128)(2,1)S(1)}, bf16[2,32,1024]{2,1,0:T(8,128)(2,1)S(1)}, u32[]{:S(2)}, u32[]{:S(2)}) collective-permute-start(bf16[2,32,1024]{2,1,0:T(8,128)(2,1)S(1)} %pad_maximum_fusion.2), channel_id=1, source_target_pairs={{16,0},{17,1},{18,2},{19,3},{20,4},{21,5},{22,6},{23,7},{24,8},{25... | collective-permute-start | bytes 393224 | tf_op jit(solution)/shard_map/ppermute | solution.py:621
  17.9 15.1 %collective-permute-start.2 = (bf16[2,64,1024]{2,1,0:T(8,128)(2,1)}, bf16[2,64,1024]{2,1,0:T(8,128)(2,1)S(1)}, u32[]{:S(2)}, u32[]{:S(2)}) collective-permute-start(bf16[2,64,1024]{2,1,0:T(8,128)(2,1)} %get-tuple-element.35), channel_id=1, source_target_pairs={{2,0},{3,1},{0,2},{1,3},{6,4},{7,5},{4,6},{5,7},{10,8},{11,9},{8,1... | collective-permute-start | bytes 786440 | tf_op jit(solution)/shard_map/ppermute | solution.py:621
  23.8 21.3 %collective-permute-start.12 = (bf16[2,256,1024]{2,1,0:T(8,128)(2,1)}, bf16[2,256,1024]{2,1,0:T(8,128)(2,1)}, u32[]{:S(2)}, u32[]{:S(2)}) collective-permute-start(bf16[2,256,1024]{2,1,0:T(8,128)(2,1)} %get-tuple-element.58), channel_id=1, source_target_pairs={{1,0},{0,1},{3,2},{2,3},{5,4},{4,5},{7,6},{6,7},{9,8},{8,9},{11,10... | collective-permute-start | bytes 3145736 | tf_op jit(solution)/shard_map/ppermute | solution.py:621
  23.9 9.8 %collective-permute-start.5 = (bf16[2,64,1024]{2,1,0:T(8,128)(2,1)S(1)}, bf16[2,64,1024]{2,1,0:T(8,128)(2,1)S(1)}, u32[]{:S(2)}, u32[]{:S(2)}) collective-permute-start(bf16[2,64,1024]{2,1,0:T(8,128)(2,1)S(1)} %collective-permute-done.4), channel_id=1, source_target_pairs={{2,0},{3,1},{0,2},{1,3},{6,4},{7,5},{4,6},{5,7},{10,8},{11,9},{8,1... | collective-permute-start | bytes 786440 | tf_op jit(solution)/shard_map/ppermute | solution.py:621
  25.4 7.0 %collective-permute-start.9 = (bf16[2,32,1024]{2,1,0:T(8,128)(2,1)S(1)}, bf16[2,32,1024]{2,1,0:T(8,128)(2,1)S(1)}, u32[]{:S(2)}, u32[]{:S(2)}) collective-permute-start(bf16[2,32,1024]{2,1,0:T(8,128)(2,1)S(1)} %collective-permute-done.8), channel_id=1, source_target_pairs={{4,0},{5,1},{6,2},{7,3},{0,4},{1,5},{2,6},{3,7},{12,8},{13,9},{14,... | collective-permute-start | bytes 393224 | tf_op jit(solution)/shard_map/ppermute | solution.py:621
  32.4 8.2 %collective-permute-start.7 = (bf16[2,64,1024]{2,1,0:T(8,128)(2,1)S(1)}, bf16[2,64,1024]{2,1,0:T(8,128)(2,1)S(1)}, u32[]{:S(2)}, u32[]{:S(2)}) collective-permute-start(bf16[2,64,1024]{2,1,0:T(8,128)(2,1)S(1)} %pad_maximum_fusion.1), channel_id=1, source_target_pairs={{4,0},{5,1},{6,2},{7,3},{0,4},{1,5},{2,6},{3,7},{12,8},{13,9},{14,... | collective-permute-start | bytes 786440 | tf_op jit(solution)/shard_map/ppermute | solution.py:621
  33.0 11.9 %collective-permute-start.10 = (bf16[2,64,1024]{2,1,0:T(8,128)(2,1)S(1)}, bf16[2,64,1024]{2,1,0:T(8,128)(2,1)S(1)}, u32[]{:S(2)}, u32[]{:S(2)}) collective-permute-start(bf16[2,64,1024]{2,1,0:T(8,128)(2,1)S(1)} %constant_dynamic-update-slice_fusion.6), channel_id=1, source_target_pairs={{2,0},{3,1},{0,2},{1,3},{6,4},{7,5},{4,6},{5,7},{10,8},{11,9},{8,1... | collective-permute-start | bytes 786440 | tf_op jit(solution)/shard_map/ppermute | solution.py:621
  33.7 11.1 %copy-start.1 = (bf16[2,256,1024]{2,1,0:T(8,128)(2,1)}, bf16[2,256,1024]{2,1,0:T(8,128)(2,1)S(1)}, u32[]{:S(2)}) copy-start(bf16[2,256,1024]{2,1,0:T(8,128)(2,1)S(1)} %constant_dynamic-update-slice_fusion.refs_0_) | copy-start | bytes 3145732
  33.7 11.4 %collective-permute-start.6 = (bf16[2,256,1024]{2,1,0:T(8,128)(2,1)S(1)}, bf16[2,256,1024]{2,1,0:T(8,128)(2,1)}, u32[]{:S(2)}, u32[]{:S(2)}) collective-permute-start(bf16[2,256,1024]{2,1,0:T(8,128)(2,1)S(1)} %constant_dynamic-update-slice_fusion.refs_0_), channel_id=1, source_target_pairs={{1,0},{0,1},{3,2},{2,3},{5,4},{4,5},{7,6},{6,7},{9,8},{8,9},{11,10... | collective-permute-start | bytes 3145736 | tf_op jit(solution)/shard_map/ppermute | solution.py:621
  45.0 2.9 %copy-start = (bf16[2,256,1024]{2,1,0:T(8,128)(2,1)}, bf16[2,256,1024]{2,1,0:T(8,128)(2,1)S(1)}, u32[]{:S(2)}) copy-start(bf16[2,256,1024]{2,1,0:T(8,128)(2,1)S(1)} %constant_dynamic-update-slice_fusion.8.refs_2_) | copy-start | bytes 3145732
  45.0 2.9 %collective-permute-start.11 = (bf16[2,256,1024]{2,1,0:T(8,128)(2,1)S(1)}, bf16[2,256,1024]{2,1,0:T(8,128)(2,1)}, u32[]{:S(2)}, u32[]{:S(2)}) collective-permute-start(bf16[2,256,1024]{2,1,0:T(8,128)(2,1)S(1)} %constant_dynamic-update-slice_fusion.8.refs_2_), channel_id=1, source_target_pairs={{1,0},{0,1},{3,2},{2,3},{5,4},{4,5},{7,6},{6,7},{9,8},{8,9},{11,10... | collective-permute-start | bytes 3145736 | tf_op jit(solution)/shard_map/ppermute | solution.py:621

commit v9 on v8

--- a/solution.py
+++ b/solution.py
@@ -671,15 +671,14 @@
     upper = [blocks[level] for level in high[1:]]
     five = gathered([arrived], 2)
     near = [near_call(after(queries, arrived), keys, values, levels, 0)]
-    upper = gathered(after(upper, near[0]), 4)
-    five_y = gathered(after(five, near[0]), 4)
+    five_y, *upper = gathered(after(five + upper, near[0]), 4)
     fourth = gathered([after(fourth, near[0])], 2)[0]
     near.append(near_call(after(queries, (near[0], five)), keys, values, levels, 1))
     upper_x = gathered(after(upper, near[1]), 2)
     low = jnp.concatenate([*after(third, near[1]), fourth], axis=1)
     low_got = moved(low, 1)
-    near.append(near_call(after(queries, (near[1], upper, five_y)), keys, values, levels, 2))
-    top = jnp.concatenate(after(five_y + upper_x, near[2]), axis=1)
+    near.append(near_call(after(queries, (near[1], upper)), keys, values, levels, 2))
+    top = jnp.concatenate(after([five_y] + upper_x, near[2]), axis=1)
     top_got = moved(top, 1)
     plan = [(2, 4, (0, 0, BLOCK))]
     for level in (3, 4):

time: 62.1 us -> 61.7 us (level)
    ppermute x13 -> x12, starting transfers between devices: 15.6 us -> 15 us  [moved(): lax.ppermute(array, 'seq', [(i ^ distance, i) for i in range(lax.axis_siz...]
    ppermute x13 -> x12, waiting for transfers between devices: 10.8 us -> 10.8 us  [moved(): lax.ppermute(array, 'seq', [(i ^ distance, i) for i in range(lax.axis_siz...]
  transfers between devices with their start and end apart: 13 -> 12, of which waited for: 3 -> 5; matrix products, arithmetic and copies ran while one was open for 2% -> 2% of each run, Pallas kernels for 24% -> 24%
where the time goes in v9:
time: 61.7 us; the launch traced here: 61.4 us
  Pallas kernels  33.4 us (54%)
  starting transfers between devices  15 us (24%)
  waiting for transfers between devices  10.8 us (18%)
  local copies, waits for them, and re-layouts  1.66 us (3%)
    ppermute x12, starting transfers between devices, moved(): lax.ppermute(array, 'seq', [(i ^ distance, i) for i in range(lax.axis_siz...  15 us
    pallas_call x3, Pallas kernels, near_call(): pl.pallas_call(functools.partial(near_kernel, levels, first, heads), in_s...  14.8 us
    pallas_call x1, Pallas kernels, far_call(): pl.pallas_call(functools.partial(far_kernel, levels, plan), in_specs=[HBM...  13.9 us
    ppermute x12, waiting for transfers between devices, moved(): lax.ppermute(array, 'seq', [(i ^ distance, i) for i in range(lax.axis_siz...  10.8 us
    pallas_call x1, Pallas kernels, pool_call(): pl.pallas_call(functools.partial(pool_kernel, levels), in_specs=[HBM] * 4...  4.71 us
  transfers between devices with their start and end apart: 12, of which 5 were waited for; matrix products, arithmetic and copies ran while one was open for 2% of the time, Pallas kernels for 24%

profile of v9, /device:TPU:0, one launch (start us, length us, event | category | flops | bytes accessed | tf_op | source)
XLA Modules:
  0.0 61.4 jit_solution(8914640060905122874)
XLA Ops:
  0.0 0.6 broadcast.1.large_ref
  0.6 4.7 %pool_keys_values.1 = (bf16[2,256,1024]{2,1,0:T(8,128)(2,1)}, bf16[2,64,1024]{2,1,0:T(8,128)(2,1)}, bf16[2,64,1024]{2,1,0:T(8,128)(2,1)}, bf16[2,64,1024]{2,1,0:T(8,128)(2,1)}, bf16[2,48,1024]{2,1,0:T(8,128)(2,1)}) custom-call(bf16[256,512]{1,0:T(8,128)(2,1)} %constant.12.small_ref, bf16[16,1024]{1,0:T(8,128)(2,1)} %broadcast.1.large_ref, ...), custom_call_target="tpu_custom_call" | custom-call | flops 1073741824 | bytes 6291456 | tf_op jit(solution)/shard_map/pool_keys_values/pallas_call | solution.py:157
  5.3 3.1 %collective-permute-start.1 = (bf16[2,48,1024]{2,1,0:T(8,128)(2,1)}, bf16[2,48,1024]{2,1,0:T(8,128)(2,1)S(1)}, u32[]{:S(2)}, u32[]{:S(2)}) collective-permute-start(bf16[2,48,1024]{2,1,0:T(8,128)(2,1)} %get-tuple-element.34), channel_id=1, source_target_pairs={{8,0},{9,1},{10,2},{11,3},{12,4},{13,5},{14,6},{15,7},{0,8},{1,9},... | collective-permute-start | bytes 589832 | tf_op jit(solution)/shard_map/ppermute | solution.py:621
  8.4 1.5 %collective-permute-start = (bf16[2,64,1024]{2,1,0:T(8,128)(2,1)}, bf16[2,64,1024]{2,1,0:T(8,128)(2,1)S(1)}, u32[]{:S(2)}, u32[]{:S(2)}) collective-permute-start(bf16[2,64,1024]{2,1,0:T(8,128)(2,1)} %get-tuple-element.32), channel_id=1, source_target_pairs={{2,0},{3,1},{0,2},{1,3},{6,4},{7,5},{4,6},{5,7},{10,8},{11,9},{8,1... | collective-permute-start | bytes 786440 | tf_op jit(solution)/shard_map/ppermute | solution.py:621
  9.9 1.5 %collective-permute-start.4 = (bf16[2,64,1024]{2,1,0:T(8,128)(2,1)}, bf16[2,64,1024]{2,1,0:T(8,128)(2,1)S(1)}, u32[]{:S(2)}, u32[]{:S(2)}) collective-permute-start(bf16[2,64,1024]{2,1,0:T(8,128)(2,1)} %get-tuple-element.46), channel_id=1, source_target_pairs={{4,0},{5,1},{6,2},{7,3},{0,4},{1,5},{2,6},{3,7},{12,8},{13,9},{14,... | collective-permute-start | bytes 786440 | tf_op jit(solution)/shard_map/ppermute | solution.py:621
  11.4 0.8 %slice.16 = bf16[2,16,1024]{2,1,0:T(8,128)(2,1)S(1)} slice(bf16[2,48,1024]{2,1,0:T(8,128)(2,1)} %get-tuple-element.34), slice={[0:2], [32:48], [0:1024]} | slice | bytes 131072 | tf_op jit(solution)/shard_map/slice | solution.py:648
  12.3 1.2 %collective-permute-done.1 = bf16[2,48,1024]{2,1,0:T(8,128)(2,1)S(1)} collective-permute-done((bf16[2,48,1024]{2,1,0:T(8,128)(2,1)}, bf16[2,48,1024]{2,1,0:T(8,128)(2,1)S(1)}, u32[]{:S(2)}, u32[]{:S(2)}) %collective-permute-start.1) | collective-permute-done | bytes 196640 | tf_op jit(solution)/shard_map/ppermute | solution.py:621
  13.5 1.7 %collective-permute-start.3 = (bf16[2,32,1024]{2,1,0:T(8,128)(2,1)S(1)}, bf16[2,32,1024]{2,1,0:T(8,128)(2,1)S(1)}, u32[]{:S(2)}, u32[]{:S(2)}) collective-permute-start(bf16[2,32,1024]{2,1,0:T(8,128)(2,1)S(1)} %slice.20), channel_id=1, source_target_pairs={{2,0},{3,1},{0,2},{1,3},{6,4},{7,5},{4,6},{5,7},{10,8},{11,9},{8,1... | collective-permute-start | bytes 393224 | tf_op jit(solution)/shard_map/ppermute | solution.py:621
  15.3 2.7 %collective-permute-start.7 = (bf16[2,32,1024]{2,1,0:T(8,128)(2,1)S(1)}, bf16[2,32,1024]{2,1,0:T(8,128)(2,1)S(1)}, u32[]{:S(2)}, u32[]{:S(2)}) collective-permute-start(bf16[2,32,1024]{2,1,0:T(8,128)(2,1)S(1)} %pad_maximum_fusion.5), channel_id=1, source_target_pairs={{16,0},{17,1},{18,2},{19,3},{20,4},{21,5},{22,6},{23,7},{24,8},{25... | collective-permute-start | bytes 393224 | tf_op jit(solution)/shard_map/ppermute | solution.py:621
  17.9 0.5 collective-permute-start.2
  18.5 5.3 %near_levels.3 = (f32[384,1024]{1,0:T(8,128)}, f32[3,8,1024]{2,1,0:T(8,128)}, bf16[768,384]{1,0:T(8,128)(2,1)}) custom-call(bf16[576,256]{1,0:T(8,128)(2,1)} %constant.14.pool_ref, bf16[1024,1024]{1,0:T(8,128)(2,1)} %q_ref.2, bf16[1024,1024]{1,0:T(8,128)(2,1)} %k_ref.5, bf16[1024,1024]{1,0:T(8,128)(2,1)} %v_ref.5), custom_call_target="tpu_custom_call" | custom-call | flops 8000000000 | bytes 4194304 | tf_op jit(solution)/shard_map/near_levels/pallas_call | solution.py:349
  23.8 0.0 collective-permute-done.4
  23.8 0.1 collective-permute-start.11
  23.9 0.0 collective-permute-done.3
  23.9 1.6 %collective-permute-start.5 = (bf16[2,64,1024]{2,1,0:T(8,128)(2,1)S(1)}, bf16[2,64,1024]{2,1,0:T(8,128)(2,1)S(1)}, u32[]{:S(2)}, u32[]{:S(2)}) collective-permute-start(bf16[2,64,1024]{2,1,0:T(8,128)(2,1)S(1)} %collective-permute-done.4), channel_id=1, source_target_pairs={{2,0},{3,1},{0,2},{1,3},{6,4},{7,5},{4,6},{5,7},{10,8},{11,9},{8,1... | collective-permute-start | bytes 786440 | tf_op jit(solution)/shard_map/ppermute | solution.py:621
  25.4 0.0 collective-permute-done.7
  25.5 1.6 %collective-permute-start.8 = (bf16[2,96,1024]{2,1,0:T(8,128)(2,1)S(1)}, bf16[2,96,1024]{2,1,0:T(8,128)(2,1)S(1)}, u32[]{:S(2)}, u32[]{:S(2)}) collective-permute-start(bf16[2,96,1024]{2,1,0:T(8,128)(2,1)S(1)} %pad_maximum_fusion.2), channel_id=1, source_target_pairs={{4,0},{5,1},{6,2},{7,3},{0,4},{1,5},{2,6},{3,7},{12,8},{13,9},{14,... | collective-permute-start | bytes 1179656 | tf_op jit(solution)/shard_map/ppermute | solution.py:621
  27.1 5.3 %near_levels.4 = (f32[384,1024]{1,0:T(8,128)}, f32[3,8,1024]{2,1,0:T(8,128)}, bf16[768,384]{1,0:T(8,128)(2,1)}) custom-call(bf16[576,256]{1,0:T(8,128)(2,1)} %constant.14.pool_ref, bf16[1024,1024]{1,0:T(8,128)(2,1)} %q_ref.2, bf16[1024,1024]{1,0:T(8,128)(2,1)} %k_ref.5, bf16[1024,1024]{1,0:T(8,128)(2,1)} %v_ref.5), custom_call_target="tpu_custom_call" | custom-call | flops 8000000000 | bytes 4194304 | tf_op jit(solution)/shard_map/near_levels/pallas_call | solution.py:349
  32.4 0.0 collective-permute-done
  32.4 0.0 collective-permute-done.2
  32.5 0.1 collective-permute-done.5
  32.6 0.0 copy-start.1
  32.6 0.1 collective-permute-start.6
  32.7 4.0 %collective-permute-done.8 = bf16[2,96,1024]{2,1,0:T(8,128)(2,1)S(1)} collective-permute-done((bf16[2,96,1024]{2,1,0:T(8,128)(2,1)S(1)}, bf16[2,96,1024]{2,1,0:T(8,128)(2,1)S(1)}, u32[]{:S(2)}, u32[]{:S(2)}) %collective-permute-start.8) | collective-permute-done | bytes 393248 | tf_op jit(solution)/shard_map/ppermute | solution.py:621
  36.8 0.6 collective-permute-start.9
  37.4 4.3 %near_levels.5 = (f32[256,1024]{1,0:T(8,128)}, f32[2,8,1024]{2,1,0:T(8,128)}, bf16[768,256]{1,0:T(8,128)(2,1)}) custom-call(bf16[576,256]{1,0:T(8,128)(2,1)} %constant.14.pool_ref, bf16[1024,1024]{1,0:T(8,128)(2,1)} %q_ref.2, bf16[1024,1024]{1,0:T(8,128)(2,1)} %k_ref.5, bf16[1024,1024]{1,0:T(8,128)(2,1)} %v_ref.5), custom_call_target="tpu_custom_call" | custom-call | flops 8000000000 | bytes 4194304 | tf_op jit(solution)/shard_map/near_levels/pallas_call | solution.py:349
  41.6 0.0 copy-done.1
  41.7 2.7 %collective-permute-done.9 = bf16[2,64,1024]{2,1,0:T(8,128)(2,1)S(1)} collective-permute-done((bf16[2,64,1024]{2,1,0:T(8,128)(2,1)S(1)}, bf16[2,64,1024]{2,1,0:T(8,128)(2,1)S(1)}, u32[]{:S(2)}, u32[]{:S(2)}) %collective-permute-start.9) | collective-permute-done | bytes 262176 | tf_op jit(solution)/shard_map/ppermute | solution.py:621
  44.5 0.0 copy-start
  44.5 0.1 collective-permute-start.10
  44.6 0.0 collective-permute-done.11.refs_4_
  44.6 0.0 collective-permute-done.6.refs_1_
  44.6 0.0 copy-start.2
  44.6 2.7 %collective-permute-done.10.refs_3_ = bf16[2,256,1024]{2,1,0:T(8,128)(2,1)} collective-permute-done((bf16[2,256,1024]{2,1,0:T(8,128)(2,1)S(1)}, bf16[2,256,1024]{2,1,0:T(8,128)(2,1)}, u32[]{:S(2)}, u32[]{:S(2)}) %collective-permute-start.10) | collective-permute-done | bytes 1048608 | tf_op jit(solution)/shard_map/ppermute | solution.py:621
  47.4 0.0 copy-done
  47.4 0.0 copy-done.2
  47.4 13.9 %far_levels_projection.1 = bf16[1024,2048]{1,0:T(8,128)(2,1)} custom-call(bf16[2,256,1024]{2,1,0:T(8,128)(2,1)} %copy-done.1, bf16[2,256,1024]{2,1,0:T(8,128)(2,1)} %copy-done.2, bf16[2,256,1024]{2,1,0:T(8,128)(2,1)} %copy-done, bf16[2,256,1024]{2,1,0:T(8,128)(2,1)} %collective-permute-done.10.refs_3_, ...), custom_call_target="tpu_custom_call" | custom-call | flops 6499999744 | bytes 18874368 | tf_op jit(solution)/shard_map/far_levels_projection/pallas_call | solution.py:592
  (16 shorter events, 0.3 us)
Async XLA Ops:
  5.3 8.2 %collective-permute-start.1 = (bf16[2,48,1024]{2,1,0:T(8,128)(2,1)}, bf16[2,48,1024]{2,1,0:T(8,128)(2,1)S(1)}, u32[]{:S(2)}, u32[]{:S(2)}) collective-permute-start(bf16[2,48,1024]{2,1,0:T(8,128)(2,1)} %get-tuple-element.34), channel_id=1, source_target_pairs={{8,0},{9,1},{10,2},{11,3},{12,4},{13,5},{14,6},{15,7},{0,8},{1,9},... | collective-permute-start | bytes 589832 | tf_op jit(solution)/shard_map/ppermute | solution.py:621
  8.4 24.0 %collective-permute-start = (bf16[2,64,1024]{2,1,0:T(8,128)(2,1)}, bf16[2,64,1024]{2,1,0:T(8,128)(2,1)S(1)}, u32[]{:S(2)}, u32[]{:S(2)}) collective-permute-start(bf16[2,64,1024]{2,1,0:T(8,128)(2,1)} %get-tuple-element.32), channel_id=1, source_target_pairs={{2,0},{3,1},{0,2},{1,3},{6,4},{7,5},{4,6},{5,7},{10,8},{11,9},{8,1... | collective-permute-start | bytes 786440 | tf_op jit(solution)/shard_map/ppermute | solution.py:621
  9.9 13.9 %collective-permute-start.4 = (bf16[2,64,1024]{2,1,0:T(8,128)(2,1)}, bf16[2,64,1024]{2,1,0:T(8,128)(2,1)S(1)}, u32[]{:S(2)}, u32[]{:S(2)}) collective-permute-start(bf16[2,64,1024]{2,1,0:T(8,128)(2,1)} %get-tuple-element.46), channel_id=1, source_target_pairs={{4,0},{5,1},{6,2},{7,3},{0,4},{1,5},{2,6},{3,7},{12,8},{13,9},{14,... | collective-permute-start | bytes 786440 | tf_op jit(solution)/shard_map/ppermute | solution.py:621
  13.5 10.3 %collective-permute-start.3 = (bf16[2,32,1024]{2,1,0:T(8,128)(2,1)S(1)}, bf16[2,32,1024]{2,1,0:T(8,128)(2,1)S(1)}, u32[]{:S(2)}, u32[]{:S(2)}) collective-permute-start(bf16[2,32,1024]{2,1,0:T(8,128)(2,1)S(1)} %slice.20), channel_id=1, source_target_pairs={{2,0},{3,1},{0,2},{1,3},{6,4},{7,5},{4,6},{5,7},{10,8},{11,9},{8,1... | collective-permute-start | bytes 393224 | tf_op jit(solution)/shard_map/ppermute | solution.py:621
  15.3 10.2 %collective-permute-start.7 = (bf16[2,32,1024]{2,1,0:T(8,128)(2,1)S(1)}, bf16[2,32,1024]{2,1,0:T(8,128)(2,1)S(1)}, u32[]{:S(2)}, u32[]{:S(2)}) collective-permute-start(bf16[2,32,1024]{2,1,0:T(8,128)(2,1)S(1)} %pad_maximum_fusion.5), channel_id=1, source_target_pairs={{16,0},{17,1},{18,2},{19,3},{20,4},{21,5},{22,6},{23,7},{24,8},{25... | collective-permute-start | bytes 393224 | tf_op jit(solution)/shard_map/ppermute | solution.py:621
  17.9 14.5 %collective-permute-start.2 = (bf16[2,64,1024]{2,1,0:T(8,128)(2,1)}, bf16[2,64,1024]{2,1,0:T(8,128)(2,1)S(1)}, u32[]{:S(2)}, u32[]{:S(2)}) collective-permute-start(bf16[2,64,1024]{2,1,0:T(8,128)(2,1)} %get-tuple-element.35), channel_id=1, source_target_pairs={{2,0},{3,1},{0,2},{1,3},{6,4},{7,5},{4,6},{5,7},{10,8},{11,9},{8,1... | collective-permute-start | bytes 786440 | tf_op jit(solution)/shard_map/ppermute | solution.py:621
  23.8 20.8 %collective-permute-start.11 = (bf16[2,256,1024]{2,1,0:T(8,128)(2,1)}, bf16[2,256,1024]{2,1,0:T(8,128)(2,1)}, u32[]{:S(2)}, u32[]{:S(2)}) collective-permute-start(bf16[2,256,1024]{2,1,0:T(8,128)(2,1)} %get-tuple-element.58), channel_id=1, source_target_pairs={{1,0},{0,1},{3,2},{2,3},{5,4},{4,5},{7,6},{6,7},{9,8},{8,9},{11,10... | collective-permute-start | bytes 3145736 | tf_op jit(solution)/shard_map/ppermute | solution.py:621
  23.9 8.7 %collective-permute-start.5 = (bf16[2,64,1024]{2,1,0:T(8,128)(2,1)S(1)}, bf16[2,64,1024]{2,1,0:T(8,128)(2,1)S(1)}, u32[]{:S(2)}, u32[]{:S(2)}) collective-permute-start(bf16[2,64,1024]{2,1,0:T(8,128)(2,1)S(1)} %collective-permute-done.4), channel_id=1, source_target_pairs={{2,0},{3,1},{0,2},{1,3},{6,4},{7,5},{4,6},{5,7},{10,8},{11,9},{8,1... | collective-permute-start | bytes 786440 | tf_op jit(solution)/shard_map/ppermute | solution.py:621
  25.5 11.2 %collective-permute-start.8 = (bf16[2,96,1024]{2,1,0:T(8,128)(2,1)S(1)}, bf16[2,96,1024]{2,1,0:T(8,128)(2,1)S(1)}, u32[]{:S(2)}, u32[]{:S(2)}) collective-permute-start(bf16[2,96,1024]{2,1,0:T(8,128)(2,1)S(1)} %pad_maximum_fusion.2), channel_id=1, source_target_pairs={{4,0},{5,1},{6,2},{7,3},{0,4},{1,5},{2,6},{3,7},{12,8},{13,9},{14,... | collective-permute-start | bytes 1179656 | tf_op jit(solution)/shard_map/ppermute | solution.py:621
  32.6 9.0 %copy-start.1 = (bf16[2,256,1024]{2,1,0:T(8,128)(2,1)}, bf16[2,256,1024]{2,1,0:T(8,128)(2,1)S(1)}, u32[]{:S(2)}) copy-start(bf16[2,256,1024]{2,1,0:T(8,128)(2,1)S(1)} %constant_dynamic-update-slice_fusion.refs_0_) | copy-start | bytes 3145732
  32.6 12.0 %collective-permute-start.6 = (bf16[2,256,1024]{2,1,0:T(8,128)(2,1)S(1)}, bf16[2,256,1024]{2,1,0:T(8,128)(2,1)S(1)}, u32[]{:S(2)}, u32[]{:S(2)}) collective-permute-start(bf16[2,256,1024]{2,1,0:T(8,128)(2,1)S(1)} %constant_dynamic-update-slice_fusion.refs_0_), channel_id=1, source_target_pairs={{1,0},{0,1},{3,2},{2,3},{5,4},{4,5},{7,6},{6,7},{9,8},{8,9},{11,10... | collective-permute-start | bytes 3145736 | tf_op jit(solution)/shard_map/ppermute | solution.py:621
  36.8 7.6 %collective-permute-start.9 = (bf16[2,64,1024]{2,1,0:T(8,128)(2,1)S(1)}, bf16[2,64,1024]{2,1,0:T(8,128)(2,1)S(1)}, u32[]{:S(2)}, u32[]{:S(2)}) collective-permute-start(bf16[2,64,1024]{2,1,0:T(8,128)(2,1)S(1)} %pad_maximum_fusion.4), channel_id=1, source_target_pairs={{2,0},{3,1},{0,2},{1,3},{6,4},{7,5},{4,6},{5,7},{10,8},{11,9},{8,1... | collective-permute-start | bytes 786440 | tf_op jit(solution)/shard_map/ppermute | solution.py:621
  44.5 2.9 %copy-start = (bf16[2,256,1024]{2,1,0:T(8,128)(2,1)}, bf16[2,256,1024]{2,1,0:T(8,128)(2,1)S(1)}, u32[]{:S(2)}) copy-start(bf16[2,256,1024]{2,1,0:T(8,128)(2,1)S(1)} %constant_dynamic-update-slice_fusion.4.refs_2_) | copy-start | bytes 3145732
  44.5 2.9 %collective-permute-start.10 = (bf16[2,256,1024]{2,1,0:T(8,128)(2,1)S(1)}, bf16[2,256,1024]{2,1,0:T(8,128)(2,1)}, u32[]{:S(2)}, u32[]{:S(2)}) collective-permute-start(bf16[2,256,1024]{2,1,0:T(8,128)(2,1)S(1)} %constant_dynamic-update-slice_fusion.4.refs_2_), channel_id=1, source_target_pairs={{1,0},{0,1},{3,2},{2,3},{5,4},{4,5},{7,6},{6,7},{9,8},{8,9},{11,10... | collective-permute-start | bytes 3145736 | tf_op jit(solution)/shard_map/ppermute | solution.py:621
  44.6 2.8 %copy-start.2 = (bf16[2,256,1024]{2,1,0:T(8,128)(2,1)}, bf16[2,256,1024]{2,1,0:T(8,128)(2,1)S(1)}, u32[]{:S(2)}) copy-start(bf16[2,256,1024]{2,1,0:T(8,128)(2,1)S(1)} %collective-permute-done.6.refs_1_) | copy-start | bytes 3145732

commit v10 on v9

--- a/solution.py
+++ b/solution.py
@@ -621,15 +621,10 @@
     return lax.ppermute(array, "seq", [(i ^ distance, i) for i in range(lax.axis_size("seq"))])
 
 
-def gathered(blocks, distance):
-    sent = jnp.concatenate(blocks, axis=1) if len(blocks) > 1 else blocks[0]
-    got = moved(sent, distance)
-    joined, start = [], 0
-    for block in blocks:
-        rows = block.shape[1]
-        joined.append(jnp.concatenate([block, got[:, start : start + rows]], axis=1))
-        start += rows
-    return joined
+def gathered(array, distances):
+    size = lax.axis_size("seq")
+    got = lax.ppermute(array, "seq", [(i ^ distances[i % 2], i) for i in range(size)])
+    return jnp.concatenate([array, got], axis=1)
 
 
 def after(arrays, others):
@@ -668,23 +663,24 @@
             third.append(moved(after(pooled[2], arrived), 2))
             second = moved(after(blocks[2], arrived), 1)
 
-    upper = [blocks[level] for level in high[1:]]
-    five = gathered([arrived], 2)
+    upper = jnp.concatenate([blocks[level] for level in high], axis=1)
     near = [near_call(after(queries, arrived), keys, values, levels, 0)]
-    five_y, *upper = gathered(after(five + upper, near[0]), 4)
-    fourth = gathered([after(fourth, near[0])], 2)[0]
-    near.append(near_call(after(queries, (near[0], five)), keys, values, levels, 1))
-    upper_x = gathered(after(upper, near[1]), 2)
+    once = gathered(after(upper, near[0]), (2, 4))
+    fourth = gathered(after(fourth, (near[0], upper)), (2, 2))
+    near.append(near_call(after(queries, (near[0], upper)), keys, values, levels, 1))
+    joined = gathered(after(once, near[1]), (4, 2))
     low = jnp.concatenate([*after(third, near[1]), fourth], axis=1)
     low_got = moved(low, 1)
-    near.append(near_call(after(queries, (near[1], upper)), keys, values, levels, 2))
-    top = jnp.concatenate(after([five_y] + upper_x, near[2]), axis=1)
+    near.append(near_call(after(queries, (near[1], once)), keys, values, levels, 2))
+    top = after(joined, near[2])
     top_got = moved(top, 1)
     plan = [(2, 4, (0, 0, BLOCK))]
     for level in (3, 4):
         plan += [(level, bundle, ((level - 3) * 128, bundle * 128, 128)) for bundle in (0, 1)]
     for level in high:
-        plan += [(level, bundle, ((level - TOP) * 128, (bundle - 2) * 128, 128)) for bundle in (2, 3)]
+        for piece in range(4):
+            start = (piece * len(high) + level - TOP) * 32
+            plan += [(level, bundle, (start, (bundle - 2) * 128 + piece * 32, 32)) for bundle in (2, 3)]
     return far_call([low, low_got, top, top_got, second], plan, near, w_out, levels)
 
 

time: 61.7 us -> 63.6 us (1.031)
  waiting for transfers between devices: 10.8 us -> 11.8 us
  Pallas kernels: 33.4 us -> 34.3 us
    ppermute x0 -> x3, waiting for transfers between devices: none -> 7.81 us  [gathered(): lax.ppermute(array, 'seq', [(i ^ distances[i % 2], i) for i in range(size)])]
    ppermute x12 -> x8, waiting for transfers between devices: 10.8 us -> 4.02 us  [moved(): lax.ppermute(array, 'seq', [(i ^ distance, i) for i in range(lax.axis_siz...]
    ppermute x0 -> x3, starting transfers between devices: none -> 4.68 us  [gathered(): lax.ppermute(array, 'seq', [(i ^ distances[i % 2], i) for i in range(size)])]
    ppermute x12 -> x8, starting transfers between devices: 15 us -> 10.6 us  [moved(): lax.ppermute(array, 'seq', [(i ^ distance, i) for i in range(lax.axis_siz...]
  transfers between devices with their start and end apart: 12 -> 11, of which waited for: 5 -> 4; matrix products, arithmetic and copies ran while one was open for 2% -> 2% of each run, Pallas kernels for 24% -> 24%
where the time goes in v10:
time: 63.6 us; the launch traced here: 63.4 us
  Pallas kernels  34.3 us (54%)
  starting transfers between devices  15.2 us (24%)
  waiting for transfers between devices  11.8 us (19%)
  local copies, waits for them, and re-layouts  1.59 us (2%)
    pallas_call x3, Pallas kernels, near_call(): pl.pallas_call(functools.partial(near_kernel, levels, first, heads), in_s...  15.2 us
    pallas_call x1, Pallas kernels, far_call(): pl.pallas_call(functools.partial(far_kernel, levels, plan), in_specs=[HBM...  14.4 us
    ppermute x8, starting transfers between devices, moved(): lax.ppermute(array, 'seq', [(i ^ distance, i) for i in range(lax.axis_siz...  10.6 us
    ppermute x3, waiting for transfers between devices, gathered(): lax.ppermute(array, 'seq', [(i ^ distances[i % 2], i) for i in range(size)])  7.81 us
    pallas_call x1, Pallas kernels, pool_call(): pl.pallas_call(functools.partial(pool_kernel, levels), in_specs=[HBM] * 4...  4.72 us
    ppermute x3, starting transfers between devices, gathered(): lax.ppermute(array, 'seq', [(i ^ distances[i % 2], i) for i in range(size)])  4.68 us
    ppermute x8, waiting for transfers between devices, moved(): lax.ppermute(array, 'seq', [(i ^ distance, i) for i in range(lax.axis_siz...  4.02 us
  transfers between devices with their start and end apart: 11, of which 4 were waited for; matrix products, arithmetic and copies ran while one was open for 2% of the time, Pallas kernels for 24%

profile of v10, /device:TPU:0, one launch (start us, length us, event | category | flops | bytes accessed | tf_op | source)
XLA Modules:
  0.0 63.4 jit_solution(2519826961042078389)
XLA Ops:
  0.0 0.6 broadcast.1.large_ref
  0.6 4.7 %pool_keys_values.1 = (bf16[2,256,1024]{2,1,0:T(8,128)(2,1)}, bf16[2,64,1024]{2,1,0:T(8,128)(2,1)}, bf16[2,64,1024]{2,1,0:T(8,128)(2,1)}, bf16[2,64,1024]{2,1,0:T(8,128)(2,1)}, bf16[2,48,1024]{2,1,0:T(8,128)(2,1)}) custom-call(bf16[256,512]{1,0:T(8,128)(2,1)} %constant.12.small_ref, bf16[16,1024]{1,0:T(8,128)(2,1)} %broadcast.1.large_ref, ...), custom_call_target="tpu_custom_call" | custom-call | flops 1073741824 | bytes 6291456 | tf_op jit(solution)/shard_map/pool_keys_values/pallas_call | solution.py:157
  5.3 3.1 %collective-permute-start.1 = (bf16[2,48,1024]{2,1,0:T(8,128)(2,1)}, bf16[2,48,1024]{2,1,0:T(8,128)(2,1)S(1)}, u32[]{:S(2)}, u32[]{:S(2)}) collective-permute-start(bf16[2,48,1024]{2,1,0:T(8,128)(2,1)} %get-tuple-element.32), channel_id=1, source_target_pairs={{8,0},{9,1},{10,2},{11,3},{12,4},{13,5},{14,6},{15,7},{0,8},{1,9},... | collective-permute-start | bytes 589832 | tf_op jit(solution)/shard_map/ppermute | solution.py:621
  8.4 1.5 %collective-permute-start = (bf16[2,64,1024]{2,1,0:T(8,128)(2,1)}, bf16[2,64,1024]{2,1,0:T(8,128)(2,1)S(1)}, u32[]{:S(2)}, u32[]{:S(2)}) collective-permute-start(bf16[2,64,1024]{2,1,0:T(8,128)(2,1)} %get-tuple-element.30), channel_id=1, source_target_pairs={{2,0},{3,1},{0,2},{1,3},{6,4},{7,5},{4,6},{5,7},{10,8},{11,9},{8,1... | collective-permute-start | bytes 786440 | tf_op jit(solution)/shard_map/ppermute | solution.py:621
  9.9 1.5 %collective-permute-start.4 = (bf16[2,64,1024]{2,1,0:T(8,128)(2,1)}, bf16[2,64,1024]{2,1,0:T(8,128)(2,1)S(1)}, u32[]{:S(2)}, u32[]{:S(2)}) collective-permute-start(bf16[2,64,1024]{2,1,0:T(8,128)(2,1)} %get-tuple-element.44), channel_id=1, source_target_pairs={{4,0},{5,1},{6,2},{7,3},{0,4},{1,5},{2,6},{3,7},{12,8},{13,9},{14,... | collective-permute-start | bytes 786440 | tf_op jit(solution)/shard_map/ppermute | solution.py:621
  11.4 0.8 %slice.10 = bf16[2,16,1024]{2,1,0:T(8,128)(2,1)S(1)} slice(bf16[2,48,1024]{2,1,0:T(8,128)(2,1)} %get-tuple-element.32), slice={[0:2], [32:48], [0:1024]} | slice | bytes 131072 | tf_op jit(solution)/shard_map/slice | solution.py:643
  12.3 1.2 %collective-permute-done.1 = bf16[2,48,1024]{2,1,0:T(8,128)(2,1)S(1)} collective-permute-done((bf16[2,48,1024]{2,1,0:T(8,128)(2,1)}, bf16[2,48,1024]{2,1,0:T(8,128)(2,1)S(1)}, u32[]{:S(2)}, u32[]{:S(2)}) %collective-permute-start.1) | collective-permute-done | bytes 196640 | tf_op jit(solution)/shard_map/ppermute | solution.py:621
  13.6 2.8 %collective-permute-start.3 = (bf16[2,32,1024]{2,1,0:T(8,128)(2,1)S(1)}, bf16[2,32,1024]{2,1,0:T(8,128)(2,1)S(1)}, u32[]{:S(2)}, u32[]{:S(2)}) collective-permute-start(bf16[2,32,1024]{2,1,0:T(8,128)(2,1)S(1)} %pad_maximum_fusion.2), channel_id=1, source_target_pairs={{16,0},{17,1},{18,2},{19,3},{20,4},{21,5},{22,6},{23,7},{24,8},{25... | collective-permute-start | bytes 393224 | tf_op jit(solution)/shard_map/ppermute | solution.py:621
  16.4 1.5 %collective-permute-start.2 = (bf16[2,64,1024]{2,1,0:T(8,128)(2,1)}, bf16[2,64,1024]{2,1,0:T(8,128)(2,1)S(1)}, u32[]{:S(2)}, u32[]{:S(2)}) collective-permute-start(bf16[2,64,1024]{2,1,0:T(8,128)(2,1)} %get-tuple-element.33), channel_id=1, source_target_pairs={{2,0},{3,1},{0,2},{1,3},{6,4},{7,5},{4,6},{5,7},{10,8},{11,9},{8,1... | collective-permute-start | bytes 786440 | tf_op jit(solution)/shard_map/ppermute | solution.py:621
  17.9 0.0 collective-permute-start.10
  17.9 5.3 %near_levels.3 = (f32[384,1024]{1,0:T(8,128)}, f32[3,8,1024]{2,1,0:T(8,128)}, bf16[768,384]{1,0:T(8,128)(2,1)}) custom-call(bf16[576,256]{1,0:T(8,128)(2,1)} %constant.14.pool_ref, bf16[1024,1024]{1,0:T(8,128)(2,1)} %q_ref.2, bf16[1024,1024]{1,0:T(8,128)(2,1)} %k_ref.5, bf16[1024,1024]{1,0:T(8,128)(2,1)} %v_ref.5), custom_call_target="tpu_custom_call" | custom-call | flops 8000000000 | bytes 4194304 | tf_op jit(solution)/shard_map/near_levels/pallas_call | solution.py:349
  23.2 0.0 collective-permute-done.3
  23.2 0.0 collective-permute-done.4
  23.2 0.6 collective-permute-start.5
  23.8 1.5 %collective-permute-start.7 = (bf16[2,64,1024]{2,1,0:T(8,128)(2,1)S(1)}, bf16[2,64,1024]{2,1,0:T(8,128)(2,1)S(1)}, u32[]{:S(2)}, u32[]{:S(2)}) collective-permute-start(bf16[2,64,1024]{2,1,0:T(8,128)(2,1)S(1)} %pad_maximum_fusion.1), channel_id=1, source_target_pairs={{2,0},{5,1},{0,2},{7,3},{6,4},{1,5},{4,6},{3,7},{10,8},{13,9},{8,1... | collective-permute-start | bytes 786440 | tf_op jit(solution)/shard_map/ppermute | solution.py:626
  25.3 5.3 %near_levels.4 = (f32[384,1024]{1,0:T(8,128)}, f32[3,8,1024]{2,1,0:T(8,128)}, bf16[768,384]{1,0:T(8,128)(2,1)}) custom-call(bf16[576,256]{1,0:T(8,128)(2,1)} %constant.14.pool_ref, bf16[1024,1024]{1,0:T(8,128)(2,1)} %q_ref.2, bf16[1024,1024]{1,0:T(8,128)(2,1)} %k_ref.5, bf16[1024,1024]{1,0:T(8,128)(2,1)} %v_ref.5), custom_call_target="tpu_custom_call" | custom-call | flops 8000000000 | bytes 4194304 | tf_op jit(solution)/shard_map/near_levels/pallas_call | solution.py:349
  30.7 0.0 collective-permute-done
  30.7 0.0 collective-permute-done.2
  30.8 5.4 %collective-permute-done.7 = bf16[2,64,1024]{2,1,0:T(8,128)(2,1)S(1)} collective-permute-done((bf16[2,64,1024]{2,1,0:T(8,128)(2,1)S(1)}, bf16[2,64,1024]{2,1,0:T(8,128)(2,1)S(1)}, u32[]{:S(2)}, u32[]{:S(2)}) %collective-permute-start.7) | collective-permute-done | bytes 262176 | tf_op jit(solution)/shard_map/ppermute | solution.py:626
  36.2 2.6 %collective-permute-start.8 = (bf16[2,128,1024]{2,1,0:T(8,128)(2,1)S(1)}, bf16[2,128,1024]{2,1,0:T(8,128)(2,1)S(1)}, u32[]{:S(2)}, u32[]{:S(2)}) collective-permute-start(bf16[2,128,1024]{2,1,0:T(8,128)(2,1)S(1)} %constant_dynamic-update-slice_fusion.4), channel_id=1, source_target_pairs={{4,0},{3,1},{6,2},{1,3},{0,4},{7,5},{2,6},{5,7},{12,8},{11,9},{14,... | collective-permute-start | bytes 1572872 | tf_op jit(solution)/shard_map/ppermute | solution.py:626
  38.8 0.0 collective-permute-done.5
  38.8 0.0 copy-start.1
  38.8 0.1 collective-permute-start.6
  38.9 4.6 %near_levels.5 = (f32[256,1024]{1,0:T(8,128)}, f32[2,8,1024]{2,1,0:T(8,128)}, bf16[768,256]{1,0:T(8,128)(2,1)}) custom-call(bf16[576,256]{1,0:T(8,128)(2,1)} %constant.14.pool_ref, bf16[1024,1024]{1,0:T(8,128)(2,1)} %q_ref.2, bf16[1024,1024]{1,0:T(8,128)(2,1)} %k_ref.5, bf16[1024,1024]{1,0:T(8,128)(2,1)} %v_ref.5), custom_call_target="tpu_custom_call" | custom-call | flops 8000000000 | bytes 4194304 | tf_op jit(solution)/shard_map/near_levels/pallas_call | solution.py:349
  43.5 0.0 copy-done.1
  43.5 2.4 %collective-permute-done.8 = bf16[2,128,1024]{2,1,0:T(8,128)(2,1)S(1)} collective-permute-done((bf16[2,128,1024]{2,1,0:T(8,128)(2,1)S(1)}, bf16[2,128,1024]{2,1,0:T(8,128)(2,1)S(1)}, u32[]{:S(2)}, u32[]{:S(2)}) %collective-permute-start.8) | collective-permute-done | bytes 524320 | tf_op jit(solution)/shard_map/ppermute | solution.py:626
  45.9 0.1 pad_maximum_fusion.refs_2_
  46.0 0.0 copy-start
  46.0 0.1 collective-permute-start.9
  46.1 0.0 collective-permute-done.10.refs_4_
  46.1 0.0 collective-permute-done.6.refs_1_
  46.1 2.8 %collective-permute-done.9.refs_3_ = bf16[2,256,1024]{2,1,0:T(8,128)(2,1)} collective-permute-done((bf16[2,256,1024]{2,1,0:T(8,128)(2,1)S(1)}, bf16[2,256,1024]{2,1,0:T(8,128)(2,1)}, u32[]{:S(2)}, u32[]{:S(2)}) %collective-permute-start.9) | collective-permute-done | bytes 1048608 | tf_op jit(solution)/shard_map/ppermute | solution.py:621
  48.9 0.0 copy-done
  48.9 14.4 %far_levels_projection.1 = bf16[1024,2048]{1,0:T(8,128)(2,1)} custom-call(bf16[2,256,1024]{2,1,0:T(8,128)(2,1)} %copy-done.1, bf16[2,256,1024]{2,1,0:T(8,128)(2,1)} %collective-permute-done.6.refs_1_, bf16[2,256,1024]{2,1,0:T(8,128)(2,1)} %copy-done, bf16[2,256,1024]{2,1,0:T(8,128)(2,1)} %collective-permute-done.9.refs_3_, ...), custom_call_target="tpu_custom_call" | custom-call | flops 6499999744 | bytes 18874368 | tf_op jit(solution)/shard_map/far_levels_projection/pallas_call | solution.py:592
  (10 shorter events, 0.2 us)
Async XLA Ops:
  5.3 8.2 %collective-permute-start.1 = (bf16[2,48,1024]{2,1,0:T(8,128)(2,1)}, bf16[2,48,1024]{2,1,0:T(8,128)(2,1)S(1)}, u32[]{:S(2)}, u32[]{:S(2)}) collective-permute-start(bf16[2,48,1024]{2,1,0:T(8,128)(2,1)} %get-tuple-element.32), channel_id=1, source_target_pairs={{8,0},{9,1},{10,2},{11,3},{12,4},{13,5},{14,6},{15,7},{0,8},{1,9},... | collective-permute-start | bytes 589832 | tf_op jit(solution)/shard_map/ppermute | solution.py:621
  8.4 22.2 %collective-permute-start = (bf16[2,64,1024]{2,1,0:T(8,128)(2,1)}, bf16[2,64,1024]{2,1,0:T(8,128)(2,1)S(1)}, u32[]{:S(2)}, u32[]{:S(2)}) collective-permute-start(bf16[2,64,1024]{2,1,0:T(8,128)(2,1)} %get-tuple-element.30), channel_id=1, source_target_pairs={{2,0},{3,1},{0,2},{1,3},{6,4},{7,5},{4,6},{5,7},{10,8},{11,9},{8,1... | collective-permute-start | bytes 786440 | tf_op jit(solution)/shard_map/ppermute | solution.py:621
  9.9 13.3 %collective-permute-start.4 = (bf16[2,64,1024]{2,1,0:T(8,128)(2,1)}, bf16[2,64,1024]{2,1,0:T(8,128)(2,1)S(1)}, u32[]{:S(2)}, u32[]{:S(2)}) collective-permute-start(bf16[2,64,1024]{2,1,0:T(8,128)(2,1)} %get-tuple-element.44), channel_id=1, source_target_pairs={{4,0},{5,1},{6,2},{7,3},{0,4},{1,5},{2,6},{3,7},{12,8},{13,9},{14,... | collective-permute-start | bytes 786440 | tf_op jit(solution)/shard_map/ppermute | solution.py:621
  13.6 9.6 %collective-permute-start.3 = (bf16[2,32,1024]{2,1,0:T(8,128)(2,1)S(1)}, bf16[2,32,1024]{2,1,0:T(8,128)(2,1)S(1)}, u32[]{:S(2)}, u32[]{:S(2)}) collective-permute-start(bf16[2,32,1024]{2,1,0:T(8,128)(2,1)S(1)} %pad_maximum_fusion.2), channel_id=1, source_target_pairs={{16,0},{17,1},{18,2},{19,3},{20,4},{21,5},{22,6},{23,7},{24,8},{25... | collective-permute-start | bytes 393224 | tf_op jit(solution)/shard_map/ppermute | solution.py:621
  16.4 14.3 %collective-permute-start.2 = (bf16[2,64,1024]{2,1,0:T(8,128)(2,1)}, bf16[2,64,1024]{2,1,0:T(8,128)(2,1)S(1)}, u32[]{:S(2)}, u32[]{:S(2)}) collective-permute-start(bf16[2,64,1024]{2,1,0:T(8,128)(2,1)} %get-tuple-element.33), channel_id=1, source_target_pairs={{2,0},{3,1},{0,2},{1,3},{6,4},{7,5},{4,6},{5,7},{10,8},{11,9},{8,1... | collective-permute-start | bytes 786440 | tf_op jit(solution)/shard_map/ppermute | solution.py:621
  17.9 28.2 %collective-permute-start.10 = (bf16[2,256,1024]{2,1,0:T(8,128)(2,1)}, bf16[2,256,1024]{2,1,0:T(8,128)(2,1)}, u32[]{:S(2)}, u32[]{:S(2)}) collective-permute-start(bf16[2,256,1024]{2,1,0:T(8,128)(2,1)} %get-tuple-element.54), channel_id=1, source_target_pairs={{1,0},{0,1},{3,2},{2,3},{5,4},{4,5},{7,6},{6,7},{9,8},{8,9},{11,10... | collective-permute-start | bytes 3145736 | tf_op jit(solution)/shard_map/ppermute | solution.py:621
  23.2 15.5 %collective-permute-start.5 = (bf16[2,64,1024]{2,1,0:T(8,128)(2,1)S(1)}, bf16[2,64,1024]{2,1,0:T(8,128)(2,1)S(1)}, u32[]{:S(2)}, u32[]{:S(2)}) collective-permute-start(bf16[2,64,1024]{2,1,0:T(8,128)(2,1)S(1)} %collective-permute-done.4), channel_id=1, source_target_pairs={{2,0},{3,1},{0,2},{1,3},{6,4},{7,5},{4,6},{5,7},{10,8},{11,9},{8,1... | collective-permute-start | bytes 786440 | tf_op jit(solution)/shard_map/ppermute | solution.py:626
  23.8 12.3 %collective-permute-start.7 = (bf16[2,64,1024]{2,1,0:T(8,128)(2,1)S(1)}, bf16[2,64,1024]{2,1,0:T(8,128)(2,1)S(1)}, u32[]{:S(2)}, u32[]{:S(2)}) collective-permute-start(bf16[2,64,1024]{2,1,0:T(8,128)(2,1)S(1)} %pad_maximum_fusion.1), channel_id=1, source_target_pairs={{2,0},{5,1},{0,2},{7,3},{6,4},{1,5},{4,6},{3,7},{10,8},{13,9},{8,1... | collective-permute-start | bytes 786440 | tf_op jit(solution)/shard_map/ppermute | solution.py:626
  36.2 9.8 %collective-permute-start.8 = (bf16[2,128,1024]{2,1,0:T(8,128)(2,1)S(1)}, bf16[2,128,1024]{2,1,0:T(8,128)(2,1)S(1)}, u32[]{:S(2)}, u32[]{:S(2)}) collective-permute-start(bf16[2,128,1024]{2,1,0:T(8,128)(2,1)S(1)} %constant_dynamic-update-slice_fusion.4), channel_id=1, source_target_pairs={{4,0},{3,1},{6,2},{1,3},{0,4},{7,5},{2,6},{5,7},{12,8},{11,9},{14,... | collective-permute-start | bytes 1572872 | tf_op jit(solution)/shard_map/ppermute | solution.py:626
  38.8 4.7 %copy-start.1 = (bf16[2,256,1024]{2,1,0:T(8,128)(2,1)}, bf16[2,256,1024]{2,1,0:T(8,128)(2,1)S(1)}, u32[]{:S(2)}) copy-start(bf16[2,256,1024]{2,1,0:T(8,128)(2,1)S(1)} %constant_dynamic-update-slice_fusion.refs_0_) | copy-start | bytes 3145732
  38.8 7.3 %collective-permute-start.6 = (bf16[2,256,1024]{2,1,0:T(8,128)(2,1)S(1)}, bf16[2,256,1024]{2,1,0:T(8,128)(2,1)}, u32[]{:S(2)}, u32[]{:S(2)}) collective-permute-start(bf16[2,256,1024]{2,1,0:T(8,128)(2,1)S(1)} %constant_dynamic-update-slice_fusion.refs_0_), channel_id=1, source_target_pairs={{1,0},{0,1},{3,2},{2,3},{5,4},{4,5},{7,6},{6,7},{9,8},{8,9},{11,10... | collective-permute-start | bytes 3145736 | tf_op jit(solution)/shard_map/ppermute | solution.py:621
  46.0 2.9 %copy-start = (bf16[2,256,1024]{2,1,0:T(8,128)(2,1)}, bf16[2,256,1024]{2,1,0:T(8,128)(2,1)S(1)}, u32[]{:S(2)}) copy-start(bf16[2,256,1024]{2,1,0:T(8,128)(2,1)S(1)} %pad_maximum_fusion.refs_2_) | copy-start | bytes 3145732
  46.0 2.9 %collective-permute-start.9 = (bf16[2,256,1024]{2,1,0:T(8,128)(2,1)S(1)}, bf16[2,256,1024]{2,1,0:T(8,128)(2,1)}, u32[]{:S(2)}, u32[]{:S(2)}) collective-permute-start(bf16[2,256,1024]{2,1,0:T(8,128)(2,1)S(1)} %pad_maximum_fusion.refs_2_), channel_id=1, source_target_pairs={{1,0},{0,1},{3,2},{2,3},{5,4},{4,5},{7,6},{6,7},{9,8},{8,9},{11,10... | collective-permute-start | bytes 3145736 | tf_op jit(solution)/shard_map/ppermute | solution.py:621

commit v11 on v8

--- a/solution.py
+++ b/solution.py
@@ -678,7 +678,7 @@
     upper_x = gathered(after(upper, near[1]), 2)
     low = jnp.concatenate([*after(third, near[1]), fourth], axis=1)
     low_got = moved(low, 1)
-    near.append(near_call(after(queries, (near[1], upper, five_y)), keys, values, levels, 2))
+    near.append(near_call(after(queries, (near[1], upper)), keys, values, levels, 2))
     top = jnp.concatenate(after(five_y + upper_x, near[2]), axis=1)
     top_got = moved(top, 1)
     plan = [(2, 4, (0, 0, BLOCK))]

time: 62.1 us -> 59 us (0.950)
  waiting for transfers between devices: 10.8 us -> 5.56 us
  local copies, waits for them, and re-layouts: 1.68 us -> 3.8 us
    ppermute x13, waiting for transfers between devices: 10.8 us -> 5.56 us  [moved(): lax.ppermute(array, 'seq', [(i ^ distance, i) for i in range(lax.axis_siz...]
    unnamed x10 -> x13, local copies, waits for them, and re-layouts: 0.13 us -> 2.26 us
  transfers between devices with their start and end apart: 13 -> 13, of which waited for: 3 -> 4; matrix products, arithmetic and copies ran while one was open for 2% -> 2% of each run, Pallas kernels for 24% -> 25%
where the time goes in v11:
time: 59 us; the launch traced here: 58.8 us
  Pallas kernels  33.4 us (57%)
  starting transfers between devices  15.5 us (26%)
  waiting for transfers between devices  5.56 us (9%)
  local copies, waits for them, and re-layouts  3.8 us (6%)
    ppermute x13, starting transfers between devices, moved(): lax.ppermute(array, 'seq', [(i ^ distance, i) for i in range(lax.axis_siz...  15.5 us
    pallas_call x3, Pallas kernels, near_call(): pl.pallas_call(functools.partial(near_kernel, levels, first, heads), in_s...  14.8 us
    pallas_call x1, Pallas kernels, far_call(): pl.pallas_call(functools.partial(far_kernel, levels, plan), in_specs=[HBM...  13.9 us
    ppermute x13, waiting for transfers between devices, moved(): lax.ppermute(array, 'seq', [(i ^ distance, i) for i in range(lax.axis_siz...  5.56 us
    pallas_call x1, Pallas kernels, pool_call(): pl.pallas_call(functools.partial(pool_kernel, levels), in_specs=[HBM] * 4...  4.73 us
    unnamed x13, local copies, waits for them, and re-layouts  2.26 us
  transfers between devices with their start and end apart: 13, of which 4 were waited for; matrix products, arithmetic and copies ran while one was open for 2% of the time, Pallas kernels for 25%

profile of v11, /device:TPU:0, one launch (start us, length us, event | category | flops | bytes accessed | tf_op | source)
XLA Modules:
  0.0 58.8 jit_solution(10530455997595562673)
XLA Ops:
  0.0 0.6 %broadcast.1.large_ref = bf16[16,1024]{1,0:T(8,128)(2,1)} broadcast(bf16[]{:T(256)} %constant.13), dimensions={} | broadcast | bytes 32770 | tf_op jit(solution)
  0.6 4.7 %pool_keys_values.1 = (bf16[2,256,1024]{2,1,0:T(8,128)(2,1)}, bf16[2,64,1024]{2,1,0:T(8,128)(2,1)}, bf16[2,64,1024]{2,1,0:T(8,128)(2,1)}, bf16[2,64,1024]{2,1,0:T(8,128)(2,1)}, bf16[2,48,1024]{2,1,0:T(8,128)(2,1)}) custom-call(bf16[256,512]{1,0:T(8,128)(2,1)} %constant.12.small_ref, bf16[16,1024]{1,0:T(8,128)(2,1)} %broadcast.1.large_ref, ...), custom_call_target="tpu_custom_call" | custom-call | flops 1073741824 | bytes 6291456 | tf_op jit(solution)/shard_map/pool_keys_values/pallas_call | solution.py:157
  5.3 3.1 %collective-permute-start.1 = (bf16[2,48,1024]{2,1,0:T(8,128)(2,1)}, bf16[2,48,1024]{2,1,0:T(8,128)(2,1)S(1)}, u32[]{:S(2)}, u32[]{:S(2)}) collective-permute-start(bf16[2,48,1024]{2,1,0:T(8,128)(2,1)} %get-tuple-element.34), channel_id=1, source_target_pairs={{8,0},{9,1},{10,2},{11,3},{12,4},{13,5},{14,6},{15,7},{0,8},{1,9},... | collective-permute-start | bytes 589832 | tf_op jit(solution)/shard_map/ppermute | solution.py:621
  8.4 1.5 %collective-permute-start = (bf16[2,64,1024]{2,1,0:T(8,128)(2,1)}, bf16[2,64,1024]{2,1,0:T(8,128)(2,1)S(1)}, u32[]{:S(2)}, u32[]{:S(2)}) collective-permute-start(bf16[2,64,1024]{2,1,0:T(8,128)(2,1)} %get-tuple-element.32), channel_id=1, source_target_pairs={{2,0},{3,1},{0,2},{1,3},{6,4},{7,5},{4,6},{5,7},{10,8},{11,9},{8,1... | collective-permute-start | bytes 786440 | tf_op jit(solution)/shard_map/ppermute | solution.py:621
  9.9 1.5 %collective-permute-start.4 = (bf16[2,64,1024]{2,1,0:T(8,128)(2,1)}, bf16[2,64,1024]{2,1,0:T(8,128)(2,1)S(1)}, u32[]{:S(2)}, u32[]{:S(2)}) collective-permute-start(bf16[2,64,1024]{2,1,0:T(8,128)(2,1)} %get-tuple-element.46), channel_id=1, source_target_pairs={{4,0},{5,1},{6,2},{7,3},{0,4},{1,5},{2,6},{3,7},{12,8},{13,9},{14,... | collective-permute-start | bytes 786440 | tf_op jit(solution)/shard_map/ppermute | solution.py:621
  11.4 0.8 %slice.10 = bf16[2,16,1024]{2,1,0:T(8,128)(2,1)S(1)} slice(bf16[2,48,1024]{2,1,0:T(8,128)(2,1)} %get-tuple-element.34), slice={[0:2], [32:48], [0:1024]} | slice | bytes 131072 | tf_op jit(solution)/shard_map/slice | solution.py:648
  12.3 1.3 %collective-permute-done.1 = bf16[2,48,1024]{2,1,0:T(8,128)(2,1)S(1)} collective-permute-done((bf16[2,48,1024]{2,1,0:T(8,128)(2,1)}, bf16[2,48,1024]{2,1,0:T(8,128)(2,1)S(1)}, u32[]{:S(2)}, u32[]{:S(2)}) %collective-permute-start.1) | collective-permute-done | bytes 196640 | tf_op jit(solution)/shard_map/ppermute | solution.py:621
  13.6 1.7 %collective-permute-start.3 = (bf16[2,32,1024]{2,1,0:T(8,128)(2,1)S(1)}, bf16[2,32,1024]{2,1,0:T(8,128)(2,1)S(1)}, u32[]{:S(2)}, u32[]{:S(2)}) collective-permute-start(bf16[2,32,1024]{2,1,0:T(8,128)(2,1)S(1)} %slice.12), channel_id=1, source_target_pairs={{2,0},{3,1},{0,2},{1,3},{6,4},{7,5},{4,6},{5,7},{10,8},{11,9},{8,1... | collective-permute-start | bytes 393224 | tf_op jit(solution)/shard_map/ppermute | solution.py:621
  15.3 2.7 %collective-permute-start.8 = (bf16[2,32,1024]{2,1,0:T(8,128)(2,1)S(1)}, bf16[2,32,1024]{2,1,0:T(8,128)(2,1)S(1)}, u32[]{:S(2)}, u32[]{:S(2)}) collective-permute-start(bf16[2,32,1024]{2,1,0:T(8,128)(2,1)S(1)} %pad_maximum_fusion.3), channel_id=1, source_target_pairs={{16,0},{17,1},{18,2},{19,3},{20,4},{21,5},{22,6},{23,7},{24,8},{25... | collective-permute-start | bytes 393224 | tf_op jit(solution)/shard_map/ppermute | solution.py:621
  18.0 0.5 collective-permute-start.2
  18.5 5.3 %near_levels.3 = (f32[384,1024]{1,0:T(8,128)}, f32[3,8,1024]{2,1,0:T(8,128)}, bf16[768,384]{1,0:T(8,128)(2,1)}) custom-call(bf16[576,256]{1,0:T(8,128)(2,1)} %constant.14.pool_ref, bf16[1024,1024]{1,0:T(8,128)(2,1)} %q_ref.2, bf16[1024,1024]{1,0:T(8,128)(2,1)} %k_ref.5, bf16[1024,1024]{1,0:T(8,128)(2,1)} %v_ref.5), custom_call_target="tpu_custom_call" | custom-call | flops 8000000000 | bytes 4194304 | tf_op jit(solution)/shard_map/near_levels/pallas_call | solution.py:349
  23.7 0.0 collective-permute-done.4
  23.8 0.1 collective-permute-start.12
  23.8 0.0 collective-permute-done.8
  23.9 1.6 %collective-permute-start.5 = (bf16[2,64,1024]{2,1,0:T(8,128)(2,1)S(1)}, bf16[2,64,1024]{2,1,0:T(8,128)(2,1)S(1)}, u32[]{:S(2)}, u32[]{:S(2)}) collective-permute-start(bf16[2,64,1024]{2,1,0:T(8,128)(2,1)S(1)} %collective-permute-done.4), channel_id=1, source_target_pairs={{2,0},{3,1},{0,2},{1,3},{6,4},{7,5},{4,6},{5,7},{10,8},{11,9},{8,1... | collective-permute-start | bytes 786440 | tf_op jit(solution)/shard_map/ppermute | solution.py:621
  25.4 0.0 collective-permute-done.3
  25.4 1.6 %collective-permute-start.9 = (bf16[2,32,1024]{2,1,0:T(8,128)(2,1)S(1)}, bf16[2,32,1024]{2,1,0:T(8,128)(2,1)S(1)}, u32[]{:S(2)}, u32[]{:S(2)}) collective-permute-start(bf16[2,32,1024]{2,1,0:T(8,128)(2,1)S(1)} %collective-permute-done.8), channel_id=1, source_target_pairs={{4,0},{5,1},{6,2},{7,3},{0,4},{1,5},{2,6},{3,7},{12,8},{13,9},{14,... | collective-permute-start | bytes 393224 | tf_op jit(solution)/shard_map/ppermute | solution.py:621
  27.0 5.3 %near_levels.4 = (f32[384,1024]{1,0:T(8,128)}, f32[3,8,1024]{2,1,0:T(8,128)}, bf16[768,384]{1,0:T(8,128)(2,1)}) custom-call(bf16[576,256]{1,0:T(8,128)(2,1)} %constant.14.pool_ref, bf16[1024,1024]{1,0:T(8,128)(2,1)} %q_ref.2, bf16[1024,1024]{1,0:T(8,128)(2,1)} %k_ref.5, bf16[1024,1024]{1,0:T(8,128)(2,1)} %v_ref.5), custom_call_target="tpu_custom_call" | custom-call | flops 8000000000 | bytes 4194304 | tf_op jit(solution)/shard_map/near_levels/pallas_call | solution.py:349
  32.3 0.0 collective-permute-done.9
  32.3 0.6 collective-permute-start.7
  32.9 0.0 collective-permute-done
  32.9 0.0 collective-permute-done.2
  32.9 0.6 %collective-permute-start.10 = (bf16[2,64,1024]{2,1,0:T(8,128)(2,1)S(1)}, bf16[2,64,1024]{2,1,0:T(8,128)(2,1)S(1)}, u32[]{:S(2)}, u32[]{:S(2)}) collective-permute-start(bf16[2,64,1024]{2,1,0:T(8,128)(2,1)S(1)} %constant_dynamic-update-slice_fusion.4), channel_id=1, source_target_pairs={{2,0},{3,1},{0,2},{1,3},{6,4},{7,5},{4,6},{5,7},{10,8},{11,9},{8,1... | collective-permute-start | bytes 786440 | tf_op jit(solution)/shard_map/ppermute | solution.py:621
  33.5 4.3 %near_levels.5 = (f32[256,1024]{1,0:T(8,128)}, f32[2,8,1024]{2,1,0:T(8,128)}, bf16[768,256]{1,0:T(8,128)(2,1)}) custom-call(bf16[576,256]{1,0:T(8,128)(2,1)} %constant.14.pool_ref, bf16[1024,1024]{1,0:T(8,128)(2,1)} %q_ref.2, bf16[1024,1024]{1,0:T(8,128)(2,1)} %k_ref.5, bf16[1024,1024]{1,0:T(8,128)(2,1)} %v_ref.5), custom_call_target="tpu_custom_call" | custom-call | flops 8000000000 | bytes 4194304 | tf_op jit(solution)/shard_map/near_levels/pallas_call | solution.py:349
  37.9 0.0 collective-permute-done.5
  37.9 0.0 copy-start.1
  37.9 0.1 collective-permute-start.6
  38.0 2.5 %collective-permute-done.7 = bf16[2,64,1024]{2,1,0:T(8,128)(2,1)S(1)} collective-permute-done((bf16[2,64,1024]{2,1,0:T(8,128)(2,1)S(1)}, bf16[2,64,1024]{2,1,0:T(8,128)(2,1)S(1)}, u32[]{:S(2)}, u32[]{:S(2)}) %collective-permute-start.7) | collective-permute-done | bytes 262176 | tf_op jit(solution)/shard_map/ppermute | solution.py:621
  40.5 0.3 collective-permute-done.10
  40.9 0.0 copy-done.1
  41.0 0.0 copy-start
  41.0 0.1 collective-permute-start.11
  41.0 0.0 collective-permute-done.12.refs_4_
  41.1 0.0 collective-permute-done.6.refs_1_
  41.1 0.0 copy-start.2
  41.1 1.1 %copy-done.2 = bf16[2,256,1024]{2,1,0:T(8,128)(2,1)} copy-done((bf16[2,256,1024]{2,1,0:T(8,128)(2,1)}, bf16[2,256,1024]{2,1,0:T(8,128)(2,1)S(1)}, u32[]{:S(2)}) %copy-start.2) | copy-done | bytes 1048600
  42.2 1.5 %collective-permute-done.11.refs_3_ = bf16[2,256,1024]{2,1,0:T(8,128)(2,1)S(1)} collective-permute-done((bf16[2,256,1024]{2,1,0:T(8,128)(2,1)S(1)}, bf16[2,256,1024]{2,1,0:T(8,128)(2,1)S(1)}, u32[]{:S(2)}, u32[]{:S(2)}) %collective-permute-start.11) | collective-permute-done | bytes 1048608 | tf_op jit(solution)/shard_map/ppermute | solution.py:621
  43.7 0.0 copy-done
  43.7 0.0 copy-start.3
  43.7 1.0 %copy-done.3 = bf16[2,256,1024]{2,1,0:T(8,128)(2,1)} copy-done((bf16[2,256,1024]{2,1,0:T(8,128)(2,1)}, bf16[2,256,1024]{2,1,0:T(8,128)(2,1)S(1)}, u32[]{:S(2)}) %copy-start.3) | copy-done | bytes 1048600
  44.7 13.9 %far_levels_projection.1 = bf16[1024,2048]{1,0:T(8,128)(2,1)} custom-call(bf16[2,256,1024]{2,1,0:T(8,128)(2,1)} %copy-done.1, bf16[2,256,1024]{2,1,0:T(8,128)(2,1)} %copy-done.2, bf16[2,256,1024]{2,1,0:T(8,128)(2,1)} %copy-done, bf16[2,256,1024]{2,1,0:T(8,128)(2,1)} %copy-done.3, bf16[2,256,1024]{2,1,0:T(8,128)(2,1)} %collective-permute-done.12.refs_4_, ...), custom_call_target="tpu_custom_call" | custom-call | flops 6499999744 | bytes 18874368 | tf_op jit(solution)/shard_map/far_levels_projection/pallas_call | solution.py:592
  (14 shorter events, 0.3 us)
Async XLA Ops:
  5.3 8.2 %collective-permute-start.1 = (bf16[2,48,1024]{2,1,0:T(8,128)(2,1)}, bf16[2,48,1024]{2,1,0:T(8,128)(2,1)S(1)}, u32[]{:S(2)}, u32[]{:S(2)}) collective-permute-start(bf16[2,48,1024]{2,1,0:T(8,128)(2,1)} %get-tuple-element.34), channel_id=1, source_target_pairs={{8,0},{9,1},{10,2},{11,3},{12,4},{13,5},{14,6},{15,7},{0,8},{1,9},... | collective-permute-start | bytes 589832 | tf_op jit(solution)/shard_map/ppermute | solution.py:621
  8.4 24.5 %collective-permute-start = (bf16[2,64,1024]{2,1,0:T(8,128)(2,1)}, bf16[2,64,1024]{2,1,0:T(8,128)(2,1)S(1)}, u32[]{:S(2)}, u32[]{:S(2)}) collective-permute-start(bf16[2,64,1024]{2,1,0:T(8,128)(2,1)} %get-tuple-element.32), channel_id=1, source_target_pairs={{2,0},{3,1},{0,2},{1,3},{6,4},{7,5},{4,6},{5,7},{10,8},{11,9},{8,1... | collective-permute-start | bytes 786440 | tf_op jit(solution)/shard_map/ppermute | solution.py:621
  9.9 13.8 %collective-permute-start.4 = (bf16[2,64,1024]{2,1,0:T(8,128)(2,1)}, bf16[2,64,1024]{2,1,0:T(8,128)(2,1)S(1)}, u32[]{:S(2)}, u32[]{:S(2)}) collective-permute-start(bf16[2,64,1024]{2,1,0:T(8,128)(2,1)} %get-tuple-element.46), channel_id=1, source_target_pairs={{4,0},{5,1},{6,2},{7,3},{0,4},{1,5},{2,6},{3,7},{12,8},{13,9},{14,... | collective-permute-start | bytes 786440 | tf_op jit(solution)/shard_map/ppermute | solution.py:621
  13.6 11.9 %collective-permute-start.3 = (bf16[2,32,1024]{2,1,0:T(8,128)(2,1)S(1)}, bf16[2,32,1024]{2,1,0:T(8,128)(2,1)S(1)}, u32[]{:S(2)}, u32[]{:S(2)}) collective-permute-start(bf16[2,32,1024]{2,1,0:T(8,128)(2,1)S(1)} %slice.12), channel_id=1, source_target_pairs={{2,0},{3,1},{0,2},{1,3},{6,4},{7,5},{4,6},{5,7},{10,8},{11,9},{8,1... | collective-permute-start | bytes 393224 | tf_op jit(solution)/shard_map/ppermute | solution.py:621
  15.3 8.5 %collective-permute-start.8 = (bf16[2,32,1024]{2,1,0:T(8,128)(2,1)S(1)}, bf16[2,32,1024]{2,1,0:T(8,128)(2,1)S(1)}, u32[]{:S(2)}, u32[]{:S(2)}) collective-permute-start(bf16[2,32,1024]{2,1,0:T(8,128)(2,1)S(1)} %pad_maximum_fusion.3), channel_id=1, source_target_pairs={{16,0},{17,1},{18,2},{19,3},{20,4},{21,5},{22,6},{23,7},{24,8},{25... | collective-permute-start | bytes 393224 | tf_op jit(solution)/shard_map/ppermute | solution.py:621
  18.0 15.0 %collective-permute-start.2 = (bf16[2,64,1024]{2,1,0:T(8,128)(2,1)}, bf16[2,64,1024]{2,1,0:T(8,128)(2,1)S(1)}, u32[]{:S(2)}, u32[]{:S(2)}) collective-permute-start(bf16[2,64,1024]{2,1,0:T(8,128)(2,1)} %get-tuple-element.35), channel_id=1, source_target_pairs={{2,0},{3,1},{0,2},{1,3},{6,4},{7,5},{4,6},{5,7},{10,8},{11,9},{8,1... | collective-permute-start | bytes 786440 | tf_op jit(solution)/shard_map/ppermute | solution.py:621
  23.8 17.3 %collective-permute-start.12 = (bf16[2,256,1024]{2,1,0:T(8,128)(2,1)}, bf16[2,256,1024]{2,1,0:T(8,128)(2,1)}, u32[]{:S(2)}, u32[]{:S(2)}) collective-permute-start(bf16[2,256,1024]{2,1,0:T(8,128)(2,1)} %get-tuple-element.58), channel_id=1, source_target_pairs={{1,0},{0,1},{3,2},{2,3},{5,4},{4,5},{7,6},{6,7},{9,8},{8,9},{11,10... | collective-permute-start | bytes 3145736 | tf_op jit(solution)/shard_map/ppermute | solution.py:621
  23.9 14.0 %collective-permute-start.5 = (bf16[2,64,1024]{2,1,0:T(8,128)(2,1)S(1)}, bf16[2,64,1024]{2,1,0:T(8,128)(2,1)S(1)}, u32[]{:S(2)}, u32[]{:S(2)}) collective-permute-start(bf16[2,64,1024]{2,1,0:T(8,128)(2,1)S(1)} %collective-permute-done.4), channel_id=1, source_target_pairs={{2,0},{3,1},{0,2},{1,3},{6,4},{7,5},{4,6},{5,7},{10,8},{11,9},{8,1... | collective-permute-start | bytes 786440 | tf_op jit(solution)/shard_map/ppermute | solution.py:621
  25.4 6.9 %collective-permute-start.9 = (bf16[2,32,1024]{2,1,0:T(8,128)(2,1)S(1)}, bf16[2,32,1024]{2,1,0:T(8,128)(2,1)S(1)}, u32[]{:S(2)}, u32[]{:S(2)}) collective-permute-start(bf16[2,32,1024]{2,1,0:T(8,128)(2,1)S(1)} %collective-permute-done.8), channel_id=1, source_target_pairs={{4,0},{5,1},{6,2},{7,3},{0,4},{1,5},{2,6},{3,7},{12,8},{13,9},{14,... | collective-permute-start | bytes 393224 | tf_op jit(solution)/shard_map/ppermute | solution.py:621
  32.3 8.2 %collective-permute-start.7 = (bf16[2,64,1024]{2,1,0:T(8,128)(2,1)S(1)}, bf16[2,64,1024]{2,1,0:T(8,128)(2,1)S(1)}, u32[]{:S(2)}, u32[]{:S(2)}) collective-permute-start(bf16[2,64,1024]{2,1,0:T(8,128)(2,1)S(1)} %pad_maximum_fusion.2), channel_id=1, source_target_pairs={{4,0},{5,1},{6,2},{7,3},{0,4},{1,5},{2,6},{3,7},{12,8},{13,9},{14,... | collective-permute-start | bytes 786440 | tf_op jit(solution)/shard_map/ppermute | solution.py:621
  32.9 7.9 %collective-permute-start.10 = (bf16[2,64,1024]{2,1,0:T(8,128)(2,1)S(1)}, bf16[2,64,1024]{2,1,0:T(8,128)(2,1)S(1)}, u32[]{:S(2)}, u32[]{:S(2)}) collective-permute-start(bf16[2,64,1024]{2,1,0:T(8,128)(2,1)S(1)} %constant_dynamic-update-slice_fusion.4), channel_id=1, source_target_pairs={{2,0},{3,1},{0,2},{1,3},{6,4},{7,5},{4,6},{5,7},{10,8},{11,9},{8,1... | collective-permute-start | bytes 786440 | tf_op jit(solution)/shard_map/ppermute | solution.py:621
  37.9 3.0 %copy-start.1 = (bf16[2,256,1024]{2,1,0:T(8,128)(2,1)}, bf16[2,256,1024]{2,1,0:T(8,128)(2,1)S(1)}, u32[]{:S(2)}) copy-start(bf16[2,256,1024]{2,1,0:T(8,128)(2,1)S(1)} %constant_dynamic-update-slice_fusion.refs_0_) | copy-start | bytes 3145732
  37.9 3.1 %collective-permute-start.6 = (bf16[2,256,1024]{2,1,0:T(8,128)(2,1)S(1)}, bf16[2,256,1024]{2,1,0:T(8,128)(2,1)S(1)}, u32[]{:S(2)}, u32[]{:S(2)}) collective-permute-start(bf16[2,256,1024]{2,1,0:T(8,128)(2,1)S(1)} %constant_dynamic-update-slice_fusion.refs_0_), channel_id=1, source_target_pairs={{1,0},{0,1},{3,2},{2,3},{5,4},{4,5},{7,6},{6,7},{9,8},{8,9},{11,10... | collective-permute-start | bytes 3145736 | tf_op jit(solution)/shard_map/ppermute | solution.py:621
  41.0 2.7 %copy-start = (bf16[2,256,1024]{2,1,0:T(8,128)(2,1)}, bf16[2,256,1024]{2,1,0:T(8,128)(2,1)S(1)}, u32[]{:S(2)}) copy-start(bf16[2,256,1024]{2,1,0:T(8,128)(2,1)S(1)} %constant_dynamic-update-slice_fusion.6.refs_2_) | copy-start | bytes 3145732
  41.0 2.7 %collective-permute-start.11 = (bf16[2,256,1024]{2,1,0:T(8,128)(2,1)S(1)}, bf16[2,256,1024]{2,1,0:T(8,128)(2,1)S(1)}, u32[]{:S(2)}, u32[]{:S(2)}) collective-permute-start(bf16[2,256,1024]{2,1,0:T(8,128)(2,1)S(1)} %constant_dynamic-update-slice_fusion.6.refs_2_), channel_id=1, source_target_pairs={{1,0},{0,1},{3,2},{2,3},{5,4},{4,5},{7,6},{6,7},{9,8},{8,9},{11,10... | collective-permute-start | bytes 3145736 | tf_op jit(solution)/shard_map/ppermute | solution.py:621
  41.1 1.1 %copy-start.2 = (bf16[2,256,1024]{2,1,0:T(8,128)(2,1)}, bf16[2,256,1024]{2,1,0:T(8,128)(2,1)S(1)}, u32[]{:S(2)}) copy-start(bf16[2,256,1024]{2,1,0:T(8,128)(2,1)S(1)} %collective-permute-done.6.refs_1_) | copy-start | bytes 3145732
  43.7 1.0 %copy-start.3 = (bf16[2,256,1024]{2,1,0:T(8,128)(2,1)}, bf16[2,256,1024]{2,1,0:T(8,128)(2,1)S(1)}, u32[]{:S(2)}) copy-start(bf16[2,256,1024]{2,1,0:T(8,128)(2,1)S(1)} %collective-permute-done.11.refs_3_) | copy-start | bytes 3145732

commit v12 on v11

--- a/solution.py
+++ b/solution.py
@@ -21,7 +21,7 @@
 SCALE = HEAD**-0.5
 LOG2E = 1.4426950408889634
 MIB = 1 << 20
-SLICES = ((0, 3), (3, 3), (6, 2))
+SLICES = ((0, 3), (3, 2), (5, 3))
 VMEM_CLAIM = 60 * MIB
 HBM = pl.BlockSpec(memory_space=pltpu.HBM)
 

time: 59 us -> 57.7 us (0.978)
  waiting for transfers between devices: 5.56 us -> 4.17 us
  starting transfers between devices: 15.5 us -> 16.3 us
  Pallas kernels: 33.4 us -> 32.8 us
    ppermute x13, waiting for transfers between devices: 5.56 us -> 4.17 us  [moved(): lax.ppermute(array, 'seq', [(i ^ distance, i) for i in range(lax.axis_siz...]
    ppermute x13, starting transfers between devices: 15.5 us -> 16.3 us  [moved(): lax.ppermute(array, 'seq', [(i ^ distance, i) for i in range(lax.axis_siz...]
  transfers between devices with their start and end apart: 13 -> 13, of which waited for: 4 -> 5; matrix products, arithmetic and copies ran while one was open for 2% -> 2% of each run, Pallas kernels for 25% -> 26%
where the time goes in v12:
time: 57.7 us; the launch traced here: 57.4 us
  Pallas kernels  32.8 us (57%)
  starting transfers between devices  16.3 us (28%)
  waiting for transfers between devices  4.17 us (7%)
  local copies, waits for them, and re-layouts  3.7 us (6%)
    ppermute x13, starting transfers between devices, moved(): lax.ppermute(array, 'seq', [(i ^ distance, i) for i in range(lax.axis_siz...  16.3 us
    pallas_call x3, Pallas kernels, near_call(): pl.pallas_call(functools.partial(near_kernel, levels, first, heads), in_s...  14.7 us
    pallas_call x1, Pallas kernels, far_call(): pl.pallas_call(functools.partial(far_kernel, levels, plan), in_specs=[HBM...  13.3 us
    pallas_call x1, Pallas kernels, pool_call(): pl.pallas_call(functools.partial(pool_kernel, levels), in_specs=[HBM] * 4...  4.73 us
    ppermute x13, waiting for transfers between devices, moved(): lax.ppermute(array, 'seq', [(i ^ distance, i) for i in range(lax.axis_siz...  4.17 us
    unnamed x13, local copies, waits for them, and re-layouts  2.16 us
  transfers between devices with their start and end apart: 13, of which 5 were waited for; matrix products, arithmetic and copies ran while one was open for 2% of the time, Pallas kernels for 26%

profile of v12, /device:TPU:0, one launch (start us, length us, event | category | flops | bytes accessed | tf_op | source)
XLA Modules:
  0.0 57.4 jit_solution(4185879792476652617)
XLA Ops:
  0.0 0.6 %broadcast.1.large_ref = bf16[16,1024]{1,0:T(8,128)(2,1)} broadcast(bf16[]{:T(256)} %constant.13), dimensions={} | broadcast | bytes 32770 | tf_op jit(solution)
  0.6 4.7 %pool_keys_values.1 = (bf16[2,256,1024]{2,1,0:T(8,128)(2,1)}, bf16[2,64,1024]{2,1,0:T(8,128)(2,1)}, bf16[2,64,1024]{2,1,0:T(8,128)(2,1)}, bf16[2,64,1024]{2,1,0:T(8,128)(2,1)}, bf16[2,48,1024]{2,1,0:T(8,128)(2,1)}) custom-call(bf16[256,512]{1,0:T(8,128)(2,1)} %constant.12.small_ref, bf16[16,1024]{1,0:T(8,128)(2,1)} %broadcast.1.large_ref, ...), custom_call_target="tpu_custom_call" | custom-call | flops 1073741824 | bytes 6291456 | tf_op jit(solution)/shard_map/pool_keys_values/pallas_call | solution.py:157
  5.3 3.1 %collective-permute-start.1 = (bf16[2,48,1024]{2,1,0:T(8,128)(2,1)}, bf16[2,48,1024]{2,1,0:T(8,128)(2,1)S(1)}, u32[]{:S(2)}, u32[]{:S(2)}) collective-permute-start(bf16[2,48,1024]{2,1,0:T(8,128)(2,1)} %get-tuple-element.34), channel_id=1, source_target_pairs={{8,0},{9,1},{10,2},{11,3},{12,4},{13,5},{14,6},{15,7},{0,8},{1,9},... | collective-permute-start | bytes 589832 | tf_op jit(solution)/shard_map/ppermute | solution.py:621
  8.4 1.5 %collective-permute-start = (bf16[2,64,1024]{2,1,0:T(8,128)(2,1)}, bf16[2,64,1024]{2,1,0:T(8,128)(2,1)S(1)}, u32[]{:S(2)}, u32[]{:S(2)}) collective-permute-start(bf16[2,64,1024]{2,1,0:T(8,128)(2,1)} %get-tuple-element.32), channel_id=1, source_target_pairs={{2,0},{3,1},{0,2},{1,3},{6,4},{7,5},{4,6},{5,7},{10,8},{11,9},{8,1... | collective-permute-start | bytes 786440 | tf_op jit(solution)/shard_map/ppermute | solution.py:621
  9.9 1.5 %collective-permute-start.4 = (bf16[2,64,1024]{2,1,0:T(8,128)(2,1)}, bf16[2,64,1024]{2,1,0:T(8,128)(2,1)S(1)}, u32[]{:S(2)}, u32[]{:S(2)}) collective-permute-start(bf16[2,64,1024]{2,1,0:T(8,128)(2,1)} %get-tuple-element.46), channel_id=1, source_target_pairs={{4,0},{5,1},{6,2},{7,3},{0,4},{1,5},{2,6},{3,7},{12,8},{13,9},{14,... | collective-permute-start | bytes 786440 | tf_op jit(solution)/shard_map/ppermute | solution.py:621
  11.4 0.8 %slice.10 = bf16[2,16,1024]{2,1,0:T(8,128)(2,1)S(1)} slice(bf16[2,48,1024]{2,1,0:T(8,128)(2,1)} %get-tuple-element.34), slice={[0:2], [32:48], [0:1024]} | slice | bytes 131072 | tf_op jit(solution)/shard_map/slice | solution.py:648
  12.3 1.3 %collective-permute-done.1 = bf16[2,48,1024]{2,1,0:T(8,128)(2,1)S(1)} collective-permute-done((bf16[2,48,1024]{2,1,0:T(8,128)(2,1)}, bf16[2,48,1024]{2,1,0:T(8,128)(2,1)S(1)}, u32[]{:S(2)}, u32[]{:S(2)}) %collective-permute-start.1) | collective-permute-done | bytes 196640 | tf_op jit(solution)/shard_map/ppermute | solution.py:621
  13.6 1.7 %collective-permute-start.3 = (bf16[2,32,1024]{2,1,0:T(8,128)(2,1)S(1)}, bf16[2,32,1024]{2,1,0:T(8,128)(2,1)S(1)}, u32[]{:S(2)}, u32[]{:S(2)}) collective-permute-start(bf16[2,32,1024]{2,1,0:T(8,128)(2,1)S(1)} %slice.12), channel_id=1, source_target_pairs={{2,0},{3,1},{0,2},{1,3},{6,4},{7,5},{4,6},{5,7},{10,8},{11,9},{8,1... | collective-permute-start | bytes 393224 | tf_op jit(solution)/shard_map/ppermute | solution.py:621
  15.3 2.7 %collective-permute-start.8 = (bf16[2,32,1024]{2,1,0:T(8,128)(2,1)S(1)}, bf16[2,32,1024]{2,1,0:T(8,128)(2,1)S(1)}, u32[]{:S(2)}, u32[]{:S(2)}) collective-permute-start(bf16[2,32,1024]{2,1,0:T(8,128)(2,1)S(1)} %pad_maximum_fusion.3), channel_id=1, source_target_pairs={{16,0},{17,1},{18,2},{19,3},{20,4},{21,5},{22,6},{23,7},{24,8},{25... | collective-permute-start | bytes 393224 | tf_op jit(solution)/shard_map/ppermute | solution.py:621
  18.0 0.5 collective-permute-start.2
  18.5 5.3 %near_levels.3 = (f32[384,1024]{1,0:T(8,128)}, f32[3,8,1024]{2,1,0:T(8,128)}, bf16[768,384]{1,0:T(8,128)(2,1)}) custom-call(bf16[576,256]{1,0:T(8,128)(2,1)} %constant.14.pool_ref, bf16[1024,1024]{1,0:T(8,128)(2,1)} %q_ref.2, bf16[1024,1024]{1,0:T(8,128)(2,1)} %k_ref.5, bf16[1024,1024]{1,0:T(8,128)(2,1)} %v_ref.5), custom_call_target="tpu_custom_call" | custom-call | flops 8000000000 | bytes 4194304 | tf_op jit(solution)/shard_map/near_levels/pallas_call | solution.py:349
  23.7 0.0 collective-permute-done.4
  23.8 0.1 collective-permute-start.12
  23.8 0.0 collective-permute-done.8
  23.9 1.6 %collective-permute-start.5 = (bf16[2,64,1024]{2,1,0:T(8,128)(2,1)S(1)}, bf16[2,64,1024]{2,1,0:T(8,128)(2,1)S(1)}, u32[]{:S(2)}, u32[]{:S(2)}) collective-permute-start(bf16[2,64,1024]{2,1,0:T(8,128)(2,1)S(1)} %collective-permute-done.4), channel_id=1, source_target_pairs={{2,0},{3,1},{0,2},{1,3},{6,4},{7,5},{4,6},{5,7},{10,8},{11,9},{8,1... | collective-permute-start | bytes 786440 | tf_op jit(solution)/shard_map/ppermute | solution.py:621
  25.4 0.0 collective-permute-done.3
  25.4 1.6 %collective-permute-start.9 = (bf16[2,32,1024]{2,1,0:T(8,128)(2,1)S(1)}, bf16[2,32,1024]{2,1,0:T(8,128)(2,1)S(1)}, u32[]{:S(2)}, u32[]{:S(2)}) collective-permute-start(bf16[2,32,1024]{2,1,0:T(8,128)(2,1)S(1)} %collective-permute-done.8), channel_id=1, source_target_pairs={{4,0},{5,1},{6,2},{7,3},{0,4},{1,5},{2,6},{3,7},{12,8},{13,9},{14,... | collective-permute-start | bytes 393224 | tf_op jit(solution)/shard_map/ppermute | solution.py:621
  27.0 4.2 %near_levels.4 = (f32[256,1024]{1,0:T(8,128)}, f32[2,8,1024]{2,1,0:T(8,128)}, bf16[768,256]{1,0:T(8,128)(2,1)}) custom-call(bf16[576,256]{1,0:T(8,128)(2,1)} %constant.14.pool_ref, bf16[1024,1024]{1,0:T(8,128)(2,1)} %q_ref.2, bf16[1024,1024]{1,0:T(8,128)(2,1)} %k_ref.5, bf16[1024,1024]{1,0:T(8,128)(2,1)} %v_ref.5), custom_call_target="tpu_custom_call" | custom-call | flops 8000000000 | bytes 4194304 | tf_op jit(solution)/shard_map/near_levels/pallas_call | solution.py:349
  31.3 0.0 collective-permute-done.9
  31.3 1.3 %collective-permute-start.7 = (bf16[2,64,1024]{2,1,0:T(8,128)(2,1)S(1)}, bf16[2,64,1024]{2,1,0:T(8,128)(2,1)S(1)}, u32[]{:S(2)}, u32[]{:S(2)}) collective-permute-start(bf16[2,64,1024]{2,1,0:T(8,128)(2,1)S(1)} %pad_maximum_fusion.2), channel_id=1, source_target_pairs={{4,0},{5,1},{6,2},{7,3},{0,4},{1,5},{2,6},{3,7},{12,8},{13,9},{14,... | collective-permute-start | bytes 786440 | tf_op jit(solution)/shard_map/ppermute | solution.py:621
  32.6 0.0 collective-permute-done
  32.6 0.0 collective-permute-done.2
  32.6 0.6 %collective-permute-start.10 = (bf16[2,64,1024]{2,1,0:T(8,128)(2,1)S(1)}, bf16[2,64,1024]{2,1,0:T(8,128)(2,1)S(1)}, u32[]{:S(2)}, u32[]{:S(2)}) collective-permute-start(bf16[2,64,1024]{2,1,0:T(8,128)(2,1)S(1)} %constant_dynamic-update-slice_fusion.4), channel_id=1, source_target_pairs={{2,0},{3,1},{0,2},{1,3},{6,4},{7,5},{4,6},{5,7},{10,8},{11,9},{8,1... | collective-permute-start | bytes 786440 | tf_op jit(solution)/shard_map/ppermute | solution.py:621
  33.2 5.3 %near_levels.5 = (f32[384,1024]{1,0:T(8,128)}, f32[3,8,1024]{2,1,0:T(8,128)}, bf16[768,384]{1,0:T(8,128)(2,1)}) custom-call(bf16[576,256]{1,0:T(8,128)(2,1)} %constant.14.pool_ref, bf16[1024,1024]{1,0:T(8,128)(2,1)} %q_ref.2, bf16[1024,1024]{1,0:T(8,128)(2,1)} %k_ref.5, bf16[1024,1024]{1,0:T(8,128)(2,1)} %v_ref.5), custom_call_target="tpu_custom_call" | custom-call | flops 8000000000 | bytes 4194304 | tf_op jit(solution)/shard_map/near_levels/pallas_call | solution.py:349
  38.6 0.0 collective-permute-done.5
  38.6 0.0 copy-start.1
  38.6 0.1 collective-permute-start.6
  38.7 0.7 %collective-permute-done.7 = bf16[2,64,1024]{2,1,0:T(8,128)(2,1)S(1)} collective-permute-done((bf16[2,64,1024]{2,1,0:T(8,128)(2,1)S(1)}, bf16[2,64,1024]{2,1,0:T(8,128)(2,1)S(1)}, u32[]{:S(2)}, u32[]{:S(2)}) %collective-permute-start.7) | collective-permute-done | bytes 262176 | tf_op jit(solution)/shard_map/ppermute | solution.py:621
  39.5 0.5 collective-permute-done.10
  40.1 0.0 copy-done.1
  40.1 0.0 copy-start
  40.1 0.1 collective-permute-start.11
  40.2 0.0 collective-permute-done.12.refs_4_
  40.2 1.2 %collective-permute-done.6.refs_1_ = bf16[2,256,1024]{2,1,0:T(8,128)(2,1)S(1)} collective-permute-done((bf16[2,256,1024]{2,1,0:T(8,128)(2,1)S(1)}, bf16[2,256,1024]{2,1,0:T(8,128)(2,1)S(1)}, u32[]{:S(2)}, u32[]{:S(2)}) %collective-permute-start.6) | collective-permute-done | bytes 1048608 | tf_op jit(solution)/shard_map/ppermute | solution.py:621
  41.4 0.0 copy-start.2
  41.4 1.0 %copy-done.2 = bf16[2,256,1024]{2,1,0:T(8,128)(2,1)} copy-done((bf16[2,256,1024]{2,1,0:T(8,128)(2,1)}, bf16[2,256,1024]{2,1,0:T(8,128)(2,1)S(1)}, u32[]{:S(2)}) %copy-start.2) | copy-done | bytes 1048600
  42.3 0.5 collective-permute-done.11.refs_3_
  42.9 0.0 copy-done
  42.9 0.0 copy-start.3
  42.9 1.1 %copy-done.3 = bf16[2,256,1024]{2,1,0:T(8,128)(2,1)} copy-done((bf16[2,256,1024]{2,1,0:T(8,128)(2,1)}, bf16[2,256,1024]{2,1,0:T(8,128)(2,1)S(1)}, u32[]{:S(2)}) %copy-start.3) | copy-done | bytes 1048600
  43.9 13.3 %far_levels_projection.1 = bf16[1024,2048]{1,0:T(8,128)(2,1)} custom-call(bf16[2,256,1024]{2,1,0:T(8,128)(2,1)} %copy-done.1, bf16[2,256,1024]{2,1,0:T(8,128)(2,1)} %copy-done.2, bf16[2,256,1024]{2,1,0:T(8,128)(2,1)} %copy-done, bf16[2,256,1024]{2,1,0:T(8,128)(2,1)} %copy-done.3, bf16[2,256,1024]{2,1,0:T(8,128)(2,1)} %collective-permute-done.12.refs_4_, ...), custom_call_target="tpu_custom_call" | custom-call | flops 6499999744 | bytes 18874368 | tf_op jit(solution)/shard_map/far_levels_projection/pallas_call | solution.py:592
  (14 shorter events, 0.3 us)
Async XLA Ops:
  5.3 8.2 %collective-permute-start.1 = (bf16[2,48,1024]{2,1,0:T(8,128)(2,1)}, bf16[2,48,1024]{2,1,0:T(8,128)(2,1)S(1)}, u32[]{:S(2)}, u32[]{:S(2)}) collective-permute-start(bf16[2,48,1024]{2,1,0:T(8,128)(2,1)} %get-tuple-element.34), channel_id=1, source_target_pairs={{8,0},{9,1},{10,2},{11,3},{12,4},{13,5},{14,6},{15,7},{0,8},{1,9},... | collective-permute-start | bytes 589832 | tf_op jit(solution)/shard_map/ppermute | solution.py:621
  8.4 24.2 %collective-permute-start = (bf16[2,64,1024]{2,1,0:T(8,128)(2,1)}, bf16[2,64,1024]{2,1,0:T(8,128)(2,1)S(1)}, u32[]{:S(2)}, u32[]{:S(2)}) collective-permute-start(bf16[2,64,1024]{2,1,0:T(8,128)(2,1)} %get-tuple-element.32), channel_id=1, source_target_pairs={{2,0},{3,1},{0,2},{1,3},{6,4},{7,5},{4,6},{5,7},{10,8},{11,9},{8,1... | collective-permute-start | bytes 786440 | tf_op jit(solution)/shard_map/ppermute | solution.py:621
  9.9 13.8 %collective-permute-start.4 = (bf16[2,64,1024]{2,1,0:T(8,128)(2,1)}, bf16[2,64,1024]{2,1,0:T(8,128)(2,1)S(1)}, u32[]{:S(2)}, u32[]{:S(2)}) collective-permute-start(bf16[2,64,1024]{2,1,0:T(8,128)(2,1)} %get-tuple-element.46), channel_id=1, source_target_pairs={{4,0},{5,1},{6,2},{7,3},{0,4},{1,5},{2,6},{3,7},{12,8},{13,9},{14,... | collective-permute-start | bytes 786440 | tf_op jit(solution)/shard_map/ppermute | solution.py:621
  13.6 11.9 %collective-permute-start.3 = (bf16[2,32,1024]{2,1,0:T(8,128)(2,1)S(1)}, bf16[2,32,1024]{2,1,0:T(8,128)(2,1)S(1)}, u32[]{:S(2)}, u32[]{:S(2)}) collective-permute-start(bf16[2,32,1024]{2,1,0:T(8,128)(2,1)S(1)} %slice.12), channel_id=1, source_target_pairs={{2,0},{3,1},{0,2},{1,3},{6,4},{7,5},{4,6},{5,7},{10,8},{11,9},{8,1... | collective-permute-start | bytes 393224 | tf_op jit(solution)/shard_map/ppermute | solution.py:621
  15.3 8.5 %collective-permute-start.8 = (bf16[2,32,1024]{2,1,0:T(8,128)(2,1)S(1)}, bf16[2,32,1024]{2,1,0:T(8,128)(2,1)S(1)}, u32[]{:S(2)}, u32[]{:S(2)}) collective-permute-start(bf16[2,32,1024]{2,1,0:T(8,128)(2,1)S(1)} %pad_maximum_fusion.3), channel_id=1, source_target_pairs={{16,0},{17,1},{18,2},{19,3},{20,4},{21,5},{22,6},{23,7},{24,8},{25... | collective-permute-start | bytes 393224 | tf_op jit(solution)/shard_map/ppermute | solution.py:621
  18.0 14.7 %collective-permute-start.2 = (bf16[2,64,1024]{2,1,0:T(8,128)(2,1)}, bf16[2,64,1024]{2,1,0:T(8,128)(2,1)S(1)}, u32[]{:S(2)}, u32[]{:S(2)}) collective-permute-start(bf16[2,64,1024]{2,1,0:T(8,128)(2,1)} %get-tuple-element.35), channel_id=1, source_target_pairs={{2,0},{3,1},{0,2},{1,3},{6,4},{7,5},{4,6},{5,7},{10,8},{11,9},{8,1... | collective-permute-start | bytes 786440 | tf_op jit(solution)/shard_map/ppermute | solution.py:621
  23.8 16.4 %collective-permute-start.12 = (bf16[2,256,1024]{2,1,0:T(8,128)(2,1)}, bf16[2,256,1024]{2,1,0:T(8,128)(2,1)}, u32[]{:S(2)}, u32[]{:S(2)}) collective-permute-start(bf16[2,256,1024]{2,1,0:T(8,128)(2,1)} %get-tuple-element.58), channel_id=1, source_target_pairs={{1,0},{0,1},{3,2},{2,3},{5,4},{4,5},{7,6},{6,7},{9,8},{8,9},{11,10... | collective-permute-start | bytes 3145736 | tf_op jit(solution)/shard_map/ppermute | solution.py:621
  23.9 14.7 %collective-permute-start.5 = (bf16[2,64,1024]{2,1,0:T(8,128)(2,1)S(1)}, bf16[2,64,1024]{2,1,0:T(8,128)(2,1)S(1)}, u32[]{:S(2)}, u32[]{:S(2)}) collective-permute-start(bf16[2,64,1024]{2,1,0:T(8,128)(2,1)S(1)} %collective-permute-done.4), channel_id=1, source_target_pairs={{2,0},{3,1},{0,2},{1,3},{6,4},{7,5},{4,6},{5,7},{10,8},{11,9},{8,1... | collective-permute-start | bytes 786440 | tf_op jit(solution)/shard_map/ppermute | solution.py:621
  25.4 5.8 %collective-permute-start.9 = (bf16[2,32,1024]{2,1,0:T(8,128)(2,1)S(1)}, bf16[2,32,1024]{2,1,0:T(8,128)(2,1)S(1)}, u32[]{:S(2)}, u32[]{:S(2)}) collective-permute-start(bf16[2,32,1024]{2,1,0:T(8,128)(2,1)S(1)} %collective-permute-done.8), channel_id=1, source_target_pairs={{4,0},{5,1},{6,2},{7,3},{0,4},{1,5},{2,6},{3,7},{12,8},{13,9},{14,... | collective-permute-start | bytes 393224 | tf_op jit(solution)/shard_map/ppermute | solution.py:621
  31.3 8.2 %collective-permute-start.7 = (bf16[2,64,1024]{2,1,0:T(8,128)(2,1)S(1)}, bf16[2,64,1024]{2,1,0:T(8,128)(2,1)S(1)}, u32[]{:S(2)}, u32[]{:S(2)}) collective-permute-start(bf16[2,64,1024]{2,1,0:T(8,128)(2,1)S(1)} %pad_maximum_fusion.2), channel_id=1, source_target_pairs={{4,0},{5,1},{6,2},{7,3},{0,4},{1,5},{2,6},{3,7},{12,8},{13,9},{14,... | collective-permute-start | bytes 786440 | tf_op jit(solution)/shard_map/ppermute | solution.py:621
  32.6 7.3 %collective-permute-start.10 = (bf16[2,64,1024]{2,1,0:T(8,128)(2,1)S(1)}, bf16[2,64,1024]{2,1,0:T(8,128)(2,1)S(1)}, u32[]{:S(2)}, u32[]{:S(2)}) collective-permute-start(bf16[2,64,1024]{2,1,0:T(8,128)(2,1)S(1)} %constant_dynamic-update-slice_fusion.4), channel_id=1, source_target_pairs={{2,0},{3,1},{0,2},{1,3},{6,4},{7,5},{4,6},{5,7},{10,8},{11,9},{8,1... | collective-permute-start | bytes 786440 | tf_op jit(solution)/shard_map/ppermute | solution.py:621
  38.6 1.4 %copy-start.1 = (bf16[2,256,1024]{2,1,0:T(8,128)(2,1)}, bf16[2,256,1024]{2,1,0:T(8,128)(2,1)S(1)}, u32[]{:S(2)}) copy-start(bf16[2,256,1024]{2,1,0:T(8,128)(2,1)S(1)} %constant_dynamic-update-slice_fusion.refs_0_) | copy-start | bytes 3145732
  38.6 2.7 %collective-permute-start.6 = (bf16[2,256,1024]{2,1,0:T(8,128)(2,1)S(1)}, bf16[2,256,1024]{2,1,0:T(8,128)(2,1)S(1)}, u32[]{:S(2)}, u32[]{:S(2)}) collective-permute-start(bf16[2,256,1024]{2,1,0:T(8,128)(2,1)S(1)} %constant_dynamic-update-slice_fusion.refs_0_), channel_id=1, source_target_pairs={{1,0},{0,1},{3,2},{2,3},{5,4},{4,5},{7,6},{6,7},{9,8},{8,9},{11,10... | collective-permute-start | bytes 3145736 | tf_op jit(solution)/shard_map/ppermute | solution.py:621
  40.1 2.8 %copy-start = (bf16[2,256,1024]{2,1,0:T(8,128)(2,1)}, bf16[2,256,1024]{2,1,0:T(8,128)(2,1)S(1)}, u32[]{:S(2)}) copy-start(bf16[2,256,1024]{2,1,0:T(8,128)(2,1)S(1)} %constant_dynamic-update-slice_fusion.6.refs_2_) | copy-start | bytes 3145732
  40.1 2.8 %collective-permute-start.11 = (bf16[2,256,1024]{2,1,0:T(8,128)(2,1)S(1)}, bf16[2,256,1024]{2,1,0:T(8,128)(2,1)S(1)}, u32[]{:S(2)}, u32[]{:S(2)}) collective-permute-start(bf16[2,256,1024]{2,1,0:T(8,128)(2,1)S(1)} %constant_dynamic-update-slice_fusion.6.refs_2_), channel_id=1, source_target_pairs={{1,0},{0,1},{3,2},{2,3},{5,4},{4,5},{7,6},{6,7},{9,8},{8,9},{11,10... | collective-permute-start | bytes 3145736 | tf_op jit(solution)/shard_map/ppermute | solution.py:621
  41.4 1.0 %copy-start.2 = (bf16[2,256,1024]{2,1,0:T(8,128)(2,1)}, bf16[2,256,1024]{2,1,0:T(8,128)(2,1)S(1)}, u32[]{:S(2)}) copy-start(bf16[2,256,1024]{2,1,0:T(8,128)(2,1)S(1)} %collective-permute-done.6.refs_1_) | copy-start | bytes 3145732
  42.9 1.1 %copy-start.3 = (bf16[2,256,1024]{2,1,0:T(8,128)(2,1)}, bf16[2,256,1024]{2,1,0:T(8,128)(2,1)S(1)}, u32[]{:S(2)}) copy-start(bf16[2,256,1024]{2,1,0:T(8,128)(2,1)S(1)} %collective-permute-done.11.refs_3_) | copy-start | bytes 3145732

commit v13 on v12

--- a/solution.py
+++ b/solution.py
@@ -21,7 +21,7 @@
 SCALE = HEAD**-0.5
 LOG2E = 1.4426950408889634
 MIB = 1 << 20
-SLICES = ((0, 3), (3, 2), (5, 3))
+SLICES = ((0, 3), (3, 1), (4, 4))
 VMEM_CLAIM = 60 * MIB
 HBM = pl.BlockSpec(memory_space=pltpu.HBM)
 

time: 57.7 us -> 59.3 us (1.028)
  Pallas kernels: 32.8 us -> 33.7 us
    pallas_call x1, Pallas kernels: 13.3 us -> 14.2 us  [far_call(): pl.pallas_call(functools.partial(far_kernel, levels, plan), in_specs=[HBM...]
  transfers between devices with their start and end apart: 13 -> 13, of which waited for: 5 -> 5; matrix products, arithmetic and copies ran while one was open for 2% -> 2% of each run, Pallas kernels for 26% -> 25%
where the time goes in v13:
time: 59.3 us; the launch traced here: 59.1 us
  Pallas kernels  33.7 us (57%)
  starting transfers between devices  16.4 us (28%)
  waiting for transfers between devices  4.45 us (8%)
  local copies, waits for them, and re-layouts  4.13 us (7%)
    ppermute x13, starting transfers between devices, moved(): lax.ppermute(array, 'seq', [(i ^ distance, i) for i in range(lax.axis_siz...  16.4 us
    pallas_call x3, Pallas kernels, near_call(): pl.pallas_call(functools.partial(near_kernel, levels, first, heads), in_s...  14.8 us
    pallas_call x1, Pallas kernels, far_call(): pl.pallas_call(functools.partial(far_kernel, levels, plan), in_specs=[HBM...  14.2 us
    pallas_call x1, Pallas kernels, pool_call(): pl.pallas_call(functools.partial(pool_kernel, levels), in_specs=[HBM] * 4...  4.71 us
    ppermute x13, waiting for transfers between devices, moved(): lax.ppermute(array, 'seq', [(i ^ distance, i) for i in range(lax.axis_siz...  4.45 us
    unnamed x13, local copies, waits for them, and re-layouts  2.59 us
  transfers between devices with their start and end apart: 13, of which 5 were waited for; matrix products, arithmetic and copies ran while one was open for 2% of the time, Pallas kernels for 25%

profile of v13, /device:TPU:0, one launch (start us, length us, event | category | flops | bytes accessed | tf_op | source)
XLA Modules:
  0.0 59.1 jit_solution(16596558077643836620)
XLA Ops:
  0.0 0.6 %broadcast.1.large_ref = bf16[16,1024]{1,0:T(8,128)(2,1)} broadcast(bf16[]{:T(256)} %constant.13), dimensions={} | broadcast | bytes 32770 | tf_op jit(solution)
  0.6 4.7 %pool_keys_values.1 = (bf16[2,256,1024]{2,1,0:T(8,128)(2,1)}, bf16[2,64,1024]{2,1,0:T(8,128)(2,1)}, bf16[2,64,1024]{2,1,0:T(8,128)(2,1)}, bf16[2,64,1024]{2,1,0:T(8,128)(2,1)}, bf16[2,48,1024]{2,1,0:T(8,128)(2,1)}) custom-call(bf16[256,512]{1,0:T(8,128)(2,1)} %constant.12.small_ref, bf16[16,1024]{1,0:T(8,128)(2,1)} %broadcast.1.large_ref, ...), custom_call_target="tpu_custom_call" | custom-call | flops 1073741824 | bytes 6291456 | tf_op jit(solution)/shard_map/pool_keys_values/pallas_call | solution.py:157
  5.3 3.1 %collective-permute-start.1 = (bf16[2,48,1024]{2,1,0:T(8,128)(2,1)}, bf16[2,48,1024]{2,1,0:T(8,128)(2,1)S(1)}, u32[]{:S(2)}, u32[]{:S(2)}) collective-permute-start(bf16[2,48,1024]{2,1,0:T(8,128)(2,1)} %get-tuple-element.34), channel_id=1, source_target_pairs={{8,0},{9,1},{10,2},{11,3},{12,4},{13,5},{14,6},{15,7},{0,8},{1,9},... | collective-permute-start | bytes 589832 | tf_op jit(solution)/shard_map/ppermute | solution.py:621
  8.4 1.5 %collective-permute-start = (bf16[2,64,1024]{2,1,0:T(8,128)(2,1)}, bf16[2,64,1024]{2,1,0:T(8,128)(2,1)S(1)}, u32[]{:S(2)}, u32[]{:S(2)}) collective-permute-start(bf16[2,64,1024]{2,1,0:T(8,128)(2,1)} %get-tuple-element.32), channel_id=1, source_target_pairs={{2,0},{3,1},{0,2},{1,3},{6,4},{7,5},{4,6},{5,7},{10,8},{11,9},{8,1... | collective-permute-start | bytes 786440 | tf_op jit(solution)/shard_map/ppermute | solution.py:621
  9.9 1.5 %collective-permute-start.4 = (bf16[2,64,1024]{2,1,0:T(8,128)(2,1)}, bf16[2,64,1024]{2,1,0:T(8,128)(2,1)S(1)}, u32[]{:S(2)}, u32[]{:S(2)}) collective-permute-start(bf16[2,64,1024]{2,1,0:T(8,128)(2,1)} %get-tuple-element.46), channel_id=1, source_target_pairs={{4,0},{5,1},{6,2},{7,3},{0,4},{1,5},{2,6},{3,7},{12,8},{13,9},{14,... | collective-permute-start | bytes 786440 | tf_op jit(solution)/shard_map/ppermute | solution.py:621
  11.4 0.8 %slice.10 = bf16[2,16,1024]{2,1,0:T(8,128)(2,1)S(1)} slice(bf16[2,48,1024]{2,1,0:T(8,128)(2,1)} %get-tuple-element.34), slice={[0:2], [32:48], [0:1024]} | slice | bytes 131072 | tf_op jit(solution)/shard_map/slice | solution.py:648
  12.3 1.3 %collective-permute-done.1 = bf16[2,48,1024]{2,1,0:T(8,128)(2,1)S(1)} collective-permute-done((bf16[2,48,1024]{2,1,0:T(8,128)(2,1)}, bf16[2,48,1024]{2,1,0:T(8,128)(2,1)S(1)}, u32[]{:S(2)}, u32[]{:S(2)}) %collective-permute-start.1) | collective-permute-done | bytes 196640 | tf_op jit(solution)/shard_map/ppermute | solution.py:621
  13.5 1.7 %collective-permute-start.3 = (bf16[2,32,1024]{2,1,0:T(8,128)(2,1)S(1)}, bf16[2,32,1024]{2,1,0:T(8,128)(2,1)S(1)}, u32[]{:S(2)}, u32[]{:S(2)}) collective-permute-start(bf16[2,32,1024]{2,1,0:T(8,128)(2,1)S(1)} %slice.12), channel_id=1, source_target_pairs={{2,0},{3,1},{0,2},{1,3},{6,4},{7,5},{4,6},{5,7},{10,8},{11,9},{8,1... | collective-permute-start | bytes 393224 | tf_op jit(solution)/shard_map/ppermute | solution.py:621
  15.3 2.6 %collective-permute-start.8 = (bf16[2,32,1024]{2,1,0:T(8,128)(2,1)S(1)}, bf16[2,32,1024]{2,1,0:T(8,128)(2,1)S(1)}, u32[]{:S(2)}, u32[]{:S(2)}) collective-permute-start(bf16[2,32,1024]{2,1,0:T(8,128)(2,1)S(1)} %pad_maximum_fusion.3), channel_id=1, source_target_pairs={{16,0},{17,1},{18,2},{19,3},{20,4},{21,5},{22,6},{23,7},{24,8},{25... | collective-permute-start | bytes 393224 | tf_op jit(solution)/shard_map/ppermute | solution.py:621
  17.9 0.5 collective-permute-start.2
  18.5 5.3 %near_levels.3 = (f32[384,1024]{1,0:T(8,128)}, f32[3,8,1024]{2,1,0:T(8,128)}, bf16[768,384]{1,0:T(8,128)(2,1)}) custom-call(bf16[576,256]{1,0:T(8,128)(2,1)} %constant.14.pool_ref, bf16[1024,1024]{1,0:T(8,128)(2,1)} %q_ref.2, bf16[1024,1024]{1,0:T(8,128)(2,1)} %k_ref.5, bf16[1024,1024]{1,0:T(8,128)(2,1)} %v_ref.5), custom_call_target="tpu_custom_call" | custom-call | flops 8000000000 | bytes 4194304 | tf_op jit(solution)/shard_map/near_levels/pallas_call | solution.py:349
  23.7 0.0 collective-permute-done.4
  23.7 0.1 collective-permute-start.12
  23.8 0.0 collective-permute-done.8
  23.8 1.6 %collective-permute-start.5 = (bf16[2,64,1024]{2,1,0:T(8,128)(2,1)S(1)}, bf16[2,64,1024]{2,1,0:T(8,128)(2,1)S(1)}, u32[]{:S(2)}, u32[]{:S(2)}) collective-permute-start(bf16[2,64,1024]{2,1,0:T(8,128)(2,1)S(1)} %collective-permute-done.4), channel_id=1, source_target_pairs={{2,0},{3,1},{0,2},{1,3},{6,4},{7,5},{4,6},{5,7},{10,8},{11,9},{8,1... | collective-permute-start | bytes 786440 | tf_op jit(solution)/shard_map/ppermute | solution.py:621
  25.4 0.0 collective-permute-done.3
  25.4 1.6 %collective-permute-start.9 = (bf16[2,32,1024]{2,1,0:T(8,128)(2,1)S(1)}, bf16[2,32,1024]{2,1,0:T(8,128)(2,1)S(1)}, u32[]{:S(2)}, u32[]{:S(2)}) collective-permute-start(bf16[2,32,1024]{2,1,0:T(8,128)(2,1)S(1)} %collective-permute-done.8), channel_id=1, source_target_pairs={{4,0},{5,1},{6,2},{7,3},{0,4},{1,5},{2,6},{3,7},{12,8},{13,9},{14,... | collective-permute-start | bytes 393224 | tf_op jit(solution)/shard_map/ppermute | solution.py:621
  27.0 3.4 %near_levels.4 = (f32[128,1024]{1,0:T(8,128)}, f32[1,8,1024]{2,1,0:T(8,128)}, bf16[768,128]{1,0:T(8,128)(2,1)}) custom-call(bf16[576,256]{1,0:T(8,128)(2,1)} %constant.14.pool_ref, bf16[1024,1024]{1,0:T(8,128)(2,1)} %q_ref.2, bf16[1024,1024]{1,0:T(8,128)(2,1)} %k_ref.5, bf16[1024,1024]{1,0:T(8,128)(2,1)} %v_ref.5), custom_call_target="tpu_custom_call" | custom-call | flops 8000000000 | bytes 4194304 | tf_op jit(solution)/shard_map/near_levels/pallas_call | solution.py:349
  30.4 0.7 %collective-permute-done.9 = bf16[2,32,1024]{2,1,0:T(8,128)(2,1)S(1)} collective-permute-done((bf16[2,32,1024]{2,1,0:T(8,128)(2,1)S(1)}, bf16[2,32,1024]{2,1,0:T(8,128)(2,1)S(1)}, u32[]{:S(2)}, u32[]{:S(2)}) %collective-permute-start.9) | collective-permute-done | bytes 131104 | tf_op jit(solution)/shard_map/ppermute | solution.py:621
  31.0 1.5 %collective-permute-start.7 = (bf16[2,64,1024]{2,1,0:T(8,128)(2,1)S(1)}, bf16[2,64,1024]{2,1,0:T(8,128)(2,1)S(1)}, u32[]{:S(2)}, u32[]{:S(2)}) collective-permute-start(bf16[2,64,1024]{2,1,0:T(8,128)(2,1)S(1)} %pad_maximum_fusion.2), channel_id=1, source_target_pairs={{4,0},{5,1},{6,2},{7,3},{0,4},{1,5},{2,6},{3,7},{12,8},{13,9},{14,... | collective-permute-start | bytes 786440 | tf_op jit(solution)/shard_map/ppermute | solution.py:621
  32.6 0.0 collective-permute-done
  32.6 0.0 collective-permute-done.2
  32.6 0.6 %collective-permute-start.10 = (bf16[2,64,1024]{2,1,0:T(8,128)(2,1)S(1)}, bf16[2,64,1024]{2,1,0:T(8,128)(2,1)S(1)}, u32[]{:S(2)}, u32[]{:S(2)}) collective-permute-start(bf16[2,64,1024]{2,1,0:T(8,128)(2,1)S(1)} %constant_dynamic-update-slice_fusion.4), channel_id=1, source_target_pairs={{2,0},{3,1},{0,2},{1,3},{6,4},{7,5},{4,6},{5,7},{10,8},{11,9},{8,1... | collective-permute-start | bytes 786440 | tf_op jit(solution)/shard_map/ppermute | solution.py:621
  33.2 6.2 %near_levels.5 = (f32[512,1024]{1,0:T(8,128)}, f32[4,8,1024]{2,1,0:T(8,128)}, bf16[768,512]{1,0:T(8,128)(2,1)}) custom-call(bf16[576,256]{1,0:T(8,128)(2,1)} %constant.14.pool_ref, bf16[1024,1024]{1,0:T(8,128)(2,1)} %q_ref.2, bf16[1024,1024]{1,0:T(8,128)(2,1)} %k_ref.5, bf16[1024,1024]{1,0:T(8,128)(2,1)} %v_ref.5), custom_call_target="tpu_custom_call" | custom-call | flops 8000000000 | bytes 4194304 | tf_op jit(solution)/shard_map/near_levels/pallas_call | solution.py:349
  39.5 0.0 collective-permute-done.5
  39.5 0.0 copy-start.1
  39.5 0.1 collective-permute-start.6
  39.6 0.0 collective-permute-done.7
  39.6 0.3 collective-permute-done.10
  40.0 0.5 copy-done.1
  40.5 0.0 copy-start
  40.5 0.0 collective-permute-start.11
  40.5 0.0 collective-permute-done.12.refs_4_
  40.5 1.7 %collective-permute-done.6.refs_1_ = bf16[2,256,1024]{2,1,0:T(8,128)(2,1)S(1)} collective-permute-done((bf16[2,256,1024]{2,1,0:T(8,128)(2,1)S(1)}, bf16[2,256,1024]{2,1,0:T(8,128)(2,1)S(1)}, u32[]{:S(2)}, u32[]{:S(2)}) %collective-permute-start.6) | collective-permute-done | bytes 1048608 | tf_op jit(solution)/shard_map/ppermute | solution.py:621
  42.2 0.0 copy-start.2
  42.2 1.0 %copy-done.2 = bf16[2,256,1024]{2,1,0:T(8,128)(2,1)} copy-done((bf16[2,256,1024]{2,1,0:T(8,128)(2,1)}, bf16[2,256,1024]{2,1,0:T(8,128)(2,1)S(1)}, u32[]{:S(2)}) %copy-start.2) | copy-done | bytes 1048600
  43.2 0.5 collective-permute-done.11.refs_3_
  43.7 0.0 copy-done
  43.7 0.0 copy-start.3
  43.7 1.0 %copy-done.3 = bf16[2,256,1024]{2,1,0:T(8,128)(2,1)} copy-done((bf16[2,256,1024]{2,1,0:T(8,128)(2,1)}, bf16[2,256,1024]{2,1,0:T(8,128)(2,1)S(1)}, u32[]{:S(2)}) %copy-start.3) | copy-done | bytes 1048600
  44.8 14.2 %far_levels_projection.1 = bf16[1024,2048]{1,0:T(8,128)(2,1)} custom-call(bf16[2,256,1024]{2,1,0:T(8,128)(2,1)} %copy-done.1, bf16[2,256,1024]{2,1,0:T(8,128)(2,1)} %copy-done.2, bf16[2,256,1024]{2,1,0:T(8,128)(2,1)} %copy-done, bf16[2,256,1024]{2,1,0:T(8,128)(2,1)} %copy-done.3, bf16[2,256,1024]{2,1,0:T(8,128)(2,1)} %collective-permute-done.12.refs_4_, ...), custom_call_target="tpu_custom_call" | custom-call | flops 6499999744 | bytes 18874368 | tf_op jit(solution)/shard_map/far_levels_projection/pallas_call | solution.py:592
  (14 shorter events, 0.3 us)
Async XLA Ops:
  5.3 8.2 %collective-permute-start.1 = (bf16[2,48,1024]{2,1,0:T(8,128)(2,1)}, bf16[2,48,1024]{2,1,0:T(8,128)(2,1)S(1)}, u32[]{:S(2)}, u32[]{:S(2)}) collective-permute-start(bf16[2,48,1024]{2,1,0:T(8,128)(2,1)} %get-tuple-element.34), channel_id=1, source_target_pairs={{8,0},{9,1},{10,2},{11,3},{12,4},{13,5},{14,6},{15,7},{0,8},{1,9},... | collective-permute-start | bytes 589832 | tf_op jit(solution)/shard_map/ppermute | solution.py:621
  8.4 24.2 %collective-permute-start = (bf16[2,64,1024]{2,1,0:T(8,128)(2,1)}, bf16[2,64,1024]{2,1,0:T(8,128)(2,1)S(1)}, u32[]{:S(2)}, u32[]{:S(2)}) collective-permute-start(bf16[2,64,1024]{2,1,0:T(8,128)(2,1)} %get-tuple-element.32), channel_id=1, source_target_pairs={{2,0},{3,1},{0,2},{1,3},{6,4},{7,5},{4,6},{5,7},{10,8},{11,9},{8,1... | collective-permute-start | bytes 786440 | tf_op jit(solution)/shard_map/ppermute | solution.py:621
  9.9 13.8 %collective-permute-start.4 = (bf16[2,64,1024]{2,1,0:T(8,128)(2,1)}, bf16[2,64,1024]{2,1,0:T(8,128)(2,1)S(1)}, u32[]{:S(2)}, u32[]{:S(2)}) collective-permute-start(bf16[2,64,1024]{2,1,0:T(8,128)(2,1)} %get-tuple-element.46), channel_id=1, source_target_pairs={{4,0},{5,1},{6,2},{7,3},{0,4},{1,5},{2,6},{3,7},{12,8},{13,9},{14,... | collective-permute-start | bytes 786440 | tf_op jit(solution)/shard_map/ppermute | solution.py:621
  13.5 11.9 %collective-permute-start.3 = (bf16[2,32,1024]{2,1,0:T(8,128)(2,1)S(1)}, bf16[2,32,1024]{2,1,0:T(8,128)(2,1)S(1)}, u32[]{:S(2)}, u32[]{:S(2)}) collective-permute-start(bf16[2,32,1024]{2,1,0:T(8,128)(2,1)S(1)} %slice.12), channel_id=1, source_target_pairs={{2,0},{3,1},{0,2},{1,3},{6,4},{7,5},{4,6},{5,7},{10,8},{11,9},{8,1... | collective-permute-start | bytes 393224 | tf_op jit(solution)/shard_map/ppermute | solution.py:621
  15.3 8.5 %collective-permute-start.8 = (bf16[2,32,1024]{2,1,0:T(8,128)(2,1)S(1)}, bf16[2,32,1024]{2,1,0:T(8,128)(2,1)S(1)}, u32[]{:S(2)}, u32[]{:S(2)}) collective-permute-start(bf16[2,32,1024]{2,1,0:T(8,128)(2,1)S(1)} %pad_maximum_fusion.3), channel_id=1, source_target_pairs={{16,0},{17,1},{18,2},{19,3},{20,4},{21,5},{22,6},{23,7},{24,8},{25... | collective-permute-start | bytes 393224 | tf_op jit(solution)/shard_map/ppermute | solution.py:621
  17.9 14.6 %collective-permute-start.2 = (bf16[2,64,1024]{2,1,0:T(8,128)(2,1)}, bf16[2,64,1024]{2,1,0:T(8,128)(2,1)S(1)}, u32[]{:S(2)}, u32[]{:S(2)}) collective-permute-start(bf16[2,64,1024]{2,1,0:T(8,128)(2,1)} %get-tuple-element.35), channel_id=1, source_target_pairs={{2,0},{3,1},{0,2},{1,3},{6,4},{7,5},{4,6},{5,7},{10,8},{11,9},{8,1... | collective-permute-start | bytes 786440 | tf_op jit(solution)/shard_map/ppermute | solution.py:621
  23.7 16.8 %collective-permute-start.12 = (bf16[2,256,1024]{2,1,0:T(8,128)(2,1)}, bf16[2,256,1024]{2,1,0:T(8,128)(2,1)}, u32[]{:S(2)}, u32[]{:S(2)}) collective-permute-start(bf16[2,256,1024]{2,1,0:T(8,128)(2,1)} %get-tuple-element.58), channel_id=1, source_target_pairs={{1,0},{0,1},{3,2},{2,3},{5,4},{4,5},{7,6},{6,7},{9,8},{8,9},{11,10... | collective-permute-start | bytes 3145736 | tf_op jit(solution)/shard_map/ppermute | solution.py:621
  23.8 15.6 %collective-permute-start.5 = (bf16[2,64,1024]{2,1,0:T(8,128)(2,1)S(1)}, bf16[2,64,1024]{2,1,0:T(8,128)(2,1)S(1)}, u32[]{:S(2)}, u32[]{:S(2)}) collective-permute-start(bf16[2,64,1024]{2,1,0:T(8,128)(2,1)S(1)} %collective-permute-done.4), channel_id=1, source_target_pairs={{2,0},{3,1},{0,2},{1,3},{6,4},{7,5},{4,6},{5,7},{10,8},{11,9},{8,1... | collective-permute-start | bytes 786440 | tf_op jit(solution)/shard_map/ppermute | solution.py:621
  25.4 5.6 %collective-permute-start.9 = (bf16[2,32,1024]{2,1,0:T(8,128)(2,1)S(1)}, bf16[2,32,1024]{2,1,0:T(8,128)(2,1)S(1)}, u32[]{:S(2)}, u32[]{:S(2)}) collective-permute-start(bf16[2,32,1024]{2,1,0:T(8,128)(2,1)S(1)} %collective-permute-done.8), channel_id=1, source_target_pairs={{4,0},{5,1},{6,2},{7,3},{0,4},{1,5},{2,6},{3,7},{12,8},{13,9},{14,... | collective-permute-start | bytes 393224 | tf_op jit(solution)/shard_map/ppermute | solution.py:621
  31.0 8.5 %collective-permute-start.7 = (bf16[2,64,1024]{2,1,0:T(8,128)(2,1)S(1)}, bf16[2,64,1024]{2,1,0:T(8,128)(2,1)S(1)}, u32[]{:S(2)}, u32[]{:S(2)}) collective-permute-start(bf16[2,64,1024]{2,1,0:T(8,128)(2,1)S(1)} %pad_maximum_fusion.2), channel_id=1, source_target_pairs={{4,0},{5,1},{6,2},{7,3},{0,4},{1,5},{2,6},{3,7},{12,8},{13,9},{14,... | collective-permute-start | bytes 786440 | tf_op jit(solution)/shard_map/ppermute | solution.py:621
  32.6 7.3 %collective-permute-start.10 = (bf16[2,64,1024]{2,1,0:T(8,128)(2,1)S(1)}, bf16[2,64,1024]{2,1,0:T(8,128)(2,1)S(1)}, u32[]{:S(2)}, u32[]{:S(2)}) collective-permute-start(bf16[2,64,1024]{2,1,0:T(8,128)(2,1)S(1)} %constant_dynamic-update-slice_fusion.4), channel_id=1, source_target_pairs={{2,0},{3,1},{0,2},{1,3},{6,4},{7,5},{4,6},{5,7},{10,8},{11,9},{8,1... | collective-permute-start | bytes 786440 | tf_op jit(solution)/shard_map/ppermute | solution.py:621
  39.5 1.0 %copy-start.1 = (bf16[2,256,1024]{2,1,0:T(8,128)(2,1)}, bf16[2,256,1024]{2,1,0:T(8,128)(2,1)S(1)}, u32[]{:S(2)}) copy-start(bf16[2,256,1024]{2,1,0:T(8,128)(2,1)S(1)} %constant_dynamic-update-slice_fusion.refs_0_) | copy-start | bytes 3145732
  39.5 2.7 %collective-permute-start.6 = (bf16[2,256,1024]{2,1,0:T(8,128)(2,1)S(1)}, bf16[2,256,1024]{2,1,0:T(8,128)(2,1)S(1)}, u32[]{:S(2)}, u32[]{:S(2)}) collective-permute-start(bf16[2,256,1024]{2,1,0:T(8,128)(2,1)S(1)} %constant_dynamic-update-slice_fusion.refs_0_), channel_id=1, source_target_pairs={{1,0},{0,1},{3,2},{2,3},{5,4},{4,5},{7,6},{6,7},{9,8},{8,9},{11,10... | collective-permute-start | bytes 3145736 | tf_op jit(solution)/shard_map/ppermute | solution.py:621
  40.5 3.2 %copy-start = (bf16[2,256,1024]{2,1,0:T(8,128)(2,1)}, bf16[2,256,1024]{2,1,0:T(8,128)(2,1)S(1)}, u32[]{:S(2)}) copy-start(bf16[2,256,1024]{2,1,0:T(8,128)(2,1)S(1)} %constant_dynamic-update-slice_fusion.6.refs_2_) | copy-start | bytes 3145732
  40.5 3.2 %collective-permute-start.11 = (bf16[2,256,1024]{2,1,0:T(8,128)(2,1)S(1)}, bf16[2,256,1024]{2,1,0:T(8,128)(2,1)S(1)}, u32[]{:S(2)}, u32[]{:S(2)}) collective-permute-start(bf16[2,256,1024]{2,1,0:T(8,128)(2,1)S(1)} %constant_dynamic-update-slice_fusion.6.refs_2_), channel_id=1, source_target_pairs={{1,0},{0,1},{3,2},{2,3},{5,4},{4,5},{7,6},{6,7},{9,8},{8,9},{11,10... | collective-permute-start | bytes 3145736 | tf_op jit(solution)/shard_map/ppermute | solution.py:621
  42.2 1.0 %copy-start.2 = (bf16[2,256,1024]{2,1,0:T(8,128)(2,1)}, bf16[2,256,1024]{2,1,0:T(8,128)(2,1)S(1)}, u32[]{:S(2)}) copy-start(bf16[2,256,1024]{2,1,0:T(8,128)(2,1)S(1)} %collective-permute-done.6.refs_1_) | copy-start | bytes 3145732
  43.7 1.0 %copy-start.3 = (bf16[2,256,1024]{2,1,0:T(8,128)(2,1)}, bf16[2,256,1024]{2,1,0:T(8,128)(2,1)S(1)}, u32[]{:S(2)}) copy-start(bf16[2,256,1024]{2,1,0:T(8,128)(2,1)S(1)} %collective-permute-done.11.refs_3_) | copy-start | bytes 3145732
